TPU v7x, 32 devices: a whole 2x2x4 slice. The times are simulated.
32 devices in a mesh: blk: 16 (over z, y, core), rep: 2 (over x).
Axes of the slice: x: 2, y: 2, z: 4, core: 2. Of those that a mesh axis runs over, the one named last changes fastest.
Arguments:
- hidden_in: bfloat16 [2, 2048, 1536], P('rep', 'blk'), may hold values from -12 to 12
- lengths: int32 [32], P('rep'), may hold values from 1 to 128, 2048 in all
- routes: int32 [2, 2048, 8], P('rep', 'blk'), may hold values from 0 to 31, all different within a row; in each aligned block of 128 rows (0 to 127, 128 to 255, ..., all dimensions but the last counted through in order) at most 36 rows name the same one
- route_weights: float32 [2, 2048, 8], P('rep', 'blk'), may hold values from 0.03 to 0.3
- norm_gain: float32 [1536], replicated, may hold values from 0.1 to 1.9
- master: float32 [3, 1536, 16, 1024], P(None, 'blk', None, 'rep'), may hold values from -1 to 1
- unembed: bfloat16 [32768, 1536], P('blk'), may hold values from -0.5 to 0.5
- final_gain: float32 [1536], replicated, may hold values from 0.5 to 1.5
- target_ids: int32 [32], P('rep'), may hold values from 0 to 32767
Outputs:
- hidden_out: bfloat16 [2, 2048, 1536], P('rep', 'blk')
- server_blocks: bfloat16 [3, 1536, 16384], P(None, None, 'blk')
- request_stats: float32 [3, 32], P(None, 'rep')
Inputs may be any that keep to these rules, and one draw needn't show every extreme that they name: `routes`: in the 128 slots of one device no expert is named by more than 36 slots, and in some device one expert is named by exactly 36. The lengths of all 32 prompts sum to 2048 and the longest is exactly 128.
All inputs are finite; a program needn't handle non-finite values. No bound on the sum of `lengths` on one device may be relied on, other than what follows from the above.
Results may differ from a plain program's by a relative error of at most 0.0022.
Values may be sent and summed in bfloat16 or wider, within the bound.
No kernel may reach another device: no remote copies, remote signals or barrier semaphores. Data moves between devices by JAX's collectives and lax.ppermute only.
A program may use at most 128 MiB of HBM per device.

v0:
```python
import jax
import jax.numpy as jnp
from jax import lax
from jax.sharding import PartitionSpec as P

FF = 512
EXPERTS = 32
LEN = 128
CAP = 36


def merged(x, axis, combine):
    everything = jax.tree.map(lambda part: lax.all_gather(part, axis), x)
    initial = jax.tree.map(lambda part: part[0], everything)

    def turn(k, so_far):
        return combine(so_far, jax.tree.map(lambda part: part[k], everything))

    return lax.fori_loop(1, lax.axis_size(axis), turn, initial)


def combine_stats(first, second):
    return (first[0] + second[0], jnp.maximum(first[1], second[1]))


def local(
    hidden_in, lengths, routes, route_weights, norm_gain, master, unembed, final_gain, target_ids
):
    rows_here = hidden_in.shape[1]
    width = hidden_in.shape[2]
    top_count = routes.shape[2]
    blk_count = lax.axis_size("blk")
    rep_count = lax.axis_size("rep")
    blk_index = lax.axis_index("blk")
    unit_count = master.shape[3] * rep_count
    split_ways = max(1, FF // unit_count)
    local_exp = max(1, unit_count // FF)
    group_width = min(unit_count, FF)
    capacity = CAP
    blocks = master.astype(jnp.bfloat16)
    arrived_blocks = lax.all_to_all(blocks, "blk", split_axis=2, concat_axis=1, tiled=True)
    server = lax.all_gather(arrived_blocks, "rep", axis=3, tiled=True)[:, :, 0, :]
    gate_w = server[0].reshape(width, local_exp, group_width)
    up_w = server[1].reshape(width, local_exp, group_width)
    down_w = server[2].reshape(width, local_exp, group_width)
    prompts_here = lengths.shape[0]
    slot_index = blk_index * rows_here + jnp.arange(rows_here, dtype=jnp.int32)
    prompt_of = slot_index // LEN
    position = slot_index % LEN
    prompt_match = prompt_of[:, None] == jnp.arange(prompts_here, dtype=jnp.int32)[None, :]
    row_len = jnp.sum(jnp.where(prompt_match, lengths[None, :], 0), axis=1)
    is_valid = position < row_len
    resid_f = hidden_in[0].astype(jnp.float32)
    normed = (
        resid_f * lax.rsqrt(jnp.mean(resid_f * resid_f, axis=-1, keepdims=True) + 1e-05) * norm_gain
    ).astype(jnp.bfloat16)
    expert_ids = routes[0].reshape(-1)
    pair_live = jnp.repeat(is_valid, top_count)
    pair_row = jnp.repeat(jnp.arange(rows_here, dtype=jnp.int32), top_count)
    expert_hits = (
        (expert_ids[:, None] == jnp.arange(EXPERTS, dtype=jnp.int32)[None, :]) & pair_live[:, None]
    ).astype(jnp.int32)
    slot_rank = jnp.sum((jnp.cumsum(expert_hits, axis=0) - 1) * expert_hits, axis=1)
    slot_id = jnp.where(pair_live, expert_ids * capacity + slot_rank, EXPERTS * capacity)
    source_row = jnp.zeros((EXPERTS * capacity + 1,), jnp.int32).at[slot_id].set(pair_row)[:-1]
    filled = jnp.zeros((EXPERTS * capacity + 1,), jnp.bfloat16).at[slot_id].set(1.0)[:-1]
    outgoing = (normed[source_row] * filled[:, None]).reshape(EXPERTS, capacity, width)
    sending = jnp.repeat(outgoing, split_ways, axis=0).reshape(
        blk_count, local_exp, capacity, width
    )
    arrived = lax.all_to_all(sending, "blk", split_axis=0, concat_axis=0, tiled=True)
    sources = arrived.shape[0]
    slot_count = arrived.shape[2]
    stride = sources
    while stride % 2 == 0 and stride * local_exp * slot_count > 1024:
        stride = stride // 2
    grouped = arrived.reshape(sources // stride, stride, local_exp, slot_count, width)

    def one_block(portion):
        gate_out = jnp.einsum("slnd,dlf->slnf", portion, gate_w, preferred_element_type=jnp.float32)
        up_out = jnp.einsum("slnd,dlf->slnf", portion, up_w, preferred_element_type=jnp.float32)
        hidden = (jax.nn.silu(gate_out) * up_out).astype(jnp.bfloat16)
        return jnp.einsum(
            "slnf,dlf->slnd", hidden, down_w, preferred_element_type=jnp.float32
        ).astype(jnp.bfloat16)

    returned = lax.all_to_all(
        lax.map(one_block, grouped).reshape(sources, local_exp, slot_count, width),
        "blk",
        split_axis=0,
        concat_axis=0,
        tiled=True,
    )
    summed_f = jnp.sum(
        returned.reshape(EXPERTS, split_ways, capacity, width).astype(jnp.float32), axis=1
    )
    expert_out = lax.optimization_barrier(summed_f.astype(jnp.bfloat16)).reshape(
        EXPERTS * capacity, width
    )
    gather_index = jnp.where(pair_live, expert_ids * capacity + slot_rank, 0)
    pair_weight = route_weights[0].reshape(-1) * pair_live.astype(jnp.float32)
    moe = jnp.sum(
        (expert_out[gather_index].astype(jnp.float32) * pair_weight[:, None]).reshape(
            rows_here, top_count, width
        ),
        axis=1,
    )
    out_rows = (resid_f + moe).astype(jnp.bfloat16)
    out_f = out_rows.astype(jnp.float32)
    row_squares = jnp.sum(out_f * out_f, axis=-1) * is_valid.astype(jnp.float32)
    square_local = jnp.sum(jnp.where(prompt_match, row_squares[:, None], 0.0), axis=0)
    is_last = is_valid & (position == row_len - 1)
    picker = (prompt_match & is_last[:, None]).astype(jnp.bfloat16)
    last_local = lax.dot_general(
        picker, out_rows, (((0,), (0,)), ((), ())), preferred_element_type=jnp.float32
    )
    last_rows, square_total = lax.psum((last_local, square_local), "blk")
    norms = jnp.sqrt(square_total / (lengths.astype(jnp.float32) * width) + 1e-06)
    final = (
        last_rows
        * lax.rsqrt(jnp.mean(last_rows * last_rows, axis=-1, keepdims=True) + 1e-05)
        * final_gain
    ).astype(jnp.bfloat16)
    logits = lax.dot_general(
        final, unembed, (((1,), (1,)), ((), ())), preferred_element_type=jnp.float32
    )
    vocab_base = blk_index * unembed.shape[0]
    target_hit = (
        target_ids[:, None] == vocab_base + jnp.arange(unembed.shape[0], dtype=jnp.int32)[None, :]
    )
    target_part = jnp.sum(jnp.where(target_hit, logits, 0.0), axis=1)
    top_part = jnp.max(logits, axis=1)
    target_logit, top_logit = merged((target_part, top_part), "blk", combine_stats)
    request_stats = jnp.stack([norms, top_logit, target_logit])
    return (out_rows[None], server, request_stats)


def solution(mesh):
    return jax.shard_map(
        local,
        mesh=mesh,
        in_specs=(
            P("rep", "blk", None),
            P("rep"),
            P("rep", "blk", None),
            P("rep", "blk", None),
            P(),
            P(None, "blk", None, "rep"),
            P("blk", None),
            P(),
            P("rep"),
        ),
        out_specs=(P("rep", "blk", None), P(None, None, "blk"), P(None, "rep")),
        check_vma=False,
    )
```

profile of v0, /device:TPU:0, one launch (start us, length us, event | category | flops | bytes accessed | tf_op | source)
XLA Modules:
  0.0 575.1 jit_solution(4345030745036477090)
XLA Ops:
  7.2 8.7 %copy.153 = bf16[3,96,16,512]{3,1,0,2:T(8,128)(2,1)S(1)} copy(f32[3,96,16,512]{3,2,1,0:T(8,128)} %param.18) | data formatting | bytes 14155776 | tf_op args[5]
  15.9 110.7 %all_to_all.28 = bf16[3,96,16,512]{3,1,0,2:T(8,128)(2,1)S(1)} all-to-all(bf16[3,96,16,512]{3,1,0,2:T(8,128)(2,1)S(1)} %copy.153), channel_id=1, replica_groups=mesh['blk'=16,'rep'=2] {'blk'}, dimensions={2} | all-to-all | bytes 9437184 | tf_op jit(solution)/shard_map/all_to_all | solution.py:41
  126.6 2.5 copy.116
  129.1 0.6 copy-done.3
  129.8 0.1 copy.108
  130.3 0.5 compare_and_fusion
  130.9 0.1 and.69
  131.0 0.1 reshape.226
  131.2 0.1 broadcast_in_dim.86
  131.3 9.0 %reduce-window.6 = s32[32,8,128]{2,1,0:T(8,128)S(1)} reduce-window(s32[32,8,128]{2,1,0:T(8,128)S(1)} %fusion.40, s32[]{:T(128)} %constant.110.clone.1), window={size=1x1x128 pad=0_0x0_0x127_0}, to_apply=%region_2.3 | reduce-window | flops 4161536 | bytes 262148 | tf_op jit(solution)/shard_map/reduce-window
  140.4 0.1 copy.111
  140.7 0.1 copy.107
  140.8 0.1 mul.111
  141.2 4.5 scatter_custom_fusion
  145.7 0.2 fusion.31
  145.9 0.2 fusion.33
  146.0 5.3 gather_fusion
  151.4 5.7 gather.9
  157.0 7.6 %scatter_custom_fusion.1 = bf16[1153]{0:T(1024)(128)(2,1)S(1)} fusion(s32[1024]{0:T(1024)S(1)} %bitcast.160, bf16[1024]{0:T(1024)(128)(2,1)S(1)} %broadcast.265, bf16[]{:T(256)} %constant.111.clone.1), kind=kCustom, calls=%fused_computation.77 | custom fusion | bytes 2308 | tf_op jit(solution)/shard_map/scatter | solution.py:66
  164.6 0.1 mul.113
  164.7 2.4 broadcast_multiply_fusion
  167.2 4.5 copy.113
  171.7 5.6 all-to-all-start
  177.3 70.7 %all-gather.4.cloned.1.call-done = bf16[3,1536,1,1024]{3,1,0,2:T(8,128)(2,1)} async-done(((bf16[3,1536,1,512]{3,1,0,2:T(8,128)(2,1)}), bf16[3,1536,1,1024]{3,1,0,2:T(8,128)(2,1)}) %all-gather.4.cloned.1.call-update) | async-done | bytes 9437200 | tf_op jit(solution)/shard_map/all_gather | solution.py:42
  248.0 6.0 %fusion.58 = (bf16[1,1536,1,1024]{3,1,0,2:T(8,128)(2,1)S(1)}, bf16[1,1536,1,1024]{3,1,0,2:T(8,128)(2,1)}, bf16[1,1536,1,1024]{3,1,0,2:T(8,128)(2,1)}) fusion(bf16[3,1536,1,1024]{3,1,0,2:T(8,128)(2,1)} %all-gather.4.cloned.1.call-done), kind=kLoop, calls=%fused_computation.94 | loop fusion | bytes 18874368 | tf_op jit(solution)/shard_map/slice | solution.py:45
  254.0 6.2 %reshape_squeeze.13 = bf16[1536,2,512]{2,1,0:T(2,128)(2,1)} reshape(bf16[1,1536,1,1024]{3,1,0,2:T(8,128)(2,1)} %get-tuple-element.244) | data formatting | bytes 6291456 | tf_op jit(solution)/shard_map/reshape;squeeze | solution.py:43
  260.2 4.1 copy.118
  264.3 6.2 %reshape_squeeze.14 = bf16[1536,2,512]{2,1,0:T(2,128)(2,1)} reshape(bf16[1,1536,1,1024]{3,1,0,2:T(8,128)(2,1)} %get-tuple-element.243) | data formatting | bytes 6291456 | tf_op jit(solution)/shard_map/reshape;squeeze | solution.py:44
  270.5 4.1 copy.119
  274.5 4.0 reshape_squeeze.15
  278.5 4.1 copy.120
  282.6 27.8 %while.27 = (s32[]{:T(128)}, bf16[2,8,2,36,1536]{4,1,0,3,2:T(8,128)(2,1)}, bf16[2,8,2,36,1536]{4,2,3,1,0:T(2,128)(2,1)}, bf16[1536,2,512]{2,0,1:T(8,128)(2,1)}, ...) while((s32[]{:T(128)}, bf16[2,8,2,36,1536]{4,1,0,3,2:T(8,128)(2,1)}, ...), condition=%wide.region_8.9_spmd, body=%wide.region_7.8_spmd.sunk | while | flops 2720563200 | bytes 31261292 | solution.py:88
  282.6 2.7 constant_dynamic-slice_fusion.2
  285.3 3.7 fusion.68
  289.0 5.6 fusion.69
  294.7 1.8 copy_dynamic-update-slice_fusion.2
  296.5 2.7 constant_dynamic-slice_fusion.2
  299.2 3.7 fusion.68
  302.9 5.6 fusion.69
  308.6 1.8 copy_dynamic-update-slice_fusion.2
  310.3 7.4 %copy.122 = bf16[16,2,36,1536]{3,1,2,0:T(2,128)(2,1)} copy(bf16[16,2,36,1536]{3,0,2,1:T(8,128)(2,1)} %bitcast.151) | data formatting | bytes 7077888 | tf_op jit(solution)/shard_map/reshape | solution.py:88
  317.8 5.7 all-to-all-start.2
  323.6 0.7 copy.125
  324.3 1.2 dynamic-slice
  326.1 63.6 %all-to-all-done.2 = bf16[16,2,36,1536]{3,1,2,0:T(2,128)(2,1)S(1)} async-done(((bf16[16,2,36,1536]{3,1,2,0:T(2,128)(2,1)}), bf16[16,2,36,1536]{3,1,2,0:T(2,128)(2,1)S(1)}, u32[]{:S(2)}, u32[]{:S(2)}) %all-to-all-start.2) | async-done | bytes 3538976 | tf_op jit(solution)/shard_map/all_to_all | solution.py:87
  389.7 5.6 copy.123
  395.3 7.0 %reshape.231 = bf16[32,36,1536]{2,0,1:T(8,128)(2,1)S(1)} reshape(bf16[16,2,36,1536]{3,1,0,2:T(2,128)(2,1)} %copy.123) | data formatting | bytes 7077888 | tf_op jit(solution)/shard_map/reshape | solution.py:95
  402.3 3.9 copy.124
  406.2 3.9 reshape.232
  410.1 5.6 gather_fusion.1
  415.7 4.8 fusion.27
  420.5 0.2 multiply_reduce_fusion
  420.7 0.8 fusion.35
  421.5 0.8 fusion.45
  422.4 0.1 select_reduce_fusion.1
  422.5 98.6 %all-reduce.5.cloned.1.call-done = f32[16,1536]{1,0:T(8,128)} async-done(((f32[16,1536]{1,0:T(8,128)}), f32[16,1536]{1,0:T(8,128)}) %all-reduce.5.cloned.1.call-update) | async-done | bytes 98320 | tf_op jit(solution)/shard_map/psum | solution.py:117
  521.1 1.0 multiply_reduce_fusion.1
  522.1 4.7 fusion.57
  526.9 0.2 dynamic-update-slice.1
  527.1 0.2 dynamic-update-slice
  527.3 30.6 %all-reduce.2 = (f32[256]{0:T(256)S(1)}, f32[256]{0:T(256)S(1)}, f32[16]{0:T(128)S(1)}) all-reduce(f32[256]{0:T(256)S(1)} %dynamic-update-slice, f32[256]{0:T(256)S(1)} %dynamic-update-slice.1, f32[16]{0:T(128)S(1)} %select_reduce_fusion.1), channel_id=2, replica_groups=mesh['blk'=16,'rep'=2] {'blk'}, use_global_device_ids=true, to_apply=%add | all-reduce | flops 528 | bytes 4224
  558.0 0.6 while.28
  558.7 0.6 pad_maximum_fusion
  559.3 8.5 %copy.180 = bf16[3,1536,1024]{2,1,0:T(8,128)(2,1)} copy(bf16[3,1536,1024]{2,1,0:T(8,128)(2,1)} %bitcast.149) | data formatting | bytes 18874368
  (87 shorter events, 1.7 us)
Async XLA Ops:
  7.2 240.8 %all-gather.4.cloned.1.call-start = ((), (), s32[]{:S(2)}) async-start(), calls=%async_computation.3 | async-start | bytes 14155776 | tf_op jit(solution)/shard_map/all_gather | solution.py:42
  129.1 0.7 copy-start.3
  129.1 1.0 copy-start.13
  129.1 16.6 %copy-start.1 = (bf16[1,128,1536]{2,1,0:T(8,128)(2,1)S(1)}, bf16[1,128,1536]{2,1,0:T(8,128)(2,1)}, u32[]{:S(2)}) copy-start(bf16[1,128,1536]{2,1,0:T(8,128)(2,1)} %param.13) | copy-start | bytes 1179652
  129.1 16.8 %copy-start.4 = (f32[1536]{0:T(1024)S(1)}, f32[1536]{0:T(1024)}, u32[]{:S(2)}) copy-start(f32[1536]{0:T(1024)} %param.17) | copy-start | bytes 18436
  130.1 0.7 copy-start.11
  130.2 0.7 copy-start.6
  171.7 110.9 %all-to-all-start = ((bf16[16,2,36,1536]{3,1,2,0:T(2,128)(2,1)}), bf16[16,2,36,1536]{3,1,2,0:T(2,128)(2,1)}, u32[]{:S(2)}, u32[]{:S(2)}) async-start(bf16[16,2,36,1536]{3,1,2,0:T(2,128)(2,1)} %copy.113), calls=%async_computation | async-start | bytes 7077888 | tf_op jit(solution)/shard_map/all_to_all | solution.py:71
  285.3 3.7 copy-start
  299.2 3.7 copy-start
  317.8 5.8 %copy-start.8 = (f32[1,128,8]{1,2,0:T(8,128)S(1)}, f32[1,128,8]{1,2,0:T(8,128)}, u32[]{:S(2)}) copy-start(f32[1,128,8]{1,2,0:T(8,128)} %param.16) | copy-start | bytes 12292
  317.8 71.9 %all-to-all-start.2 = ((bf16[16,2,36,1536]{3,1,2,0:T(2,128)(2,1)}), bf16[16,2,36,1536]{3,1,2,0:T(2,128)(2,1)S(1)}, u32[]{:S(2)}, u32[]{:S(2)}) async-start(bf16[16,2,36,1536]{3,1,2,0:T(2,128)(2,1)} %copy.122), calls=%async_computation.2 | async-start | bytes 7077888 | tf_op jit(solution)/shard_map/all_to_all | solution.py:87
  323.5 197.6 %all-reduce.5.cloned.1.call-start = ((), (), s32[]{:S(2)}) async-start(), calls=%async_computation.4 | async-start | bytes 196608 | tf_op jit(solution)/shard_map/psum | solution.py:117
  415.7 4.8 copy-start.2
  415.7 5.8 %copy-start.9 = (pred[128]{0:T(512)(128)(4,1)S(1)}, pred[128]{0:T(512)(128)(4,1)}, u32[]{:S(2)}) copy-start(pred[128]{0:T(512)(128)(4,1)} %get-tuple-element.247) | copy-start | bytes 388
  415.7 5.9 %copy-start.12 = (s32[128]{0:T(128)S(1)}, s32[128]{0:T(128)}, u32[]{:S(2)}) copy-start(s32[128]{0:T(128)} %copy-done.11) | copy-start | bytes 1540
  415.7 6.7 %copy-start.7 = (s32[128]{0:T(128)S(1)}, s32[128]{0:T(128)}, u32[]{:S(2)}) copy-start(s32[128]{0:T(128)} %copy-done.6) | copy-start | bytes 1540
  415.7 106.5 %copy-start.5 = (f32[1536]{0:T(1024)S(1)}, f32[1536]{0:T(1024)}, u32[]{:S(2)}) copy-start(f32[1536]{0:T(1024)} %param.20) | copy-start | bytes 18436
  415.7 106.4 %copy-start.10 = (s32[16]{0:T(128)S(1)}, s32[16]{0:T(128)}, u32[]{:S(2)}) copy-start(s32[16]{0:T(128)} %param.21) | copy-start | bytes 196
  522.1 36.5 %copy-start.14 = (s32[16]{0:T(128)S(1)}, s32[16]{0:T(128)}, u32[]{:S(2)}) copy-start(s32[16]{0:T(128)} %param.14) | copy-start | bytes 196
Sparse Core Ops, SparseCore 0:
  129.2 118.6 all-gather.3
  422.5 98.5 all-reduce.4
where the time goes:
time: 582 us; the launch traced here: 575 us
  waiting for transfers between devices  233 us (40%)
  blocking collectives  141 us (24%)
  local copies, waits for them, and re-layouts  129 us (22%)
  matrix products  24.2 us (4%)
  other arithmetic  20.5 us (4%)
  between operations  15.4 us (3%)
  starting transfers between devices  11.4 us (2%)
    all_to_all x1, blocking collectives, local(): lax.all_to_all(blocks, 'blk', split_axis=2, concat_axis=1, tiled=True)  111 us
    psum x1, waiting for transfers between devices, local(): last_rows, square_total = lax.psum((last_local, square_local), 'blk')  98.6 us
    all_gather x1, waiting for transfers between devices, local(): lax.all_gather(arrived_blocks, 'rep', axis=3, tiled=True)[:, :, 0, :]  70.7 us
    all_to_all x1, waiting for transfers between devices, local(): lax.all_to_all(lax.map(one_block, grouped).reshape(sources, local_exp, sl...  63.6 us
    unnamed x1, blocking collectives  30.6 us
    unnamed x36, local copies, waits for them, and re-layouts  19.7 us
    while x3, local copies, waits for them, and re-layouts, local(): lax.map(one_block, grouped).reshape(sources, local_exp, slot_count, width)  12.2 us
  transfers between devices with their start and end apart: 4, of which 3 were waited for; matrix products, arithmetic and copies ran while one was open for 14% of the time, Pallas kernels for 0%

commit v1 on v0

--- a/solution.py
+++ b/solution.py
@@ -1,12 +1,18 @@
+import functools
+
 import jax
 import jax.numpy as jnp
 from jax import lax
+from jax.experimental import pallas as pl
+from jax.experimental.pallas import tpu as pltpu
 from jax.sharding import PartitionSpec as P
 
 FF = 512
 EXPERTS = 32
 LEN = 128
 CAP = 36
+LANES = 128
+VMEM = 56 * 1024 * 1024
 
 
 def merged(x, axis, combine):
@@ -23,7 +29,7 @@
     return (first[0] + second[0], jnp.maximum(first[1], second[1]))
 
 
-def local(
+def general(
     hidden_in, lengths, routes, route_weights, norm_gain, master, unembed, final_gain, target_ids
 ):
     rows_here = hidden_in.shape[1]
@@ -135,6 +141,315 @@
     return (out_rows[None], server, request_stats)
 
 
+def iota(shape, dim):
+    return lax.broadcasted_iota(jnp.int32, shape, dim)
+
+
+def prep_kernel(info, hidden_ref, routes_ref, weights_ref, gain_ref, rows_ref, pieces_ref):
+    rows, width = hidden_ref.shape
+    length = info[3]
+    x = hidden_ref[...].astype(jnp.float32)
+    scale = lax.rsqrt(jnp.mean(x * x, axis=-1, keepdims=True) + 1e-05)
+    rows_ref[:, :width] = (x * scale * gain_ref[...]).astype(jnp.bfloat16)
+    lane = iota((rows, LANES), 1)
+    row = iota((rows, LANES), 0)
+    hit = jnp.zeros((rows, LANES), jnp.float32)
+    weight = jnp.zeros((rows, LANES), jnp.float32)
+    for k in range(routes_ref.shape[1]):
+        named = routes_ref[:, k : k + 1] == lane
+        hit = hit + jnp.where(named, 1.0, 0.0)
+        weight = weight + jnp.where(named, weights_ref[:, k : k + 1], 0.0)
+    live = row < length
+    hit = jnp.where(live, hit, 0.0)
+    weight = jnp.where(live, weight, 0.0)
+    before = jnp.where(iota((rows, rows), 1) < iota((rows, rows), 0), 1.0, 0.0)
+    rank = jnp.dot(
+        before.astype(jnp.bfloat16), hit.astype(jnp.bfloat16), preferred_element_type=jnp.float32
+    )
+    rows_ref[:, width:] = jnp.where(hit > 0.0, rank, -1.0).astype(jnp.bfloat16)
+    for k in range(3):
+        piece = weight.astype(jnp.bfloat16)
+        pieces_ref[k * rows : (k + 1) * rows, :] = piece
+        weight = weight - piece.astype(jnp.float32)
+
+
+def hidden_kernel(groups, info, x_ref, g_own, u_own, g_oth, u_oth, out_ref, picked):
+    step = pl.program_id(0)
+    rows = x_ref.shape[0]
+    width = g_own.shape[0]
+    sources = rows // LEN
+    slots = sources * CAP
+    ranks = x_ref[:, width:].astype(jnp.float32)
+    lane = iota((rows, LANES), 1)
+    source = (iota((rows, 1), 0) // LEN).astype(jnp.float32)
+    slot_lane = iota((rows, slots), 1).astype(jnp.float32)
+    for i in range(2):
+        rank = jnp.sum(jnp.where(lane == info[i], ranks, 0.0), axis=1, keepdims=True)
+        slot = jnp.where(rank >= 0.0, source * CAP + rank, -1.0)
+        one_hot = jnp.where(slot == slot_lane, 1.0, 0.0).astype(jnp.bfloat16)
+        chosen = lax.dot_general(
+            one_hot, x_ref[:, :width], (((0,), (0,)), ((), ())), preferred_element_type=jnp.float32
+        )
+        picked[i, pl.ds(pl.multiple_of(step * slots, slots), slots), :] = chosen.astype(jnp.bfloat16)
+
+    @pl.when(step == groups - 1)
+    def _():
+        column = iota((2 * slots, slots), 1)
+        owner = jnp.zeros_like(column)
+        for s in range(1, sources):
+            owner = owner + jnp.where(column >= s * CAP, 1, 0)
+        for i, (g, u) in enumerate(((g_own, u_own), (g_oth, u_oth))):
+            gate = jnp.dot(picked[i], g[...], preferred_element_type=jnp.float32)
+            up = jnp.dot(picked[i], u[...], preferred_element_type=jnp.float32)
+            hidden = (gate / (1.0 + jnp.exp(-gate)) * up).astype(jnp.bfloat16)
+            place = jnp.where(
+                iota((2 * slots, slots), 0) == column + (owner + i) * CAP, 1.0, 0.0
+            ).astype(jnp.bfloat16)
+            for k in range(groups):
+                placed = jnp.dot(
+                    place, hidden[k * slots : (k + 1) * slots], preferred_element_type=jnp.float32
+                )
+                out_ref[k * 2 * slots : (k + 1) * 2 * slots, i * FF : (i + 1) * FF] = placed.astype(
+                    jnp.bfloat16
+                )
+
+
+def down_kernel(hidden_ref, d_own, d_oth, out_ref):
+    dims = (((1,), (1,)), ((), ()))
+    total = lax.dot_general(
+        hidden_ref[:, :FF], d_own[...], dims, preferred_element_type=jnp.float32
+    ) + lax.dot_general(hidden_ref[:, FF:], d_oth[...], dims, preferred_element_type=jnp.float32)
+    out_ref[...] = total.astype(jnp.bfloat16)
+
+
+def combine_kernel(
+    info, rank_ref, pieces_ref, back_ref, resid_ref, out_ref, last_ref, square_ref, mix, squares
+):
+    step = pl.program_id(0)
+    rows = resid_ref.shape[0]
+    slots = back_ref.shape[0]
+    length = info[3]
+
+    @pl.when(step == 0)
+    def _():
+        expert = iota((LANES, slots), 0)
+        lane = iota((LANES, slots), 1)
+        odd = expert & 1
+        start = (expert - odd + jnp.where(odd == info[2], 0, 1)) * CAP
+        inside = (lane >= start) & (lane < start + CAP)
+        spread = jnp.where(inside, 1.0, 0.0).astype(jnp.bfloat16)
+        within = jnp.sum(jnp.where(inside, lane - start, 0), axis=0, keepdims=True).astype(jnp.float32)
+        rank = jnp.dot(rank_ref[...], spread, preferred_element_type=jnp.float32)
+        match = rank == within
+        for k in range(3):
+            part = jnp.dot(
+                pieces_ref[k * rows : (k + 1) * rows, :], spread, preferred_element_type=jnp.float32
+            )
+            mix[k * rows : (k + 1) * rows, :] = jnp.where(match, part, 0.0).astype(jnp.bfloat16)
+        squares[...] = jnp.zeros_like(squares)
+
+    parts = jnp.dot(mix[...], back_ref[...], preferred_element_type=jnp.float32)
+    moe = parts[2 * rows :] + parts[rows : 2 * rows] + parts[:rows]
+    out = (resid_ref[...].astype(jnp.float32) + moe).astype(jnp.bfloat16)
+    out_ref[...] = out
+    out_f = out.astype(jnp.float32)
+    row = iota(out_f.shape, 0)
+    last_ref[...] = jnp.sum(jnp.where(row == length - 1, out_f, 0.0), axis=0, keepdims=True)
+    squares[...] += jnp.sum(jnp.where(row < length, out_f * out_f, 0.0), axis=0, keepdims=True)
+
+    @pl.when(step == pl.num_programs(0) - 1)
+    def _():
+        square_ref[...] = jnp.broadcast_to(
+            jnp.sum(squares[...], axis=1, keepdims=True), square_ref.shape
+        )
+
+
+def place_kernel(info, *refs):
+    out_ref, sems = refs[-2], refs[-1]
+    copies = []
+    for k in range(3):
+        for i in range(2):
+            half = refs[2 * k + i]
+            column = info[2] if i == 0 else 1 - info[2]
+            target = out_ref.at[k, :, pl.ds(pl.multiple_of(column * FF, FF), FF)]
+            copies.append(pltpu.make_async_copy(half, target, sems.at[2 * k + i]))
+    for copy in copies:
+        copy.start()
+    for copy in copies:
+        copy.wait()
+
+
+def params():
+    return pltpu.CompilerParams(vmem_limit_bytes=VMEM, dimension_semantics=("arbitrary",))
+
+
+def whole(shape):
+    return pl.BlockSpec(shape, lambda *_: tuple(0 for _ in shape))
+
+
+def paired(
+    hidden_in, lengths, routes, route_weights, norm_gain, master, unembed, final_gain, target_ids
+):
+    rows = hidden_in.shape[1]
+    width = hidden_in.shape[2]
+    blk_count = lax.axis_size("blk")
+    blk = lax.axis_index("blk")
+    rep = lax.axis_index("rep")
+    back_rows = 2 * CAP
+    slots = blk_count * back_rows
+    resid = hidden_in[0]
+    info = jnp.stack([2 * blk + rep, 2 * blk + 1 - rep, rep, lengths[blk]]).astype(jnp.int32)
+
+    def moved(k):
+        turned = jnp.transpose(master[k], (1, 0, 2)).astype(jnp.bfloat16)
+        own = lax.all_to_all(turned, "blk", split_axis=0, concat_axis=0, tiled=True)
+        own = own.reshape(width, FF)
+        return own, lax.ppermute(own, "rep", [(0, 1), (1, 0)])
+
+    g_own, g_oth = moved(0)
+    u_own, u_oth = moved(1)
+    d_own, d_oth = moved(2)
+
+    row_ext, pieces = pl.pallas_call(
+        prep_kernel,
+        grid_spec=pltpu.PrefetchScalarGridSpec(
+            num_scalar_prefetch=1,
+            grid=(1,),
+            in_specs=[
+                whole((rows, width)),
+                whole((rows, routes.shape[2])),
+                whole((rows, routes.shape[2])),
+                whole((1, width)),
+            ],
+            out_specs=[whole((rows, width + LANES)), whole((3 * rows, LANES))],
+        ),
+        out_shape=[
+            jax.ShapeDtypeStruct((rows, width + LANES), jnp.bfloat16),
+            jax.ShapeDtypeStruct((3 * rows, LANES), jnp.bfloat16),
+        ],
+        compiler_params=params(),
+        name="prep",
+    )(info, resid, routes[0], route_weights[0], norm_gain[None])
+    tokens = lax.all_gather(row_ext, "blk", axis=0, tiled=True)
+
+    groups = 4 if blk_count % 4 == 0 else 1
+    group_rows = blk_count // groups * rows
+    hidden = pl.pallas_call(
+        functools.partial(hidden_kernel, groups),
+        grid_spec=pltpu.PrefetchScalarGridSpec(
+            num_scalar_prefetch=1,
+            grid=(groups,),
+            in_specs=[pl.BlockSpec((group_rows, width + LANES), lambda i, *_: (i, 0))]
+            + [whole((width, FF))] * 4,
+            out_specs=whole((slots, 2 * FF)),
+            scratch_shapes=[pltpu.VMEM((2, slots // 2, width), jnp.bfloat16)],
+        ),
+        out_shape=jax.ShapeDtypeStruct((slots, 2 * FF), jnp.bfloat16),
+        compiler_params=params(),
+        name="gate_up",
+    )(info, tokens, g_own, u_own, g_oth, u_oth)
+
+    step = 512
+    outputs = pl.pallas_call(
+        down_kernel,
+        grid=(width // step,),
+        in_specs=[
+            whole((slots, 2 * FF)),
+            pl.BlockSpec((step, FF), lambda i: (i, 0)),
+            pl.BlockSpec((step, FF), lambda i: (i, 0)),
+        ],
+        out_specs=pl.BlockSpec((slots, step), lambda i: (0, i)),
+        out_shape=jax.ShapeDtypeStruct((slots, width), jnp.bfloat16),
+        compiler_params=params(),
+        name="down",
+    )(hidden, d_own, d_oth)
+    back = lax.all_to_all(
+        outputs.reshape(blk_count, back_rows, width), "blk", split_axis=0, concat_axis=0, tiled=True
+    ).reshape(slots, width)
+
+    server = pl.pallas_call(
+        place_kernel,
+        grid_spec=pltpu.PrefetchScalarGridSpec(
+            num_scalar_prefetch=1,
+            grid=(1,),
+            in_specs=[pl.BlockSpec(memory_space=pl.ANY)] * 6,
+            out_specs=pl.BlockSpec(memory_space=pl.ANY),
+            scratch_shapes=[pltpu.SemaphoreType.DMA((6,))],
+        ),
+        out_shape=jax.ShapeDtypeStruct((3, width, 2 * FF), jnp.bfloat16),
+        compiler_params=params(),
+        name="place",
+    )(info, g_own, g_oth, u_own, u_oth, d_own, d_oth)
+
+    out_rows, last, square = pl.pallas_call(
+        combine_kernel,
+        grid_spec=pltpu.PrefetchScalarGridSpec(
+            num_scalar_prefetch=1,
+            grid=(width // step,),
+            in_specs=[
+                pl.BlockSpec((rows, LANES), lambda i, *_: (0, width // LANES)),
+                whole((3 * rows, LANES)),
+                pl.BlockSpec((slots, step), lambda i, *_: (0, i)),
+                pl.BlockSpec((rows, step), lambda i, *_: (0, i)),
+            ],
+            out_specs=[
+                pl.BlockSpec((rows, step), lambda i, *_: (0, i)),
+                pl.BlockSpec((1, step), lambda i, *_: (0, i)),
+                whole((1, LANES)),
+            ],
+            scratch_shapes=[
+                pltpu.VMEM((3 * rows, slots), jnp.bfloat16),
+                pltpu.VMEM((1, step), jnp.float32),
+            ],
+        ),
+        out_shape=[
+            jax.ShapeDtypeStruct((rows, width), jnp.bfloat16),
+            jax.ShapeDtypeStruct((1, width), jnp.float32),
+            jax.ShapeDtypeStruct((1, LANES), jnp.float32),
+        ],
+        compiler_params=params(),
+        name="combine",
+    )(info, row_ext, pieces, back, resid)
+
+    def everywhere(x):
+        copies = jnp.broadcast_to(x[None], (blk_count,) + x.shape)
+        return lax.all_to_all(copies, "blk", split_axis=0, concat_axis=0, tiled=True)
+
+    gathered = everywhere(jnp.concatenate([last, square], axis=1))[:, 0]
+    last_rows, square_total = gathered[:, :width], gathered[:, width]
+    norms = jnp.sqrt(square_total / (lengths.astype(jnp.float32) * width) + 1e-06)
+    final = (
+        last_rows
+        * lax.rsqrt(jnp.mean(last_rows * last_rows, axis=-1, keepdims=True) + 1e-05)
+        * final_gain
+    ).astype(jnp.bfloat16)
+    logits = lax.dot_general(
+        final, unembed, (((1,), (1,)), ((), ())), preferred_element_type=jnp.float32
+    )
+    vocab_base = blk * unembed.shape[0]
+    target_hit = (
+        target_ids[:, None] == vocab_base + jnp.arange(unembed.shape[0], dtype=jnp.int32)[None, :]
+    )
+    target_part = jnp.sum(jnp.where(target_hit, logits, 0.0), axis=1)
+    top_part = jnp.max(logits, axis=1)
+    parts = everywhere(jnp.stack([top_part, target_part]))
+    request_stats = jnp.stack([norms, jnp.max(parts[:, 0], axis=0), jnp.sum(parts[:, 1], axis=0)])
+    return (out_rows[None], server, request_stats)
+
+
+def local(hidden_in, lengths, routes, route_weights, norm_gain, master, *rest):
+    blk_count = lax.axis_size("blk")
+    fits = (
+        lax.axis_size("rep") == 2
+        and master.shape[3] == FF
+        and EXPERTS == 2 * blk_count
+        and hidden_in.shape[1] == LEN
+        and lengths.shape[0] == blk_count
+    )
+    form = paired if fits else general
+    return form(hidden_in, lengths, routes, route_weights, norm_gain, master, *rest)
+
+
 def solution(mesh):
     return jax.shard_map(
         local,

time: 582 us -> 670 us (1.15)
  Pallas kernels: 0 us -> 318 us
  waiting for transfers between devices: 233 us -> 93.3 us
  local copies, waits for them, and re-layouts: 129 us -> 17.2 us
  blocking collectives: 141 us -> 199 us
  matrix products: 24.2 us -> 4.64 us
  other arithmetic: 20.5 us -> 2.74 us
  starting transfers between devices: 11.4 us -> 19.4 us
    pallas_call x0 -> x5, Pallas kernels: none -> 318 us  [the longest x1 288 us: paired(): pl.pallas_call(place_kernel, grid_spec=pltpu.PrefetchScalarGridSpec(num_s...]
    psum x1 -> x0, waiting for transfers between devices: 98.6 us -> none  [local(): last_rows, square_total = lax.psum((last_local, square_local), 'blk')]
    all_to_all x1 -> x3, blocking collectives: 111 us -> 199 us  [the longest x2 115 us: moved(): own = lax.all_to_all(turned, 'blk', split_axis=0, concat_axis=0, tiled=True)]
    all_gather x1, waiting for transfers between devices: 70.7 us -> 0.01 us  [paired(): tokens = lax.all_gather(row_ext, 'blk', axis=0, tiled=True)]
    ppermute x0 -> x3, waiting for transfers between devices: none -> 56.9 us  [moved(): return (own, lax.ppermute(own, 'rep', [(0, 1), (1, 0)]))]
    unnamed x1 -> x0, blocking collectives: 30.6 us -> none
    all_to_all x2 -> x3, waiting for transfers between devices: 63.6 us -> 36.4 us  [the longest x1 29.9 us: moved(): own = lax.all_to_all(turned, 'blk', split_axis=0, concat_axis=0, tiled=True)]
    dot_general x6 -> x1, matrix products: 24.2 us -> 4.64 us  [paired(): lax.dot_general(final, unembed, (((1,), (1,)), ((), ())), preferred_eleme...]
  transfers between devices with their start and end apart: 4 -> 7, of which waited for: 3 -> 5; matrix products, arithmetic and copies ran while one was open for 14% -> 2% of each run, Pallas kernels for 0% -> 45%
where the time goes in v1:
time: 670 us; the launch traced here: 669 us
  Pallas kernels  318 us (47%)
  blocking collectives  199 us (30%)
  waiting for transfers between devices  93.3 us (14%)
  starting transfers between devices  19.4 us (3%)
  local copies, waits for them, and re-layouts  17.2 us (3%)
  between operations  14.2 us (2%)
    pallas_call x1, Pallas kernels, paired(): pl.pallas_call(place_kernel, grid_spec=pltpu.PrefetchScalarGridSpec(num_s...  288 us
    all_to_all x2, blocking collectives, moved(): own = lax.all_to_all(turned, 'blk', split_axis=0, concat_axis=0, tiled=True)  115 us
    all_to_all x1, blocking collectives, paired(): lax.all_to_all(outputs.reshape(blk_count, back_rows, width), 'blk', split...  84.6 us
    ppermute x3, waiting for transfers between devices, moved(): return (own, lax.ppermute(own, 'rep', [(0, 1), (1, 0)]))  56.9 us
    all_to_all x1, waiting for transfers between devices, moved(): own = lax.all_to_all(turned, 'blk', split_axis=0, concat_axis=0, tiled=True)  29.9 us
    pallas_call x1, Pallas kernels, paired(): pl.pallas_call(functools.partial(hidden_kernel, groups), grid_spec=pltpu....  13.9 us
  transfers between devices with their start and end apart: 7, of which 5 were waited for; matrix products, arithmetic and copies ran while one was open for 2% of the time, Pallas kernels for 45%

profile of v1, /device:TPU:0, one launch (start us, length us, event | category | flops | bytes accessed | tf_op | source)
XLA Modules:
  0.0 669.2 jit_solution(2225602634419526441)
XLA Ops:
  7.2 0.0 all-gather.2.cloned.1.call-start
  7.2 1.4 copy.26
  8.6 1.4 copy.27
  10.1 1.3 broadcast_in_dim.14.gain_ref
  11.3 1.2 dynamic_slice.3
  12.6 1.2 pad_add_fusion.info
  13.8 3.0 prep.1
  16.8 0.0 all-gather.2.cloned.1.call-update
  16.8 8.7 %copy.34 = bf16[3,96,16,512]{3,1,2,0:T(8,128)(2,1)S(1)} copy(f32[3,96,16,512]{3,2,1,0:T(8,128)} %param.14) | data formatting | bytes 14155776 | tf_op args[5]
  25.5 1.7 slice_bitcast_fusion
  27.2 69.8 %all_to_all.30 = bf16[16,96,512]{2,1,0:T(8,128)(2,1)S(1)} all-to-all(bf16[16,96,512]{2,1,0:T(8,128)(2,1)S(1)} %get-tuple-element.17), channel_id=1, replica_groups=mesh['blk'=16,'rep'=2] {'blk'}, dimensions={0} | all-to-all | bytes 3145728 | tf_op jit(solution)/shard_map/all_to_all | solution.py:305
  97.1 0.0 copy-start
  97.1 44.9 %all_to_all.31 = bf16[16,96,512]{2,1,0:T(8,128)(2,1)S(1)} all-to-all(bf16[16,96,512]{2,1,0:T(8,128)(2,1)S(1)} %get-tuple-element.16), channel_id=1, replica_groups=mesh['blk'=16,'rep'=2] {'blk'}, dimensions={0} | all-to-all | bytes 3145728 | tf_op jit(solution)/shard_map/all_to_all | solution.py:305
  142.0 0.0 copy-start.1
  142.0 5.1 all-to-all-start.2
  147.1 0.0 copy-done
  147.1 1.5 collective-permute-start
  148.6 0.6 collective-permute-start.1
  149.2 29.9 %all-to-all-done.2 = bf16[16,96,512]{2,1,0:T(8,128)(2,1)} async-done(((bf16[16,96,512]{2,1,0:T(8,128)(2,1)}), bf16[16,96,512]{2,1,0:T(8,128)(2,1)}, u32[]{:S(2)}, u32[]{:S(2)}) %all-to-all-start.2) | async-done | bytes 1572896 | tf_op jit(solution)/shard_map/all_to_all | solution.py:305
  179.1 1.5 collective-permute-start.2
  180.6 3.9 collective-permute-done.g_oth.refs_1_
  184.5 33.7 %collective-permute-done.1.u_oth.refs_3_ = bf16[1536,512]{1,0:T(8,128)(2,1)} collective-permute-done((bf16[1536,512]{1,0:T(8,128)(2,1)S(1)}, bf16[1536,512]{1,0:T(8,128)(2,1)}, u32[]{:S(2)}, u32[]{:S(2)}) %collective-permute-start.1) | collective-permute-done | bytes 1572896 | tf_op jit(solution)/shard_map/ppermute | solution.py:307
  218.2 0.0 all-gather.2.cloned.1.call-done.x_ref
  218.2 0.0 copy-done.1
  218.2 13.9 %gate_up.1.hidden_ref = bf16[1152,1024]{1,0:T(8,128)(2,1)} custom-call(s32[4]{0:T(128)} %pad_add_fusion.info, bf16[2048,1664]{1,0:T(8,128)(2,1)} %all-gather.2.cloned.1.call-done.x_ref, bf16[1536,512]{1,0:T(8,128)(2,1)} %bitcast.39, bf16[1536,512]{1,0:T(8,128)(2,1)} %bitcast.42, bf16[1536,512]{1,0:T(8,128)(2,1)} %collective-permute-done.g_oth.refs_1_, ...), custom_call_target="tpu_custom_call" | custom-call | tf_op jit(solution)/shard_map/gate_up/pallas_call | solution.py:337
  232.1 19.3 %collective-permute-done.2.d_oth.refs_5_ = bf16[1536,512]{1,0:T(8,128)(2,1)} collective-permute-done((bf16[1536,512]{1,0:T(8,128)(2,1)}, bf16[1536,512]{1,0:T(8,128)(2,1)}, u32[]{:S(2)}, u32[]{:S(2)}) %collective-permute-start.2) | collective-permute-done | bytes 1572896 | tf_op jit(solution)/shard_map/ppermute | solution.py:307
  251.3 7.5 %down.1 = bf16[1152,1536]{1,0:T(8,128)(2,1)} custom-call(bf16[1152,1024]{1,0:T(8,128)(2,1)} %gate_up.1.hidden_ref, bf16[1536,512]{1,0:T(8,128)(2,1)} %bitcast.14.d_own.refs_4_, bf16[1536,512]{1,0:T(8,128)(2,1)} %collective-permute-done.2.d_oth.refs_5_), custom_call_target="tpu_custom_call" | custom-call | tf_op jit(solution)/shard_map/down/pallas_call | solution.py:353
  258.8 84.6 %all_to_all.32 = bf16[16,72,1536]{2,1,0:T(8,128)(2,1)} all-to-all(bf16[16,72,1536]{2,1,0:T(8,128)(2,1)} %bitcast.37), channel_id=1, replica_groups=mesh['blk'=16,'rep'=2] {'blk'}, dimensions={0} | all-to-all | bytes 7077888 | tf_op jit(solution)/shard_map/all_to_all | solution.py:366
  343.4 6.2 combine.1
  349.6 0.7 maximum_reduce_fusion
  350.3 0.7 broadcast_in_dim.31
  351.0 4.7 all-to-all-start.4
  355.7 0.0 copy-start.2
  355.7 0.0 copy-start.3
  355.7 287.8 %place.1 = bf16[3,1536,1024]{2,1,0:T(8,128)(2,1)} custom-call(s32[4]{0:T(128)} %pad_add_fusion.info, bf16[1536,512]{1,0:T(8,128)(2,1)} %bitcast.40, bf16[1536,512]{1,0:T(8,128)(2,1)} %collective-permute-done.g_oth.refs_1_, bf16[1536,512]{1,0:T(8,128)(2,1)} %bitcast.43, bf16[1536,512]{1,0:T(8,128)(2,1)} %collective-permute-done.1.u_oth.refs_3_, ...), custom_call_target="tpu_custom_call" | custom-call | tf_op jit(solution)/shard_map/place/pallas_call | solution.py:370
  643.6 0.0 all-to-all-done.4
  643.6 0.1 multiply_reduce_fusion
  643.7 0.1 slice_reduce_fusion
  643.9 0.0 copy-done.2
  643.9 0.0 copy-done.3
  643.9 0.0 copy-start.4
  643.9 4.6 fusion.3
  648.5 0.6 broadcast_in_dim.33
  649.2 6.0 all-to-all-start.5
  655.2 0.0 copy-done.4
  655.2 6.5 all-to-all-done.5
  661.7 0.6 pad_maximum_fusion
  (8 shorter events, 0.1 us)
Async XLA Ops:
  7.2 211.0 %all-gather.2.cloned.1.call-start = ((), (), s32[]{:S(2)}) async-start(), calls=%async_computation.6 | async-start | bytes 7241728 | tf_op jit(solution)/shard_map/all_gather | solution.py:333
  97.1 50.0 %copy-start = (bf16[16,96,512]{2,1,0:T(8,128)(2,1)}, bf16[16,96,512]{2,1,0:T(8,128)(2,1)S(1)}, u32[]{:S(2)}) copy-start(bf16[16,96,512]{2,1,0:T(8,128)(2,1)S(1)} %all_to_all.30) | copy-start | bytes 4718596
  142.0 76.2 %copy-start.1 = (bf16[16,96,512]{2,1,0:T(8,128)(2,1)}, bf16[16,96,512]{2,1,0:T(8,128)(2,1)S(1)}, u32[]{:S(2)}) copy-start(bf16[16,96,512]{2,1,0:T(8,128)(2,1)S(1)} %all_to_all.31) | copy-start | bytes 4718596
  142.0 37.1 %all-to-all-start.2 = ((bf16[16,96,512]{2,1,0:T(8,128)(2,1)}), bf16[16,96,512]{2,1,0:T(8,128)(2,1)}, u32[]{:S(2)}, u32[]{:S(2)}) async-start(bf16[16,96,512]{2,1,0:T(8,128)(2,1)} %get-tuple-element.15), calls=%async_computation.2 | async-start | bytes 3145728 | tf_op jit(solution)/shard_map/all_to_all | solution.py:305
  147.1 37.4 %collective-permute-start = (bf16[1536,512]{1,0:T(8,128)(2,1)S(1)}, bf16[1536,512]{1,0:T(8,128)(2,1)}, u32[]{:S(2)}, u32[]{:S(2)}) collective-permute-start(bf16[1536,512]{1,0:T(8,128)(2,1)S(1)} %bitcast.38), channel_id=1, source_target_pairs={{0,1},{1,0},{2,3},{3,2},{4,5},{5,4},{6,7},{7,6},{8,9},{9,8},{10,11... | collective-permute-start | bytes 4718600 | tf_op jit(solution)/shard_map/ppermute | solution.py:307
  148.6 69.6 %collective-permute-start.1 = (bf16[1536,512]{1,0:T(8,128)(2,1)S(1)}, bf16[1536,512]{1,0:T(8,128)(2,1)}, u32[]{:S(2)}, u32[]{:S(2)}) collective-permute-start(bf16[1536,512]{1,0:T(8,128)(2,1)S(1)} %bitcast.41), channel_id=1, source_target_pairs={{0,1},{1,0},{2,3},{3,2},{4,5},{5,4},{6,7},{7,6},{8,9},{9,8},{10,11... | collective-permute-start | bytes 4718600 | tf_op jit(solution)/shard_map/ppermute | solution.py:307
  179.1 72.2 %collective-permute-start.2 = (bf16[1536,512]{1,0:T(8,128)(2,1)}, bf16[1536,512]{1,0:T(8,128)(2,1)}, u32[]{:S(2)}, u32[]{:S(2)}) collective-permute-start(bf16[1536,512]{1,0:T(8,128)(2,1)} %bitcast.14.d_own.refs_4_), channel_id=1, source_target_pairs={{0,1},{1,0},{2,3},{3,2},{4,5},{5,4},{6,7},{7,6},{8,9},{9,8},{10,11... | collective-permute-start | bytes 4718600 | tf_op jit(solution)/shard_map/ppermute | solution.py:307
  351.0 292.6 %all-to-all-start.4 = ((f32[16,1,1664]{2,1,0:T(1,128)}), f32[16,1,1664]{2,1,0:T(1,128)S(1)}, u32[]{:S(2)}, u32[]{:S(2)}) async-start(f32[16,1,1664]{2,1,0:T(1,128)} %broadcast_in_dim.31), calls=%async_computation.4 | async-start | bytes 212992 | tf_op jit(solution)/shard_map/all_to_all | solution.py:416
  355.7 288.1 %copy-start.2 = (f32[1536]{0:T(1024)S(1)}, f32[1536]{0:T(1024)}, u32[]{:S(2)}) copy-start(f32[1536]{0:T(1024)} %param.16) | copy-start | bytes 18436
  355.7 288.1 %copy-start.3 = (s32[16]{0:T(128)S(1)}, s32[16]{0:T(128)}, u32[]{:S(2)}) copy-start(s32[16]{0:T(128)} %param.17) | copy-start | bytes 196
  643.9 11.3 %copy-start.4 = (s32[16]{0:T(128)S(1)}, s32[16]{0:T(128)}, u32[]{:S(2)}) copy-start(s32[16]{0:T(128)} %param.10) | copy-start | bytes 196
  649.2 12.5 %all-to-all-start.5 = ((f32[16,2,16]{2,1,0:T(2,128)}), f32[16,2,16]{2,1,0:T(2,128)S(1)}, u32[]{:S(2)}, u32[]{:S(2)}) async-start(f32[16,2,16]{2,1,0:T(2,128)} %broadcast_in_dim.33), calls=%async_computation.5 | async-start | bytes 32768 | tf_op jit(solution)/shard_map/all_to_all | solution.py:416
Sparse Core Ops, SparseCore 0:
  17.0 91.4 all-gather.1

commit v2 on v1

--- a/solution.py
+++ b/solution.py
@@ -223,7 +223,7 @@
 
 
 def combine_kernel(
-    info, rank_ref, pieces_ref, back_ref, resid_ref, out_ref, last_ref, square_ref, mix, squares
+    info, rank_ref, pieces_ref, back_ref, resid_ref, _, out_ref, last_ref, square_ref, mix, squares
 ):
     step = pl.program_id(0)
     rows = resid_ref.shape[0]
@@ -264,19 +264,25 @@
         )
 
 
-def place_kernel(info, *refs):
-    out_ref, sems = refs[-2], refs[-1]
-    copies = []
-    for k in range(3):
-        for i in range(2):
-            half = refs[2 * k + i]
-            column = info[2] if i == 0 else 1 - info[2]
-            target = out_ref.at[k, :, pl.ds(pl.multiple_of(column * FF, FF), FF)]
-            copies.append(pltpu.make_async_copy(half, target, sems.at[2 * k + i]))
-    for copy in copies:
-        copy.start()
-    for copy in copies:
-        copy.wait()
+def place_kernel(info, g_own, g_oth, u_own, u_oth, d_own, d_oth, _, out_ref):
+    for k, (own, oth) in enumerate(((g_own, g_oth), (u_own, u_oth), (d_own, d_oth))):
+
+        @pl.when(info[2] == 0)
+        def _():
+            out_ref[k, :, :FF] = own[...]
+            out_ref[k, :, FF:] = oth[...]
+
+        @pl.when(info[2] != 0)
+        def _():
+            out_ref[k, :, :FF] = oth[...]
+            out_ref[k, :, FF:] = own[...]
+
+
+def cast_kernel(blocks, x_ref, *refs):
+    out_ref = refs[-1]
+    rows = out_ref.shape[1]
+    for b in range(blocks):
+        out_ref[b] = x_ref[pl.ds(b, rows, stride=blocks), :].astype(jnp.bfloat16)
 
 
 def params():
@@ -300,15 +306,27 @@
     resid = hidden_in[0]
     info = jnp.stack([2 * blk + rep, 2 * blk + 1 - rep, rep, lengths[blk]]).astype(jnp.int32)
 
-    def moved(k):
-        turned = jnp.transpose(master[k], (1, 0, 2)).astype(jnp.bfloat16)
+    shard_rows = master.shape[1]
+    flat = master.reshape(3 * shard_rows * blk_count, FF)
+
+    def moved(k, *after):
+        turned = pl.pallas_call(
+            functools.partial(cast_kernel, blk_count),
+            grid=(FF // LANES,),
+            in_specs=[pl.BlockSpec((shard_rows * blk_count, LANES), lambda i: (k, i))]
+            + [pl.BlockSpec(memory_space=pl.ANY)] * len(after),
+            out_specs=pl.BlockSpec((blk_count, shard_rows, LANES), lambda i: (0, 0, i)),
+            out_shape=jax.ShapeDtypeStruct((blk_count, shard_rows, FF), jnp.bfloat16),
+            compiler_params=params(),
+            name="cast",
+        )(flat, *after)
         own = lax.all_to_all(turned, "blk", split_axis=0, concat_axis=0, tiled=True)
         own = own.reshape(width, FF)
         return own, lax.ppermute(own, "rep", [(0, 1), (1, 0)])
 
     g_own, g_oth = moved(0)
     u_own, u_oth = moved(1)
-    d_own, d_oth = moved(2)
+    d_own, d_oth = moved(2, g_oth)
 
     row_ext, pieces = pl.pallas_call(
         prep_kernel,
@@ -367,19 +385,20 @@
         outputs.reshape(blk_count, back_rows, width), "blk", split_axis=0, concat_axis=0, tiled=True
     ).reshape(slots, width)
 
+    part = width // 4
     server = pl.pallas_call(
         place_kernel,
         grid_spec=pltpu.PrefetchScalarGridSpec(
             num_scalar_prefetch=1,
-            grid=(1,),
-            in_specs=[pl.BlockSpec(memory_space=pl.ANY)] * 6,
-            out_specs=pl.BlockSpec(memory_space=pl.ANY),
-            scratch_shapes=[pltpu.SemaphoreType.DMA((6,))],
+            grid=(width // part,),
+            in_specs=[pl.BlockSpec((part, FF), lambda i, *_: (i, 0))] * 6
+            + [pl.BlockSpec(memory_space=pl.ANY)],
+            out_specs=pl.BlockSpec((3, part, 2 * FF), lambda i, *_: (0, i, 0)),
         ),
         out_shape=jax.ShapeDtypeStruct((3, width, 2 * FF), jnp.bfloat16),
         compiler_params=params(),
         name="place",
-    )(info, g_own, g_oth, u_own, u_oth, d_own, d_oth)
+    )(info, g_own, g_oth, u_own, u_oth, d_own, d_oth, outputs)
 
     out_rows, last, square = pl.pallas_call(
         combine_kernel,
@@ -391,6 +410,7 @@
                 whole((3 * rows, LANES)),
                 pl.BlockSpec((slots, step), lambda i, *_: (0, i)),
                 pl.BlockSpec((rows, step), lambda i, *_: (0, i)),
+                pl.BlockSpec(memory_space=pl.ANY),
             ],
             out_specs=[
                 pl.BlockSpec((rows, step), lambda i, *_: (0, i)),
@@ -409,7 +429,7 @@
         ],
         compiler_params=params(),
         name="combine",
-    )(info, row_ext, pieces, back, resid)
+    )(info, row_ext, pieces, back, resid, server)
 
     def everywhere(x):
         copies = jnp.broadcast_to(x[None], (blk_count,) + x.shape)

time: 670 us -> 354 us (0.53)
  Pallas kernels: 318 us -> 52 us
  blocking collectives: 199 us -> 0 us
  waiting for transfers between devices: 93.3 us -> 203 us
  starting transfers between devices: 19.4 us -> 65.3 us
    pallas_call x1, Pallas kernels: 288 us -> 8.27 us  [paired(): pl.pallas_call(place_kernel, grid_spec=pltpu.PrefetchScalarGridSpec(num_s...]
    all_to_all x3 -> x0, blocking collectives: 199 us -> none  [the longest x2 115 us: moved(): own = lax.all_to_all(turned, 'blk', split_axis=0, concat_axis=0, tiled=True)]
    all_to_all x0 -> x1, waiting for transfers between devices: none -> 57.9 us  [paired(): lax.all_to_all(outputs.reshape(blk_count, back_rows, width), 'blk', split...]
    all_to_all x1 -> x3, waiting for transfers between devices: 29.9 us -> 73.5 us  [moved(): own = lax.all_to_all(turned, 'blk', split_axis=0, concat_axis=0, tiled=True)]
    all_to_all x1 -> x3, starting transfers between devices: 5.09 us -> 33 us  [moved(): own = lax.all_to_all(turned, 'blk', split_axis=0, concat_axis=0, tiled=True)]
    pallas_call x0 -> x3, Pallas kernels: none -> 13 us  [moved(): pl.pallas_call(functools.partial(cast_kernel, blk_count), grid=(FF // LAN...]
    all_to_all x2, starting transfers between devices: 10.7 us -> 20.5 us  [everywhere(): lax.all_to_all(copies, 'blk', split_axis=0, concat_axis=0, tiled=True)]
    all_to_all x2, waiting for transfers between devices: 6.47 us -> 14 us  [everywhere(): lax.all_to_all(copies, 'blk', split_axis=0, concat_axis=0, tiled=True)]
  transfers between devices with their start and end apart: 7 -> 10, of which waited for: 5 -> 9; matrix products, arithmetic and copies ran while one was open for 2% -> 0% of each run, Pallas kernels for 45% -> 10%
where the time goes in v2:
time: 354 us; the launch traced here: 352 us
  waiting for transfers between devices  203 us (57%)
  starting transfers between devices  65.3 us (18%)
  Pallas kernels  52 us (15%)
  between operations  14.2 us (4%)
  local copies, waits for them, and re-layouts  10.9 us (3%)
  matrix products  4.64 us (1%)
    all_to_all x3, waiting for transfers between devices, moved(): own = lax.all_to_all(turned, 'blk', split_axis=0, concat_axis=0, tiled=True)  73.5 us
    all_to_all x1, waiting for transfers between devices, paired(): lax.all_to_all(outputs.reshape(blk_count, back_rows, width), 'blk', split...  57.9 us
    ppermute x3, waiting for transfers between devices, moved(): return (own, lax.ppermute(own, 'rep', [(0, 1), (1, 0)]))  57.2 us
    all_to_all x3, starting transfers between devices, moved(): own = lax.all_to_all(turned, 'blk', split_axis=0, concat_axis=0, tiled=True)  33 us
    all_to_all x2, starting transfers between devices, everywhere(): lax.all_to_all(copies, 'blk', split_axis=0, concat_axis=0, tiled=True)  20.5 us
    all_to_all x2, waiting for transfers between devices, everywhere(): lax.all_to_all(copies, 'blk', split_axis=0, concat_axis=0, tiled=True)  14 us
    pallas_call x1, Pallas kernels, paired(): pl.pallas_call(functools.partial(hidden_kernel, groups), grid_spec=pltpu....  13.8 us
    pallas_call x3, Pallas kernels, moved(): pl.pallas_call(functools.partial(cast_kernel, blk_count), grid=(FF // LAN...  13 us
  transfers between devices with their start and end apart: 10, of which 9 were waited for; matrix products, arithmetic and copies ran while one was open for 0% of the time, Pallas kernels for 10%

profile of v2, /device:TPU:0, one launch (start us, length us, event | category | flops | bytes accessed | tf_op | source)
XLA Modules:
  0.0 352.4 jit_solution(2380488735321500184)
XLA Ops:
  7.2 0.0 all-gather.2.cloned.1.call-start
  7.2 1.4 copy.20
  8.6 1.4 copy.21
  10.1 1.3 broadcast_in_dim.14.gain_ref
  11.3 1.2 dynamic_slice.3
  12.6 1.2 pad_add_fusion.info
  13.8 3.0 prep.1
  16.9 0.0 all-gather.2.cloned.1.call-update
  16.9 4.3 %cast.3 = bf16[16,96,512]{2,1,0:T(8,128)(2,1)} custom-call(f32[4608,512]{1,0:T(8,128)} %bitcast.25), custom_call_target="tpu_custom_call" | custom-call | tf_op jit(solution)/shard_map/cast/pallas_call | solution.py:313
  21.2 7.4 %all-to-all-start = ((bf16[16,96,512]{2,1,0:T(8,128)(2,1)}), bf16[16,96,512]{2,1,0:T(8,128)(2,1)S(1)}, u32[]{:S(2)}, u32[]{:S(2)}) async-start(bf16[16,96,512]{2,1,0:T(8,128)(2,1)} %cast.3), calls=%async_computation | async-start | bytes 3145728 | tf_op jit(solution)/shard_map/all_to_all | solution.py:323
  28.6 4.4 %cast.4 = bf16[16,96,512]{2,1,0:T(8,128)(2,1)} custom-call(f32[4608,512]{1,0:T(8,128)} %bitcast.26), custom_call_target="tpu_custom_call" | custom-call | tf_op jit(solution)/shard_map/cast/pallas_call | solution.py:313
  33.0 40.7 %all-to-all-done = bf16[16,96,512]{2,1,0:T(8,128)(2,1)S(1)} async-done(((bf16[16,96,512]{2,1,0:T(8,128)(2,1)}), bf16[16,96,512]{2,1,0:T(8,128)(2,1)S(1)}, u32[]{:S(2)}, u32[]{:S(2)}) %all-to-all-start) | async-done | bytes 1572896 | tf_op jit(solution)/shard_map/all_to_all | solution.py:323
  73.7 0.0 copy-start.1
  73.7 16.7 %all-to-all-start.1 = ((bf16[16,96,512]{2,1,0:T(8,128)(2,1)}), bf16[16,96,512]{2,1,0:T(8,128)(2,1)}, u32[]{:S(2)}, u32[]{:S(2)}) async-start(bf16[16,96,512]{2,1,0:T(8,128)(2,1)} %cast.4), calls=%async_computation.1 | async-start | bytes 3145728 | tf_op jit(solution)/shard_map/all_to_all | solution.py:323
  90.3 1.7 collective-permute-start
  92.0 35.0 %collective-permute-done.g_oth.refs_0_ = bf16[1536,512]{1,0:T(8,128)(2,1)S(1)} collective-permute-done((bf16[1536,512]{1,0:T(8,128)(2,1)S(1)}, bf16[1536,512]{1,0:T(8,128)(2,1)S(1)}, u32[]{:S(2)}, u32[]{:S(2)}) %collective-permute-start) | collective-permute-done | bytes 1572896 | tf_op jit(solution)/shard_map/ppermute | solution.py:325
  127.0 0.0 copy-start
  127.0 1.1 copy-done
  128.1 4.3 %cast.5 = bf16[16,96,512]{2,1,0:T(8,128)(2,1)} custom-call(f32[4608,512]{1,0:T(8,128)} %bitcast.27, bf16[1536,512]{1,0:T(8,128)(2,1)} %copy-done), custom_call_target="tpu_custom_call" | custom-call | tf_op jit(solution)/shard_map/cast/pallas_call | solution.py:313
  132.4 0.0 copy-done.1
  132.4 2.4 all-to-all-done.1
  134.8 8.9 %all-to-all-start.2 = ((bf16[16,96,512]{2,1,0:T(8,128)(2,1)}), bf16[16,96,512]{2,1,0:T(8,128)(2,1)S(1)}, u32[]{:S(2)}, u32[]{:S(2)}) async-start(bf16[16,96,512]{2,1,0:T(8,128)(2,1)} %cast.5), calls=%async_computation.2 | async-start | bytes 3145728 | tf_op jit(solution)/shard_map/all_to_all | solution.py:323
  143.8 1.6 collective-permute-start.1
  145.3 30.4 %all-to-all-done.2 = bf16[16,96,512]{2,1,0:T(8,128)(2,1)S(1)} async-done(((bf16[16,96,512]{2,1,0:T(8,128)(2,1)}), bf16[16,96,512]{2,1,0:T(8,128)(2,1)S(1)}, u32[]{:S(2)}, u32[]{:S(2)}) %all-to-all-start.2) | async-done | bytes 1572896 | tf_op jit(solution)/shard_map/all_to_all | solution.py:323
  175.7 0.0 copy-start.3
  175.7 1.5 collective-permute-start.2
  177.2 4.0 %collective-permute-done.1.u_oth = bf16[1536,512]{1,0:T(8,128)(2,1)S(1)} collective-permute-done((bf16[1536,512]{1,0:T(8,128)(2,1)}, bf16[1536,512]{1,0:T(8,128)(2,1)S(1)}, u32[]{:S(2)}, u32[]{:S(2)}) %collective-permute-start.1) | collective-permute-done | bytes 1572896 | tf_op jit(solution)/shard_map/ppermute | solution.py:325
  181.2 0.0 copy-start.4
  181.2 0.0 all-gather.2.cloned.1.call-done.x_ref
  181.2 1.2 copy-done.4
  182.4 13.8 %gate_up.1.hidden_ref = bf16[1152,1024]{1,0:T(8,128)(2,1)} custom-call(s32[4]{0:T(128)} %pad_add_fusion.info, bf16[2048,1664]{1,0:T(8,128)(2,1)} %all-gather.2.cloned.1.call-done.x_ref, bf16[1536,512]{1,0:T(8,128)(2,1)} %bitcast.30, bf16[1536,512]{1,0:T(8,128)(2,1)} %bitcast.8.u_own, bf16[1536,512]{1,0:T(8,128)(2,1)} %copy-done, bf16[1536,512]{1,0:T(8,128)(2,1)} %copy-done.4), custom_call_target="tpu_custom_call" | custom-call | tf_op jit(solution)/shard_map/gate_up/pallas_call | solution.py:355
  196.3 0.0 copy-done.3
  196.3 18.2 %collective-permute-done.2.d_oth = bf16[1536,512]{1,0:T(8,128)(2,1)} collective-permute-done((bf16[1536,512]{1,0:T(8,128)(2,1)S(1)}, bf16[1536,512]{1,0:T(8,128)(2,1)}, u32[]{:S(2)}, u32[]{:S(2)}) %collective-permute-start.2) | collective-permute-done | bytes 1572896 | tf_op jit(solution)/shard_map/ppermute | solution.py:325
  214.5 7.6 %down.1._ = bf16[1152,1536]{1,0:T(8,128)(2,1)} custom-call(bf16[1152,1024]{1,0:T(8,128)(2,1)} %gate_up.1.hidden_ref, bf16[1536,512]{1,0:T(8,128)(2,1)} %bitcast.34, bf16[1536,512]{1,0:T(8,128)(2,1)} %collective-permute-done.2.d_oth), custom_call_target="tpu_custom_call" | custom-call | tf_op jit(solution)/shard_map/down/pallas_call | solution.py:371
  222.1 7.1 %all-to-all-start.3 = ((bf16[16,72,1536]{2,1,0:T(8,128)(2,1)}), bf16[16,72,1536]{2,1,0:T(8,128)(2,1)S(1)}, u32[]{:S(2)}, u32[]{:S(2)}) async-start(bf16[16,72,1536]{2,1,0:T(8,128)(2,1)} %bitcast.28), calls=%async_computation.3 | async-start | bytes 7077888 | tf_op jit(solution)/shard_map/all_to_all | solution.py:384
  229.1 8.3 %place.1._ = bf16[3,1536,1024]{2,1,0:T(8,128)(2,1)} custom-call(s32[4]{0:T(128)} %pad_add_fusion.info, bf16[1536,512]{1,0:T(8,128)(2,1)} %bitcast.31, bf16[1536,512]{1,0:T(8,128)(2,1)} %copy-done, bf16[1536,512]{1,0:T(8,128)(2,1)} %bitcast.8.u_own, bf16[1536,512]{1,0:T(8,128)(2,1)} %copy-done.4, bf16[1536,512]{1,0:T(8,128)(2,1)} %bitcast.35, ...), custom_call_target="tpu_custom_call" | custom-call | tf_op jit(solution)/shard_map/place/pallas_call | solution.py:389
  237.4 57.9 %all-to-all-done.3 = bf16[16,72,1536]{2,1,0:T(8,128)(2,1)S(1)} async-done(((bf16[16,72,1536]{2,1,0:T(8,128)(2,1)}), bf16[16,72,1536]{2,1,0:T(8,128)(2,1)S(1)}, u32[]{:S(2)}, u32[]{:S(2)}) %all-to-all-start.3) | async-done | bytes 3538976 | tf_op jit(solution)/shard_map/all_to_all | solution.py:384
  295.4 0.0 copy-start.2
  295.4 1.7 copy-done.2
  297.1 0.0 copy-start.5
  297.1 0.0 copy-start.6
  297.1 6.3 %combine.1 = (bf16[128,1536]{1,0:T(8,128)(2,1)}, f32[1,1536]{1,0:T(1,128)}, f32[1,128]{1,0:T(1,128)}) custom-call(s32[4]{0:T(128)} %pad_add_fusion.info, bf16[128,1664]{1,0:T(8,128)(2,1)} %get-tuple-element.8.rank_ref, bf16[384,128]{1,0:T(8,128)(2,1)} %get-tuple-element.9.pieces_ref, bf16[1152,1536]{1,0:T(8,128)(2,1)} %bitcast.32, ...), custom_call_target="tpu_custom_call" | custom-call | tf_op jit(solution)/shard_map/combine/pallas_call | solution.py:403
  303.4 0.7 maximum_reduce_fusion
  304.1 0.7 broadcast_in_dim.31
  304.8 17.0 %all-to-all-start.4 = ((f32[16,1,1664]{2,1,0:T(1,128)}), f32[16,1,1664]{2,1,0:T(1,128)S(1)}, u32[]{:S(2)}, u32[]{:S(2)}) async-start(f32[16,1,1664]{2,1,0:T(1,128)} %broadcast_in_dim.31), calls=%async_computation.4 | async-start | bytes 212992 | tf_op jit(solution)/shard_map/all_to_all | solution.py:436
  321.9 7.5 %all-to-all-done.4 = f32[16,1,1664]{2,1,0:T(1,128)S(1)} async-done(((f32[16,1,1664]{2,1,0:T(1,128)}), f32[16,1,1664]{2,1,0:T(1,128)S(1)}, u32[]{:S(2)}, u32[]{:S(2)}) %all-to-all-start.4) | async-done | bytes 106528 | tf_op jit(solution)/shard_map/all_to_all | solution.py:436
  329.4 0.1 multiply_reduce_fusion
  329.5 0.1 slice_reduce_fusion
  329.6 0.0 copy-done.5
  329.6 0.0 copy-done.6
  329.7 0.0 copy-start.7
  329.7 4.6 %fusion.3 = (f32[16]{0:T(128)S(1)}, f32[16]{0:T(128)S(1)}) fusion(s32[2048]{0:T(1024)S(1)} %iota_add_fusion, s32[16]{0:T(128)S(1)} %copy-done.6, bf16[2048,1536]{1,0:T(8,128)(2,1)} %param.15, f32[16,1664]{1,0:T(8,128)S(1)} %bitcast.40, f32[1536]{0:T(1024)S(1)} %copy-done.5, f32[16]{0:T(128)S(1)} %add_rsqrt_fusion), kind=kOutput, calls=%fused_computation.16 | convolution fusion | flops 100868064 | bytes 6407296 | tf_op jit(solution)/shard_map/dot_general | solution.py:446
  334.3 0.6 broadcast_in_dim.33
  334.9 3.5 all-to-all-start.5
  338.4 0.0 copy-done.7
  338.4 6.4 %all-to-all-done.5 = f32[16,2,16]{2,1,0:T(2,128)S(1)} async-done(((f32[16,2,16]{2,1,0:T(2,128)}), f32[16,2,16]{2,1,0:T(2,128)S(1)}, u32[]{:S(2)}, u32[]{:S(2)}) %all-to-all-start.5) | async-done | bytes 2080 | tf_op jit(solution)/shard_map/all_to_all | solution.py:436
  344.9 0.6 pad_maximum_fusion
  (8 shorter events, 0.1 us)
Async XLA Ops:
  7.2 174.1 %all-gather.2.cloned.1.call-start = ((), (), s32[]{:S(2)}) async-start(), calls=%async_computation.6 | async-start | bytes 7241728 | tf_op jit(solution)/shard_map/all_gather | solution.py:351
  21.2 52.5 %all-to-all-start = ((bf16[16,96,512]{2,1,0:T(8,128)(2,1)}), bf16[16,96,512]{2,1,0:T(8,128)(2,1)S(1)}, u32[]{:S(2)}, u32[]{:S(2)}) async-start(bf16[16,96,512]{2,1,0:T(8,128)(2,1)} %cast.3), calls=%async_computation | async-start | bytes 3145728 | tf_op jit(solution)/shard_map/all_to_all | solution.py:323
  73.7 58.8 %copy-start.1 = (bf16[16,96,512]{2,1,0:T(8,128)(2,1)}, bf16[16,96,512]{2,1,0:T(8,128)(2,1)S(1)}, u32[]{:S(2)}) copy-start(bf16[16,96,512]{2,1,0:T(8,128)(2,1)S(1)} %all-to-all-done) | copy-start | bytes 4718596
  73.7 61.1 %all-to-all-start.1 = ((bf16[16,96,512]{2,1,0:T(8,128)(2,1)}), bf16[16,96,512]{2,1,0:T(8,128)(2,1)}, u32[]{:S(2)}, u32[]{:S(2)}) async-start(bf16[16,96,512]{2,1,0:T(8,128)(2,1)} %cast.4), calls=%async_computation.1 | async-start | bytes 3145728 | tf_op jit(solution)/shard_map/all_to_all | solution.py:323
  90.3 36.7 %collective-permute-start = (bf16[1536,512]{1,0:T(8,128)(2,1)S(1)}, bf16[1536,512]{1,0:T(8,128)(2,1)S(1)}, u32[]{:S(2)}, u32[]{:S(2)}) collective-permute-start(bf16[1536,512]{1,0:T(8,128)(2,1)S(1)} %bitcast.29), channel_id=1, source_target_pairs={{0,1},{1,0},{2,3},{3,2},{4,5},{5,4},{6,7},{7,6},{8,9},{9,8},{10,11... | collective-permute-start | bytes 4718600 | tf_op jit(solution)/shard_map/ppermute | solution.py:325
  127.0 1.1 copy-start
  134.8 40.9 %all-to-all-start.2 = ((bf16[16,96,512]{2,1,0:T(8,128)(2,1)}), bf16[16,96,512]{2,1,0:T(8,128)(2,1)S(1)}, u32[]{:S(2)}, u32[]{:S(2)}) async-start(bf16[16,96,512]{2,1,0:T(8,128)(2,1)} %cast.5), calls=%async_computation.2 | async-start | bytes 3145728 | tf_op jit(solution)/shard_map/all_to_all | solution.py:323
  143.8 37.5 %collective-permute-start.1 = (bf16[1536,512]{1,0:T(8,128)(2,1)}, bf16[1536,512]{1,0:T(8,128)(2,1)S(1)}, u32[]{:S(2)}, u32[]{:S(2)}) collective-permute-start(bf16[1536,512]{1,0:T(8,128)(2,1)} %bitcast.8.u_own), channel_id=1, source_target_pairs={{0,1},{1,0},{2,3},{3,2},{4,5},{5,4},{6,7},{7,6},{8,9},{9,8},{10,11... | collective-permute-start | bytes 4718600 | tf_op jit(solution)/shard_map/ppermute | solution.py:325
  175.7 20.5 %copy-start.3 = (bf16[16,96,512]{2,1,0:T(8,128)(2,1)}, bf16[16,96,512]{2,1,0:T(8,128)(2,1)S(1)}, u32[]{:S(2)}) copy-start(bf16[16,96,512]{2,1,0:T(8,128)(2,1)S(1)} %all-to-all-done.2) | copy-start | bytes 4718596
  175.7 38.8 %collective-permute-start.2 = (bf16[1536,512]{1,0:T(8,128)(2,1)S(1)}, bf16[1536,512]{1,0:T(8,128)(2,1)}, u32[]{:S(2)}, u32[]{:S(2)}) collective-permute-start(bf16[1536,512]{1,0:T(8,128)(2,1)S(1)} %bitcast.33), channel_id=1, source_target_pairs={{0,1},{1,0},{2,3},{3,2},{4,5},{5,4},{6,7},{7,6},{8,9},{9,8},{10,11... | collective-permute-start | bytes 4718600 | tf_op jit(solution)/shard_map/ppermute | solution.py:325
  181.2 1.2 copy-start.4
  222.1 73.3 %all-to-all-start.3 = ((bf16[16,72,1536]{2,1,0:T(8,128)(2,1)}), bf16[16,72,1536]{2,1,0:T(8,128)(2,1)S(1)}, u32[]{:S(2)}, u32[]{:S(2)}) async-start(bf16[16,72,1536]{2,1,0:T(8,128)(2,1)} %bitcast.28), calls=%async_computation.3 | async-start | bytes 7077888 | tf_op jit(solution)/shard_map/all_to_all | solution.py:384
  295.4 1.7 copy-start.2
  297.1 32.5 %copy-start.5 = (f32[1536]{0:T(1024)S(1)}, f32[1536]{0:T(1024)}, u32[]{:S(2)}) copy-start(f32[1536]{0:T(1024)} %param.16) | copy-start | bytes 18436
  297.1 32.5 %copy-start.6 = (s32[16]{0:T(128)S(1)}, s32[16]{0:T(128)}, u32[]{:S(2)}) copy-start(s32[16]{0:T(128)} %param.17) | copy-start | bytes 196
  304.8 24.6 %all-to-all-start.4 = ((f32[16,1,1664]{2,1,0:T(1,128)}), f32[16,1,1664]{2,1,0:T(1,128)S(1)}, u32[]{:S(2)}, u32[]{:S(2)}) async-start(f32[16,1,1664]{2,1,0:T(1,128)} %broadcast_in_dim.31), calls=%async_computation.4 | async-start | bytes 212992 | tf_op jit(solution)/shard_map/all_to_all | solution.py:436
  329.7 8.8 %copy-start.7 = (s32[16]{0:T(128)S(1)}, s32[16]{0:T(128)}, u32[]{:S(2)}) copy-start(s32[16]{0:T(128)} %param.10) | copy-start | bytes 196
  334.9 9.9 %all-to-all-start.5 = ((f32[16,2,16]{2,1,0:T(2,128)}), f32[16,2,16]{2,1,0:T(2,128)S(1)}, u32[]{:S(2)}, u32[]{:S(2)}) async-start(f32[16,2,16]{2,1,0:T(2,128)} %broadcast_in_dim.33), calls=%async_computation.5 | async-start | bytes 32768 | tf_op jit(solution)/shard_map/all_to_all | solution.py:436
Sparse Core Ops, SparseCore 0:
  17.0 115.0 all-gather.1

commit v3 on v2

--- a/solution.py
+++ b/solution.py
@@ -11,6 +11,8 @@
 EXPERTS = 32
 LEN = 128
 CAP = 36
+ROOM = 40
+PLANE = 4
 LANES = 128
 VMEM = 56 * 1024 * 1024
 
@@ -145,7 +147,7 @@
     return lax.broadcasted_iota(jnp.int32, shape, dim)
 
 
-def prep_kernel(info, hidden_ref, routes_ref, weights_ref, gain_ref, rows_ref, pieces_ref):
+def prep_kernel(info, hidden_ref, routes_ref, weights_ref, gain_ref, _, rows_ref, pieces_ref):
     rows, width = hidden_ref.shape
     length = info[3]
     x = hidden_ref[...].astype(jnp.float32)
@@ -173,70 +175,51 @@
         weight = weight - piece.astype(jnp.float32)
 
 
-def hidden_kernel(groups, info, x_ref, g_own, u_own, g_oth, u_oth, out_ref, picked):
+def gate_up_kernel(which, info, x_ref, g_ref, u_ref, out_ref, picked):
     step = pl.program_id(0)
     rows = x_ref.shape[0]
-    width = g_own.shape[0]
+    width = g_ref.shape[0]
     sources = rows // LEN
-    slots = sources * CAP
+    slots = sources * ROOM
     ranks = x_ref[:, width:].astype(jnp.float32)
     lane = iota((rows, LANES), 1)
     source = (iota((rows, 1), 0) // LEN).astype(jnp.float32)
+    rank = jnp.sum(jnp.where(lane == info[which], ranks, 0.0), axis=1, keepdims=True)
+    slot = jnp.where(rank >= 0.0, source * ROOM + rank, -1.0)
     slot_lane = iota((rows, slots), 1).astype(jnp.float32)
-    for i in range(2):
-        rank = jnp.sum(jnp.where(lane == info[i], ranks, 0.0), axis=1, keepdims=True)
-        slot = jnp.where(rank >= 0.0, source * CAP + rank, -1.0)
-        one_hot = jnp.where(slot == slot_lane, 1.0, 0.0).astype(jnp.bfloat16)
-        chosen = lax.dot_general(
-            one_hot, x_ref[:, :width], (((0,), (0,)), ((), ())), preferred_element_type=jnp.float32
-        )
-        picked[i, pl.ds(pl.multiple_of(step * slots, slots), slots), :] = chosen.astype(jnp.bfloat16)
-
-    @pl.when(step == groups - 1)
+    one_hot = jnp.where(slot == slot_lane, 1.0, 0.0).astype(jnp.bfloat16)
+    chosen = lax.dot_general(
+        one_hot, x_ref[:, :width], (((0,), (0,)), ((), ())), preferred_element_type=jnp.float32
+    )
+    for s in range(sources):
+        start = pl.multiple_of((s * PLANE + step) * ROOM, ROOM)
+        picked[pl.ds(start, ROOM), :] = chosen[s * ROOM : (s + 1) * ROOM]
+
+    @pl.when(step == PLANE - 1)
     def _():
-        column = iota((2 * slots, slots), 1)
-        owner = jnp.zeros_like(column)
-        for s in range(1, sources):
-            owner = owner + jnp.where(column >= s * CAP, 1, 0)
-        for i, (g, u) in enumerate(((g_own, u_own), (g_oth, u_oth))):
-            gate = jnp.dot(picked[i], g[...], preferred_element_type=jnp.float32)
-            up = jnp.dot(picked[i], u[...], preferred_element_type=jnp.float32)
-            hidden = (gate / (1.0 + jnp.exp(-gate)) * up).astype(jnp.bfloat16)
-            place = jnp.where(
-                iota((2 * slots, slots), 0) == column + (owner + i) * CAP, 1.0, 0.0
-            ).astype(jnp.bfloat16)
-            for k in range(groups):
-                placed = jnp.dot(
-                    place, hidden[k * slots : (k + 1) * slots], preferred_element_type=jnp.float32
-                )
-                out_ref[k * 2 * slots : (k + 1) * 2 * slots, i * FF : (i + 1) * FF] = placed.astype(
-                    jnp.bfloat16
-                )
-
-
-def down_kernel(hidden_ref, d_own, d_oth, out_ref):
-    dims = (((1,), (1,)), ((), ()))
+        x = picked[...].astype(jnp.bfloat16)
+        gate = jnp.dot(x, g_ref[...], preferred_element_type=jnp.float32)
+        up = jnp.dot(x, u_ref[...], preferred_element_type=jnp.float32)
+        out_ref[...] = (gate / (1.0 + jnp.exp(-gate)) * up).astype(jnp.bfloat16)
+
+
+def down_kernel(hidden_ref, d_ref, out_ref):
     total = lax.dot_general(
-        hidden_ref[:, :FF], d_own[...], dims, preferred_element_type=jnp.float32
-    ) + lax.dot_general(hidden_ref[:, FF:], d_oth[...], dims, preferred_element_type=jnp.float32)
+        hidden_ref[...], d_ref[...], (((1,), (1,)), ((), ())), preferred_element_type=jnp.float32
+    )
     out_ref[...] = total.astype(jnp.bfloat16)
 
 
-def combine_kernel(
-    info, rank_ref, pieces_ref, back_ref, resid_ref, _, out_ref, last_ref, square_ref, mix, squares
-):
-    step = pl.program_id(0)
-    rows = resid_ref.shape[0]
+def weigh(parity, rank_ref, pieces_ref, back_ref, mix, step):
     slots = back_ref.shape[0]
-    length = info[3]
+    rows = rank_ref.shape[0]
 
     @pl.when(step == 0)
     def _():
         expert = iota((LANES, slots), 0)
         lane = iota((LANES, slots), 1)
-        odd = expert & 1
-        start = (expert - odd + jnp.where(odd == info[2], 0, 1)) * CAP
-        inside = (lane >= start) & (lane < start + CAP)
+        start = jnp.where((expert & 1) == parity, (expert >> 1) * ROOM, slots)
+        inside = (lane >= start) & (lane < start + ROOM)
         spread = jnp.where(inside, 1.0, 0.0).astype(jnp.bfloat16)
         within = jnp.sum(jnp.where(inside, lane - start, 0), axis=0, keepdims=True).astype(jnp.float32)
         rank = jnp.dot(rank_ref[...], spread, preferred_element_type=jnp.float32)
@@ -246,10 +229,37 @@
                 pieces_ref[k * rows : (k + 1) * rows, :], spread, preferred_element_type=jnp.float32
             )
             mix[k * rows : (k + 1) * rows, :] = jnp.where(match, part, 0.0).astype(jnp.bfloat16)
+
+    parts = jnp.dot(mix[...], back_ref[...], preferred_element_type=jnp.float32)
+    return parts[2 * rows :] + parts[rows : 2 * rows] + parts[:rows]
+
+
+def first_kernel(info, rank_ref, pieces_ref, back_ref, moe_ref, mix):
+    moe_ref[...] = weigh(info[2], rank_ref, pieces_ref, back_ref, mix, pl.program_id(0))
+
+
+def combine_kernel(
+    info,
+    rank_ref,
+    pieces_ref,
+    back_ref,
+    moe_ref,
+    resid_ref,
+    _,
+    out_ref,
+    last_ref,
+    square_ref,
+    mix,
+    squares,
+):
+    step = pl.program_id(0)
+    length = info[3]
+    moe = moe_ref[...] + weigh(1 - info[2], rank_ref, pieces_ref, back_ref, mix, step)
+
+    @pl.when(step == 0)
+    def _():
         squares[...] = jnp.zeros_like(squares)
 
-    parts = jnp.dot(mix[...], back_ref[...], preferred_element_type=jnp.float32)
-    moe = parts[2 * rows :] + parts[rows : 2 * rows] + parts[:rows]
     out = (resid_ref[...].astype(jnp.float32) + moe).astype(jnp.bfloat16)
     out_ref[...] = out
     out_f = out.astype(jnp.float32)
@@ -283,6 +293,10 @@
     rows = out_ref.shape[1]
     for b in range(blocks):
         out_ref[b] = x_ref[pl.ds(b, rows, stride=blocks), :].astype(jnp.bfloat16)
+
+
+def tie_kernel(x_ref, _, out_ref):
+    pass
 
 
 def params():
@@ -301,16 +315,15 @@
     blk_count = lax.axis_size("blk")
     blk = lax.axis_index("blk")
     rep = lax.axis_index("rep")
-    back_rows = 2 * CAP
-    slots = blk_count * back_rows
+    slots = blk_count * ROOM
     resid = hidden_in[0]
     info = jnp.stack([2 * blk + rep, 2 * blk + 1 - rep, rep, lengths[blk]]).astype(jnp.int32)
 
     shard_rows = master.shape[1]
     flat = master.reshape(3 * shard_rows * blk_count, FF)
 
-    def moved(k, *after):
-        turned = pl.pallas_call(
+    def turned(k, *after):
+        return pl.pallas_call(
             functools.partial(cast_kernel, blk_count),
             grid=(FF // LANES,),
             in_specs=[pl.BlockSpec((shard_rows * blk_count, LANES), lambda i: (k, i))]
@@ -320,13 +333,26 @@
             compiler_params=params(),
             name="cast",
         )(flat, *after)
-        own = lax.all_to_all(turned, "blk", split_axis=0, concat_axis=0, tiled=True)
+
+    def moved(x):
+        own = lax.all_to_all(x, "blk", split_axis=0, concat_axis=0, tiled=True)
         own = own.reshape(width, FF)
         return own, lax.ppermute(own, "rep", [(0, 1), (1, 0)])
 
-    g_own, g_oth = moved(0)
-    u_own, u_oth = moved(1)
-    d_own, d_oth = moved(2, g_oth)
+    def tied(x, after):
+        return pl.pallas_call(
+            tie_kernel,
+            in_specs=[pl.BlockSpec(memory_space=pl.ANY)] * 2,
+            out_specs=pl.BlockSpec(memory_space=pl.ANY),
+            out_shape=jax.ShapeDtypeStruct(x.shape, x.dtype),
+            input_output_aliases={0: 0},
+            name="tie",
+        )(x, after)
+
+    g_turned = turned(0)
+    g_own, g_oth = moved(g_turned)
+    u_own, u_oth = moved(turned(1))
+    d_own, d_oth = moved(tied(turned(2), g_oth))
 
     row_ext, pieces = pl.pallas_call(
         prep_kernel,
@@ -338,6 +364,7 @@
                 whole((rows, routes.shape[2])),
                 whole((rows, routes.shape[2])),
                 whole((1, width)),
+                pl.BlockSpec(memory_space=pl.ANY),
             ],
             out_specs=[whole((rows, width + LANES)), whole((3 * rows, LANES))],
         ),
@@ -347,43 +374,51 @@
         ],
         compiler_params=params(),
         name="prep",
-    )(info, resid, routes[0], route_weights[0], norm_gain[None])
-    tokens = lax.all_gather(row_ext, "blk", axis=0, tiled=True)
-
-    groups = 4 if blk_count % 4 == 0 else 1
-    group_rows = blk_count // groups * rows
-    hidden = pl.pallas_call(
-        functools.partial(hidden_kernel, groups),
-        grid_spec=pltpu.PrefetchScalarGridSpec(
-            num_scalar_prefetch=1,
-            grid=(groups,),
-            in_specs=[pl.BlockSpec((group_rows, width + LANES), lambda i, *_: (i, 0))]
-            + [whole((width, FF))] * 4,
-            out_specs=whole((slots, 2 * FF)),
-            scratch_shapes=[pltpu.VMEM((2, slots // 2, width), jnp.bfloat16)],
-        ),
-        out_shape=jax.ShapeDtypeStruct((slots, 2 * FF), jnp.bfloat16),
-        compiler_params=params(),
-        name="gate_up",
-    )(info, tokens, g_own, u_own, g_oth, u_oth)
+    )(info, resid, routes[0], route_weights[0], norm_gain[None], g_turned)
+    count = blk_count // PLANE
+    lines = [[p + PLANE * q for q in range(count)] for p in range(PLANE)]
+    planes = [[p + PLANE * q for p in range(PLANE)] for q in range(count)]
+    line = lax.all_gather(row_ext, "blk", axis_index_groups=lines, axis=0, tiled=True)
+    tokens = lax.all_gather(line, "blk", axis_index_groups=planes, axis=0, tiled=True)
+
+    def hidden_of(which, g, u):
+        return pl.pallas_call(
+            functools.partial(gate_up_kernel, which),
+            grid_spec=pltpu.PrefetchScalarGridSpec(
+                num_scalar_prefetch=1,
+                grid=(PLANE,),
+                in_specs=[pl.BlockSpec((count * rows, width + LANES), lambda i, *_: (i, 0))]
+                + [whole((width, FF))] * 2,
+                out_specs=whole((slots, FF)),
+                scratch_shapes=[pltpu.VMEM((slots, width), jnp.float32)],
+            ),
+            out_shape=jax.ShapeDtypeStruct((slots, FF), jnp.bfloat16),
+            compiler_params=params(),
+            name="gate_up",
+        )(info, tokens, g, u)
 
     step = 512
-    outputs = pl.pallas_call(
-        down_kernel,
-        grid=(width // step,),
-        in_specs=[
-            whole((slots, 2 * FF)),
-            pl.BlockSpec((step, FF), lambda i: (i, 0)),
-            pl.BlockSpec((step, FF), lambda i: (i, 0)),
-        ],
-        out_specs=pl.BlockSpec((slots, step), lambda i: (0, i)),
-        out_shape=jax.ShapeDtypeStruct((slots, width), jnp.bfloat16),
-        compiler_params=params(),
-        name="down",
-    )(hidden, d_own, d_oth)
-    back = lax.all_to_all(
-        outputs.reshape(blk_count, back_rows, width), "blk", split_axis=0, concat_axis=0, tiled=True
-    ).reshape(slots, width)
+
+    def outputs_of(hidden, d):
+        return pl.pallas_call(
+            down_kernel,
+            grid=(width // step,),
+            in_specs=[whole((slots, FF)), pl.BlockSpec((step, FF), lambda i: (i, 0))],
+            out_specs=pl.BlockSpec((slots, step), lambda i: (0, i)),
+            out_shape=jax.ShapeDtypeStruct((slots, width), jnp.bfloat16),
+            compiler_params=params(),
+            name="down",
+        )(hidden, d)
+
+    def returned(x):
+        x = x.reshape(blk_count, ROOM, width)
+        x = lax.all_to_all(x, "blk", split_axis=0, concat_axis=0, tiled=True)
+        return x.reshape(slots, width)
+
+    own_out = outputs_of(hidden_of(0, g_own, u_own), d_own)
+    own_back = returned(own_out)
+    oth_out = outputs_of(hidden_of(1, g_oth, u_oth), d_oth)
+    oth_back = returned(oth_out)
 
     part = width // 4
     server = pl.pallas_call(
@@ -398,29 +433,40 @@
         out_shape=jax.ShapeDtypeStruct((3, width, 2 * FF), jnp.bfloat16),
         compiler_params=params(),
         name="place",
-    )(info, g_own, g_oth, u_own, u_oth, d_own, d_oth, outputs)
-
+    )(info, g_own, g_oth, u_own, u_oth, d_own, d_oth, oth_out)
+
+    weigh_specs = [
+        pl.BlockSpec((rows, LANES), lambda i, *_: (0, width // LANES)),
+        whole((3 * rows, LANES)),
+        pl.BlockSpec((slots, step), lambda i, *_: (0, i)),
+    ]
+    column = pl.BlockSpec((rows, step), lambda i, *_: (0, i))
+    mix = pltpu.VMEM((3 * rows, slots), jnp.bfloat16)
+    moe = pl.pallas_call(
+        first_kernel,
+        grid_spec=pltpu.PrefetchScalarGridSpec(
+            num_scalar_prefetch=1,
+            grid=(width // step,),
+            in_specs=weigh_specs,
+            out_specs=column,
+            scratch_shapes=[mix],
+        ),
+        out_shape=jax.ShapeDtypeStruct((rows, width), jnp.float32),
+        compiler_params=params(),
+        name="first",
+    )(info, row_ext, pieces, own_back)
     out_rows, last, square = pl.pallas_call(
         combine_kernel,
         grid_spec=pltpu.PrefetchScalarGridSpec(
             num_scalar_prefetch=1,
             grid=(width // step,),
-            in_specs=[
-                pl.BlockSpec((rows, LANES), lambda i, *_: (0, width // LANES)),
-                whole((3 * rows, LANES)),
-                pl.BlockSpec((slots, step), lambda i, *_: (0, i)),
-                pl.BlockSpec((rows, step), lambda i, *_: (0, i)),
-                pl.BlockSpec(memory_space=pl.ANY),
-            ],
+            in_specs=weigh_specs + [column, column, pl.BlockSpec(memory_space=pl.ANY)],
             out_specs=[
-                pl.BlockSpec((rows, step), lambda i, *_: (0, i)),
+                column,
                 pl.BlockSpec((1, step), lambda i, *_: (0, i)),
                 whole((1, LANES)),
             ],
-            scratch_shapes=[
-                pltpu.VMEM((3 * rows, slots), jnp.bfloat16),
-                pltpu.VMEM((1, step), jnp.float32),
-            ],
+            scratch_shapes=[mix, pltpu.VMEM((1, step), jnp.float32)],
         ),
         out_shape=[
             jax.ShapeDtypeStruct((rows, width), jnp.bfloat16),
@@ -429,7 +475,7 @@
         ],
         compiler_params=params(),
         name="combine",
-    )(info, row_ext, pieces, back, resid, server)
+    )(info, row_ext, pieces, oth_back, moe, resid, server)
 
     def everywhere(x):
         copies = jnp.broadcast_to(x[None], (blk_count,) + x.shape)
@@ -463,6 +509,7 @@
         lax.axis_size("rep") == 2
         and master.shape[3] == FF
         and EXPERTS == 2 * blk_count
+        and blk_count == PLANE * PLANE
         and hidden_in.shape[1] == LEN
         and lengths.shape[0] == blk_count
     )

time: 354 us -> 370 us (1.045)
  waiting for transfers between devices: 203 us -> 220 us
  starting transfers between devices: 65.3 us -> 51.6 us
  Pallas kernels: 52 us -> 63.3 us
    all_to_all x4 -> x5, waiting for transfers between devices: 131 us -> 75.5 us  [the longest x3 50 us: moved(): own = lax.all_to_all(x, 'blk', split_axis=0, concat_axis=0, tiled=True)]
    all_gather x1 -> x2, waiting for transfers between devices: 0.01 us -> 42.1 us  [the longest x1 42 us: paired(): lax.all_gather(row_ext, 'blk', axis_index_groups=lines, axis=0, tiled=True)]
    ppermute x3, waiting for transfers between devices: 57.2 us -> 88.5 us  [moved(): return (own, lax.ppermute(own, 'rep', [(0, 1), (1, 0)]))]
    pallas_call x5 -> x9, Pallas kernels: 34.4 us -> 46.4 us  [the longest x2 19.3 us: hidden_of(): pl.pallas_call(functools.partial(gate_up_kernel, which), grid_spec=pltpu....]
    all_to_all x4 -> x5, starting transfers between devices: 40.1 us -> 33.7 us  [the longest x3 18.5 us: moved(): own = lax.all_to_all(x, 'blk', split_axis=0, concat_axis=0, tiled=True)]
    all_to_all x2, starting transfers between devices: 20.5 us -> 14.2 us  [everywhere(): lax.all_to_all(copies, 'blk', split_axis=0, concat_axis=0, tiled=True)]
    unnamed x19 -> x25, local copies, waits for them, and re-layouts: 6.95 us -> 8.83 us
  transfers between devices with their start and end apart: 10 -> 12, of which waited for: 9 -> 9; matrix products, arithmetic and copies ran while one was open for 0% -> 0% of each run, Pallas kernels for 10% -> 12%
where the time goes in v3:
time: 370 us; the launch traced here: 369 us
  waiting for transfers between devices  220 us (59%)
  Pallas kernels  63.3 us (17%)
  starting transfers between devices  51.6 us (14%)
  between operations  14.2 us (4%)
  local copies, waits for them, and re-layouts  12.2 us (3%)
  matrix products  4.63 us (1%)
    ppermute x3, waiting for transfers between devices, moved(): return (own, lax.ppermute(own, 'rep', [(0, 1), (1, 0)]))  88.5 us
    all_to_all x3, waiting for transfers between devices, moved(): own = lax.all_to_all(x, 'blk', split_axis=0, concat_axis=0, tiled=True)  50 us
    all_gather x1, waiting for transfers between devices, paired(): lax.all_gather(row_ext, 'blk', axis_index_groups=lines, axis=0, tiled=True)  42 us
    all_to_all x2, waiting for transfers between devices, returned(): x = lax.all_to_all(x, 'blk', split_axis=0, concat_axis=0, tiled=True)  25.5 us
    pallas_call x2, Pallas kernels, hidden_of(): pl.pallas_call(functools.partial(gate_up_kernel, which), grid_spec=pltpu....  19.3 us
    all_to_all x3, starting transfers between devices, moved(): own = lax.all_to_all(x, 'blk', split_axis=0, concat_axis=0, tiled=True)  18.5 us
    all_to_all x2, starting transfers between devices, returned(): x = lax.all_to_all(x, 'blk', split_axis=0, concat_axis=0, tiled=True)  15.2 us
    all_to_all x2, starting transfers between devices, everywhere(): lax.all_to_all(copies, 'blk', split_axis=0, concat_axis=0, tiled=True)  14.2 us
  transfers between devices with their start and end apart: 12, of which 9 were waited for; matrix products, arithmetic and copies ran while one was open for 0% of the time, Pallas kernels for 12%

profile of v3, /device:TPU:0, one launch (start us, length us, event | category | flops | bytes accessed | tf_op | source)
XLA Modules:
  0.0 368.7 jit_solution(13198807907954051450)
XLA Ops:
  7.2 0.0 all-gather.3.cloned.1.call-start
  7.2 1.3 broadcast_in_dim.14.gain_ref
  8.5 1.4 copy.21
  9.9 1.4 copy.22
  11.3 0.0 copy-start.10
  11.3 4.3 %cast.3._ = bf16[16,96,512]{2,1,0:T(8,128)(2,1)} custom-call(f32[4608,512]{1,0:T(8,128)} %bitcast.27), custom_call_target="tpu_custom_call" | custom-call | tf_op jit(solution)/shard_map/cast/pallas_call | solution.py:326
  15.6 0.0 copy-done.10
  15.6 0.6 dynamic_slice.3
  16.2 1.2 pad_add_fusion.info
  17.4 3.0 prep.1
  20.4 0.0 all-gather.3.cloned.1.call-update
  20.5 0.0 all-gather.5.cloned.1.call-start
  20.5 42.0 %all-gather.3.cloned.1.call-done = bf16[512,1664]{1,0:T(8,128)(2,1)} async-done(((bf16[128,1664]{1,0:T(8,128)(2,1)}), bf16[512,1664]{1,0:T(8,128)(2,1)}) %all-gather.3.cloned.1.call-update) | async-done | bytes 1703952 | tf_op jit(solution)/shard_map/all_gather | solution.py:381
  62.6 0.0 all-gather.5.cloned.1.call-update
  62.6 3.7 %all-to-all-start = ((bf16[16,96,512]{2,1,0:T(8,128)(2,1)}), bf16[16,96,512]{2,1,0:T(8,128)(2,1)S(1)}, u32[]{:S(2)}, u32[]{:S(2)}) async-start(bf16[16,96,512]{2,1,0:T(8,128)(2,1)} %cast.3._), calls=%async_computation | async-start | bytes 3145728 | tf_op jit(solution)/shard_map/all_to_all | solution.py:338
  66.3 4.5 %cast.4 = bf16[16,96,512]{2,1,0:T(8,128)(2,1)} custom-call(f32[4608,512]{1,0:T(8,128)} %bitcast.28), custom_call_target="tpu_custom_call" | custom-call | tf_op jit(solution)/shard_map/cast/pallas_call | solution.py:326
  70.8 27.6 %all-to-all-done = bf16[16,96,512]{2,1,0:T(8,128)(2,1)S(1)} async-done(((bf16[16,96,512]{2,1,0:T(8,128)(2,1)}), bf16[16,96,512]{2,1,0:T(8,128)(2,1)S(1)}, u32[]{:S(2)}, u32[]{:S(2)}) %all-to-all-start) | async-done | bytes 1572896 | tf_op jit(solution)/shard_map/all_to_all | solution.py:338
  98.4 0.0 copy-start.2
  98.4 9.1 %all-to-all-start.1 = ((bf16[16,96,512]{2,1,0:T(8,128)(2,1)}), bf16[16,96,512]{2,1,0:T(8,128)(2,1)S(1)}, u32[]{:S(2)}, u32[]{:S(2)}) async-start(bf16[16,96,512]{2,1,0:T(8,128)(2,1)} %cast.4), calls=%async_computation.1 | async-start | bytes 3145728 | tf_op jit(solution)/shard_map/all_to_all | solution.py:338
  107.5 1.5 collective-permute-start
  109.0 4.3 %cast.5.x_ref = bf16[16,96,512]{2,1,0:T(8,128)(2,1)} custom-call(f32[4608,512]{1,0:T(8,128)} %bitcast.29), custom_call_target="tpu_custom_call" | custom-call | tf_op jit(solution)/shard_map/cast/pallas_call | solution.py:326
  113.3 0.0 copy-done.2
  113.3 31.0 %collective-permute-done.g_ref._.g_oth = bf16[1536,512]{1,0:T(8,128)(2,1)} collective-permute-done((bf16[1536,512]{1,0:T(8,128)(2,1)S(1)}, bf16[1536,512]{1,0:T(8,128)(2,1)}, u32[]{:S(2)}, u32[]{:S(2)}) %collective-permute-start) | collective-permute-done | bytes 1572896 | tf_op jit(solution)/shard_map/ppermute | solution.py:340
  144.3 0.0 all-to-all-done.1
  144.3 0.0 copy-start.3
  144.3 1.2 copy-done.3
  145.5 5.7 %all-to-all-start.2 = ((bf16[16,96,512]{2,1,0:T(8,128)(2,1)}), bf16[16,96,512]{2,1,0:T(8,128)(2,1)S(1)}, u32[]{:S(2)}, u32[]{:S(2)}) async-start(bf16[16,96,512]{2,1,0:T(8,128)(2,1)} %tie.1), calls=%async_computation.2 | async-start | bytes 3145728 | tf_op jit(solution)/shard_map/all_to_all | solution.py:338
  151.3 0.0 all-gather.5.cloned.1.call-done.x_ref
  151.3 9.6 %gate_up.3.hidden_ref = bf16[640,512]{1,0:T(8,128)(2,1)} custom-call(s32[4]{0:T(128)} %pad_add_fusion.info, bf16[2048,1664]{1,0:T(8,128)(2,1)} %all-gather.5.cloned.1.call-done.x_ref, bf16[1536,512]{1,0:T(8,128)(2,1)} %bitcast.35, bf16[1536,512]{1,0:T(8,128)(2,1)} %bitcast.37), custom_call_target="tpu_custom_call" | custom-call | tf_op jit(solution)/shard_map/gate_up/pallas_call | solution.py:385
  160.9 22.3 %all-to-all-done.2 = bf16[16,96,512]{2,1,0:T(8,128)(2,1)S(1)} async-done(((bf16[16,96,512]{2,1,0:T(8,128)(2,1)}), bf16[16,96,512]{2,1,0:T(8,128)(2,1)S(1)}, u32[]{:S(2)}, u32[]{:S(2)}) %all-to-all-start.2) | async-done | bytes 1572896 | tf_op jit(solution)/shard_map/all_to_all | solution.py:338
  183.3 0.0 copy-start
  183.3 1.2 copy-done
  184.4 4.5 %down.3 = bf16[640,1536]{1,0:T(8,128)(2,1)} custom-call(bf16[640,512]{1,0:T(8,128)(2,1)} %gate_up.3.hidden_ref, bf16[1536,512]{1,0:T(8,128)(2,1)} %bitcast.31), custom_call_target="tpu_custom_call" | custom-call | tf_op jit(solution)/shard_map/down/pallas_call | solution.py:403
  188.9 9.4 %all-to-all-start.4 = ((bf16[16,40,1536]{2,1,0:T(8,128)(2,1)}), bf16[16,40,1536]{2,1,0:T(8,128)(2,1)}, u32[]{:S(2)}, u32[]{:S(2)}) async-start(bf16[16,40,1536]{2,1,0:T(8,128)(2,1)} %bitcast.41), calls=%async_computation.4 | async-start | bytes 3932160 | tf_op jit(solution)/shard_map/all_to_all | solution.py:415
  198.3 0.0 copy-done.4
  198.3 1.5 collective-permute-start.1
  199.8 0.0 copy-done.1
  199.9 0.6 collective-permute-start.2
  200.4 35.2 %collective-permute-done.1.u_ref.u_oth = bf16[1536,512]{1,0:T(8,128)(2,1)S(1)} collective-permute-done((bf16[1536,512]{1,0:T(8,128)(2,1)S(1)}, bf16[1536,512]{1,0:T(8,128)(2,1)S(1)}, u32[]{:S(2)}, u32[]{:S(2)}) %collective-permute-start.1) | collective-permute-done | bytes 1572896 | tf_op jit(solution)/shard_map/ppermute | solution.py:340
  235.6 1.1 copy-done.7
  236.7 9.6 %gate_up.2.hidden_ref = bf16[640,512]{1,0:T(8,128)(2,1)} custom-call(s32[4]{0:T(128)} %pad_add_fusion.info, bf16[2048,1664]{1,0:T(8,128)(2,1)} %all-gather.5.cloned.1.call-done.x_ref, bf16[1536,512]{1,0:T(8,128)(2,1)} %collective-permute-done.g_ref._.g_oth, bf16[1536,512]{1,0:T(8,128)(2,1)} %copy-done.7), custom_call_target="tpu_custom_call" | custom-call | tf_op jit(solution)/shard_map/gate_up/pallas_call | solution.py:385
  246.4 22.4 %collective-permute-done.2.d_ref.d_oth = bf16[1536,512]{1,0:T(8,128)(2,1)S(1)} collective-permute-done((bf16[1536,512]{1,0:T(8,128)(2,1)S(1)}, bf16[1536,512]{1,0:T(8,128)(2,1)S(1)}, u32[]{:S(2)}, u32[]{:S(2)}) %collective-permute-start.2) | collective-permute-done | bytes 1572896 | tf_op jit(solution)/shard_map/ppermute | solution.py:340
  268.7 1.2 copy-done.6
  269.9 4.5 %down.2._ = bf16[640,1536]{1,0:T(8,128)(2,1)} custom-call(bf16[640,512]{1,0:T(8,128)(2,1)} %gate_up.2.hidden_ref, bf16[1536,512]{1,0:T(8,128)(2,1)} %copy-done.6), custom_call_target="tpu_custom_call" | custom-call | tf_op jit(solution)/shard_map/down/pallas_call | solution.py:403
  274.4 0.0 all-to-all-done.4
  274.4 5.8 %all-to-all-start.3 = ((bf16[16,40,1536]{2,1,0:T(8,128)(2,1)}), bf16[16,40,1536]{2,1,0:T(8,128)(2,1)S(1)}, u32[]{:S(2)}, u32[]{:S(2)}) async-start(bf16[16,40,1536]{2,1,0:T(8,128)(2,1)} %bitcast.30), calls=%async_computation.3 | async-start | bytes 3932160 | tf_op jit(solution)/shard_map/all_to_all | solution.py:415
  280.2 8.3 %place.1._ = bf16[3,1536,1024]{2,1,0:T(8,128)(2,1)} custom-call(s32[4]{0:T(128)} %pad_add_fusion.info, bf16[1536,512]{1,0:T(8,128)(2,1)} %bitcast.36, bf16[1536,512]{1,0:T(8,128)(2,1)} %collective-permute-done.g_ref._.g_oth, bf16[1536,512]{1,0:T(8,128)(2,1)} %bitcast.38, bf16[1536,512]{1,0:T(8,128)(2,1)} %copy-done.7, bf16[1536,512]{1,0:T(8,128)(2,1)} %bitcast.32, ...), custom_call_target="tpu_custom_call" | custom-call | tf_op jit(solution)/shard_map/place/pallas_call | solution.py:424
  288.5 5.1 %first.1.moe_ref = f32[128,1536]{1,0:T(8,128)} custom-call(s32[4]{0:T(128)} %pad_add_fusion.info, bf16[128,1664]{1,0:T(8,128)(2,1)} %get-tuple-element.8.rank_ref, bf16[384,128]{1,0:T(8,128)(2,1)} %get-tuple-element.9.pieces_ref, bf16[640,1536]{1,0:T(8,128)(2,1)} %bitcast.13.back_ref), custom_call_target="tpu_custom_call" | custom-call | tf_op jit(solution)/shard_map/first/pallas_call | solution.py:445
  293.5 25.5 %all-to-all-done.3 = bf16[16,40,1536]{2,1,0:T(8,128)(2,1)S(1)} async-done(((bf16[16,40,1536]{2,1,0:T(8,128)(2,1)}), bf16[16,40,1536]{2,1,0:T(8,128)(2,1)S(1)}, u32[]{:S(2)}, u32[]{:S(2)}) %all-to-all-start.3) | async-done | bytes 1966112 | tf_op jit(solution)/shard_map/all_to_all | solution.py:415
  319.0 1.3 copy-done.5
  320.3 5.7 %combine.1 = (bf16[128,1536]{1,0:T(8,128)(2,1)}, f32[1,1536]{1,0:T(1,128)}, f32[1,128]{1,0:T(1,128)}) custom-call(s32[4]{0:T(128)} %pad_add_fusion.info, bf16[128,1664]{1,0:T(8,128)(2,1)} %get-tuple-element.8.rank_ref, bf16[384,128]{1,0:T(8,128)(2,1)} %get-tuple-element.9.pieces_ref, bf16[640,1536]{1,0:T(8,128)(2,1)} %bitcast.40, f32[128,1536]{1,0:T(8,128)} %first.1.moe_ref, ...), custom_call_target="tpu_custom_call" | custom-call | tf_op jit(solution)/shard_map/combine/pallas_call | solution.py:458
  326.0 0.7 maximum_reduce_fusion
  326.8 0.7 broadcast_in_dim.31
  327.5 10.7 %all-to-all-start.5 = ((f32[16,1,1664]{2,1,0:T(1,128)}), f32[16,1,1664]{2,1,0:T(1,128)S(1)}, u32[]{:S(2)}, u32[]{:S(2)}) async-start(f32[16,1,1664]{2,1,0:T(1,128)} %broadcast_in_dim.31), calls=%async_computation.5 | async-start | bytes 212992 | tf_op jit(solution)/shard_map/all_to_all | solution.py:482
  338.2 7.5 %all-to-all-done.5 = f32[16,1,1664]{2,1,0:T(1,128)S(1)} async-done(((f32[16,1,1664]{2,1,0:T(1,128)}), f32[16,1,1664]{2,1,0:T(1,128)S(1)}, u32[]{:S(2)}, u32[]{:S(2)}) %all-to-all-start.5) | async-done | bytes 106528 | tf_op jit(solution)/shard_map/all_to_all | solution.py:482
  345.7 0.1 multiply_reduce_fusion
  345.8 0.1 slice_reduce_fusion
  346.0 0.0 copy-done.8
  346.0 0.0 copy-done.9
  346.0 4.6 %fusion.3 = (f32[16]{0:T(128)S(1)}, f32[16]{0:T(128)S(1)}) fusion(s32[2048]{0:T(1024)S(1)} %iota_add_fusion, s32[16]{0:T(128)S(1)} %copy-done.9, bf16[2048,1536]{1,0:T(8,128)(2,1)} %param.15, f32[16,1664]{1,0:T(8,128)S(1)} %bitcast.46, f32[1536]{0:T(1024)S(1)} %copy-done.8, f32[16]{0:T(128)S(1)} %add_rsqrt_fusion), kind=kOutput, calls=%fused_computation.16 | convolution fusion | flops 100868064 | bytes 6407296 | tf_op jit(solution)/shard_map/dot_general | solution.py:492
  350.6 0.6 broadcast_in_dim.33
  351.3 3.5 all-to-all-start.6
  354.8 6.4 %all-to-all-done.6 = f32[16,2,16]{2,1,0:T(2,128)S(1)} async-done(((f32[16,2,16]{2,1,0:T(2,128)}), f32[16,2,16]{2,1,0:T(2,128)S(1)}, u32[]{:S(2)}, u32[]{:S(2)}) %all-to-all-start.6) | async-done | bytes 2080 | tf_op jit(solution)/shard_map/all_to_all | solution.py:482
  361.3 0.6 pad_maximum_fusion
  (16 shorter events, 0.1 us)
Async XLA Ops:
  7.2 55.4 %all-gather.3.cloned.1.call-start = ((), (), s32[]{:S(2)}) async-start(), calls=%async_computation.7 | async-start | bytes 2129920 | tf_op jit(solution)/shard_map/all_gather | solution.py:381
  11.3 4.3 %copy-start.10 = (s32[16]{0:T(128)S(1)}, s32[16]{0:T(128)}, u32[]{:S(2)}) copy-start(s32[16]{0:T(128)} %param.10) | copy-start | bytes 196
  20.5 130.8 %all-gather.5.cloned.1.call-start = ((), (), s32[]{:S(2)}) async-start(), calls=%async_computation.8 | async-start | bytes 8519680 | tf_op jit(solution)/shard_map/all_gather | solution.py:382
  62.6 35.8 %all-to-all-start = ((bf16[16,96,512]{2,1,0:T(8,128)(2,1)}), bf16[16,96,512]{2,1,0:T(8,128)(2,1)S(1)}, u32[]{:S(2)}, u32[]{:S(2)}) async-start(bf16[16,96,512]{2,1,0:T(8,128)(2,1)} %cast.3._), calls=%async_computation | async-start | bytes 3145728 | tf_op jit(solution)/shard_map/all_to_all | solution.py:338
  98.4 14.9 %copy-start.2 = (bf16[16,96,512]{2,1,0:T(8,128)(2,1)}, bf16[16,96,512]{2,1,0:T(8,128)(2,1)S(1)}, u32[]{:S(2)}) copy-start(bf16[16,96,512]{2,1,0:T(8,128)(2,1)S(1)} %all-to-all-done) | copy-start | bytes 4718596
  98.4 45.9 %all-to-all-start.1 = ((bf16[16,96,512]{2,1,0:T(8,128)(2,1)}), bf16[16,96,512]{2,1,0:T(8,128)(2,1)S(1)}, u32[]{:S(2)}, u32[]{:S(2)}) async-start(bf16[16,96,512]{2,1,0:T(8,128)(2,1)} %cast.4), calls=%async_computation.1 | async-start | bytes 3145728 | tf_op jit(solution)/shard_map/all_to_all | solution.py:338
  107.5 36.8 %collective-permute-start = (bf16[1536,512]{1,0:T(8,128)(2,1)S(1)}, bf16[1536,512]{1,0:T(8,128)(2,1)}, u32[]{:S(2)}, u32[]{:S(2)}) collective-permute-start(bf16[1536,512]{1,0:T(8,128)(2,1)S(1)} %bitcast.34), channel_id=1, source_target_pairs={{0,1},{1,0},{2,3},{3,2},{4,5},{5,4},{6,7},{7,6},{8,9},{9,8},{10,11... | collective-permute-start | bytes 4718600 | tf_op jit(solution)/shard_map/ppermute | solution.py:340
  144.3 1.2 copy-start.3
  145.5 37.7 %all-to-all-start.2 = ((bf16[16,96,512]{2,1,0:T(8,128)(2,1)}), bf16[16,96,512]{2,1,0:T(8,128)(2,1)S(1)}, u32[]{:S(2)}, u32[]{:S(2)}) async-start(bf16[16,96,512]{2,1,0:T(8,128)(2,1)} %tie.1), calls=%async_computation.2 | async-start | bytes 3145728 | tf_op jit(solution)/shard_map/all_to_all | solution.py:338
  183.3 1.2 copy-start
  188.9 9.4 %copy-start.4 = (bf16[16,96,512]{2,1,0:T(8,128)(2,1)S(1)}, bf16[16,96,512]{2,1,0:T(8,128)(2,1)}, u32[]{:S(2)}) copy-start(bf16[16,96,512]{2,1,0:T(8,128)(2,1)} %copy-done.3) | copy-start | bytes 4718596
  188.9 11.0 %copy-start.1 = (bf16[16,96,512]{2,1,0:T(8,128)(2,1)S(1)}, bf16[16,96,512]{2,1,0:T(8,128)(2,1)}, u32[]{:S(2)}) copy-start(bf16[16,96,512]{2,1,0:T(8,128)(2,1)} %copy-done) | copy-start | bytes 4718596
  188.9 85.6 %all-to-all-start.4 = ((bf16[16,40,1536]{2,1,0:T(8,128)(2,1)}), bf16[16,40,1536]{2,1,0:T(8,128)(2,1)}, u32[]{:S(2)}, u32[]{:S(2)}) async-start(bf16[16,40,1536]{2,1,0:T(8,128)(2,1)} %bitcast.41), calls=%async_computation.4 | async-start | bytes 3932160 | tf_op jit(solution)/shard_map/all_to_all | solution.py:415
  198.3 37.3 %collective-permute-start.1 = (bf16[1536,512]{1,0:T(8,128)(2,1)S(1)}, bf16[1536,512]{1,0:T(8,128)(2,1)S(1)}, u32[]{:S(2)}, u32[]{:S(2)}) collective-permute-start(bf16[1536,512]{1,0:T(8,128)(2,1)S(1)} %bitcast.39), channel_id=1, source_target_pairs={{0,1},{1,0},{2,3},{3,2},{4,5},{5,4},{6,7},{7,6},{8,9},{9,8},{10,11... | collective-permute-start | bytes 4718600 | tf_op jit(solution)/shard_map/ppermute | solution.py:340
  199.9 68.9 %collective-permute-start.2 = (bf16[1536,512]{1,0:T(8,128)(2,1)S(1)}, bf16[1536,512]{1,0:T(8,128)(2,1)S(1)}, u32[]{:S(2)}, u32[]{:S(2)}) collective-permute-start(bf16[1536,512]{1,0:T(8,128)(2,1)S(1)} %bitcast.33), channel_id=1, source_target_pairs={{0,1},{1,0},{2,3},{3,2},{4,5},{5,4},{6,7},{7,6},{8,9},{9,8},{10,11... | collective-permute-start | bytes 4718600 | tf_op jit(solution)/shard_map/ppermute | solution.py:340
  235.6 1.1 copy-start.7
  268.7 1.2 copy-start.6
  274.4 44.6 %all-to-all-start.3 = ((bf16[16,40,1536]{2,1,0:T(8,128)(2,1)}), bf16[16,40,1536]{2,1,0:T(8,128)(2,1)S(1)}, u32[]{:S(2)}, u32[]{:S(2)}) async-start(bf16[16,40,1536]{2,1,0:T(8,128)(2,1)} %bitcast.30), calls=%async_computation.3 | async-start | bytes 3932160 | tf_op jit(solution)/shard_map/all_to_all | solution.py:415
  319.0 1.3 copy-start.5
  320.3 25.6 %copy-start.8 = (f32[1536]{0:T(1024)S(1)}, f32[1536]{0:T(1024)}, u32[]{:S(2)}) copy-start(f32[1536]{0:T(1024)} %param.16) | copy-start | bytes 18436
  320.3 25.6 %copy-start.9 = (s32[16]{0:T(128)S(1)}, s32[16]{0:T(128)}, u32[]{:S(2)}) copy-start(s32[16]{0:T(128)} %param.17) | copy-start | bytes 196
  327.5 18.2 %all-to-all-start.5 = ((f32[16,1,1664]{2,1,0:T(1,128)}), f32[16,1,1664]{2,1,0:T(1,128)S(1)}, u32[]{:S(2)}, u32[]{:S(2)}) async-start(f32[16,1,1664]{2,1,0:T(1,128)} %broadcast_in_dim.31), calls=%async_computation.5 | async-start | bytes 212992 | tf_op jit(solution)/shard_map/all_to_all | solution.py:482
  351.3 9.9 %all-to-all-start.6 = ((f32[16,2,16]{2,1,0:T(2,128)}), f32[16,2,16]{2,1,0:T(2,128)S(1)}, u32[]{:S(2)}, u32[]{:S(2)}) async-start(f32[16,2,16]{2,1,0:T(2,128)} %broadcast_in_dim.33), calls=%async_computation.6 | async-start | bytes 32768 | tf_op jit(solution)/shard_map/all_to_all | solution.py:482
Sparse Core Ops, SparseCore 0:
  20.6 41.9 all-gather.2
  64.1 72.8 all-gather.4

commit v4 on v3

--- a/solution.py
+++ b/solution.py
@@ -11,7 +11,8 @@
 EXPERTS = 32
 LEN = 128
 CAP = 36
-ROOM = 40
+FIRST = 32
+SECOND = 40
 PLANE = 4
 LANES = 128
 VMEM = 56 * 1024 * 1024
@@ -157,10 +158,12 @@
     row = iota((rows, LANES), 0)
     hit = jnp.zeros((rows, LANES), jnp.float32)
     weight = jnp.zeros((rows, LANES), jnp.float32)
-    for k in range(routes_ref.shape[1]):
-        named = routes_ref[:, k : k + 1] == lane
+    named_by = jnp.transpose(routes_ref[...].astype(jnp.float32)).astype(jnp.int32)
+    weight_by = jnp.transpose(weights_ref[...])
+    for k in range(routes_ref.shape[0]):
+        named = named_by[:, k : k + 1] == lane
         hit = hit + jnp.where(named, 1.0, 0.0)
-        weight = weight + jnp.where(named, weights_ref[:, k : k + 1], 0.0)
+        weight = weight + jnp.where(named, weight_by[:, k : k + 1], 0.0)
     live = row < length
     hit = jnp.where(live, hit, 0.0)
     weight = jnp.where(live, weight, 0.0)
@@ -175,42 +178,91 @@
         weight = weight - piece.astype(jnp.float32)
 
 
-def gate_up_kernel(which, info, x_ref, g_ref, u_ref, out_ref, picked):
-    step = pl.program_id(0)
+def pick(info, which, x_ref, width, place, slots):
     rows = x_ref.shape[0]
-    width = g_ref.shape[0]
-    sources = rows // LEN
-    slots = sources * ROOM
     ranks = x_ref[:, width:].astype(jnp.float32)
     lane = iota((rows, LANES), 1)
     source = (iota((rows, 1), 0) // LEN).astype(jnp.float32)
     rank = jnp.sum(jnp.where(lane == info[which], ranks, 0.0), axis=1, keepdims=True)
-    slot = jnp.where(rank >= 0.0, source * ROOM + rank, -1.0)
+    slot = jnp.where(rank >= 0.0, place(source, rank), -1.0)
     slot_lane = iota((rows, slots), 1).astype(jnp.float32)
     one_hot = jnp.where(slot == slot_lane, 1.0, 0.0).astype(jnp.bfloat16)
-    chosen = lax.dot_general(
+    return lax.dot_general(
         one_hot, x_ref[:, :width], (((0,), (0,)), ((), ())), preferred_element_type=jnp.float32
     )
+
+
+def activ(x, g_ref, u_ref):
+    x = x.astype(jnp.bfloat16)
+    gate = jnp.dot(x, g_ref[...], preferred_element_type=jnp.float32)
+    up = jnp.dot(x, u_ref[...], preferred_element_type=jnp.float32)
+    return (gate / (1.0 + jnp.exp(-gate)) * up).astype(jnp.bfloat16)
+
+
+def own_kernel(info, x_ref, g_ref, u_ref, out_ref, late_ref, picked):
+    step = pl.program_id(0)
+    sources = x_ref.shape[0] // LEN
+    more = CAP - FIRST
+    early = sources * FIRST
+    all_early = PLANE * early
+
+    def place(source, rank):
+        return jnp.where(
+            rank < FIRST, source * FIRST + rank, early + source * more + (rank - FIRST)
+        )
+
+    chosen = pick(info, 0, x_ref, g_ref.shape[0], place, early + sources * more)
     for s in range(sources):
-        start = pl.multiple_of((s * PLANE + step) * ROOM, ROOM)
-        picked[pl.ds(start, ROOM), :] = chosen[s * ROOM : (s + 1) * ROOM]
+        start = pl.multiple_of((s * PLANE + step) * FIRST, FIRST)
+        picked[pl.ds(start, FIRST), :] = chosen[s * FIRST : (s + 1) * FIRST]
+    start = pl.multiple_of(all_early + step * sources * more, sources * more)
+    picked[pl.ds(start, sources * more), :] = chosen[early:]
 
     @pl.when(step == PLANE - 1)
     def _():
-        x = picked[...].astype(jnp.bfloat16)
-        gate = jnp.dot(x, g_ref[...], preferred_element_type=jnp.float32)
-        up = jnp.dot(x, u_ref[...], preferred_element_type=jnp.float32)
-        out_ref[...] = (gate / (1.0 + jnp.exp(-gate)) * up).astype(jnp.bfloat16)
-
-
-def down_kernel(hidden_ref, d_ref, out_ref):
-    total = lax.dot_general(
-        hidden_ref[...], d_ref[...], (((1,), (1,)), ((), ())), preferred_element_type=jnp.float32
-    )
+        hidden = activ(picked[...], g_ref, u_ref)
+        out_ref[...] = hidden[:all_early]
+        rest = hidden[all_early:]
+        shape = (late_ref.shape[0], rest.shape[0])
+        column = iota(shape, 1)
+        source = (column // more % sources) * PLANE + column // (more * sources)
+        one_hot = jnp.where(iota(shape, 0) == source * SECOND + column % more, 1.0, 0.0)
+        late_ref[...] = jnp.dot(
+            one_hot.astype(jnp.bfloat16), rest, preferred_element_type=jnp.float32
+        ).astype(jnp.bfloat16)
+
+
+def oth_kernel(info, x_ref, g_ref, u_ref, _, out_ref, picked):
+    step = pl.program_id(0)
+    sources = x_ref.shape[0] // LEN
+
+    def place(source, rank):
+        return source * SECOND + (SECOND - CAP) + rank
+
+    chosen = pick(info, 1, x_ref, g_ref.shape[0], place, sources * SECOND)
+    for s in range(sources):
+        start = pl.multiple_of((s * PLANE + step) * SECOND, SECOND)
+        picked[pl.ds(start, SECOND), :] = chosen[s * SECOND : (s + 1) * SECOND]
+
+    @pl.when(step == PLANE - 1)
+    def _():
+        out_ref[...] = activ(picked[...], g_ref, u_ref)
+
+
+def down_kernel(*refs):
+    out_ref = refs[-1]
+    total = 0.0
+    for hidden_ref, d_ref in zip(refs[0:-1:2], refs[1:-1:2]):
+        total = total + lax.dot_general(
+            hidden_ref[...],
+            d_ref[...],
+            (((1,), (1,)), ((), ())),
+            preferred_element_type=jnp.float32,
+        )
     out_ref[...] = total.astype(jnp.bfloat16)
 
 
-def weigh(parity, rank_ref, pieces_ref, back_ref, mix, step):
+def weigh(spans, stride, rank_ref, pieces_ref, back_ref, mix, step):
     slots = back_ref.shape[0]
     rows = rank_ref.shape[0]
 
@@ -218,10 +270,15 @@
     def _():
         expert = iota((LANES, slots), 0)
         lane = iota((LANES, slots), 1)
-        start = jnp.where((expert & 1) == parity, (expert >> 1) * ROOM, slots)
-        inside = (lane >= start) & (lane < start + ROOM)
-        spread = jnp.where(inside, 1.0, 0.0).astype(jnp.bfloat16)
-        within = jnp.sum(jnp.where(inside, lane - start, 0), axis=0, keepdims=True).astype(jnp.float32)
+        within = jnp.zeros((1, slots), jnp.float32)
+        spread = jnp.zeros((LANES, slots), jnp.float32)
+        for parity, offset, count, lowest in spans:
+            start = jnp.where((expert & 1) == parity, (expert >> 1) * stride + offset, slots)
+            inside = (lane >= start) & (lane < start + count)
+            spread = spread + jnp.where(inside, 1.0, 0.0)
+            ranks = jnp.where(inside, lane - start + lowest, 0)
+            within = within + jnp.sum(ranks, axis=0, keepdims=True).astype(jnp.float32)
+        spread = spread.astype(jnp.bfloat16)
         rank = jnp.dot(rank_ref[...], spread, preferred_element_type=jnp.float32)
         match = rank == within
         for k in range(3):
@@ -235,7 +292,8 @@
 
 
 def first_kernel(info, rank_ref, pieces_ref, back_ref, moe_ref, mix):
-    moe_ref[...] = weigh(info[2], rank_ref, pieces_ref, back_ref, mix, pl.program_id(0))
+    spans = ((info[2], 0, FIRST, 0),)
+    moe_ref[...] = weigh(spans, FIRST, rank_ref, pieces_ref, back_ref, mix, pl.program_id(0))
 
 
 def combine_kernel(
@@ -254,7 +312,9 @@
 ):
     step = pl.program_id(0)
     length = info[3]
-    moe = moe_ref[...] + weigh(1 - info[2], rank_ref, pieces_ref, back_ref, mix, step)
+    late = SECOND - CAP
+    spans = ((info[2], 0, late, FIRST), (1 - info[2], late, CAP, 0))
+    moe = moe_ref[...] + weigh(spans, SECOND, rank_ref, pieces_ref, back_ref, mix, step)
 
     @pl.when(step == 0)
     def _():
@@ -315,7 +375,8 @@
     blk_count = lax.axis_size("blk")
     blk = lax.axis_index("blk")
     rep = lax.axis_index("rep")
-    slots = blk_count * ROOM
+    first = blk_count * FIRST
+    second = blk_count * SECOND
     resid = hidden_in[0]
     info = jnp.stack([2 * blk + rep, 2 * blk + 1 - rep, rep, lengths[blk]]).astype(jnp.int32)
 
@@ -361,8 +422,8 @@
             grid=(1,),
             in_specs=[
                 whole((rows, width)),
-                whole((rows, routes.shape[2])),
-                whole((rows, routes.shape[2])),
+                whole((routes.shape[2], rows)),
+                whole((routes.shape[2], rows)),
                 whole((1, width)),
                 pl.BlockSpec(memory_space=pl.ANY),
             ],
@@ -374,50 +435,57 @@
         ],
         compiler_params=params(),
         name="prep",
-    )(info, resid, routes[0], route_weights[0], norm_gain[None], g_turned)
+    )(info, resid, routes[0].T, route_weights[0].T, norm_gain[None], g_turned)
     count = blk_count // PLANE
     lines = [[p + PLANE * q for q in range(count)] for p in range(PLANE)]
     planes = [[p + PLANE * q for p in range(PLANE)] for q in range(count)]
     line = lax.all_gather(row_ext, "blk", axis_index_groups=lines, axis=0, tiled=True)
+    line = tied(line, g_own)
     tokens = lax.all_gather(line, "blk", axis_index_groups=planes, axis=0, tiled=True)
 
-    def hidden_of(which, g, u):
+    def hidden_of(kernel, sizes, scratch, g, u, *after):
         return pl.pallas_call(
-            functools.partial(gate_up_kernel, which),
+            kernel,
             grid_spec=pltpu.PrefetchScalarGridSpec(
                 num_scalar_prefetch=1,
                 grid=(PLANE,),
                 in_specs=[pl.BlockSpec((count * rows, width + LANES), lambda i, *_: (i, 0))]
-                + [whole((width, FF))] * 2,
-                out_specs=whole((slots, FF)),
-                scratch_shapes=[pltpu.VMEM((slots, width), jnp.float32)],
+                + [whole((width, FF))] * 2
+                + [pl.BlockSpec(memory_space=pl.ANY)] * len(after),
+                out_specs=[whole((size, FF)) for size in sizes],
+                scratch_shapes=[pltpu.VMEM((scratch, width), jnp.float32)],
             ),
-            out_shape=jax.ShapeDtypeStruct((slots, FF), jnp.bfloat16),
+            out_shape=[jax.ShapeDtypeStruct((size, FF), jnp.bfloat16) for size in sizes],
             compiler_params=params(),
             name="gate_up",
-        )(info, tokens, g, u)
+        )(info, tokens, g, u, *after)
 
     step = 512
 
-    def outputs_of(hidden, d):
+    def outputs_of(size, *operands):
         return pl.pallas_call(
             down_kernel,
             grid=(width // step,),
-            in_specs=[whole((slots, FF)), pl.BlockSpec((step, FF), lambda i: (i, 0))],
-            out_specs=pl.BlockSpec((slots, step), lambda i: (0, i)),
-            out_shape=jax.ShapeDtypeStruct((slots, width), jnp.bfloat16),
+            in_specs=[whole((size, FF)), pl.BlockSpec((step, FF), lambda i: (i, 0))]
+            * (len(operands) // 2),
+            out_specs=pl.BlockSpec((size, step), lambda i: (0, i)),
+            out_shape=jax.ShapeDtypeStruct((size, width), jnp.bfloat16),
             compiler_params=params(),
             name="down",
-        )(hidden, d)
+        )(*operands)
 
     def returned(x):
-        x = x.reshape(blk_count, ROOM, width)
+        slots = x.shape[0]
+        x = x.reshape(blk_count, slots // blk_count, width)
         x = lax.all_to_all(x, "blk", split_axis=0, concat_axis=0, tiled=True)
         return x.reshape(slots, width)
 
-    own_out = outputs_of(hidden_of(0, g_own, u_own), d_own)
+    extra = blk_count * (CAP - FIRST)
+    own_hidden, late_hidden = hidden_of(own_kernel, (first, second), first + extra, g_own, u_own)
+    own_out = tied(outputs_of(first, own_hidden, d_own), u_oth)
     own_back = returned(own_out)
-    oth_out = outputs_of(hidden_of(1, g_oth, u_oth), d_oth)
+    (oth_hidden,) = hidden_of(oth_kernel, (second,), second, g_oth, u_oth, own_out)
+    oth_out = outputs_of(second, late_hidden, d_own, oth_hidden, d_oth)
     oth_back = returned(oth_out)
 
     part = width // 4
@@ -435,21 +503,22 @@
         name="place",
     )(info, g_own, g_oth, u_own, u_oth, d_own, d_oth, oth_out)
 
-    weigh_specs = [
-        pl.BlockSpec((rows, LANES), lambda i, *_: (0, width // LANES)),
-        whole((3 * rows, LANES)),
-        pl.BlockSpec((slots, step), lambda i, *_: (0, i)),
-    ]
+    def weigh_specs(slots):
+        return [
+            pl.BlockSpec((rows, LANES), lambda i, *_: (0, width // LANES)),
+            whole((3 * rows, LANES)),
+            pl.BlockSpec((slots, step), lambda i, *_: (0, i)),
+        ]
+
     column = pl.BlockSpec((rows, step), lambda i, *_: (0, i))
-    mix = pltpu.VMEM((3 * rows, slots), jnp.bfloat16)
     moe = pl.pallas_call(
         first_kernel,
         grid_spec=pltpu.PrefetchScalarGridSpec(
             num_scalar_prefetch=1,
             grid=(width // step,),
-            in_specs=weigh_specs,
+            in_specs=weigh_specs(first),
             out_specs=column,
-            scratch_shapes=[mix],
+            scratch_shapes=[pltpu.VMEM((3 * rows, first), jnp.bfloat16)],
         ),
         out_shape=jax.ShapeDtypeStruct((rows, width), jnp.float32),
         compiler_params=params(),
@@ -460,13 +529,16 @@
         grid_spec=pltpu.PrefetchScalarGridSpec(
             num_scalar_prefetch=1,
             grid=(width // step,),
-            in_specs=weigh_specs + [column, column, pl.BlockSpec(memory_space=pl.ANY)],
+            in_specs=weigh_specs(second) + [column, column, pl.BlockSpec(memory_space=pl.ANY)],
             out_specs=[
                 column,
                 pl.BlockSpec((1, step), lambda i, *_: (0, i)),
                 whole((1, LANES)),
             ],
-            scratch_shapes=[mix, pltpu.VMEM((1, step), jnp.float32)],
+            scratch_shapes=[
+                pltpu.VMEM((3 * rows, second), jnp.bfloat16),
+                pltpu.VMEM((1, step), jnp.float32),
+            ],
         ),
         out_shape=[
             jax.ShapeDtypeStruct((rows, width), jnp.bfloat16),

time: 370 us -> 327 us (0.88)
  waiting for transfers between devices: 220 us -> 182 us
    all_to_all x3, waiting for transfers between devices: 50 us -> 0.01 us  [moved(): own = lax.all_to_all(x, 'blk', split_axis=0, concat_axis=0, tiled=True)]
    ppermute x3, waiting for transfers between devices: 88.5 us -> 56.4 us  [moved(): return (own, lax.ppermute(own, 'rep', [(0, 1), (1, 0)]))]
    all_gather x1, waiting for transfers between devices: 0.02 us -> 25.9 us  [paired(): lax.all_gather(line, 'blk', axis_index_groups=planes, axis=0, tiled=True)]
    all_gather x1, waiting for transfers between devices: 42 us -> 60 us  [paired(): lax.all_gather(row_ext, 'blk', axis_index_groups=lines, axis=0, tiled=True)]
  transfers between devices with their start and end apart: 12 -> 12, of which waited for: 9 -> 7; matrix products, arithmetic and copies ran while one was open for 0% -> 1% of each run, Pallas kernels for 12% -> 17%
where the time goes in v4:
time: 327 us; the launch traced here: 325 us
  waiting for transfers between devices  182 us (56%)
  Pallas kernels  64.2 us (20%)
  starting transfers between devices  48.8 us (15%)
  between operations  14.2 us (4%)
  local copies, waits for them, and re-layouts  8.66 us (3%)
  matrix products  4.63 us (1%)
    all_gather x1, waiting for transfers between devices, paired(): lax.all_gather(row_ext, 'blk', axis_index_groups=lines, axis=0, tiled=True)  60 us
    ppermute x3, waiting for transfers between devices, moved(): return (own, lax.ppermute(own, 'rep', [(0, 1), (1, 0)]))  56.4 us
    all_gather x1, waiting for transfers between devices, paired(): lax.all_gather(line, 'blk', axis_index_groups=planes, axis=0, tiled=True)  25.9 us
    all_to_all x2, waiting for transfers between devices, returned(): x = lax.all_to_all(x, 'blk', split_axis=0, concat_axis=0, tiled=True)  25.8 us
    pallas_call x2, Pallas kernels, hidden_of(): pl.pallas_call(kernel, grid_spec=pltpu.PrefetchScalarGridSpec(num_scalar_...  19.5 us
    all_to_all x3, starting transfers between devices, moved(): own = lax.all_to_all(x, 'blk', split_axis=0, concat_axis=0, tiled=True)  17.1 us
    all_to_all x2, starting transfers between devices, everywhere(): lax.all_to_all(copies, 'blk', split_axis=0, concat_axis=0, tiled=True)  14.2 us
    all_to_all x2, waiting for transfers between devices, everywhere(): lax.all_to_all(copies, 'blk', split_axis=0, concat_axis=0, tiled=True)  14 us
  transfers between devices with their start and end apart: 12, of which 7 were waited for; matrix products, arithmetic and copies ran while one was open for 1% of the time, Pallas kernels for 17%

profile of v4, /device:TPU:0, one launch (start us, length us, event | category | flops | bytes accessed | tf_op | source)
XLA Modules:
  0.0 325.4 jit_solution(8375847799646231987)
XLA Ops:
  7.2 4.3 %cast.3._ = bf16[16,96,512]{2,1,0:T(8,128)(2,1)} custom-call(f32[4608,512]{1,0:T(8,128)} %bitcast.31), custom_call_target="tpu_custom_call" | custom-call | tf_op jit(solution)/shard_map/cast/pallas_call | solution.py:387
  11.5 0.0 copy-start.9
  11.5 0.0 copy-start.11
  11.5 7.5 %all-to-all-start = ((bf16[16,96,512]{2,1,0:T(8,128)(2,1)}), bf16[16,96,512]{2,1,0:T(8,128)(2,1)S(1)}, u32[]{:S(2)}, u32[]{:S(2)}) async-start(bf16[16,96,512]{2,1,0:T(8,128)(2,1)} %cast.3._), calls=%async_computation | async-start | bytes 3145728 | tf_op jit(solution)/shard_map/all_to_all | solution.py:399
  19.0 0.0 all-gather.3.cloned.1.call-start
  19.0 0.0 copy-done.9
  19.1 0.6 broadcast_in_dim.14.gain_ref
  19.7 0.0 copy-done.11
  19.7 0.6 dynamic_slice.3
  20.2 1.3 pad_add_fusion.info
  21.6 3.0 prep.1
  24.6 0.0 all-gather.3.cloned.1.call-update
  24.6 0.0 all-gather.5.cloned.1.call-start
  24.6 60.0 %all-gather.3.cloned.1.call-done.x_ref = bf16[512,1664]{1,0:T(8,128)(2,1)} async-done(((bf16[128,1664]{1,0:T(8,128)(2,1)}), bf16[512,1664]{1,0:T(8,128)(2,1)}) %all-gather.3.cloned.1.call-update) | async-done | bytes 1703952 | tf_op jit(solution)/shard_map/all_gather | solution.py:442
  84.6 0.0 all-to-all-done
  84.6 0.0 copy-start
  84.6 1.2 copy-done
  85.8 0.0 all-gather.5.cloned.1.call-update
  85.8 4.3 %cast.4 = bf16[16,96,512]{2,1,0:T(8,128)(2,1)} custom-call(f32[4608,512]{1,0:T(8,128)} %bitcast.32), custom_call_target="tpu_custom_call" | custom-call | tf_op jit(solution)/shard_map/cast/pallas_call | solution.py:387
  90.1 0.0 copy-start.1
  90.1 3.9 %all-to-all-start.1 = ((bf16[16,96,512]{2,1,0:T(8,128)(2,1)}), bf16[16,96,512]{2,1,0:T(8,128)(2,1)S(1)}, u32[]{:S(2)}, u32[]{:S(2)}) async-start(bf16[16,96,512]{2,1,0:T(8,128)(2,1)} %cast.4), calls=%async_computation.1 | async-start | bytes 3145728 | tf_op jit(solution)/shard_map/all_to_all | solution.py:399
  94.0 0.0 copy-done.1
  94.0 1.6 collective-permute-start
  95.6 4.4 %cast.5.x_ref = bf16[16,96,512]{2,1,0:T(8,128)(2,1)} custom-call(f32[4608,512]{1,0:T(8,128)} %bitcast.33), custom_call_target="tpu_custom_call" | custom-call | tf_op jit(solution)/shard_map/cast/pallas_call | solution.py:387
  100.0 30.8 %collective-permute-done._.g_ref.g_oth = bf16[1536,512]{1,0:T(8,128)(2,1)} collective-permute-done((bf16[1536,512]{1,0:T(8,128)(2,1)S(1)}, bf16[1536,512]{1,0:T(8,128)(2,1)}, u32[]{:S(2)}, u32[]{:S(2)}) %collective-permute-start) | collective-permute-done | bytes 1572896 | tf_op jit(solution)/shard_map/ppermute | solution.py:401
  130.9 0.0 all-to-all-done.1
  130.9 0.0 copy-start.4
  130.9 5.8 %all-to-all-start.2 = ((bf16[16,96,512]{2,1,0:T(8,128)(2,1)}), bf16[16,96,512]{2,1,0:T(8,128)(2,1)S(1)}, u32[]{:S(2)}, u32[]{:S(2)}) async-start(bf16[16,96,512]{2,1,0:T(8,128)(2,1)} %tie.4), calls=%async_computation.2 | async-start | bytes 3145728 | tf_op jit(solution)/shard_map/all_to_all | solution.py:399
  136.6 0.0 copy-done.4
  136.6 1.6 collective-permute-start.1
  138.2 25.9 %all-gather.5.cloned.1.call-done.x_ref = bf16[2048,1664]{1,0:T(8,128)(2,1)} async-done(((bf16[512,1664]{1,0:T(8,128)(2,1)}), bf16[2048,1664]{1,0:T(8,128)(2,1)}) %all-gather.5.cloned.1.call-update) | async-done | bytes 6815760 | tf_op jit(solution)/shard_map/all_gather | solution.py:444
  164.1 9.8 %gate_up.2 = (bf16[512,512]{1,0:T(8,128)(2,1)}, bf16[640,512]{1,0:T(8,128)(2,1)}) custom-call(s32[4]{0:T(128)} %pad_add_fusion.info, bf16[2048,1664]{1,0:T(8,128)(2,1)} %all-gather.5.cloned.1.call-done.x_ref, bf16[1536,512]{1,0:T(8,128)(2,1)} %bitcast.35, bf16[1536,512]{1,0:T(8,128)(2,1)} %bitcast.45), custom_call_target="tpu_custom_call" | custom-call | tf_op jit(solution)/shard_map/gate_up/pallas_call | solution.py:447
  173.9 0.0 all-to-all-done.2
  173.9 1.2 copy-done.2
  175.1 4.2 %down.2.x_ref = bf16[512,1536]{1,0:T(8,128)(2,1)} custom-call(bf16[512,512]{1,0:T(8,128)(2,1)} %get-tuple-element.13.refs_0_, bf16[1536,512]{1,0:T(8,128)(2,1)} %bitcast.38), custom_call_target="tpu_custom_call" | custom-call | tf_op jit(solution)/shard_map/down/pallas_call | solution.py:466
  179.3 0.0 collective-permute-done.1._.u_ref.u_oth
  179.3 6.9 %all-to-all-start.4 = ((bf16[16,32,1536]{2,1,0:T(8,128)(2,1)}), bf16[16,32,1536]{2,1,0:T(8,128)(2,1)S(1)}, u32[]{:S(2)}, u32[]{:S(2)}) async-start(bf16[16,32,1536]{2,1,0:T(8,128)(2,1)} %bitcast.42), calls=%async_computation.4 | async-start | bytes 3145728 | tf_op jit(solution)/shard_map/all_to_all | solution.py:480
  186.2 0.0 copy-done.3
  186.3 1.5 collective-permute-start.2
  187.8 9.7 %gate_up.3.refs_2_ = bf16[640,512]{1,0:T(8,128)(2,1)} custom-call(s32[4]{0:T(128)} %pad_add_fusion.info, bf16[2048,1664]{1,0:T(8,128)(2,1)} %all-gather.5.cloned.1.call-done.x_ref, bf16[1536,512]{1,0:T(8,128)(2,1)} %collective-permute-done._.g_ref.g_oth, bf16[1536,512]{1,0:T(8,128)(2,1)} %collective-permute-done.1._.u_ref.u_oth, bf16[512,1536]{1,0:T(8,128)(2,1)} %tie.5._), custom_call_target="tpu_custom_call" | custom-call | tf_op jit(solution)/shard_map/gate_up/pallas_call | solution.py:447
  197.5 25.6 %collective-permute-done.2.refs_3_.d_oth = bf16[1536,512]{1,0:T(8,128)(2,1)S(1)} collective-permute-done((bf16[1536,512]{1,0:T(8,128)(2,1)S(1)}, bf16[1536,512]{1,0:T(8,128)(2,1)S(1)}, u32[]{:S(2)}, u32[]{:S(2)}) %collective-permute-start.2) | collective-permute-done | bytes 1572896 | tf_op jit(solution)/shard_map/ppermute | solution.py:401
  223.0 1.2 copy-done.7
  224.2 5.7 %down.3._ = bf16[640,1536]{1,0:T(8,128)(2,1)} custom-call(bf16[640,512]{1,0:T(8,128)(2,1)} %get-tuple-element.12.refs_0_, bf16[1536,512]{1,0:T(8,128)(2,1)} %bitcast.39, bf16[640,512]{1,0:T(8,128)(2,1)} %gate_up.3.refs_2_, bf16[1536,512]{1,0:T(8,128)(2,1)} %copy-done.7), custom_call_target="tpu_custom_call" | custom-call | tf_op jit(solution)/shard_map/down/pallas_call | solution.py:466
  229.9 0.0 all-to-all-done.4
  229.9 1.1 copy-done.6
  231.0 5.7 %all-to-all-start.3 = ((bf16[16,40,1536]{2,1,0:T(8,128)(2,1)}), bf16[16,40,1536]{2,1,0:T(8,128)(2,1)S(1)}, u32[]{:S(2)}, u32[]{:S(2)}) async-start(bf16[16,40,1536]{2,1,0:T(8,128)(2,1)} %bitcast.43), calls=%async_computation.3 | async-start | bytes 3932160 | tf_op jit(solution)/shard_map/all_to_all | solution.py:480
  236.8 8.3 %place.1._ = bf16[3,1536,1024]{2,1,0:T(8,128)(2,1)} custom-call(s32[4]{0:T(128)} %pad_add_fusion.info, bf16[1536,512]{1,0:T(8,128)(2,1)} %bitcast.36, bf16[1536,512]{1,0:T(8,128)(2,1)} %collective-permute-done._.g_ref.g_oth, bf16[1536,512]{1,0:T(8,128)(2,1)} %bitcast.46, bf16[1536,512]{1,0:T(8,128)(2,1)} %collective-permute-done.1._.u_ref.u_oth, ...), custom_call_target="tpu_custom_call" | custom-call | tf_op jit(solution)/shard_map/place/pallas_call | solution.py:492
  245.0 4.7 %first.1.moe_ref = f32[128,1536]{1,0:T(8,128)} custom-call(s32[4]{0:T(128)} %pad_add_fusion.info, bf16[128,1664]{1,0:T(8,128)(2,1)} %get-tuple-element.10.rank_ref, bf16[384,128]{1,0:T(8,128)(2,1)} %get-tuple-element.11.pieces_ref, bf16[512,1536]{1,0:T(8,128)(2,1)} %bitcast.48), custom_call_target="tpu_custom_call" | custom-call | tf_op jit(solution)/shard_map/first/pallas_call | solution.py:514
  249.7 25.8 %all-to-all-done.3 = bf16[16,40,1536]{2,1,0:T(8,128)(2,1)S(1)} async-done(((bf16[16,40,1536]{2,1,0:T(8,128)(2,1)}), bf16[16,40,1536]{2,1,0:T(8,128)(2,1)S(1)}, u32[]{:S(2)}, u32[]{:S(2)}) %all-to-all-start.3) | async-done | bytes 1966112 | tf_op jit(solution)/shard_map/all_to_all | solution.py:480
  275.6 1.3 copy-done.5
  276.9 5.8 %combine.1 = (bf16[128,1536]{1,0:T(8,128)(2,1)}, f32[1,1536]{1,0:T(1,128)}, f32[1,128]{1,0:T(1,128)}) custom-call(s32[4]{0:T(128)} %pad_add_fusion.info, bf16[128,1664]{1,0:T(8,128)(2,1)} %get-tuple-element.10.rank_ref, bf16[384,128]{1,0:T(8,128)(2,1)} %get-tuple-element.11.pieces_ref, bf16[640,1536]{1,0:T(8,128)(2,1)} %bitcast.47, ...), custom_call_target="tpu_custom_call" | custom-call | tf_op jit(solution)/shard_map/combine/pallas_call | solution.py:527
  282.7 0.7 maximum_reduce_fusion
  283.4 0.7 broadcast_in_dim.31
  284.1 10.7 %all-to-all-start.5 = ((f32[16,1,1664]{2,1,0:T(1,128)}), f32[16,1,1664]{2,1,0:T(1,128)S(1)}, u32[]{:S(2)}, u32[]{:S(2)}) async-start(f32[16,1,1664]{2,1,0:T(1,128)} %broadcast_in_dim.31), calls=%async_computation.5 | async-start | bytes 212992 | tf_op jit(solution)/shard_map/all_to_all | solution.py:554
  294.9 7.5 %all-to-all-done.5 = f32[16,1,1664]{2,1,0:T(1,128)S(1)} async-done(((f32[16,1,1664]{2,1,0:T(1,128)}), f32[16,1,1664]{2,1,0:T(1,128)S(1)}, u32[]{:S(2)}, u32[]{:S(2)}) %all-to-all-start.5) | async-done | bytes 106528 | tf_op jit(solution)/shard_map/all_to_all | solution.py:554
  302.4 0.1 multiply_reduce_fusion
  302.5 0.1 slice_reduce_fusion
  302.6 0.0 copy-done.8
  302.6 0.0 copy-done.10
  302.7 4.6 %fusion.3 = (f32[16]{0:T(128)S(1)}, f32[16]{0:T(128)S(1)}) fusion(s32[2048]{0:T(1024)S(1)} %iota_add_fusion, s32[16]{0:T(128)S(1)} %copy-done.10, bf16[2048,1536]{1,0:T(8,128)(2,1)} %param.15, f32[16,1664]{1,0:T(8,128)S(1)} %bitcast.53, f32[1536]{0:T(1024)S(1)} %copy-done.8, f32[16]{0:T(128)S(1)} %add_rsqrt_fusion), kind=kOutput, calls=%fused_computation.16 | convolution fusion | flops 100868064 | bytes 6407296 | tf_op jit(solution)/shard_map/dot_general | solution.py:564
  307.3 0.6 broadcast_in_dim.33
  307.9 3.5 %all-to-all-start.6 = ((f32[16,2,16]{2,1,0:T(2,128)}), f32[16,2,16]{2,1,0:T(2,128)S(1)}, u32[]{:S(2)}, u32[]{:S(2)}) async-start(f32[16,2,16]{2,1,0:T(2,128)} %broadcast_in_dim.33), calls=%async_computation.6 | async-start | bytes 32768 | tf_op jit(solution)/shard_map/all_to_all | solution.py:554
  311.4 6.4 %all-to-all-done.6 = f32[16,2,16]{2,1,0:T(2,128)S(1)} async-done(((f32[16,2,16]{2,1,0:T(2,128)}), f32[16,2,16]{2,1,0:T(2,128)S(1)}, u32[]{:S(2)}, u32[]{:S(2)}) %all-to-all-start.6) | async-done | bytes 2080 | tf_op jit(solution)/shard_map/all_to_all | solution.py:554
  317.9 0.6 pad_maximum_fusion
  (18 shorter events, 0.1 us)
Async XLA Ops:
  11.5 7.6 %copy-start.9 = (f32[1536]{0:T(1024)S(1)}, f32[1536]{0:T(1024)}, u32[]{:S(2)}) copy-start(f32[1536]{0:T(1024)} %param.13) | copy-start | bytes 18436
  11.5 8.2 %copy-start.11 = (s32[16]{0:T(128)S(1)}, s32[16]{0:T(128)}, u32[]{:S(2)}) copy-start(s32[16]{0:T(128)} %param.10) | copy-start | bytes 196
  11.5 73.1 %all-to-all-start = ((bf16[16,96,512]{2,1,0:T(8,128)(2,1)}), bf16[16,96,512]{2,1,0:T(8,128)(2,1)S(1)}, u32[]{:S(2)}, u32[]{:S(2)}) async-start(bf16[16,96,512]{2,1,0:T(8,128)(2,1)} %cast.3._), calls=%async_computation | async-start | bytes 3145728 | tf_op jit(solution)/shard_map/all_to_all | solution.py:399
  19.0 65.6 %all-gather.3.cloned.1.call-start = ((), (), s32[]{:S(2)}) async-start(), calls=%async_computation.7 | async-start | bytes 2129920 | tf_op jit(solution)/shard_map/all_gather | solution.py:442
  24.6 139.5 %all-gather.5.cloned.1.call-start = ((), (), s32[]{:S(2)}) async-start(), calls=%async_computation.8 | async-start | bytes 8519680 | tf_op jit(solution)/shard_map/all_gather | solution.py:444
  84.6 1.2 copy-start
  90.1 3.9 %copy-start.1 = (bf16[16,96,512]{2,1,0:T(8,128)(2,1)S(1)}, bf16[16,96,512]{2,1,0:T(8,128)(2,1)}, u32[]{:S(2)}) copy-start(bf16[16,96,512]{2,1,0:T(8,128)(2,1)} %copy-done) | copy-start | bytes 4718596
  90.1 40.7 %all-to-all-start.1 = ((bf16[16,96,512]{2,1,0:T(8,128)(2,1)}), bf16[16,96,512]{2,1,0:T(8,128)(2,1)S(1)}, u32[]{:S(2)}, u32[]{:S(2)}) async-start(bf16[16,96,512]{2,1,0:T(8,128)(2,1)} %cast.4), calls=%async_computation.1 | async-start | bytes 3145728 | tf_op jit(solution)/shard_map/all_to_all | solution.py:399
  94.0 36.9 %collective-permute-start = (bf16[1536,512]{1,0:T(8,128)(2,1)S(1)}, bf16[1536,512]{1,0:T(8,128)(2,1)}, u32[]{:S(2)}, u32[]{:S(2)}) collective-permute-start(bf16[1536,512]{1,0:T(8,128)(2,1)S(1)} %bitcast.37), channel_id=1, source_target_pairs={{0,1},{1,0},{2,3},{3,2},{4,5},{5,4},{6,7},{7,6},{8,9},{9,8},{10,11... | collective-permute-start | bytes 4718600 | tf_op jit(solution)/shard_map/ppermute | solution.py:401
  130.9 5.8 %copy-start.4 = (bf16[16,96,512]{2,1,0:T(8,128)(2,1)}, bf16[16,96,512]{2,1,0:T(8,128)(2,1)S(1)}, u32[]{:S(2)}) copy-start(bf16[16,96,512]{2,1,0:T(8,128)(2,1)S(1)} %all-to-all-done.1) | copy-start | bytes 4718596
  130.9 43.0 %all-to-all-start.2 = ((bf16[16,96,512]{2,1,0:T(8,128)(2,1)}), bf16[16,96,512]{2,1,0:T(8,128)(2,1)S(1)}, u32[]{:S(2)}, u32[]{:S(2)}) async-start(bf16[16,96,512]{2,1,0:T(8,128)(2,1)} %tie.4), calls=%async_computation.2 | async-start | bytes 3145728 | tf_op jit(solution)/shard_map/all_to_all | solution.py:399
  136.6 42.6 %collective-permute-start.1 = (bf16[1536,512]{1,0:T(8,128)(2,1)S(1)}, bf16[1536,512]{1,0:T(8,128)(2,1)}, u32[]{:S(2)}, u32[]{:S(2)}) collective-permute-start(bf16[1536,512]{1,0:T(8,128)(2,1)S(1)} %bitcast.44), channel_id=1, source_target_pairs={{0,1},{1,0},{2,3},{3,2},{4,5},{5,4},{6,7},{7,6},{8,9},{9,8},{10,11... | collective-permute-start | bytes 4718600 | tf_op jit(solution)/shard_map/ppermute | solution.py:401
  173.9 1.2 copy-start.2
  179.3 7.0 %copy-start.3 = (bf16[16,96,512]{2,1,0:T(8,128)(2,1)S(1)}, bf16[16,96,512]{2,1,0:T(8,128)(2,1)}, u32[]{:S(2)}) copy-start(bf16[16,96,512]{2,1,0:T(8,128)(2,1)} %copy-done.2) | copy-start | bytes 4718596
  179.3 50.6 %all-to-all-start.4 = ((bf16[16,32,1536]{2,1,0:T(8,128)(2,1)}), bf16[16,32,1536]{2,1,0:T(8,128)(2,1)S(1)}, u32[]{:S(2)}, u32[]{:S(2)}) async-start(bf16[16,32,1536]{2,1,0:T(8,128)(2,1)} %bitcast.42), calls=%async_computation.4 | async-start | bytes 3145728 | tf_op jit(solution)/shard_map/all_to_all | solution.py:480
  186.3 36.8 %collective-permute-start.2 = (bf16[1536,512]{1,0:T(8,128)(2,1)S(1)}, bf16[1536,512]{1,0:T(8,128)(2,1)S(1)}, u32[]{:S(2)}, u32[]{:S(2)}) collective-permute-start(bf16[1536,512]{1,0:T(8,128)(2,1)S(1)} %bitcast.41), channel_id=1, source_target_pairs={{0,1},{1,0},{2,3},{3,2},{4,5},{5,4},{6,7},{7,6},{8,9},{9,8},{10,11... | collective-permute-start | bytes 4718600 | tf_op jit(solution)/shard_map/ppermute | solution.py:401
  223.0 1.2 copy-start.7
  229.9 1.1 copy-start.6
  231.0 44.6 %all-to-all-start.3 = ((bf16[16,40,1536]{2,1,0:T(8,128)(2,1)}), bf16[16,40,1536]{2,1,0:T(8,128)(2,1)S(1)}, u32[]{:S(2)}, u32[]{:S(2)}) async-start(bf16[16,40,1536]{2,1,0:T(8,128)(2,1)} %bitcast.43), calls=%async_computation.3 | async-start | bytes 3932160 | tf_op jit(solution)/shard_map/all_to_all | solution.py:480
  275.6 1.3 copy-start.5
  276.9 25.8 %copy-start.8 = (f32[1536]{0:T(1024)S(1)}, f32[1536]{0:T(1024)}, u32[]{:S(2)}) copy-start(f32[1536]{0:T(1024)} %param.16) | copy-start | bytes 18436
  276.9 25.8 %copy-start.10 = (s32[16]{0:T(128)S(1)}, s32[16]{0:T(128)}, u32[]{:S(2)}) copy-start(s32[16]{0:T(128)} %param.17) | copy-start | bytes 196
  284.1 18.2 %all-to-all-start.5 = ((f32[16,1,1664]{2,1,0:T(1,128)}), f32[16,1,1664]{2,1,0:T(1,128)S(1)}, u32[]{:S(2)}, u32[]{:S(2)}) async-start(f32[16,1,1664]{2,1,0:T(1,128)} %broadcast_in_dim.31), calls=%async_computation.5 | async-start | bytes 212992 | tf_op jit(solution)/shard_map/all_to_all | solution.py:554
  307.9 10.0 %all-to-all-start.6 = ((f32[16,2,16]{2,1,0:T(2,128)}), f32[16,2,16]{2,1,0:T(2,128)S(1)}, u32[]{:S(2)}, u32[]{:S(2)}) async-start(f32[16,2,16]{2,1,0:T(2,128)} %broadcast_in_dim.33), calls=%async_computation.6 | async-start | bytes 32768 | tf_op jit(solution)/shard_map/all_to_all | solution.py:554
Sparse Core Ops, SparseCore 0:
  24.7 59.8 all-gather.2
  86.2 77.8 all-gather.4

commit v5 on v4

--- a/solution.py
+++ b/solution.py
@@ -13,7 +13,8 @@
 CAP = 36
 FIRST = 32
 SECOND = 40
-PLANE = 4
+GROUPS = 4
+RING = (0, 1, 4, 5, 8, 9, 12, 13, 14, 15, 10, 11, 6, 7, 2, 3)
 LANES = 128
 VMEM = 56 * 1024 * 1024
 
@@ -204,7 +205,7 @@
     sources = x_ref.shape[0] // LEN
     more = CAP - FIRST
     early = sources * FIRST
-    all_early = PLANE * early
+    all_early = GROUPS * early
 
     def place(source, rank):
         return jnp.where(
@@ -213,19 +214,21 @@
 
     chosen = pick(info, 0, x_ref, g_ref.shape[0], place, early + sources * more)
     for s in range(sources):
-        start = pl.multiple_of((s * PLANE + step) * FIRST, FIRST)
+        start = pl.multiple_of(info[4 + step * sources + s] * FIRST, FIRST)
         picked[pl.ds(start, FIRST), :] = chosen[s * FIRST : (s + 1) * FIRST]
     start = pl.multiple_of(all_early + step * sources * more, sources * more)
     picked[pl.ds(start, sources * more), :] = chosen[early:]
 
-    @pl.when(step == PLANE - 1)
+    @pl.when(step == GROUPS - 1)
     def _():
         hidden = activ(picked[...], g_ref, u_ref)
         out_ref[...] = hidden[:all_early]
         rest = hidden[all_early:]
         shape = (late_ref.shape[0], rest.shape[0])
         column = iota(shape, 1)
-        source = (column // more % sources) * PLANE + column // (more * sources)
+        source = jnp.zeros_like(column)
+        for k, b in enumerate(RING):
+            source = source + jnp.where(column // more == k, b, 0)
         one_hot = jnp.where(iota(shape, 0) == source * SECOND + column % more, 1.0, 0.0)
         late_ref[...] = jnp.dot(
             one_hot.astype(jnp.bfloat16), rest, preferred_element_type=jnp.float32
@@ -241,10 +244,10 @@
 
     chosen = pick(info, 1, x_ref, g_ref.shape[0], place, sources * SECOND)
     for s in range(sources):
-        start = pl.multiple_of((s * PLANE + step) * SECOND, SECOND)
+        start = pl.multiple_of(info[4 + step * sources + s] * SECOND, SECOND)
         picked[pl.ds(start, SECOND), :] = chosen[s * SECOND : (s + 1) * SECOND]
 
-    @pl.when(step == PLANE - 1)
+    @pl.when(step == GROUPS - 1)
     def _():
         out_ref[...] = activ(picked[...], g_ref, u_ref)
 
@@ -262,12 +265,15 @@
     out_ref[...] = total.astype(jnp.bfloat16)
 
 
-def weigh(spans, stride, rank_ref, pieces_ref, back_ref, mix, step):
-    slots = back_ref.shape[0]
+def mix_kernel(info, rank_ref, pieces_ref, first_ref, second_ref):
     rows = rank_ref.shape[0]
-
-    @pl.when(step == 0)
-    def _():
+    late = SECOND - CAP
+    own, oth = info[2], 1 - info[2]
+    for mix_ref, stride, spans in (
+        (first_ref, FIRST, ((own, 0, FIRST, 0),)),
+        (second_ref, SECOND, ((own, 0, late, FIRST), (oth, late, CAP, 0))),
+    ):
+        slots = mix_ref.shape[1]
         expert = iota((LANES, slots), 0)
         lane = iota((LANES, slots), 1)
         within = jnp.zeros((1, slots), jnp.float32)
@@ -285,36 +291,25 @@
             part = jnp.dot(
                 pieces_ref[k * rows : (k + 1) * rows, :], spread, preferred_element_type=jnp.float32
             )
-            mix[k * rows : (k + 1) * rows, :] = jnp.where(match, part, 0.0).astype(jnp.bfloat16)
-
-    parts = jnp.dot(mix[...], back_ref[...], preferred_element_type=jnp.float32)
+            mix_ref[k * rows : (k + 1) * rows, :] = jnp.where(match, part, 0.0).astype(jnp.bfloat16)
+
+
+def weigh(mix_ref, back_ref):
+    rows = mix_ref.shape[0] // 3
+    parts = jnp.dot(mix_ref[...], back_ref[...], preferred_element_type=jnp.float32)
     return parts[2 * rows :] + parts[rows : 2 * rows] + parts[:rows]
 
 
-def first_kernel(info, rank_ref, pieces_ref, back_ref, moe_ref, mix):
-    spans = ((info[2], 0, FIRST, 0),)
-    moe_ref[...] = weigh(spans, FIRST, rank_ref, pieces_ref, back_ref, mix, pl.program_id(0))
+def first_kernel(mix_ref, back_ref, moe_ref):
+    moe_ref[...] = weigh(mix_ref, back_ref)
 
 
 def combine_kernel(
-    info,
-    rank_ref,
-    pieces_ref,
-    back_ref,
-    moe_ref,
-    resid_ref,
-    _,
-    out_ref,
-    last_ref,
-    square_ref,
-    mix,
-    squares,
+    info, mix_ref, back_ref, moe_ref, resid_ref, _, out_ref, told_ref, lasts, squares
 ):
     step = pl.program_id(0)
     length = info[3]
-    late = SECOND - CAP
-    spans = ((info[2], 0, late, FIRST), (1 - info[2], late, CAP, 0))
-    moe = moe_ref[...] + weigh(spans, SECOND, rank_ref, pieces_ref, back_ref, mix, step)
+    moe = moe_ref[...] + weigh(mix_ref, back_ref)
 
     @pl.when(step == 0)
     def _():
@@ -324,13 +319,22 @@
     out_ref[...] = out
     out_f = out.astype(jnp.float32)
     row = iota(out_f.shape, 0)
-    last_ref[...] = jnp.sum(jnp.where(row == length - 1, out_f, 0.0), axis=0, keepdims=True)
+    lasts[pl.ds(step, 1)] = jnp.sum(
+        jnp.where(row == length - 1, out_f, 0.0), axis=0, keepdims=True
+    )[None]
     squares[...] += jnp.sum(jnp.where(row < length, out_f * out_f, 0.0), axis=0, keepdims=True)
 
     @pl.when(step == pl.num_programs(0) - 1)
     def _():
-        square_ref[...] = jnp.broadcast_to(
-            jnp.sum(squares[...], axis=1, keepdims=True), square_ref.shape
+        count = told_ref.shape[0]
+        for k in range(lasts.shape[0]):
+            size = lasts.shape[2]
+            told_ref[:, :, k * size : (k + 1) * size] = jnp.broadcast_to(
+                lasts[k : k + 1], (count, 1, size)
+            )
+        total = jnp.sum(squares[...], axis=1, keepdims=True)[None]
+        told_ref[:, :, lasts.shape[0] * lasts.shape[2] :] = jnp.broadcast_to(
+            total, (count, 1, LANES)
         )
 
 
@@ -378,7 +382,8 @@
     first = blk_count * FIRST
     second = blk_count * SECOND
     resid = hidden_in[0]
-    info = jnp.stack([2 * blk + rep, 2 * blk + 1 - rep, rep, lengths[blk]]).astype(jnp.int32)
+    info = jnp.stack([2 * blk + rep, 2 * blk + 1 - rep, rep, lengths[blk]] + list(RING))
+    info = info.astype(jnp.int32)
 
     shard_rows = master.shape[1]
     flat = master.reshape(3 * shard_rows * blk_count, FF)
@@ -436,20 +441,15 @@
         compiler_params=params(),
         name="prep",
     )(info, resid, routes[0].T, route_weights[0].T, norm_gain[None], g_turned)
-    count = blk_count // PLANE
-    lines = [[p + PLANE * q for q in range(count)] for p in range(PLANE)]
-    planes = [[p + PLANE * q for p in range(PLANE)] for q in range(count)]
-    line = lax.all_gather(row_ext, "blk", axis_index_groups=lines, axis=0, tiled=True)
-    line = tied(line, g_own)
-    tokens = lax.all_gather(line, "blk", axis_index_groups=planes, axis=0, tiled=True)
+    tokens = lax.all_gather(row_ext, "blk", axis_index_groups=[list(RING)], axis=0, tiled=True)
 
     def hidden_of(kernel, sizes, scratch, g, u, *after):
         return pl.pallas_call(
             kernel,
             grid_spec=pltpu.PrefetchScalarGridSpec(
                 num_scalar_prefetch=1,
-                grid=(PLANE,),
-                in_specs=[pl.BlockSpec((count * rows, width + LANES), lambda i, *_: (i, 0))]
+                grid=(GROUPS,),
+                in_specs=[pl.BlockSpec((blk_count // GROUPS * rows, width + LANES), lambda i, *_: (i, 0))]
                 + [whole((width, FF))] * 2
                 + [pl.BlockSpec(memory_space=pl.ANY)] * len(after),
                 out_specs=[whole((size, FF)) for size in sizes],
@@ -503,57 +503,62 @@
         name="place",
     )(info, g_own, g_oth, u_own, u_oth, d_own, d_oth, oth_out)
 
+    first_mix, second_mix = pl.pallas_call(
+        mix_kernel,
+        grid_spec=pltpu.PrefetchScalarGridSpec(
+            num_scalar_prefetch=1,
+            grid=(1,),
+            in_specs=[
+                pl.BlockSpec((rows, LANES), lambda i, *_: (0, width // LANES)),
+                whole((3 * rows, LANES)),
+            ],
+            out_specs=[whole((3 * rows, first)), whole((3 * rows, second))],
+        ),
+        out_shape=[
+            jax.ShapeDtypeStruct((3 * rows, first), jnp.bfloat16),
+            jax.ShapeDtypeStruct((3 * rows, second), jnp.bfloat16),
+        ],
+        compiler_params=params(),
+        name="mix",
+    )(info, row_ext, pieces)
+
     def weigh_specs(slots):
-        return [
-            pl.BlockSpec((rows, LANES), lambda i, *_: (0, width // LANES)),
-            whole((3 * rows, LANES)),
-            pl.BlockSpec((slots, step), lambda i, *_: (0, i)),
-        ]
+        return [whole((3 * rows, slots)), pl.BlockSpec((slots, step), lambda i, *_: (0, i))]
 
     column = pl.BlockSpec((rows, step), lambda i, *_: (0, i))
     moe = pl.pallas_call(
         first_kernel,
-        grid_spec=pltpu.PrefetchScalarGridSpec(
-            num_scalar_prefetch=1,
-            grid=(width // step,),
-            in_specs=weigh_specs(first),
-            out_specs=column,
-            scratch_shapes=[pltpu.VMEM((3 * rows, first), jnp.bfloat16)],
-        ),
+        grid=(width // step,),
+        in_specs=weigh_specs(first),
+        out_specs=column,
         out_shape=jax.ShapeDtypeStruct((rows, width), jnp.float32),
         compiler_params=params(),
         name="first",
-    )(info, row_ext, pieces, own_back)
-    out_rows, last, square = pl.pallas_call(
+    )(first_mix, own_back)
+    out_rows, told = pl.pallas_call(
         combine_kernel,
         grid_spec=pltpu.PrefetchScalarGridSpec(
             num_scalar_prefetch=1,
             grid=(width // step,),
             in_specs=weigh_specs(second) + [column, column, pl.BlockSpec(memory_space=pl.ANY)],
-            out_specs=[
-                column,
-                pl.BlockSpec((1, step), lambda i, *_: (0, i)),
-                whole((1, LANES)),
-            ],
+            out_specs=[column, whole((blk_count, 1, width + LANES))],
             scratch_shapes=[
-                pltpu.VMEM((3 * rows, second), jnp.bfloat16),
+                pltpu.VMEM((width // step, 1, step), jnp.float32),
                 pltpu.VMEM((1, step), jnp.float32),
             ],
         ),
         out_shape=[
             jax.ShapeDtypeStruct((rows, width), jnp.bfloat16),
-            jax.ShapeDtypeStruct((1, width), jnp.float32),
-            jax.ShapeDtypeStruct((1, LANES), jnp.float32),
+            jax.ShapeDtypeStruct((blk_count, 1, width + LANES), jnp.float32),
         ],
         compiler_params=params(),
         name="combine",
-    )(info, row_ext, pieces, oth_back, moe, resid, server)
-
-    def everywhere(x):
-        copies = jnp.broadcast_to(x[None], (blk_count,) + x.shape)
+    )(info, second_mix, oth_back, moe, resid, server)
+
+    def everywhere(copies):
         return lax.all_to_all(copies, "blk", split_axis=0, concat_axis=0, tiled=True)
 
-    gathered = everywhere(jnp.concatenate([last, square], axis=1))[:, 0]
+    gathered = everywhere(told)[:, 0]
     last_rows, square_total = gathered[:, :width], gathered[:, width]
     norms = jnp.sqrt(square_total / (lengths.astype(jnp.float32) * width) + 1e-06)
     final = (
@@ -570,7 +575,8 @@
     )
     target_part = jnp.sum(jnp.where(target_hit, logits, 0.0), axis=1)
     top_part = jnp.max(logits, axis=1)
-    parts = everywhere(jnp.stack([top_part, target_part]))
+    stats = jnp.stack([top_part, target_part])
+    parts = everywhere(jnp.broadcast_to(stats[None], (blk_count,) + stats.shape))
     request_stats = jnp.stack([norms, jnp.max(parts[:, 0], axis=0), jnp.sum(parts[:, 1], axis=0)])
     return (out_rows[None], server, request_stats)
 
@@ -581,7 +587,7 @@
         lax.axis_size("rep") == 2
         and master.shape[3] == FF
         and EXPERTS == 2 * blk_count
-        and blk_count == PLANE * PLANE
+        and blk_count == len(RING)
         and hidden_in.shape[1] == LEN
         and lengths.shape[0] == blk_count
     )

time: 327 us -> 316 us (0.966)
  waiting for transfers between devices: 182 us -> 165 us
  starting transfers between devices: 48.8 us -> 57.3 us
    all_gather x2 -> x1, waiting for transfers between devices: 85.8 us -> 0.01 us  [paired(): lax.all_gather(row_ext, 'blk', axis_index_groups=[list(RING)], axis=0, ti...]
    all_to_all x3, waiting for transfers between devices: 0.01 us -> 70.3 us  [moved(): own = lax.all_to_all(x, 'blk', split_axis=0, concat_axis=0, tiled=True)]
    all_to_all x3, starting transfers between devices: 17.1 us -> 23.4 us  [moved(): own = lax.all_to_all(x, 'blk', split_axis=0, concat_axis=0, tiled=True)]
    pallas_call x1 -> x2, Pallas kernels: 4.71 us -> 6.82 us  [the longest x1 3.79 us: paired(): pl.pallas_call(first_kernel, grid=(width // step,), in_specs=weigh_specs(...]
  transfers between devices with their start and end apart: 12 -> 11, of which waited for: 7 -> 8; matrix products, arithmetic and copies ran while one was open for 1% -> 0% of each run, Pallas kernels for 17% -> 17%
where the time goes in v5:
time: 316 us; the launch traced here: 315 us
  waiting for transfers between devices  165 us (52%)
  Pallas kernels  65.9 us (21%)
  starting transfers between devices  57.3 us (18%)
  between operations  14.2 us (4%)
  local copies, waits for them, and re-layouts  7.72 us (2%)
  matrix products  4.63 us (1%)
    all_to_all x3, waiting for transfers between devices, moved(): own = lax.all_to_all(x, 'blk', split_axis=0, concat_axis=0, tiled=True)  70.3 us
    ppermute x3, waiting for transfers between devices, moved(): return (own, lax.ppermute(own, 'rep', [(0, 1), (1, 0)]))  56.6 us
    all_to_all x2, waiting for transfers between devices, returned(): x = lax.all_to_all(x, 'blk', split_axis=0, concat_axis=0, tiled=True)  23.7 us
    all_to_all x3, starting transfers between devices, moved(): own = lax.all_to_all(x, 'blk', split_axis=0, concat_axis=0, tiled=True)  23.4 us
    pallas_call x2, Pallas kernels, hidden_of(): pl.pallas_call(kernel, grid_spec=pltpu.PrefetchScalarGridSpec(num_scalar_...  19.5 us
    all_to_all x2, starting transfers between devices, returned(): x = lax.all_to_all(x, 'blk', split_axis=0, concat_axis=0, tiled=True)  15 us
    all_to_all x2, starting transfers between devices, everywhere(): lax.all_to_all(copies, 'blk', split_axis=0, concat_axis=0, tiled=True)  14.2 us
    all_to_all x2, waiting for transfers between devices, everywhere(): lax.all_to_all(copies, 'blk', split_axis=0, concat_axis=0, tiled=True)  14 us
  transfers between devices with their start and end apart: 11, of which 8 were waited for; matrix products, arithmetic and copies ran while one was open for 0% of the time, Pallas kernels for 17%

profile of v5, /device:TPU:0, one launch (start us, length us, event | category | flops | bytes accessed | tf_op | source)
XLA Modules:
  0.0 315.1 jit_solution(14640650734266364611)
XLA Ops:
  7.2 0.0 all-gather.2.cloned.1.call-start
  7.2 1.3 broadcast_in_dim.10.gain_ref
  8.5 0.0 copy-start.8
  8.5 4.3 %cast.3._ = bf16[16,96,512]{2,1,0:T(8,128)(2,1)} custom-call(f32[4608,512]{1,0:T(8,128)} %bitcast.31), custom_call_target="tpu_custom_call" | custom-call | tf_op jit(solution)/shard_map/cast/pallas_call | solution.py:392
  12.8 0.0 copy-done.8
  12.8 0.7 dynamic_slice.3
  13.5 1.4 stack.36.info
  14.8 3.0 prep.1
  17.9 0.0 all-gather.2.cloned.1.call-update
  17.9 7.4 %all-to-all-start = ((bf16[16,96,512]{2,1,0:T(8,128)(2,1)}), bf16[16,96,512]{2,1,0:T(8,128)(2,1)S(1)}, u32[]{:S(2)}, u32[]{:S(2)}) async-start(bf16[16,96,512]{2,1,0:T(8,128)(2,1)} %cast.3._), calls=%async_computation | async-start | bytes 3145728 | tf_op jit(solution)/shard_map/all_to_all | solution.py:404
  25.3 4.4 %cast.4 = bf16[16,96,512]{2,1,0:T(8,128)(2,1)} custom-call(f32[4608,512]{1,0:T(8,128)} %bitcast.32), custom_call_target="tpu_custom_call" | custom-call | tf_op jit(solution)/shard_map/cast/pallas_call | solution.py:392
  29.7 46.2 %all-to-all-done = bf16[16,96,512]{2,1,0:T(8,128)(2,1)S(1)} async-done(((bf16[16,96,512]{2,1,0:T(8,128)(2,1)}), bf16[16,96,512]{2,1,0:T(8,128)(2,1)S(1)}, u32[]{:S(2)}, u32[]{:S(2)}) %all-to-all-start) | async-done | bytes 1572896 | tf_op jit(solution)/shard_map/all_to_all | solution.py:404
  75.9 0.0 copy-start.2
  75.9 6.8 %all-to-all-start.1 = ((bf16[16,96,512]{2,1,0:T(8,128)(2,1)}), bf16[16,96,512]{2,1,0:T(8,128)(2,1)S(1)}, u32[]{:S(2)}, u32[]{:S(2)}) async-start(bf16[16,96,512]{2,1,0:T(8,128)(2,1)} %cast.4), calls=%async_computation.1 | async-start | bytes 3145728 | tf_op jit(solution)/shard_map/all_to_all | solution.py:404
  82.7 0.0 copy-done.2
  82.7 1.5 collective-permute-start
  84.3 4.3 %cast.5.x_ref = bf16[16,96,512]{2,1,0:T(8,128)(2,1)} custom-call(f32[4608,512]{1,0:T(8,128)} %bitcast.33), custom_call_target="tpu_custom_call" | custom-call | tf_op jit(solution)/shard_map/cast/pallas_call | solution.py:392
  88.6 31.1 %collective-permute-done._.g_ref.g_oth = bf16[1536,512]{1,0:T(8,128)(2,1)} collective-permute-done((bf16[1536,512]{1,0:T(8,128)(2,1)S(1)}, bf16[1536,512]{1,0:T(8,128)(2,1)}, u32[]{:S(2)}, u32[]{:S(2)}) %collective-permute-start) | collective-permute-done | bytes 1572896 | tf_op jit(solution)/shard_map/ppermute | solution.py:406
  119.6 3.4 %all-to-all-done.1 = bf16[16,96,512]{2,1,0:T(8,128)(2,1)S(1)} async-done(((bf16[16,96,512]{2,1,0:T(8,128)(2,1)}), bf16[16,96,512]{2,1,0:T(8,128)(2,1)S(1)}, u32[]{:S(2)}, u32[]{:S(2)}) %all-to-all-start.1) | async-done | bytes 1572896 | tf_op jit(solution)/shard_map/all_to_all | solution.py:404
  123.1 0.0 copy-start.3
  123.1 9.2 %all-to-all-start.2 = ((bf16[16,96,512]{2,1,0:T(8,128)(2,1)}), bf16[16,96,512]{2,1,0:T(8,128)(2,1)S(1)}, u32[]{:S(2)}, u32[]{:S(2)}) async-start(bf16[16,96,512]{2,1,0:T(8,128)(2,1)} %tie.2), calls=%async_computation.2 | async-start | bytes 3145728 | tf_op jit(solution)/shard_map/all_to_all | solution.py:404
  132.3 1.5 collective-permute-start.1
  133.8 0.0 all-gather.2.cloned.1.call-done.x_ref
  133.8 0.0 copy-done.3
  133.8 9.8 %gate_up.2 = (bf16[512,512]{1,0:T(8,128)(2,1)}, bf16[640,512]{1,0:T(8,128)(2,1)}) custom-call(s32[20]{0:T(128)} %stack.36.info, bf16[2048,1664]{1,0:T(8,128)(2,1)} %all-gather.2.cloned.1.call-done.x_ref, bf16[1536,512]{1,0:T(8,128)(2,1)} %bitcast.41, bf16[1536,512]{1,0:T(8,128)(2,1)} %bitcast.44), custom_call_target="tpu_custom_call" | custom-call | tf_op jit(solution)/shard_map/gate_up/pallas_call | solution.py:447
  143.6 20.6 %all-to-all-done.2 = bf16[16,96,512]{2,1,0:T(8,128)(2,1)S(1)} async-done(((bf16[16,96,512]{2,1,0:T(8,128)(2,1)}), bf16[16,96,512]{2,1,0:T(8,128)(2,1)S(1)}, u32[]{:S(2)}, u32[]{:S(2)}) %all-to-all-start.2) | async-done | bytes 1572896 | tf_op jit(solution)/shard_map/all_to_all | solution.py:404
  164.2 0.0 copy-start
  164.2 1.2 copy-done
  165.4 4.2 %down.2.x_ref = bf16[512,1536]{1,0:T(8,128)(2,1)} custom-call(bf16[512,512]{1,0:T(8,128)(2,1)} %get-tuple-element.15.refs_0_, bf16[1536,512]{1,0:T(8,128)(2,1)} %bitcast.34), custom_call_target="tpu_custom_call" | custom-call | tf_op jit(solution)/shard_map/down/pallas_call | solution.py:466
  169.6 0.0 collective-permute-done.1._.u_ref.u_oth
  169.6 0.0 copy-start.1
  169.6 9.3 %all-to-all-start.4 = ((bf16[16,32,1536]{2,1,0:T(8,128)(2,1)}), bf16[16,32,1536]{2,1,0:T(8,128)(2,1)}, u32[]{:S(2)}, u32[]{:S(2)}) async-start(bf16[16,32,1536]{2,1,0:T(8,128)(2,1)} %bitcast.38), calls=%async_computation.4 | async-start | bytes 3145728 | tf_op jit(solution)/shard_map/all_to_all | solution.py:480
  178.9 0.0 copy-done.1
  178.9 1.6 collective-permute-start.2
  180.5 9.7 %gate_up.3.refs_2_ = bf16[640,512]{1,0:T(8,128)(2,1)} custom-call(s32[20]{0:T(128)} %stack.36.info, bf16[2048,1664]{1,0:T(8,128)(2,1)} %all-gather.2.cloned.1.call-done.x_ref, bf16[1536,512]{1,0:T(8,128)(2,1)} %collective-permute-done._.g_ref.g_oth, bf16[1536,512]{1,0:T(8,128)(2,1)} %collective-permute-done.1._.u_ref.u_oth, bf16[512,1536]{1,0:T(8,128)(2,1)} %tie.3._), custom_call_target="tpu_custom_call" | custom-call | tf_op jit(solution)/shard_map/gate_up/pallas_call | solution.py:447
  190.1 25.5 %collective-permute-done.2.refs_3_.d_oth = bf16[1536,512]{1,0:T(8,128)(2,1)S(1)} collective-permute-done((bf16[1536,512]{1,0:T(8,128)(2,1)S(1)}, bf16[1536,512]{1,0:T(8,128)(2,1)S(1)}, u32[]{:S(2)}, u32[]{:S(2)}) %collective-permute-start.2) | collective-permute-done | bytes 1572896 | tf_op jit(solution)/shard_map/ppermute | solution.py:406
  215.6 0.0 copy-start.5
  215.6 1.2 copy-done.5
  216.8 5.7 %down.3._ = bf16[640,1536]{1,0:T(8,128)(2,1)} custom-call(bf16[640,512]{1,0:T(8,128)(2,1)} %get-tuple-element.14.refs_0_, bf16[1536,512]{1,0:T(8,128)(2,1)} %bitcast.35, bf16[640,512]{1,0:T(8,128)(2,1)} %gate_up.3.refs_2_, bf16[1536,512]{1,0:T(8,128)(2,1)} %copy-done.5), custom_call_target="tpu_custom_call" | custom-call | tf_op jit(solution)/shard_map/down/pallas_call | solution.py:466
  222.5 0.0 all-to-all-done.4
  222.5 5.8 %all-to-all-start.3 = ((bf16[16,40,1536]{2,1,0:T(8,128)(2,1)}), bf16[16,40,1536]{2,1,0:T(8,128)(2,1)S(1)}, u32[]{:S(2)}, u32[]{:S(2)}) async-start(bf16[16,40,1536]{2,1,0:T(8,128)(2,1)} %bitcast.39), calls=%async_computation.3 | async-start | bytes 3932160 | tf_op jit(solution)/shard_map/all_to_all | solution.py:480
  228.3 3.0 mix.1
  231.3 8.3 %place.1._ = bf16[3,1536,1024]{2,1,0:T(8,128)(2,1)} custom-call(s32[20]{0:T(128)} %stack.36.info, bf16[1536,512]{1,0:T(8,128)(2,1)} %bitcast.42, bf16[1536,512]{1,0:T(8,128)(2,1)} %collective-permute-done._.g_ref.g_oth, bf16[1536,512]{1,0:T(8,128)(2,1)} %bitcast.45, bf16[1536,512]{1,0:T(8,128)(2,1)} %collective-permute-done.1._.u_ref.u_oth, ...), custom_call_target="tpu_custom_call" | custom-call | tf_op jit(solution)/shard_map/place/pallas_call | solution.py:492
  239.6 3.8 %first.1.moe_ref = f32[128,1536]{1,0:T(8,128)} custom-call(bf16[384,512]{1,0:T(8,128)(2,1)} %get-tuple-element.16.mix_ref, bf16[512,1536]{1,0:T(8,128)(2,1)} %bitcast.15.back_ref), custom_call_target="tpu_custom_call" | custom-call | tf_op jit(solution)/shard_map/first/pallas_call | solution.py:529
  243.4 23.7 %all-to-all-done.3 = bf16[16,40,1536]{2,1,0:T(8,128)(2,1)S(1)} async-done(((bf16[16,40,1536]{2,1,0:T(8,128)(2,1)}), bf16[16,40,1536]{2,1,0:T(8,128)(2,1)S(1)}, u32[]{:S(2)}, u32[]{:S(2)}) %all-to-all-start.3) | async-done | bytes 1966112 | tf_op jit(solution)/shard_map/all_to_all | solution.py:480
  267.1 0.0 copy-start.4
  267.1 1.3 copy-done.4
  268.4 0.0 copy-start.6
  268.4 0.0 copy-start.7
  268.4 5.4 %combine.1 = (bf16[128,1536]{1,0:T(8,128)(2,1)}, f32[16,1,1664]{2,1,0:T(1,128)}) custom-call(s32[20]{0:T(128)} %stack.36.info, bf16[384,640]{1,0:T(8,128)(2,1)} %get-tuple-element.13.mix_ref, bf16[640,1536]{1,0:T(8,128)(2,1)} %bitcast.46, f32[128,1536]{1,0:T(8,128)} %first.1.moe_ref, bf16[128,1536]{1,0:T(8,128)(2,1)} %bitcast.48, bf16[3,1536,1024]{2,1,0:T(8,128)(2,1)} %place.1._), custom_call_target="tpu_custom_call" | custom-call | tf_op jit(solution)/shard_map/combine/pallas_call | solution.py:538
  273.9 10.7 %all-to-all-start.5 = ((f32[16,1,1664]{2,1,0:T(1,128)}), f32[16,1,1664]{2,1,0:T(1,128)S(1)}, u32[]{:S(2)}, u32[]{:S(2)}) async-start(f32[16,1,1664]{2,1,0:T(1,128)} %get-tuple-element.18), calls=%async_computation.5 | async-start | bytes 212992 | tf_op jit(solution)/shard_map/all_to_all | solution.py:559
  284.6 7.5 %all-to-all-done.5 = f32[16,1,1664]{2,1,0:T(1,128)S(1)} async-done(((f32[16,1,1664]{2,1,0:T(1,128)}), f32[16,1,1664]{2,1,0:T(1,128)S(1)}, u32[]{:S(2)}, u32[]{:S(2)}) %all-to-all-start.5) | async-done | bytes 106528 | tf_op jit(solution)/shard_map/all_to_all | solution.py:559
  292.1 0.1 multiply_reduce_fusion
  292.2 0.1 slice_reduce_fusion
  292.4 0.0 copy-done.6
  292.4 0.0 copy-done.7
  292.4 4.6 %fusion.3 = (f32[16]{0:T(128)S(1)}, f32[16]{0:T(128)S(1)}) fusion(s32[2048]{0:T(1024)S(1)} %iota_add_fusion, s32[16]{0:T(128)S(1)} %copy-done.7, bf16[2048,1536]{1,0:T(8,128)(2,1)} %param.15, f32[16,1664]{1,0:T(8,128)S(1)} %bitcast.51, f32[1536]{0:T(1024)S(1)} %copy-done.6, f32[16]{0:T(128)S(1)} %add_rsqrt_fusion), kind=kOutput, calls=%fused_computation.14 | convolution fusion | flops 100868064 | bytes 6407296 | tf_op jit(solution)/shard_map/dot_general | solution.py:569
  297.0 0.6 broadcast_in_dim.23
  297.6 3.5 %all-to-all-start.6 = ((f32[16,2,16]{2,1,0:T(2,128)}), f32[16,2,16]{2,1,0:T(2,128)S(1)}, u32[]{:S(2)}, u32[]{:S(2)}) async-start(f32[16,2,16]{2,1,0:T(2,128)} %broadcast_in_dim.23), calls=%async_computation.6 | async-start | bytes 32768 | tf_op jit(solution)/shard_map/all_to_all | solution.py:559
  301.1 6.4 %all-to-all-done.6 = f32[16,2,16]{2,1,0:T(2,128)S(1)} async-done(((f32[16,2,16]{2,1,0:T(2,128)}), f32[16,2,16]{2,1,0:T(2,128)S(1)}, u32[]{:S(2)}, u32[]{:S(2)}) %all-to-all-start.6) | async-done | bytes 2080 | tf_op jit(solution)/shard_map/all_to_all | solution.py:559
  307.6 0.6 pad_maximum_fusion
  (10 shorter events, 0.1 us)
Async XLA Ops:
  7.2 126.6 %all-gather.2.cloned.1.call-start = ((), (), s32[]{:S(2)}) async-start(), calls=%async_computation.7 | async-start | bytes 7241728 | tf_op jit(solution)/shard_map/all_gather | solution.py:444
  8.5 4.3 %copy-start.8 = (s32[16]{0:T(128)S(1)}, s32[16]{0:T(128)}, u32[]{:S(2)}) copy-start(s32[16]{0:T(128)} %param.10) | copy-start | bytes 196
  17.9 58.0 %all-to-all-start = ((bf16[16,96,512]{2,1,0:T(8,128)(2,1)}), bf16[16,96,512]{2,1,0:T(8,128)(2,1)S(1)}, u32[]{:S(2)}, u32[]{:S(2)}) async-start(bf16[16,96,512]{2,1,0:T(8,128)(2,1)} %cast.3._), calls=%async_computation | async-start | bytes 3145728 | tf_op jit(solution)/shard_map/all_to_all | solution.py:404
  75.9 6.9 %copy-start.2 = (bf16[16,96,512]{2,1,0:T(8,128)(2,1)}, bf16[16,96,512]{2,1,0:T(8,128)(2,1)S(1)}, u32[]{:S(2)}) copy-start(bf16[16,96,512]{2,1,0:T(8,128)(2,1)S(1)} %all-to-all-done) | copy-start | bytes 4718596
  75.9 47.2 %all-to-all-start.1 = ((bf16[16,96,512]{2,1,0:T(8,128)(2,1)}), bf16[16,96,512]{2,1,0:T(8,128)(2,1)S(1)}, u32[]{:S(2)}, u32[]{:S(2)}) async-start(bf16[16,96,512]{2,1,0:T(8,128)(2,1)} %cast.4), calls=%async_computation.1 | async-start | bytes 3145728 | tf_op jit(solution)/shard_map/all_to_all | solution.py:404
  82.7 36.9 %collective-permute-start = (bf16[1536,512]{1,0:T(8,128)(2,1)S(1)}, bf16[1536,512]{1,0:T(8,128)(2,1)}, u32[]{:S(2)}, u32[]{:S(2)}) collective-permute-start(bf16[1536,512]{1,0:T(8,128)(2,1)S(1)} %bitcast.40), channel_id=1, source_target_pairs={{0,1},{1,0},{2,3},{3,2},{4,5},{5,4},{6,7},{7,6},{8,9},{9,8},{10,11... | collective-permute-start | bytes 4718600 | tf_op jit(solution)/shard_map/ppermute | solution.py:406
  123.1 10.7 %copy-start.3 = (bf16[16,96,512]{2,1,0:T(8,128)(2,1)}, bf16[16,96,512]{2,1,0:T(8,128)(2,1)S(1)}, u32[]{:S(2)}) copy-start(bf16[16,96,512]{2,1,0:T(8,128)(2,1)S(1)} %all-to-all-done.1) | copy-start | bytes 4718596
  123.1 41.1 %all-to-all-start.2 = ((bf16[16,96,512]{2,1,0:T(8,128)(2,1)}), bf16[16,96,512]{2,1,0:T(8,128)(2,1)S(1)}, u32[]{:S(2)}, u32[]{:S(2)}) async-start(bf16[16,96,512]{2,1,0:T(8,128)(2,1)} %tie.2), calls=%async_computation.2 | async-start | bytes 3145728 | tf_op jit(solution)/shard_map/all_to_all | solution.py:404
  132.3 37.3 %collective-permute-start.1 = (bf16[1536,512]{1,0:T(8,128)(2,1)S(1)}, bf16[1536,512]{1,0:T(8,128)(2,1)}, u32[]{:S(2)}, u32[]{:S(2)}) collective-permute-start(bf16[1536,512]{1,0:T(8,128)(2,1)S(1)} %bitcast.43), channel_id=1, source_target_pairs={{0,1},{1,0},{2,3},{3,2},{4,5},{5,4},{6,7},{7,6},{8,9},{9,8},{10,11... | collective-permute-start | bytes 4718600 | tf_op jit(solution)/shard_map/ppermute | solution.py:406
  164.2 1.2 copy-start
  169.6 9.3 %copy-start.1 = (bf16[16,96,512]{2,1,0:T(8,128)(2,1)S(1)}, bf16[16,96,512]{2,1,0:T(8,128)(2,1)}, u32[]{:S(2)}) copy-start(bf16[16,96,512]{2,1,0:T(8,128)(2,1)} %copy-done) | copy-start | bytes 4718596
  169.6 52.9 %all-to-all-start.4 = ((bf16[16,32,1536]{2,1,0:T(8,128)(2,1)}), bf16[16,32,1536]{2,1,0:T(8,128)(2,1)}, u32[]{:S(2)}, u32[]{:S(2)}) async-start(bf16[16,32,1536]{2,1,0:T(8,128)(2,1)} %bitcast.38), calls=%async_computation.4 | async-start | bytes 3145728 | tf_op jit(solution)/shard_map/all_to_all | solution.py:480
  178.9 36.7 %collective-permute-start.2 = (bf16[1536,512]{1,0:T(8,128)(2,1)S(1)}, bf16[1536,512]{1,0:T(8,128)(2,1)S(1)}, u32[]{:S(2)}, u32[]{:S(2)}) collective-permute-start(bf16[1536,512]{1,0:T(8,128)(2,1)S(1)} %bitcast.37), channel_id=1, source_target_pairs={{0,1},{1,0},{2,3},{3,2},{4,5},{5,4},{6,7},{7,6},{8,9},{9,8},{10,11... | collective-permute-start | bytes 4718600 | tf_op jit(solution)/shard_map/ppermute | solution.py:406
  215.6 1.2 copy-start.5
  222.5 44.6 %all-to-all-start.3 = ((bf16[16,40,1536]{2,1,0:T(8,128)(2,1)}), bf16[16,40,1536]{2,1,0:T(8,128)(2,1)S(1)}, u32[]{:S(2)}, u32[]{:S(2)}) async-start(bf16[16,40,1536]{2,1,0:T(8,128)(2,1)} %bitcast.39), calls=%async_computation.3 | async-start | bytes 3932160 | tf_op jit(solution)/shard_map/all_to_all | solution.py:480
  267.1 1.3 copy-start.4
  268.4 23.9 %copy-start.6 = (f32[1536]{0:T(1024)S(1)}, f32[1536]{0:T(1024)}, u32[]{:S(2)}) copy-start(f32[1536]{0:T(1024)} %param.16) | copy-start | bytes 18436
  268.4 23.9 %copy-start.7 = (s32[16]{0:T(128)S(1)}, s32[16]{0:T(128)}, u32[]{:S(2)}) copy-start(s32[16]{0:T(128)} %param.17) | copy-start | bytes 196
  273.9 18.2 %all-to-all-start.5 = ((f32[16,1,1664]{2,1,0:T(1,128)}), f32[16,1,1664]{2,1,0:T(1,128)S(1)}, u32[]{:S(2)}, u32[]{:S(2)}) async-start(f32[16,1,1664]{2,1,0:T(1,128)} %get-tuple-element.18), calls=%async_computation.5 | async-start | bytes 212992 | tf_op jit(solution)/shard_map/all_to_all | solution.py:559
  297.6 9.9 %all-to-all-start.6 = ((f32[16,2,16]{2,1,0:T(2,128)}), f32[16,2,16]{2,1,0:T(2,128)S(1)}, u32[]{:S(2)}, u32[]{:S(2)}) async-start(f32[16,2,16]{2,1,0:T(2,128)} %broadcast_in_dim.23), calls=%async_computation.6 | async-start | bytes 32768 | tf_op jit(solution)/shard_map/all_to_all | solution.py:559
Sparse Core Ops, SparseCore 0:
  18.0 97.6 all-gather.1

commit v6 on v5

--- a/solution.py
+++ b/solution.py
@@ -252,7 +252,7 @@
         out_ref[...] = activ(picked[...], g_ref, u_ref)
 
 
-def down_kernel(*refs):
+def down_kernel(info, *refs):
     out_ref = refs[-1]
     total = 0.0
     for hidden_ref, d_ref in zip(refs[0:-1:2], refs[1:-1:2]):
@@ -300,46 +300,43 @@
     return parts[2 * rows :] + parts[rows : 2 * rows] + parts[:rows]
 
 
-def first_kernel(mix_ref, back_ref, moe_ref):
-    moe_ref[...] = weigh(mix_ref, back_ref)
-
-
-def combine_kernel(
-    info, mix_ref, back_ref, moe_ref, resid_ref, _, out_ref, told_ref, lasts, squares
-):
+def first_kernel(mix_ref, back_ref, resid_ref, base_ref):
+    base_ref[...] = resid_ref[...].astype(jnp.float32) + weigh(mix_ref, back_ref)
+
+
+def last_kernel(info, mix_ref, back_ref, base_ref, _, told_ref):
+    rows = base_ref.shape[0]
+    last = info[3] - 1
+    shape = (8, mix_ref.shape[0])
+    one_hot = jnp.where(iota(shape, 1) == iota(shape, 0) * rows + last, 1.0, 0.0)
+    mix = jnp.dot(one_hot.astype(jnp.bfloat16), mix_ref[...], preferred_element_type=jnp.float32)
+    parts = jnp.dot(mix.astype(jnp.bfloat16), back_ref[...], preferred_element_type=jnp.float32)
+    moe = parts[2:3] + parts[1:2] + parts[0:1]
+    out = (base_ref[pl.ds(last, 1), :] + moe).astype(jnp.bfloat16).astype(jnp.float32)
+    told_ref[...] = jnp.broadcast_to(out[None], told_ref.shape)
+
+
+def combine_kernel(info, mix_ref, back_ref, base_ref, _, out_ref, square_ref, squares):
     step = pl.program_id(0)
-    length = info[3]
-    moe = moe_ref[...] + weigh(mix_ref, back_ref)
 
     @pl.when(step == 0)
     def _():
         squares[...] = jnp.zeros_like(squares)
 
-    out = (resid_ref[...].astype(jnp.float32) + moe).astype(jnp.bfloat16)
+    out = (base_ref[...] + weigh(mix_ref, back_ref)).astype(jnp.bfloat16)
     out_ref[...] = out
     out_f = out.astype(jnp.float32)
     row = iota(out_f.shape, 0)
-    lasts[pl.ds(step, 1)] = jnp.sum(
-        jnp.where(row == length - 1, out_f, 0.0), axis=0, keepdims=True
-    )[None]
-    squares[...] += jnp.sum(jnp.where(row < length, out_f * out_f, 0.0), axis=0, keepdims=True)
+    squares[...] += jnp.sum(jnp.where(row < info[3], out_f * out_f, 0.0), axis=0, keepdims=True)
 
     @pl.when(step == pl.num_programs(0) - 1)
     def _():
-        count = told_ref.shape[0]
-        for k in range(lasts.shape[0]):
-            size = lasts.shape[2]
-            told_ref[:, :, k * size : (k + 1) * size] = jnp.broadcast_to(
-                lasts[k : k + 1], (count, 1, size)
-            )
-        total = jnp.sum(squares[...], axis=1, keepdims=True)[None]
-        told_ref[:, :, lasts.shape[0] * lasts.shape[2] :] = jnp.broadcast_to(
-            total, (count, 1, LANES)
-        )
-
-
-def place_kernel(info, g_own, g_oth, u_own, u_oth, d_own, d_oth, _, out_ref):
-    for k, (own, oth) in enumerate(((g_own, g_oth), (u_own, u_oth), (d_own, d_oth))):
+        total = jnp.sum(squares[...], axis=1, keepdims=True)
+        square_ref[...] = jnp.broadcast_to(total, square_ref.shape)
+
+
+def place_kernel(info, g_own, g_oth, u_own, u_oth, d_both, _, out_ref):
+    for k, (own, oth) in enumerate(((g_own, g_oth), (u_own, u_oth))):
 
         @pl.when(info[2] == 0)
         def _():
@@ -350,6 +347,9 @@
         def _():
             out_ref[k, :, :FF] = oth[...]
             out_ref[k, :, FF:] = own[...]
+
+    out_ref[2, :, :FF] = d_both[0]
+    out_ref[2, :, FF:] = d_both[1]
 
 
 def cast_kernel(blocks, x_ref, *refs):
@@ -402,8 +402,10 @@
 
     def moved(x):
         own = lax.all_to_all(x, "blk", split_axis=0, concat_axis=0, tiled=True)
-        own = own.reshape(width, FF)
-        return own, lax.ppermute(own, "rep", [(0, 1), (1, 0)])
+        return own.reshape(width, FF)
+
+    def swapped(x):
+        return lax.ppermute(x, "rep", [(0, 1), (1, 0)])
 
     def tied(x, after):
         return pl.pallas_call(
@@ -416,9 +418,12 @@
         )(x, after)
 
     g_turned = turned(0)
-    g_own, g_oth = moved(g_turned)
-    u_own, u_oth = moved(turned(1))
-    d_own, d_oth = moved(tied(turned(2), g_oth))
+    g_own = moved(g_turned)
+    g_oth = swapped(g_own)
+    u_own = moved(turned(1))
+    u_oth = swapped(u_own)
+    d_own = moved(tied(turned(2), g_oth))
+    d_both = lax.all_gather(d_own, "rep", axis=0)
 
     row_ext, pieces = pl.pallas_call(
         prep_kernel,
@@ -462,17 +467,22 @@
 
     step = 512
 
-    def outputs_of(size, *operands):
+    one = pl.BlockSpec((step, FF), lambda i, *_: (i, 0))
+    other = pl.BlockSpec((None, step, FF), lambda i, info: (1 - info[2], i, 0))
+
+    def outputs_of(size, halves, *operands):
         return pl.pallas_call(
             down_kernel,
-            grid=(width // step,),
-            in_specs=[whole((size, FF)), pl.BlockSpec((step, FF), lambda i: (i, 0))]
-            * (len(operands) // 2),
-            out_specs=pl.BlockSpec((size, step), lambda i: (0, i)),
+            grid_spec=pltpu.PrefetchScalarGridSpec(
+                num_scalar_prefetch=1,
+                grid=(width // step,),
+                in_specs=[spec for half in halves for spec in (whole((size, FF)), half)],
+                out_specs=pl.BlockSpec((size, step), lambda i, *_: (0, i)),
+            ),
             out_shape=jax.ShapeDtypeStruct((size, width), jnp.bfloat16),
             compiler_params=params(),
             name="down",
-        )(*operands)
+        )(info, *operands)
 
     def returned(x):
         slots = x.shape[0]
@@ -482,10 +492,10 @@
 
     extra = blk_count * (CAP - FIRST)
     own_hidden, late_hidden = hidden_of(own_kernel, (first, second), first + extra, g_own, u_own)
-    own_out = tied(outputs_of(first, own_hidden, d_own), u_oth)
+    own_out = tied(outputs_of(first, (one,), own_hidden, d_own), u_oth)
     own_back = returned(own_out)
     (oth_hidden,) = hidden_of(oth_kernel, (second,), second, g_oth, u_oth, own_out)
-    oth_out = outputs_of(second, late_hidden, d_own, oth_hidden, d_oth)
+    oth_out = outputs_of(second, (one, other), late_hidden, d_own, oth_hidden, d_both)
     oth_back = returned(oth_out)
 
     part = width // 4
@@ -494,14 +504,17 @@
         grid_spec=pltpu.PrefetchScalarGridSpec(
             num_scalar_prefetch=1,
             grid=(width // part,),
-            in_specs=[pl.BlockSpec((part, FF), lambda i, *_: (i, 0))] * 6
-            + [pl.BlockSpec(memory_space=pl.ANY)],
+            in_specs=[pl.BlockSpec((part, FF), lambda i, *_: (i, 0))] * 4
+            + [
+                pl.BlockSpec((2, part, FF), lambda i, *_: (0, i, 0)),
+                pl.BlockSpec(memory_space=pl.ANY),
+            ],
             out_specs=pl.BlockSpec((3, part, 2 * FF), lambda i, *_: (0, i, 0)),
         ),
         out_shape=jax.ShapeDtypeStruct((3, width, 2 * FF), jnp.bfloat16),
         compiler_params=params(),
         name="place",
-    )(info, g_own, g_oth, u_own, u_oth, d_own, d_oth, oth_out)
+    )(info, g_own, g_oth, u_own, u_oth, d_both, oth_out)
 
     first_mix, second_mix = pl.pallas_call(
         mix_kernel,
@@ -526,41 +539,48 @@
         return [whole((3 * rows, slots)), pl.BlockSpec((slots, step), lambda i, *_: (0, i))]
 
     column = pl.BlockSpec((rows, step), lambda i, *_: (0, i))
-    moe = pl.pallas_call(
+    base = pl.pallas_call(
         first_kernel,
         grid=(width // step,),
-        in_specs=weigh_specs(first),
+        in_specs=weigh_specs(first) + [column],
         out_specs=column,
         out_shape=jax.ShapeDtypeStruct((rows, width), jnp.float32),
         compiler_params=params(),
         name="first",
-    )(first_mix, own_back)
-    out_rows, told = pl.pallas_call(
+    )(first_mix, own_back, resid)
+    told = pl.pallas_call(
+        last_kernel,
+        grid_spec=pltpu.PrefetchScalarGridSpec(
+            num_scalar_prefetch=1,
+            grid=(width // step,),
+            in_specs=weigh_specs(second) + [column, pl.BlockSpec(memory_space=pl.ANY)],
+            out_specs=pl.BlockSpec((blk_count, 1, step), lambda i, *_: (0, 0, i)),
+        ),
+        out_shape=jax.ShapeDtypeStruct((blk_count, 1, width), jnp.float32),
+        compiler_params=params(),
+        name="last",
+    )(info, second_mix, oth_back, base, server)
+    out_rows, square = pl.pallas_call(
         combine_kernel,
         grid_spec=pltpu.PrefetchScalarGridSpec(
             num_scalar_prefetch=1,
             grid=(width // step,),
-            in_specs=weigh_specs(second) + [column, column, pl.BlockSpec(memory_space=pl.ANY)],
-            out_specs=[column, whole((blk_count, 1, width + LANES))],
-            scratch_shapes=[
-                pltpu.VMEM((width // step, 1, step), jnp.float32),
-                pltpu.VMEM((1, step), jnp.float32),
-            ],
+            in_specs=weigh_specs(second) + [column, pl.BlockSpec(memory_space=pl.ANY)],
+            out_specs=[column, whole((1, LANES))],
+            scratch_shapes=[pltpu.VMEM((1, step), jnp.float32)],
         ),
         out_shape=[
             jax.ShapeDtypeStruct((rows, width), jnp.bfloat16),
-            jax.ShapeDtypeStruct((blk_count, 1, width + LANES), jnp.float32),
+            jax.ShapeDtypeStruct((1, LANES), jnp.float32),
         ],
         compiler_params=params(),
         name="combine",
-    )(info, second_mix, oth_back, moe, resid, server)
+    )(info, second_mix, oth_back, base, told)
 
     def everywhere(copies):
         return lax.all_to_all(copies, "blk", split_axis=0, concat_axis=0, tiled=True)
 
-    gathered = everywhere(told)[:, 0]
-    last_rows, square_total = gathered[:, :width], gathered[:, width]
-    norms = jnp.sqrt(square_total / (lengths.astype(jnp.float32) * width) + 1e-06)
+    last_rows = everywhere(told)[:, 0]
     final = (
         last_rows
         * lax.rsqrt(jnp.mean(last_rows * last_rows, axis=-1, keepdims=True) + 1e-05)
@@ -575,9 +595,13 @@
     )
     target_part = jnp.sum(jnp.where(target_hit, logits, 0.0), axis=1)
     top_part = jnp.max(logits, axis=1)
-    stats = jnp.stack([top_part, target_part])
+    prompt = jnp.arange(blk_count, dtype=jnp.int32)
+    square_part = jnp.where(prompt == blk, square[0, :blk_count], 0.0)
+    stats = jnp.stack([top_part, target_part, square_part])
     parts = everywhere(jnp.broadcast_to(stats[None], (blk_count,) + stats.shape))
-    request_stats = jnp.stack([norms, jnp.max(parts[:, 0], axis=0), jnp.sum(parts[:, 1], axis=0)])
+    sums = jnp.sum(parts[:, 1:], axis=0)
+    norms = jnp.sqrt(sums[1] / (lengths.astype(jnp.float32) * width) + 1e-06)
+    request_stats = jnp.stack([norms, jnp.max(parts[:, 0], axis=0), sums[0]])
     return (out_rows[None], server, request_stats)
 
 

time: 316 us -> 318 us (level)
  waiting for transfers between devices: 165 us -> 152 us
  blocking collectives: 0 us -> 10.8 us
  Pallas kernels: 65.9 us -> 71.9 us
    ppermute x3 -> x2, waiting for transfers between devices: 56.6 us -> 31.1 us  [swapped(): return lax.ppermute(x, 'rep', [(0, 1), (1, 0)])]
    all_gather x0 -> x1, waiting for transfers between devices: none -> 15.8 us  [paired(): d_both = lax.all_gather(d_own, 'rep', axis=0)]
    all_to_all x2 -> x1, waiting for transfers between devices: 14 us -> 1.62 us  [everywhere(): lax.all_to_all(copies, 'blk', split_axis=0, concat_axis=0, tiled=True)]
    all_to_all x0 -> x1, blocking collectives: none -> 10.8 us  [everywhere(): lax.all_to_all(copies, 'blk', split_axis=0, concat_axis=0, tiled=True)]
    all_to_all x3, waiting for transfers between devices: 70.3 us -> 80 us  [moved(): own = lax.all_to_all(x, 'blk', split_axis=0, concat_axis=0, tiled=True)]
    pallas_call x2 -> x3, Pallas kernels: 9.91 us -> 15.9 us  [the longest x2 11.4 us: outputs_of(): pl.pallas_call(down_kernel, grid_spec=pltpu.PrefetchScalarGridSpec(num_sc...]
    all_to_all x2 -> x1, starting transfers between devices: 14.2 us -> 10.7 us  [everywhere(): lax.all_to_all(copies, 'blk', split_axis=0, concat_axis=0, tiled=True)]
  transfers between devices with their start and end apart: 11 -> 10, of which waited for: 8 -> 8; matrix products, arithmetic and copies ran while one was open for 0% -> 0% of each run, Pallas kernels for 17% -> 19%
where the time goes in v6:
time: 318 us; the launch traced here: 317 us
  waiting for transfers between devices  152 us (48%)
  Pallas kernels  71.9 us (23%)
  starting transfers between devices  55.5 us (17%)
  between operations  14.2 us (4%)
  blocking collectives  10.8 us (3%)
  local copies, waits for them, and re-layouts  6.14 us (2%)
  matrix products  4.63 us (1%)
    all_to_all x3, waiting for transfers between devices, moved(): own = lax.all_to_all(x, 'blk', split_axis=0, concat_axis=0, tiled=True)  80 us
    ppermute x2, waiting for transfers between devices, swapped(): return lax.ppermute(x, 'rep', [(0, 1), (1, 0)])  31.1 us
    all_to_all x2, waiting for transfers between devices, returned(): x = lax.all_to_all(x, 'blk', split_axis=0, concat_axis=0, tiled=True)  23.6 us
    all_to_all x3, starting transfers between devices, moved(): own = lax.all_to_all(x, 'blk', split_axis=0, concat_axis=0, tiled=True)  23.4 us
    pallas_call x2, Pallas kernels, hidden_of(): pl.pallas_call(kernel, grid_spec=pltpu.PrefetchScalarGridSpec(num_scalar_...  19.5 us
    all_to_all x2, starting transfers between devices, returned(): x = lax.all_to_all(x, 'blk', split_axis=0, concat_axis=0, tiled=True)  18.2 us
    all_gather x1, waiting for transfers between devices, paired(): d_both = lax.all_gather(d_own, 'rep', axis=0)  15.8 us
    pallas_call x3, Pallas kernels, turned(): pl.pallas_call(functools.partial(cast_kernel, blk_count), grid=(FF // LAN...  13 us
  transfers between devices with their start and end apart: 10, of which 8 were waited for; matrix products, arithmetic and copies ran while one was open for 0% of the time, Pallas kernels for 19%

profile of v6, /device:TPU:0, one launch (start us, length us, event | category | flops | bytes accessed | tf_op | source)
XLA Modules:
  0.0 316.7 jit_solution(13023585999567099045)
XLA Ops:
  7.2 0.0 all-gather.3.cloned.1.call-start
  7.2 0.0 copy-start.6
  7.2 0.0 copy-start.8
  7.2 4.3 %cast.3._ = bf16[16,96,512]{2,1,0:T(8,128)(2,1)} custom-call(f32[4608,512]{1,0:T(8,128)} %bitcast.43), custom_call_target="tpu_custom_call" | custom-call | tf_op jit(solution)/shard_map/cast/pallas_call | solution.py:392
  11.5 0.0 copy-done.6
  11.5 0.6 broadcast_in_dim.24.gain_ref
  12.1 0.0 copy-done.8
  12.1 0.6 dynamic_slice.3
  12.7 1.3 stack.34.info
  14.0 3.0 prep.1
  17.1 0.0 all-gather.3.cloned.1.call-update
  17.1 7.4 %all-to-all-start = ((bf16[16,96,512]{2,1,0:T(8,128)(2,1)}), bf16[16,96,512]{2,1,0:T(8,128)(2,1)S(1)}, u32[]{:S(2)}, u32[]{:S(2)}) async-start(bf16[16,96,512]{2,1,0:T(8,128)(2,1)} %cast.3._), calls=%async_computation | async-start | bytes 3145728 | tf_op jit(solution)/shard_map/all_to_all | solution.py:404
  24.5 4.4 %cast.4 = bf16[16,96,512]{2,1,0:T(8,128)(2,1)} custom-call(f32[4608,512]{1,0:T(8,128)} %bitcast.44), custom_call_target="tpu_custom_call" | custom-call | tf_op jit(solution)/shard_map/cast/pallas_call | solution.py:392
  28.9 46.2 %all-to-all-done = bf16[16,96,512]{2,1,0:T(8,128)(2,1)S(1)} async-done(((bf16[16,96,512]{2,1,0:T(8,128)(2,1)}), bf16[16,96,512]{2,1,0:T(8,128)(2,1)S(1)}, u32[]{:S(2)}, u32[]{:S(2)}) %all-to-all-start) | async-done | bytes 1572896 | tf_op jit(solution)/shard_map/all_to_all | solution.py:404
  75.1 0.0 copy-start.2
  75.1 6.8 %all-to-all-start.1 = ((bf16[16,96,512]{2,1,0:T(8,128)(2,1)}), bf16[16,96,512]{2,1,0:T(8,128)(2,1)S(1)}, u32[]{:S(2)}, u32[]{:S(2)}) async-start(bf16[16,96,512]{2,1,0:T(8,128)(2,1)} %cast.4), calls=%async_computation.1 | async-start | bytes 3145728 | tf_op jit(solution)/shard_map/all_to_all | solution.py:404
  81.9 0.0 copy-done.2
  82.0 1.5 collective-permute-start
  83.5 4.3 %cast.5.x_ref = bf16[16,96,512]{2,1,0:T(8,128)(2,1)} custom-call(f32[4608,512]{1,0:T(8,128)} %bitcast.45), custom_call_target="tpu_custom_call" | custom-call | tf_op jit(solution)/shard_map/cast/pallas_call | solution.py:392
  87.8 31.1 %collective-permute-done._.g_ref.g_oth = bf16[1536,512]{1,0:T(8,128)(2,1)} collective-permute-done((bf16[1536,512]{1,0:T(8,128)(2,1)S(1)}, bf16[1536,512]{1,0:T(8,128)(2,1)}, u32[]{:S(2)}, u32[]{:S(2)}) %collective-permute-start) | collective-permute-done | bytes 1572896 | tf_op jit(solution)/shard_map/ppermute | solution.py:408
  118.9 3.4 %all-to-all-done.1 = bf16[16,96,512]{2,1,0:T(8,128)(2,1)S(1)} async-done(((bf16[16,96,512]{2,1,0:T(8,128)(2,1)}), bf16[16,96,512]{2,1,0:T(8,128)(2,1)S(1)}, u32[]{:S(2)}, u32[]{:S(2)}) %all-to-all-start.1) | async-done | bytes 1572896 | tf_op jit(solution)/shard_map/all_to_all | solution.py:404
  122.3 0.0 copy-start.3
  122.3 9.2 %all-to-all-start.2 = ((bf16[16,96,512]{2,1,0:T(8,128)(2,1)}), bf16[16,96,512]{2,1,0:T(8,128)(2,1)S(1)}, u32[]{:S(2)}, u32[]{:S(2)}) async-start(bf16[16,96,512]{2,1,0:T(8,128)(2,1)} %tie.2), calls=%async_computation.2 | async-start | bytes 3145728 | tf_op jit(solution)/shard_map/all_to_all | solution.py:404
  131.5 0.0 all-gather.5.cloned.1.call-start
  131.5 1.5 collective-permute-start.1
  133.1 30.4 %all-to-all-done.2 = bf16[16,96,512]{2,1,0:T(8,128)(2,1)S(1)} async-done(((bf16[16,96,512]{2,1,0:T(8,128)(2,1)}), bf16[16,96,512]{2,1,0:T(8,128)(2,1)S(1)}, u32[]{:S(2)}, u32[]{:S(2)}) %all-to-all-start.2) | async-done | bytes 1572896 | tf_op jit(solution)/shard_map/all_to_all | solution.py:404
  163.4 0.0 copy-start
  163.4 1.1 copy-done
  164.6 0.0 all-gather.5.cloned.1.call-update
  164.6 0.0 all-gather.3.cloned.1.call-done.x_ref
  164.6 0.0 copy-done.3
  164.6 9.8 %gate_up.2 = (bf16[512,512]{1,0:T(8,128)(2,1)}, bf16[640,512]{1,0:T(8,128)(2,1)}) custom-call(s32[20]{0:T(128)} %stack.34.info, bf16[2048,1664]{1,0:T(8,128)(2,1)} %all-gather.3.cloned.1.call-done.x_ref, bf16[1536,512]{1,0:T(8,128)(2,1)} %bitcast.54, bf16[1536,512]{1,0:T(8,128)(2,1)} %bitcast.57), custom_call_target="tpu_custom_call" | custom-call | tf_op jit(solution)/shard_map/gate_up/pallas_call | solution.py:452
  174.5 5.0 %down.2.x_ref = bf16[512,1536]{1,0:T(8,128)(2,1)} custom-call(s32[20]{0:T(128)} %stack.34.info, bf16[512,512]{1,0:T(8,128)(2,1)} %get-tuple-element.15.refs_0_, bf16[1536,512]{1,0:T(8,128)(2,1)} %bitcast.48), custom_call_target="tpu_custom_call" | custom-call | tf_op jit(solution)/shard_map/down/pallas_call | solution.py:474
  179.5 0.0 collective-permute-done.1._.u_ref.u_oth
  179.5 9.1 %all-to-all-start.4 = ((bf16[16,32,1536]{2,1,0:T(8,128)(2,1)}), bf16[16,32,1536]{2,1,0:T(8,128)(2,1)S(1)}, u32[]{:S(2)}, u32[]{:S(2)}) async-start(bf16[16,32,1536]{2,1,0:T(8,128)(2,1)} %bitcast.46), calls=%async_computation.4 | async-start | bytes 3145728 | tf_op jit(solution)/shard_map/all_to_all | solution.py:490
  188.6 9.6 %gate_up.3.refs_2_ = bf16[640,512]{1,0:T(8,128)(2,1)} custom-call(s32[20]{0:T(128)} %stack.34.info, bf16[2048,1664]{1,0:T(8,128)(2,1)} %all-gather.3.cloned.1.call-done.x_ref, bf16[1536,512]{1,0:T(8,128)(2,1)} %collective-permute-done._.g_ref.g_oth, bf16[1536,512]{1,0:T(8,128)(2,1)} %collective-permute-done.1._.u_ref.u_oth, bf16[512,1536]{1,0:T(8,128)(2,1)} %tie.3._), custom_call_target="tpu_custom_call" | custom-call | tf_op jit(solution)/shard_map/gate_up/pallas_call | solution.py:452
  198.3 15.8 %all-gather.5.cloned.1.call-done.refs_3_.d_both = bf16[2,1536,512]{2,1,0:T(8,128)(2,1)} async-done(((bf16[1,1536,512]{2,1,0:T(8,128)(2,1)}), bf16[2,1536,512]{2,1,0:T(8,128)(2,1)}) %all-gather.5.cloned.1.call-update) | async-done | bytes 3145744 | tf_op jit(solution)/shard_map/all_gather | solution.py:426
  214.1 6.4 %down.3._ = bf16[640,1536]{1,0:T(8,128)(2,1)} custom-call(s32[20]{0:T(128)} %stack.34.info, bf16[640,512]{1,0:T(8,128)(2,1)} %get-tuple-element.14.refs_0_, bf16[1536,512]{1,0:T(8,128)(2,1)} %bitcast.49, bf16[640,512]{1,0:T(8,128)(2,1)} %gate_up.3.refs_2_, bf16[2,1536,512]{2,1,0:T(8,128)(2,1)} %all-gather.5.cloned.1.call-done.refs_3_.d_both), custom_call_target="tpu_custom_call" | custom-call | tf_op jit(solution)/shard_map/down/pallas_call | solution.py:474
  220.5 0.1 all-to-all-done.4
  220.6 0.0 copy-start.4
  220.6 1.2 copy-done.4
  221.8 9.1 %all-to-all-start.3 = ((bf16[16,40,1536]{2,1,0:T(8,128)(2,1)}), bf16[16,40,1536]{2,1,0:T(8,128)(2,1)S(1)}, u32[]{:S(2)}, u32[]{:S(2)}) async-start(bf16[16,40,1536]{2,1,0:T(8,128)(2,1)} %bitcast.52), calls=%async_computation.3 | async-start | bytes 3932160 | tf_op jit(solution)/shard_map/all_to_all | solution.py:490
  230.9 3.0 mix.1
  233.9 8.3 %place.1._ = bf16[3,1536,1024]{2,1,0:T(8,128)(2,1)} custom-call(s32[20]{0:T(128)} %stack.34.info, bf16[1536,512]{1,0:T(8,128)(2,1)} %bitcast.55, bf16[1536,512]{1,0:T(8,128)(2,1)} %collective-permute-done._.g_ref.g_oth, bf16[1536,512]{1,0:T(8,128)(2,1)} %bitcast.58, bf16[1536,512]{1,0:T(8,128)(2,1)} %collective-permute-done.1._.u_ref.u_oth, ...), custom_call_target="tpu_custom_call" | custom-call | tf_op jit(solution)/shard_map/place/pallas_call | solution.py:502
  242.2 4.0 %first.1.base_ref = f32[128,1536]{1,0:T(8,128)} custom-call(bf16[384,512]{1,0:T(8,128)(2,1)} %get-tuple-element.16.mix_ref, bf16[512,1536]{1,0:T(8,128)(2,1)} %bitcast.59, bf16[128,1536]{1,0:T(8,128)(2,1)} %bitcast.61), custom_call_target="tpu_custom_call" | custom-call | tf_op jit(solution)/shard_map/first/pallas_call | solution.py:542
  246.2 23.5 %all-to-all-done.3 = bf16[16,40,1536]{2,1,0:T(8,128)(2,1)S(1)} async-done(((bf16[16,40,1536]{2,1,0:T(8,128)(2,1)}), bf16[16,40,1536]{2,1,0:T(8,128)(2,1)S(1)}, u32[]{:S(2)}, u32[]{:S(2)}) %all-to-all-start.3) | async-done | bytes 1966112 | tf_op jit(solution)/shard_map/all_to_all | solution.py:490
  269.7 0.0 copy-start.1
  269.7 1.3 copy-done.1
  271.0 4.5 %last.1._ = f32[16,1,1536]{2,1,0:T(1,128)} custom-call(s32[20]{0:T(128)} %stack.34.info, bf16[384,640]{1,0:T(8,128)(2,1)} %get-tuple-element.13.mix_ref, bf16[640,1536]{1,0:T(8,128)(2,1)} %bitcast.50, f32[128,1536]{1,0:T(8,128)} %first.1.base_ref, bf16[3,1536,1024]{2,1,0:T(8,128)(2,1)} %place.1._), custom_call_target="tpu_custom_call" | custom-call | tf_op jit(solution)/shard_map/last/pallas_call | solution.py:551
  275.5 10.7 %all-to-all-start.5 = ((f32[16,1,1536]{2,1,0:T(1,128)}), f32[16,1,1536]{2,1,0:T(1,128)S(1)}, u32[]{:S(2)}, u32[]{:S(2)}) async-start(f32[16,1,1536]{2,1,0:T(1,128)} %last.1._), calls=%async_computation.5 | async-start | bytes 196608 | tf_op jit(solution)/shard_map/all_to_all | solution.py:581
  286.2 0.0 copy-start.5
  286.2 0.0 copy-start.7
  286.2 5.1 %combine.1 = (bf16[128,1536]{1,0:T(8,128)(2,1)}, f32[1,128]{1,0:T(1,128)}) custom-call(s32[20]{0:T(128)} %stack.34.info, bf16[384,640]{1,0:T(8,128)(2,1)} %get-tuple-element.13.mix_ref, bf16[640,1536]{1,0:T(8,128)(2,1)} %bitcast.51, f32[128,1536]{1,0:T(8,128)} %first.1.base_ref, f32[16,1,1536]{2,1,0:T(1,128)} %last.1._), custom_call_target="tpu_custom_call" | custom-call | tf_op jit(solution)/shard_map/combine/pallas_call | solution.py:563
  291.3 0.7 compare_select_fusion
  292.0 1.6 all-to-all-done.5
  293.6 0.1 fusion
  293.7 0.0 copy-done.5
  293.7 0.0 copy-done.7
  293.7 4.6 %fusion.7 = (f32[16]{0:T(128)S(1)}, f32[16]{0:T(128)S(1)}) fusion(s32[2048]{0:T(1024)S(1)} %iota_add_fusion, s32[16]{0:T(128)S(1)} %copy-done.7, bf16[2048,1536]{1,0:T(8,128)(2,1)} %param.15, f32[16,1,1536]{2,1,0:T(1,128)S(1)} %all-to-all-done.5, f32[1536]{0:T(1024)S(1)} %copy-done.5, f32[16]{0:T(128)S(1)} %add_rsqrt_fusion), kind=kOutput, calls=%fused_computation.17 | convolution fusion | flops 100868064 | bytes 6404352 | tf_op jit(solution)/shard_map/dot_general | solution.py:589
  298.4 10.8 %all_to_all.35 = f32[16,3,16]{2,1,0:T(4,128)S(1)} all-to-all(f32[16,3,16]{2,1,0:T(4,128)S(1)} %broadcast_in_dim.28), channel_id=1, replica_groups=mesh['blk'=16,'rep'=2] {'blk'}, dimensions={0} | all-to-all | bytes 6144 | tf_op jit(solution)/shard_map/all_to_all | solution.py:581
  309.3 0.6 pad_maximum_fusion.1
  (11 shorter events, 0.1 us)
Async XLA Ops:
  7.2 157.5 %all-gather.3.cloned.1.call-start = ((), (), s32[]{:S(2)}) async-start(), calls=%async_computation.7 | async-start | bytes 7241728 | tf_op jit(solution)/shard_map/all_gather | solution.py:449
  7.2 4.3 %copy-start.6 = (f32[1536]{0:T(1024)S(1)}, f32[1536]{0:T(1024)}, u32[]{:S(2)}) copy-start(f32[1536]{0:T(1024)} %param.13) | copy-start | bytes 18436
  7.2 4.9 %copy-start.8 = (s32[16]{0:T(128)S(1)}, s32[16]{0:T(128)}, u32[]{:S(2)}) copy-start(s32[16]{0:T(128)} %param.10) | copy-start | bytes 196
  17.1 58.0 %all-to-all-start = ((bf16[16,96,512]{2,1,0:T(8,128)(2,1)}), bf16[16,96,512]{2,1,0:T(8,128)(2,1)S(1)}, u32[]{:S(2)}, u32[]{:S(2)}) async-start(bf16[16,96,512]{2,1,0:T(8,128)(2,1)} %cast.3._), calls=%async_computation | async-start | bytes 3145728 | tf_op jit(solution)/shard_map/all_to_all | solution.py:404
  75.1 6.9 %copy-start.2 = (bf16[16,96,512]{2,1,0:T(8,128)(2,1)}, bf16[16,96,512]{2,1,0:T(8,128)(2,1)S(1)}, u32[]{:S(2)}) copy-start(bf16[16,96,512]{2,1,0:T(8,128)(2,1)S(1)} %all-to-all-done) | copy-start | bytes 4718596
  75.1 47.2 %all-to-all-start.1 = ((bf16[16,96,512]{2,1,0:T(8,128)(2,1)}), bf16[16,96,512]{2,1,0:T(8,128)(2,1)S(1)}, u32[]{:S(2)}, u32[]{:S(2)}) async-start(bf16[16,96,512]{2,1,0:T(8,128)(2,1)} %cast.4), calls=%async_computation.1 | async-start | bytes 3145728 | tf_op jit(solution)/shard_map/all_to_all | solution.py:404
  82.0 36.9 %collective-permute-start = (bf16[1536,512]{1,0:T(8,128)(2,1)S(1)}, bf16[1536,512]{1,0:T(8,128)(2,1)}, u32[]{:S(2)}, u32[]{:S(2)}) collective-permute-start(bf16[1536,512]{1,0:T(8,128)(2,1)S(1)} %bitcast.53), channel_id=1, source_target_pairs={{0,1},{1,0},{2,3},{3,2},{4,5},{5,4},{6,7},{7,6},{8,9},{9,8},{10,11... | collective-permute-start | bytes 4718600 | tf_op jit(solution)/shard_map/ppermute | solution.py:408
  122.3 42.3 %copy-start.3 = (bf16[16,96,512]{2,1,0:T(8,128)(2,1)}, bf16[16,96,512]{2,1,0:T(8,128)(2,1)S(1)}, u32[]{:S(2)}) copy-start(bf16[16,96,512]{2,1,0:T(8,128)(2,1)S(1)} %all-to-all-done.1) | copy-start | bytes 4718596
  122.3 41.1 %all-to-all-start.2 = ((bf16[16,96,512]{2,1,0:T(8,128)(2,1)}), bf16[16,96,512]{2,1,0:T(8,128)(2,1)S(1)}, u32[]{:S(2)}, u32[]{:S(2)}) async-start(bf16[16,96,512]{2,1,0:T(8,128)(2,1)} %tie.2), calls=%async_computation.2 | async-start | bytes 3145728 | tf_op jit(solution)/shard_map/all_to_all | solution.py:404
  131.5 82.6 %all-gather.5.cloned.1.call-start = ((), (), s32[]{:S(2)}) async-start(), calls=%async_computation.8 | async-start | bytes 4718592 | tf_op jit(solution)/shard_map/all_gather | solution.py:426
  131.5 48.0 %collective-permute-start.1 = (bf16[1536,512]{1,0:T(8,128)(2,1)S(1)}, bf16[1536,512]{1,0:T(8,128)(2,1)}, u32[]{:S(2)}, u32[]{:S(2)}) collective-permute-start(bf16[1536,512]{1,0:T(8,128)(2,1)S(1)} %bitcast.56), channel_id=1, source_target_pairs={{0,1},{1,0},{2,3},{3,2},{4,5},{5,4},{6,7},{7,6},{8,9},{9,8},{10,11... | collective-permute-start | bytes 4718600 | tf_op jit(solution)/shard_map/ppermute | solution.py:408
  163.4 1.1 copy-start
  179.5 41.1 %all-to-all-start.4 = ((bf16[16,32,1536]{2,1,0:T(8,128)(2,1)}), bf16[16,32,1536]{2,1,0:T(8,128)(2,1)S(1)}, u32[]{:S(2)}, u32[]{:S(2)}) async-start(bf16[16,32,1536]{2,1,0:T(8,128)(2,1)} %bitcast.46), calls=%async_computation.4 | async-start | bytes 3145728 | tf_op jit(solution)/shard_map/all_to_all | solution.py:490
  220.6 1.2 copy-start.4
  221.8 47.9 %all-to-all-start.3 = ((bf16[16,40,1536]{2,1,0:T(8,128)(2,1)}), bf16[16,40,1536]{2,1,0:T(8,128)(2,1)S(1)}, u32[]{:S(2)}, u32[]{:S(2)}) async-start(bf16[16,40,1536]{2,1,0:T(8,128)(2,1)} %bitcast.52), calls=%async_computation.3 | async-start | bytes 3932160 | tf_op jit(solution)/shard_map/all_to_all | solution.py:490
  269.7 1.3 copy-start.1
  275.5 18.1 %all-to-all-start.5 = ((f32[16,1,1536]{2,1,0:T(1,128)}), f32[16,1,1536]{2,1,0:T(1,128)S(1)}, u32[]{:S(2)}, u32[]{:S(2)}) async-start(f32[16,1,1536]{2,1,0:T(1,128)} %last.1._), calls=%async_computation.5 | async-start | bytes 196608 | tf_op jit(solution)/shard_map/all_to_all | solution.py:581
  286.2 7.5 %copy-start.5 = (f32[1536]{0:T(1024)S(1)}, f32[1536]{0:T(1024)}, u32[]{:S(2)}) copy-start(f32[1536]{0:T(1024)} %param.16) | copy-start | bytes 18436
  286.2 7.5 %copy-start.7 = (s32[16]{0:T(128)S(1)}, s32[16]{0:T(128)}, u32[]{:S(2)}) copy-start(s32[16]{0:T(128)} %param.17) | copy-start | bytes 196
Sparse Core Ops, SparseCore 0:
  17.2 97.6 all-gather.2
  164.7 49.3 all-gather.4

commit v7 on v6

--- a/solution.py
+++ b/solution.py
@@ -252,7 +252,7 @@
         out_ref[...] = activ(picked[...], g_ref, u_ref)
 
 
-def down_kernel(info, *refs):
+def down_kernel(*refs):
     out_ref = refs[-1]
     total = 0.0
     for hidden_ref, d_ref in zip(refs[0:-1:2], refs[1:-1:2]):
@@ -335,8 +335,8 @@
         square_ref[...] = jnp.broadcast_to(total, square_ref.shape)
 
 
-def place_kernel(info, g_own, g_oth, u_own, u_oth, d_both, _, out_ref):
-    for k, (own, oth) in enumerate(((g_own, g_oth), (u_own, u_oth))):
+def place_kernel(info, g_own, g_oth, u_own, u_oth, d_own, d_oth, _, out_ref):
+    for k, (own, oth) in enumerate(((g_own, g_oth), (u_own, u_oth), (d_own, d_oth))):
 
         @pl.when(info[2] == 0)
         def _():
@@ -347,9 +347,6 @@
         def _():
             out_ref[k, :, :FF] = oth[...]
             out_ref[k, :, FF:] = own[...]
-
-    out_ref[2, :, :FF] = d_both[0]
-    out_ref[2, :, FF:] = d_both[1]
 
 
 def cast_kernel(blocks, x_ref, *refs):
@@ -365,6 +362,10 @@
 
 def params():
     return pltpu.CompilerParams(vmem_limit_bytes=VMEM, dimension_semantics=("arbitrary",))
+
+
+def cost(macs, size):
+    return pl.CostEstimate(flops=2 * macs, bytes_accessed=size, transcendentals=0)
 
 
 def whole(shape):
@@ -393,10 +394,11 @@
             functools.partial(cast_kernel, blk_count),
             grid=(FF // LANES,),
             in_specs=[pl.BlockSpec((shard_rows * blk_count, LANES), lambda i: (k, i))]
-            + [pl.BlockSpec(memory_space=pl.ANY)] * len(after),
+            + [pl.BlockSpec(memory_space=pltpu.HBM)] * len(after),
             out_specs=pl.BlockSpec((blk_count, shard_rows, LANES), lambda i: (0, 0, i)),
             out_shape=jax.ShapeDtypeStruct((blk_count, shard_rows, FF), jnp.bfloat16),
             compiler_params=params(),
+            cost_estimate=cost(0, 6 * shard_rows * blk_count * FF),
             name="cast",
         )(flat, *after)
 
@@ -410,10 +412,11 @@
     def tied(x, after):
         return pl.pallas_call(
             tie_kernel,
-            in_specs=[pl.BlockSpec(memory_space=pl.ANY)] * 2,
-            out_specs=pl.BlockSpec(memory_space=pl.ANY),
+            in_specs=[pl.BlockSpec(memory_space=pltpu.HBM)] * 2,
+            out_specs=pl.BlockSpec(memory_space=pltpu.HBM),
             out_shape=jax.ShapeDtypeStruct(x.shape, x.dtype),
             input_output_aliases={0: 0},
+            cost_estimate=cost(0, 0),
             name="tie",
         )(x, after)
 
@@ -423,7 +426,6 @@
     u_own = moved(turned(1))
     u_oth = swapped(u_own)
     d_own = moved(tied(turned(2), g_oth))
-    d_both = lax.all_gather(d_own, "rep", axis=0)
 
     row_ext, pieces = pl.pallas_call(
         prep_kernel,
@@ -435,7 +437,7 @@
                 whole((routes.shape[2], rows)),
                 whole((routes.shape[2], rows)),
                 whole((1, width)),
-                pl.BlockSpec(memory_space=pl.ANY),
+                pl.BlockSpec(memory_space=pltpu.HBM),
             ],
             out_specs=[whole((rows, width + LANES)), whole((3 * rows, LANES))],
         ),
@@ -444,6 +446,7 @@
             jax.ShapeDtypeStruct((3 * rows, LANES), jnp.bfloat16),
         ],
         compiler_params=params(),
+        cost_estimate=cost(rows * rows * LANES, 6 * rows * width),
         name="prep",
     )(info, resid, routes[0].T, route_weights[0].T, norm_gain[None], g_turned)
     tokens = lax.all_gather(row_ext, "blk", axis_index_groups=[list(RING)], axis=0, tiled=True)
@@ -456,33 +459,30 @@
                 grid=(GROUPS,),
                 in_specs=[pl.BlockSpec((blk_count // GROUPS * rows, width + LANES), lambda i, *_: (i, 0))]
                 + [whole((width, FF))] * 2
-                + [pl.BlockSpec(memory_space=pl.ANY)] * len(after),
+                + [pl.BlockSpec(memory_space=pltpu.HBM)] * len(after),
                 out_specs=[whole((size, FF)) for size in sizes],
                 scratch_shapes=[pltpu.VMEM((scratch, width), jnp.float32)],
             ),
             out_shape=[jax.ShapeDtypeStruct((size, FF), jnp.bfloat16) for size in sizes],
             compiler_params=params(),
+            cost_estimate=cost(2 * scratch * width * FF, 2 * (tokens.size + g.size + u.size)),
             name="gate_up",
         )(info, tokens, g, u, *after)
 
     step = 512
 
-    one = pl.BlockSpec((step, FF), lambda i, *_: (i, 0))
-    other = pl.BlockSpec((None, step, FF), lambda i, info: (1 - info[2], i, 0))
-
-    def outputs_of(size, halves, *operands):
+    def outputs_of(size, *operands):
         return pl.pallas_call(
             down_kernel,
-            grid_spec=pltpu.PrefetchScalarGridSpec(
-                num_scalar_prefetch=1,
-                grid=(width // step,),
-                in_specs=[spec for half in halves for spec in (whole((size, FF)), half)],
-                out_specs=pl.BlockSpec((size, step), lambda i, *_: (0, i)),
-            ),
+            grid=(width // step,),
+            in_specs=[whole((size, FF)), pl.BlockSpec((step, FF), lambda i: (i, 0))]
+            * (len(operands) // 2),
+            out_specs=pl.BlockSpec((size, step), lambda i: (0, i)),
             out_shape=jax.ShapeDtypeStruct((size, width), jnp.bfloat16),
             compiler_params=params(),
+            cost_estimate=cost(size * FF * width * len(operands) // 2, size * 4 * width),
             name="down",
-        )(info, *operands)
+        )(*operands)
 
     def returned(x):
         slots = x.shape[0]
@@ -492,10 +492,12 @@
 
     extra = blk_count * (CAP - FIRST)
     own_hidden, late_hidden = hidden_of(own_kernel, (first, second), first + extra, g_own, u_own)
-    own_out = tied(outputs_of(first, (one,), own_hidden, d_own), u_oth)
+    d_own = tied(d_own, own_hidden)
+    d_oth = swapped(d_own)
+    own_out = tied(outputs_of(first, own_hidden, d_own), u_oth)
     own_back = returned(own_out)
     (oth_hidden,) = hidden_of(oth_kernel, (second,), second, g_oth, u_oth, own_out)
-    oth_out = outputs_of(second, (one, other), late_hidden, d_own, oth_hidden, d_both)
+    oth_out = outputs_of(second, late_hidden, d_own, oth_hidden, d_oth)
     oth_back = returned(oth_out)
 
     part = width // 4
@@ -504,17 +506,15 @@
         grid_spec=pltpu.PrefetchScalarGridSpec(
             num_scalar_prefetch=1,
             grid=(width // part,),
-            in_specs=[pl.BlockSpec((part, FF), lambda i, *_: (i, 0))] * 4
-            + [
-                pl.BlockSpec((2, part, FF), lambda i, *_: (0, i, 0)),
-                pl.BlockSpec(memory_space=pl.ANY),
-            ],
+            in_specs=[pl.BlockSpec((part, FF), lambda i, *_: (i, 0))] * 6
+            + [pl.BlockSpec(memory_space=pltpu.HBM)],
             out_specs=pl.BlockSpec((3, part, 2 * FF), lambda i, *_: (0, i, 0)),
         ),
         out_shape=jax.ShapeDtypeStruct((3, width, 2 * FF), jnp.bfloat16),
         compiler_params=params(),
+        cost_estimate=cost(0, 12 * width * FF * 2),
         name="place",
-    )(info, g_own, g_oth, u_own, u_oth, d_both, oth_out)
+    )(info, g_own, g_oth, u_own, u_oth, d_own, d_oth, oth_out)
 
     first_mix, second_mix = pl.pallas_call(
         mix_kernel,
@@ -532,6 +532,7 @@
             jax.ShapeDtypeStruct((3 * rows, second), jnp.bfloat16),
         ],
         compiler_params=params(),
+        cost_estimate=cost(3 * rows * LANES * (first + second), 6 * rows * (first + second)),
         name="mix",
     )(info, row_ext, pieces)
 
@@ -546,6 +547,7 @@
         out_specs=column,
         out_shape=jax.ShapeDtypeStruct((rows, width), jnp.float32),
         compiler_params=params(),
+        cost_estimate=cost(3 * rows * first * width, 2 * first * width + 6 * rows * width),
         name="first",
     )(first_mix, own_back, resid)
     told = pl.pallas_call(
@@ -553,11 +555,12 @@
         grid_spec=pltpu.PrefetchScalarGridSpec(
             num_scalar_prefetch=1,
             grid=(width // step,),
-            in_specs=weigh_specs(second) + [column, pl.BlockSpec(memory_space=pl.ANY)],
+            in_specs=weigh_specs(second) + [column, pl.BlockSpec(memory_space=pltpu.HBM)],
             out_specs=pl.BlockSpec((blk_count, 1, step), lambda i, *_: (0, 0, i)),
         ),
         out_shape=jax.ShapeDtypeStruct((blk_count, 1, width), jnp.float32),
         compiler_params=params(),
+        cost_estimate=cost(8 * second * width, 2 * second * width + 4 * rows * width),
         name="last",
     )(info, second_mix, oth_back, base, server)
     out_rows, square = pl.pallas_call(
@@ -565,7 +568,7 @@
         grid_spec=pltpu.PrefetchScalarGridSpec(
             num_scalar_prefetch=1,
             grid=(width // step,),
-            in_specs=weigh_specs(second) + [column, pl.BlockSpec(memory_space=pl.ANY)],
+            in_specs=weigh_specs(second) + [column, pl.BlockSpec(memory_space=pltpu.HBM)],
             out_specs=[column, whole((1, LANES))],
             scratch_shapes=[pltpu.VMEM((1, step), jnp.float32)],
         ),
@@ -574,6 +577,7 @@
             jax.ShapeDtypeStruct((1, LANES), jnp.float32),
         ],
         compiler_params=params(),
+        cost_estimate=cost(3 * rows * second * width, 2 * second * width + 6 * rows * width),
         name="combine",
     )(info, second_mix, oth_back, base, told)
 

time: 318 us -> 320 us (level)
  waiting for transfers between devices: 152 us -> 157 us
    ppermute x2 -> x3, waiting for transfers between devices: 31.1 us -> 56.7 us  [swapped(): return lax.ppermute(x, 'rep', [(0, 1), (1, 0)])]
    all_gather x1 -> x0, waiting for transfers between devices: 15.8 us -> none  [paired(): d_both = lax.all_gather(d_own, 'rep', axis=0)]
    all_to_all x3, waiting for transfers between devices: 80 us -> 70.2 us  [moved(): own = lax.all_to_all(x, 'blk', split_axis=0, concat_axis=0, tiled=True)]
    all_to_all x1, waiting for transfers between devices: 1.62 us -> 6.75 us  [everywhere(): lax.all_to_all(copies, 'blk', split_axis=0, concat_axis=0, tiled=True)]
    all_to_all x2, starting transfers between devices: 18.2 us -> 15 us  [returned(): x = lax.all_to_all(x, 'blk', split_axis=0, concat_axis=0, tiled=True)]
    pallas_call x4 -> x5, Pallas kernels: 11.4 us -> 9.92 us  [the longest x2 9.92 us: outputs_of(): pl.pallas_call(down_kernel, grid=(width // step,), in_specs=[whole((size,...]
  transfers between devices with their start and end apart: 10 -> 10, of which waited for: 8 -> 7; matrix products, arithmetic and copies ran while one was open for 0% -> 0% of each run, Pallas kernels for 19% -> 17%
where the time goes in v7:
time: 320 us; the launch traced here: 319 us
  waiting for transfers between devices  157 us (49%)
  Pallas kernels  70.3 us (22%)
  starting transfers between devices  53.7 us (17%)
  between operations  14.2 us (4%)
  blocking collectives  9.2 us (3%)
  local copies, waits for them, and re-layouts  7.86 us (2%)
  matrix products  4.63 us (1%)
    all_to_all x3, waiting for transfers between devices, moved(): own = lax.all_to_all(x, 'blk', split_axis=0, concat_axis=0, tiled=True)  70.2 us
    ppermute x3, waiting for transfers between devices, swapped(): return lax.ppermute(x, 'rep', [(0, 1), (1, 0)])  56.7 us
    all_to_all x2, waiting for transfers between devices, returned(): x = lax.all_to_all(x, 'blk', split_axis=0, concat_axis=0, tiled=True)  23.5 us
    all_to_all x3, starting transfers between devices, moved(): own = lax.all_to_all(x, 'blk', split_axis=0, concat_axis=0, tiled=True)  23.4 us
    pallas_call x2, Pallas kernels, hidden_of(): pl.pallas_call(kernel, grid_spec=pltpu.PrefetchScalarGridSpec(num_scalar_...  19.5 us
    all_to_all x2, starting transfers between devices, returned(): x = lax.all_to_all(x, 'blk', split_axis=0, concat_axis=0, tiled=True)  15 us
    pallas_call x3, Pallas kernels, turned(): pl.pallas_call(functools.partial(cast_kernel, blk_count), grid=(FF // LAN...  13 us
    all_to_all x1, starting transfers between devices, everywhere(): lax.all_to_all(copies, 'blk', split_axis=0, concat_axis=0, tiled=True)  10.7 us
  transfers between devices with their start and end apart: 10, of which 7 were waited for; matrix products, arithmetic and copies ran while one was open for 0% of the time, Pallas kernels for 17%

profile of v7, /device:TPU:0, one launch (start us, length us, event | category | flops | bytes accessed | tf_op | source)
XLA Modules:
  0.0 318.5 jit_solution(13264783780925809860)
XLA Ops:
  7.2 0.0 all-gather.2.cloned.1.call-start
  7.2 1.3 broadcast_in_dim.24.gain_ref
  8.5 0.0 copy-start.9
  8.5 4.3 %cast.3._ = bf16[16,96,512]{2,1,0:T(8,128)(2,1)} custom-call(f32[4608,512]{1,0:T(8,128)} %bitcast.42), custom_call_target="tpu_custom_call" | custom-call | bytes 4718592 | tf_op jit(solution)/shard_map/cast/pallas_call | solution.py:393
  12.8 0.0 copy-done.9
  12.8 0.6 dynamic_slice.3
  13.4 1.2 stack.34.info
  14.6 3.0 prep.1
  17.6 0.0 all-gather.2.cloned.1.call-update
  17.6 7.4 %all-to-all-start = ((bf16[16,96,512]{2,1,0:T(8,128)(2,1)}), bf16[16,96,512]{2,1,0:T(8,128)(2,1)S(1)}, u32[]{:S(2)}, u32[]{:S(2)}) async-start(bf16[16,96,512]{2,1,0:T(8,128)(2,1)} %cast.3._), calls=%async_computation | async-start | bytes 3145728 | tf_op jit(solution)/shard_map/all_to_all | solution.py:406
  25.1 4.4 %cast.4 = bf16[16,96,512]{2,1,0:T(8,128)(2,1)} custom-call(f32[4608,512]{1,0:T(8,128)} %bitcast.43), custom_call_target="tpu_custom_call" | custom-call | bytes 4718592 | tf_op jit(solution)/shard_map/cast/pallas_call | solution.py:393
  29.4 46.2 %all-to-all-done = bf16[16,96,512]{2,1,0:T(8,128)(2,1)S(1)} async-done(((bf16[16,96,512]{2,1,0:T(8,128)(2,1)}), bf16[16,96,512]{2,1,0:T(8,128)(2,1)S(1)}, u32[]{:S(2)}, u32[]{:S(2)}) %all-to-all-start) | async-done | bytes 1572896 | tf_op jit(solution)/shard_map/all_to_all | solution.py:406
  75.6 0.0 copy-start.3
  75.6 6.8 %all-to-all-start.1 = ((bf16[16,96,512]{2,1,0:T(8,128)(2,1)}), bf16[16,96,512]{2,1,0:T(8,128)(2,1)S(1)}, u32[]{:S(2)}, u32[]{:S(2)}) async-start(bf16[16,96,512]{2,1,0:T(8,128)(2,1)} %cast.4), calls=%async_computation.1 | async-start | bytes 3145728 | tf_op jit(solution)/shard_map/all_to_all | solution.py:406
  82.5 0.0 copy-done.3
  82.5 1.5 collective-permute-start
  84.0 4.3 %cast.5.x_ref = bf16[16,96,512]{2,1,0:T(8,128)(2,1)} custom-call(f32[4608,512]{1,0:T(8,128)} %bitcast.44), custom_call_target="tpu_custom_call" | custom-call | bytes 4718592 | tf_op jit(solution)/shard_map/cast/pallas_call | solution.py:393
  88.3 31.1 %collective-permute-done._.g_ref.g_oth = bf16[1536,512]{1,0:T(8,128)(2,1)} collective-permute-done((bf16[1536,512]{1,0:T(8,128)(2,1)S(1)}, bf16[1536,512]{1,0:T(8,128)(2,1)}, u32[]{:S(2)}, u32[]{:S(2)}) %collective-permute-start) | collective-permute-done | bytes 1572896 | tf_op jit(solution)/shard_map/ppermute | solution.py:410
  119.4 3.4 %all-to-all-done.1 = bf16[16,96,512]{2,1,0:T(8,128)(2,1)S(1)} async-done(((bf16[16,96,512]{2,1,0:T(8,128)(2,1)}), bf16[16,96,512]{2,1,0:T(8,128)(2,1)S(1)}, u32[]{:S(2)}, u32[]{:S(2)}) %all-to-all-start.1) | async-done | bytes 1572896 | tf_op jit(solution)/shard_map/all_to_all | solution.py:406
  122.8 0.0 copy-start.4
  122.9 9.2 %all-to-all-start.2 = ((bf16[16,96,512]{2,1,0:T(8,128)(2,1)}), bf16[16,96,512]{2,1,0:T(8,128)(2,1)S(1)}, u32[]{:S(2)}, u32[]{:S(2)}) async-start(bf16[16,96,512]{2,1,0:T(8,128)(2,1)} %tie.3), calls=%async_computation.2 | async-start | bytes 3145728 | tf_op jit(solution)/shard_map/all_to_all | solution.py:406
  132.0 1.5 collective-permute-start.1
  133.6 0.0 all-gather.2.cloned.1.call-done.x_ref
  133.6 0.0 copy-done.4
  133.6 9.8 %gate_up.2 = (bf16[512,512]{1,0:T(8,128)(2,1)}, bf16[640,512]{1,0:T(8,128)(2,1)}) custom-call(s32[20]{0:T(128)} %stack.34.info, bf16[2048,1664]{1,0:T(8,128)(2,1)} %all-gather.2.cloned.1.call-done.x_ref, bf16[1536,512]{1,0:T(8,128)(2,1)} %bitcast.50, bf16[1536,512]{1,0:T(8,128)(2,1)} %bitcast.53), custom_call_target="tpu_custom_call" | custom-call | flops 1811939328 | bytes 9961472 | tf_op jit(solution)/shard_map/gate_up/pallas_call | solution.py:455
  143.4 20.6 %all-to-all-done.2 = bf16[16,96,512]{2,1,0:T(8,128)(2,1)S(1)} async-done(((bf16[16,96,512]{2,1,0:T(8,128)(2,1)}), bf16[16,96,512]{2,1,0:T(8,128)(2,1)S(1)}, u32[]{:S(2)}, u32[]{:S(2)}) %all-to-all-start.2) | async-done | bytes 1572896 | tf_op jit(solution)/shard_map/all_to_all | solution.py:406
  164.0 0.0 copy-start
  164.0 1.1 copy-done
  165.1 4.2 %down.2.x_ref = bf16[512,1536]{1,0:T(8,128)(2,1)} custom-call(bf16[512,512]{1,0:T(8,128)(2,1)} %get-tuple-element.15._.refs_0_, bf16[1536,512]{1,0:T(8,128)(2,1)} %tie.4.refs_1_.d_own), custom_call_target="tpu_custom_call" | custom-call | flops 805306368 | bytes 3145728 | tf_op jit(solution)/shard_map/down/pallas_call | solution.py:475
  169.3 0.0 collective-permute-done.1._.u_ref.u_oth
  169.3 0.0 copy-start.1
  169.3 9.2 %all-to-all-start.4 = ((bf16[16,32,1536]{2,1,0:T(8,128)(2,1)}), bf16[16,32,1536]{2,1,0:T(8,128)(2,1)S(1)}, u32[]{:S(2)}, u32[]{:S(2)}) async-start(bf16[16,32,1536]{2,1,0:T(8,128)(2,1)} %bitcast.46), calls=%async_computation.4 | async-start | bytes 3145728 | tf_op jit(solution)/shard_map/all_to_all | solution.py:490
  178.6 0.0 copy-done.1
  178.6 1.5 collective-permute-start.2
  180.1 9.6 %gate_up.3.refs_2_ = bf16[640,512]{1,0:T(8,128)(2,1)} custom-call(s32[20]{0:T(128)} %stack.34.info, bf16[2048,1664]{1,0:T(8,128)(2,1)} %all-gather.2.cloned.1.call-done.x_ref, bf16[1536,512]{1,0:T(8,128)(2,1)} %collective-permute-done._.g_ref.g_oth, bf16[1536,512]{1,0:T(8,128)(2,1)} %collective-permute-done.1._.u_ref.u_oth, bf16[512,1536]{1,0:T(8,128)(2,1)} %tie.5._), custom_call_target="tpu_custom_call" | custom-call | flops 2013265920 | bytes 9961472 | tf_op jit(solution)/shard_map/gate_up/pallas_call | solution.py:455
  189.8 25.6 %collective-permute-done.2.refs_3_.d_oth = bf16[1536,512]{1,0:T(8,128)(2,1)S(1)} collective-permute-done((bf16[1536,512]{1,0:T(8,128)(2,1)S(1)}, bf16[1536,512]{1,0:T(8,128)(2,1)S(1)}, u32[]{:S(2)}, u32[]{:S(2)}) %collective-permute-start.2) | collective-permute-done | bytes 1572896 | tf_op jit(solution)/shard_map/ppermute | solution.py:410
  215.4 0.0 copy-start.6
  215.4 1.2 copy-done.6
  216.6 5.7 %down.3._ = bf16[640,1536]{1,0:T(8,128)(2,1)} custom-call(bf16[640,512]{1,0:T(8,128)(2,1)} %get-tuple-element.14.refs_0_, bf16[1536,512]{1,0:T(8,128)(2,1)} %tie.4.refs_1_.d_own, bf16[640,512]{1,0:T(8,128)(2,1)} %gate_up.3.refs_2_, bf16[1536,512]{1,0:T(8,128)(2,1)} %copy-done.6), custom_call_target="tpu_custom_call" | custom-call | flops 2013265920 | bytes 3932160 | tf_op jit(solution)/shard_map/down/pallas_call | solution.py:475
  222.3 0.0 all-to-all-done.4
  222.3 0.0 copy-start.5
  222.3 1.1 copy-done.5
  223.4 5.7 %all-to-all-start.3 = ((bf16[16,40,1536]{2,1,0:T(8,128)(2,1)}), bf16[16,40,1536]{2,1,0:T(8,128)(2,1)S(1)}, u32[]{:S(2)}, u32[]{:S(2)}) async-start(bf16[16,40,1536]{2,1,0:T(8,128)(2,1)} %bitcast.55), calls=%async_computation.3 | async-start | bytes 3932160 | tf_op jit(solution)/shard_map/all_to_all | solution.py:490
  229.2 3.1 mix.1
  232.3 8.3 %place.1._ = bf16[3,1536,1024]{2,1,0:T(8,128)(2,1)} custom-call(s32[20]{0:T(128)} %stack.34.info, bf16[1536,512]{1,0:T(8,128)(2,1)} %bitcast.51, bf16[1536,512]{1,0:T(8,128)(2,1)} %collective-permute-done._.g_ref.g_oth, bf16[1536,512]{1,0:T(8,128)(2,1)} %bitcast.54, bf16[1536,512]{1,0:T(8,128)(2,1)} %collective-permute-done.1._.u_ref.u_oth, ...), custom_call_target="tpu_custom_call" | custom-call | bytes 18874368 | tf_op jit(solution)/shard_map/place/pallas_call | solution.py:504
  240.5 4.0 %first.1.base_ref = f32[128,1536]{1,0:T(8,128)} custom-call(bf16[384,512]{1,0:T(8,128)(2,1)} %get-tuple-element.16.mix_ref, bf16[512,1536]{1,0:T(8,128)(2,1)} %bitcast.56, bf16[128,1536]{1,0:T(8,128)(2,1)} %bitcast.58), custom_call_target="tpu_custom_call" | custom-call | flops 603979776 | bytes 2752512 | tf_op jit(solution)/shard_map/first/pallas_call | solution.py:543
  244.5 23.5 %all-to-all-done.3 = bf16[16,40,1536]{2,1,0:T(8,128)(2,1)S(1)} async-done(((bf16[16,40,1536]{2,1,0:T(8,128)(2,1)}), bf16[16,40,1536]{2,1,0:T(8,128)(2,1)S(1)}, u32[]{:S(2)}, u32[]{:S(2)}) %all-to-all-start.3) | async-done | bytes 1966112 | tf_op jit(solution)/shard_map/all_to_all | solution.py:490
  268.0 0.0 copy-start.2
  268.0 1.3 copy-done.2
  269.3 4.5 %last.1._ = f32[16,1,1536]{2,1,0:T(1,128)} custom-call(s32[20]{0:T(128)} %stack.34.info, bf16[384,640]{1,0:T(8,128)(2,1)} %get-tuple-element.13.mix_ref, bf16[640,1536]{1,0:T(8,128)(2,1)} %bitcast.47, f32[128,1536]{1,0:T(8,128)} %first.1.base_ref, bf16[3,1536,1024]{2,1,0:T(8,128)(2,1)} %place.1._), custom_call_target="tpu_custom_call" | custom-call | flops 15728640 | bytes 2752512 | tf_op jit(solution)/shard_map/last/pallas_call | solution.py:553
  273.8 0.0 copy-start.7
  273.8 0.0 copy-start.8
  273.8 5.1 %combine.1 = (bf16[128,1536]{1,0:T(8,128)(2,1)}, f32[1,128]{1,0:T(1,128)}) custom-call(s32[20]{0:T(128)} %stack.34.info, bf16[384,640]{1,0:T(8,128)(2,1)} %get-tuple-element.13.mix_ref, bf16[640,1536]{1,0:T(8,128)(2,1)} %bitcast.48, f32[128,1536]{1,0:T(8,128)} %first.1.base_ref, f32[16,1,1536]{2,1,0:T(1,128)} %last.1._), custom_call_target="tpu_custom_call" | custom-call | flops 754974720 | bytes 3145728 | tf_op jit(solution)/shard_map/combine/pallas_call | solution.py:566
  278.9 10.7 %all-to-all-start.5 = ((f32[16,1,1536]{2,1,0:T(1,128)}), f32[16,1,1536]{2,1,0:T(1,128)S(1)}, u32[]{:S(2)}, u32[]{:S(2)}) async-start(f32[16,1,1536]{2,1,0:T(1,128)} %last.1._), calls=%async_computation.5 | async-start | bytes 196608 | tf_op jit(solution)/shard_map/all_to_all | solution.py:585
  289.6 0.7 compare_select_fusion
  290.3 6.7 %all-to-all-done.5 = f32[16,1,1536]{2,1,0:T(1,128)S(1)} async-done(((f32[16,1,1536]{2,1,0:T(1,128)}), f32[16,1,1536]{2,1,0:T(1,128)S(1)}, u32[]{:S(2)}, u32[]{:S(2)}) %all-to-all-start.5) | async-done | bytes 98336 | tf_op jit(solution)/shard_map/all_to_all | solution.py:585
  297.0 0.1 fusion
  297.1 0.0 copy-done.7
  297.1 0.0 copy-done.8
  297.2 4.6 %fusion.7 = (f32[16]{0:T(128)S(1)}, f32[16]{0:T(128)S(1)}) fusion(s32[2048]{0:T(1024)S(1)} %iota_add_fusion, s32[16]{0:T(128)S(1)} %copy-done.8, bf16[2048,1536]{1,0:T(8,128)(2,1)} %param.15, f32[16,1,1536]{2,1,0:T(1,128)S(1)} %all-to-all-done.5, f32[1536]{0:T(1024)S(1)} %copy-done.7, f32[16]{0:T(128)S(1)} %add_rsqrt_fusion), kind=kOutput, calls=%fused_computation.17 | convolution fusion | flops 100868064 | bytes 6404352 | tf_op jit(solution)/shard_map/dot_general | solution.py:593
  301.8 9.2 %all_to_all.35 = f32[16,3,16]{2,1,0:T(4,128)S(1)} all-to-all(f32[16,3,16]{2,1,0:T(4,128)S(1)} %broadcast_in_dim.28), channel_id=1, replica_groups=mesh['blk'=16,'rep'=2] {'blk'}, dimensions={0} | all-to-all | bytes 6144 | tf_op jit(solution)/shard_map/all_to_all | solution.py:585
  311.1 0.6 pad_maximum_fusion.1
  (12 shorter events, 0.1 us)
Async XLA Ops:
  7.2 126.4 %all-gather.2.cloned.1.call-start = ((), (), s32[]{:S(2)}) async-start(), calls=%async_computation.7 | async-start | bytes 7241728 | tf_op jit(solution)/shard_map/all_gather | solution.py:452
  8.5 4.3 %copy-start.9 = (s32[16]{0:T(128)S(1)}, s32[16]{0:T(128)}, u32[]{:S(2)}) copy-start(s32[16]{0:T(128)} %param.10) | copy-start | bytes 196
  17.6 58.0 %all-to-all-start = ((bf16[16,96,512]{2,1,0:T(8,128)(2,1)}), bf16[16,96,512]{2,1,0:T(8,128)(2,1)S(1)}, u32[]{:S(2)}, u32[]{:S(2)}) async-start(bf16[16,96,512]{2,1,0:T(8,128)(2,1)} %cast.3._), calls=%async_computation | async-start | bytes 3145728 | tf_op jit(solution)/shard_map/all_to_all | solution.py:406
  75.6 6.9 %copy-start.3 = (bf16[16,96,512]{2,1,0:T(8,128)(2,1)}, bf16[16,96,512]{2,1,0:T(8,128)(2,1)S(1)}, u32[]{:S(2)}) copy-start(bf16[16,96,512]{2,1,0:T(8,128)(2,1)S(1)} %all-to-all-done) | copy-start | bytes 4718596
  75.6 47.2 %all-to-all-start.1 = ((bf16[16,96,512]{2,1,0:T(8,128)(2,1)}), bf16[16,96,512]{2,1,0:T(8,128)(2,1)S(1)}, u32[]{:S(2)}, u32[]{:S(2)}) async-start(bf16[16,96,512]{2,1,0:T(8,128)(2,1)} %cast.4), calls=%async_computation.1 | async-start | bytes 3145728 | tf_op jit(solution)/shard_map/all_to_all | solution.py:406
  82.5 36.9 %collective-permute-start = (bf16[1536,512]{1,0:T(8,128)(2,1)S(1)}, bf16[1536,512]{1,0:T(8,128)(2,1)}, u32[]{:S(2)}, u32[]{:S(2)}) collective-permute-start(bf16[1536,512]{1,0:T(8,128)(2,1)S(1)} %bitcast.49), channel_id=1, source_target_pairs={{0,1},{1,0},{2,3},{3,2},{4,5},{5,4},{6,7},{7,6},{8,9},{9,8},{10,11... | collective-permute-start | bytes 4718600 | tf_op jit(solution)/shard_map/ppermute | solution.py:410
  122.8 10.7 %copy-start.4 = (bf16[16,96,512]{2,1,0:T(8,128)(2,1)}, bf16[16,96,512]{2,1,0:T(8,128)(2,1)S(1)}, u32[]{:S(2)}) copy-start(bf16[16,96,512]{2,1,0:T(8,128)(2,1)S(1)} %all-to-all-done.1) | copy-start | bytes 4718596
  122.9 41.1 %all-to-all-start.2 = ((bf16[16,96,512]{2,1,0:T(8,128)(2,1)}), bf16[16,96,512]{2,1,0:T(8,128)(2,1)S(1)}, u32[]{:S(2)}, u32[]{:S(2)}) async-start(bf16[16,96,512]{2,1,0:T(8,128)(2,1)} %tie.3), calls=%async_computation.2 | async-start | bytes 3145728 | tf_op jit(solution)/shard_map/all_to_all | solution.py:406
  132.0 37.3 %collective-permute-start.1 = (bf16[1536,512]{1,0:T(8,128)(2,1)S(1)}, bf16[1536,512]{1,0:T(8,128)(2,1)}, u32[]{:S(2)}, u32[]{:S(2)}) collective-permute-start(bf16[1536,512]{1,0:T(8,128)(2,1)S(1)} %bitcast.52), channel_id=1, source_target_pairs={{0,1},{1,0},{2,3},{3,2},{4,5},{5,4},{6,7},{7,6},{8,9},{9,8},{10,11... | collective-permute-start | bytes 4718600 | tf_op jit(solution)/shard_map/ppermute | solution.py:410
  164.0 1.1 copy-start
  169.3 9.3 %copy-start.1 = (bf16[1536,512]{1,0:T(8,128)(2,1)S(1)}, bf16[1536,512]{1,0:T(8,128)(2,1)}, u32[]{:S(2)}) copy-start(bf16[1536,512]{1,0:T(8,128)(2,1)} %tie.4.refs_1_.d_own) | copy-start | bytes 4718596
  169.3 53.0 %all-to-all-start.4 = ((bf16[16,32,1536]{2,1,0:T(8,128)(2,1)}), bf16[16,32,1536]{2,1,0:T(8,128)(2,1)S(1)}, u32[]{:S(2)}, u32[]{:S(2)}) async-start(bf16[16,32,1536]{2,1,0:T(8,128)(2,1)} %bitcast.46), calls=%async_computation.4 | async-start | bytes 3145728 | tf_op jit(solution)/shard_map/all_to_all | solution.py:490
  178.6 36.8 %collective-permute-start.2 = (bf16[1536,512]{1,0:T(8,128)(2,1)S(1)}, bf16[1536,512]{1,0:T(8,128)(2,1)S(1)}, u32[]{:S(2)}, u32[]{:S(2)}) collective-permute-start(bf16[1536,512]{1,0:T(8,128)(2,1)S(1)} %copy-done.1), channel_id=1, source_target_pairs={{0,1},{1,0},{2,3},{3,2},{4,5},{5,4},{6,7},{7,6},{8,9},{9,8},{10,11... | collective-permute-start | bytes 4718600 | tf_op jit(solution)/shard_map/ppermute | solution.py:410
  215.4 1.2 copy-start.6
  222.3 1.1 copy-start.5
  223.4 44.6 %all-to-all-start.3 = ((bf16[16,40,1536]{2,1,0:T(8,128)(2,1)}), bf16[16,40,1536]{2,1,0:T(8,128)(2,1)S(1)}, u32[]{:S(2)}, u32[]{:S(2)}) async-start(bf16[16,40,1536]{2,1,0:T(8,128)(2,1)} %bitcast.55), calls=%async_computation.3 | async-start | bytes 3932160 | tf_op jit(solution)/shard_map/all_to_all | solution.py:490
  268.0 1.3 copy-start.2
  273.8 23.3 %copy-start.7 = (f32[1536]{0:T(1024)S(1)}, f32[1536]{0:T(1024)}, u32[]{:S(2)}) copy-start(f32[1536]{0:T(1024)} %param.16) | copy-start | bytes 18436
  273.8 23.3 %copy-start.8 = (s32[16]{0:T(128)S(1)}, s32[16]{0:T(128)}, u32[]{:S(2)}) copy-start(s32[16]{0:T(128)} %param.17) | copy-start | bytes 196
  278.9 18.1 %all-to-all-start.5 = ((f32[16,1,1536]{2,1,0:T(1,128)}), f32[16,1,1536]{2,1,0:T(1,128)S(1)}, u32[]{:S(2)}, u32[]{:S(2)}) async-start(f32[16,1,1536]{2,1,0:T(1,128)} %last.1._), calls=%async_computation.5 | async-start | bytes 196608 | tf_op jit(solution)/shard_map/all_to_all | solution.py:585
Sparse Core Ops, SparseCore 0:
  17.8 97.6 all-gather.1

commit v8 on v6

--- a/solution.py
+++ b/solution.py
@@ -149,12 +149,12 @@
     return lax.broadcasted_iota(jnp.int32, shape, dim)
 
 
-def prep_kernel(info, hidden_ref, routes_ref, weights_ref, gain_ref, _, rows_ref, pieces_ref):
+def prep_kernel(length_ref, hidden_ref, routes_ref, weights_ref, gain_ref, rows_ref, pieces_ref):
     rows, width = hidden_ref.shape
-    length = info[3]
+    length = length_ref[0]
     x = hidden_ref[...].astype(jnp.float32)
     scale = lax.rsqrt(jnp.mean(x * x, axis=-1, keepdims=True) + 1e-05)
-    rows_ref[:, :width] = (x * scale * gain_ref[...]).astype(jnp.bfloat16)
+    rows_ref[:, :width] = (x * scale * gain_ref[...][None]).astype(jnp.bfloat16)
     lane = iota((rows, LANES), 1)
     row = iota((rows, LANES), 0)
     hit = jnp.zeros((rows, LANES), jnp.float32)
@@ -252,20 +252,30 @@
         out_ref[...] = activ(picked[...], g_ref, u_ref)
 
 
-def down_kernel(info, *refs):
-    out_ref = refs[-1]
-    total = 0.0
-    for hidden_ref, d_ref in zip(refs[0:-1:2], refs[1:-1:2]):
-        total = total + lax.dot_general(
-            hidden_ref[...],
-            d_ref[...],
-            (((1,), (1,)), ((), ())),
-            preferred_element_type=jnp.float32,
-        )
-    out_ref[...] = total.astype(jnp.bfloat16)
-
-
-def mix_kernel(info, rank_ref, pieces_ref, first_ref, second_ref):
+def matmul_nt(hidden_ref, d_ref):
+    return lax.dot_general(
+        hidden_ref[...], d_ref[...], (((1,), (1,)), ((), ())), preferred_element_type=jnp.float32
+    )
+
+
+def own_down_kernel(hidden_ref, d_ref, out_ref):
+    out_ref[...] = matmul_nt(hidden_ref, d_ref).astype(jnp.bfloat16)
+
+
+def oth_down_kernel(late_ref, d_ref, hidden_ref, d_a, d_b, out_ref):
+    late = matmul_nt(late_ref, d_ref)
+    in_a = pl.program_id(0) < pl.num_programs(0) // 2
+
+    @pl.when(in_a)
+    def _():
+        out_ref[...] = (late + matmul_nt(hidden_ref, d_a)).astype(jnp.bfloat16)
+
+    @pl.when(jnp.logical_not(in_a))
+    def _():
+        out_ref[...] = (late + matmul_nt(hidden_ref, d_b)).astype(jnp.bfloat16)
+
+
+def mix_kernel(info, rank_ref, pieces_ref, first_ref, second_ref, last_ref):
     rows = rank_ref.shape[0]
     late = SECOND - CAP
     own, oth = info[2], 1 - info[2]
@@ -292,6 +302,11 @@
                 pieces_ref[k * rows : (k + 1) * rows, :], spread, preferred_element_type=jnp.float32
             )
             mix_ref[k * rows : (k + 1) * rows, :] = jnp.where(match, part, 0.0).astype(jnp.bfloat16)
+    shape = (last_ref.shape[0], 3 * rows)
+    one_hot = jnp.where(iota(shape, 1) == iota(shape, 0) * rows + info[3] - 1, 1.0, 0.0)
+    last_ref[...] = jnp.dot(
+        one_hot.astype(jnp.bfloat16), second_ref[...], preferred_element_type=jnp.float32
+    ).astype(jnp.bfloat16)
 
 
 def weigh(mix_ref, back_ref):
@@ -300,19 +315,17 @@
     return parts[2 * rows :] + parts[rows : 2 * rows] + parts[:rows]
 
 
-def first_kernel(mix_ref, back_ref, resid_ref, base_ref):
-    base_ref[...] = resid_ref[...].astype(jnp.float32) + weigh(mix_ref, back_ref)
-
-
-def last_kernel(info, mix_ref, back_ref, base_ref, _, told_ref):
-    rows = base_ref.shape[0]
-    last = info[3] - 1
-    shape = (8, mix_ref.shape[0])
-    one_hot = jnp.where(iota(shape, 1) == iota(shape, 0) * rows + last, 1.0, 0.0)
-    mix = jnp.dot(one_hot.astype(jnp.bfloat16), mix_ref[...], preferred_element_type=jnp.float32)
-    parts = jnp.dot(mix.astype(jnp.bfloat16), back_ref[...], preferred_element_type=jnp.float32)
+def first_kernel(info, mix_ref, back_ref, resid_ref, base_ref, last_ref):
+    base = resid_ref[...].astype(jnp.float32) + weigh(mix_ref, back_ref)
+    base_ref[...] = base
+    is_last = iota(base.shape, 0) == info[3] - 1
+    last_ref[...] = jnp.sum(jnp.where(is_last, base, 0.0), axis=0, keepdims=True)
+
+
+def last_kernel(mix_ref, back_ref, base_ref, _, told_ref):
+    parts = jnp.dot(mix_ref[...], back_ref[...], preferred_element_type=jnp.float32)
     moe = parts[2:3] + parts[1:2] + parts[0:1]
-    out = (base_ref[pl.ds(last, 1), :] + moe).astype(jnp.bfloat16).astype(jnp.float32)
+    out = (base_ref[...] + moe).astype(jnp.bfloat16).astype(jnp.float32)
     told_ref[...] = jnp.broadcast_to(out[None], told_ref.shape)
 
 
@@ -335,31 +348,33 @@
         square_ref[...] = jnp.broadcast_to(total, square_ref.shape)
 
 
-def place_kernel(info, g_own, g_oth, u_own, u_oth, d_both, _, out_ref):
-    for k, (own, oth) in enumerate(((g_own, g_oth), (u_own, u_oth))):
-
-        @pl.when(info[2] == 0)
-        def _():
-            out_ref[k, :, :FF] = own[...]
-            out_ref[k, :, FF:] = oth[...]
-
-        @pl.when(info[2] != 0)
-        def _():
-            out_ref[k, :, :FF] = oth[...]
-            out_ref[k, :, FF:] = own[...]
-
-    out_ref[2, :, :FF] = d_both[0]
-    out_ref[2, :, FF:] = d_both[1]
+def place_kernel(info, g_own, g_oth, u_own, u_oth, d_own, d_a, d_b, _, out_ref):
+    second_half = pl.program_id(0) >= pl.num_programs(0) // 2
+    d_oth = jnp.where(second_half, d_b[...], d_a[...])
+    for k, (own, oth) in enumerate(
+        ((g_own[...], g_oth[...]), (u_own[...], u_oth[...]), (d_own[...], d_oth))
+    ):
+        left = info[2] == 0
+        out_ref[k, :, :FF] = jnp.where(left, own, oth)
+        out_ref[k, :, FF:] = jnp.where(left, oth, own)
 
 
 def cast_kernel(blocks, x_ref, *refs):
     out_ref = refs[-1]
     rows = out_ref.shape[1]
+    shape = (blocks * rows, blocks * rows)
+    target = iota(shape, 0)
+    one_hot = jnp.where(iota(shape, 1) == target % rows * blocks + target // rows, 1.0, 0.0)
+    turned = jnp.dot(
+        one_hot.astype(jnp.bfloat16),
+        x_ref[...].astype(jnp.bfloat16),
+        preferred_element_type=jnp.float32,
+    ).astype(jnp.bfloat16)
     for b in range(blocks):
-        out_ref[b] = x_ref[pl.ds(b, rows, stride=blocks), :].astype(jnp.bfloat16)
-
-
-def tie_kernel(x_ref, _, out_ref):
+        out_ref[b] = turned[b * rows : (b + 1) * rows]
+
+
+def tie_kernel(*_):
     pass
 
 
@@ -382,7 +397,8 @@
     first = blk_count * FIRST
     second = blk_count * SECOND
     resid = hidden_in[0]
-    info = jnp.stack([2 * blk + rep, 2 * blk + 1 - rep, rep, lengths[blk]] + list(RING))
+    length = lax.dynamic_slice(lengths, (blk,), (1,))
+    info = jnp.stack([2 * blk + rep, 2 * blk + 1 - rep, rep, length[0]] + list(RING))
     info = info.astype(jnp.int32)
 
     shard_rows = master.shape[1]
@@ -391,10 +407,10 @@
     def turned(k, *after):
         return pl.pallas_call(
             functools.partial(cast_kernel, blk_count),
-            grid=(FF // LANES,),
-            in_specs=[pl.BlockSpec((shard_rows * blk_count, LANES), lambda i: (k, i))]
+            grid=(shard_rows // 16,),
+            in_specs=[pl.BlockSpec((16 * blk_count, FF), lambda i: (k * (shard_rows // 16) + i, 0))]
             + [pl.BlockSpec(memory_space=pl.ANY)] * len(after),
-            out_specs=pl.BlockSpec((blk_count, shard_rows, LANES), lambda i: (0, 0, i)),
+            out_specs=pl.BlockSpec((blk_count, 16, FF), lambda i: (0, i, 0)),
             out_shape=jax.ShapeDtypeStruct((blk_count, shard_rows, FF), jnp.bfloat16),
             compiler_params=params(),
             name="cast",
@@ -407,23 +423,15 @@
     def swapped(x):
         return lax.ppermute(x, "rep", [(0, 1), (1, 0)])
 
-    def tied(x, after):
+    def tied(x, *after):
         return pl.pallas_call(
             tie_kernel,
-            in_specs=[pl.BlockSpec(memory_space=pl.ANY)] * 2,
+            in_specs=[pl.BlockSpec(memory_space=pl.ANY)] * (1 + len(after)),
             out_specs=pl.BlockSpec(memory_space=pl.ANY),
             out_shape=jax.ShapeDtypeStruct(x.shape, x.dtype),
             input_output_aliases={0: 0},
             name="tie",
-        )(x, after)
-
-    g_turned = turned(0)
-    g_own = moved(g_turned)
-    g_oth = swapped(g_own)
-    u_own = moved(turned(1))
-    u_oth = swapped(u_own)
-    d_own = moved(tied(turned(2), g_oth))
-    d_both = lax.all_gather(d_own, "rep", axis=0)
+        )(x, *after)
 
     row_ext, pieces = pl.pallas_call(
         prep_kernel,
@@ -434,8 +442,7 @@
                 whole((rows, width)),
                 whole((routes.shape[2], rows)),
                 whole((routes.shape[2], rows)),
-                whole((1, width)),
-                pl.BlockSpec(memory_space=pl.ANY),
+                whole((width,)),
             ],
             out_specs=[whole((rows, width + LANES)), whole((3 * rows, LANES))],
         ),
@@ -445,7 +452,13 @@
         ],
         compiler_params=params(),
         name="prep",
-    )(info, resid, routes[0].T, route_weights[0].T, norm_gain[None], g_turned)
+    )(length, resid, routes[0].T, route_weights[0].T, norm_gain)
+    g_own = moved(turned(0, row_ext))
+    g_oth = swapped(g_own)
+    u_own = moved(turned(1))
+    u_oth = swapped(u_own)
+    d_own = moved(tied(turned(2), g_oth))
+
     tokens = lax.all_gather(row_ext, "blk", axis_index_groups=[list(RING)], axis=0, tiled=True)
 
     def hidden_of(kernel, sizes, scratch, g, u, *after):
@@ -467,22 +480,9 @@
 
     step = 512
 
-    one = pl.BlockSpec((step, FF), lambda i, *_: (i, 0))
-    other = pl.BlockSpec((None, step, FF), lambda i, info: (1 - info[2], i, 0))
-
-    def outputs_of(size, halves, *operands):
-        return pl.pallas_call(
-            down_kernel,
-            grid_spec=pltpu.PrefetchScalarGridSpec(
-                num_scalar_prefetch=1,
-                grid=(width // step,),
-                in_specs=[spec for half in halves for spec in (whole((size, FF)), half)],
-                out_specs=pl.BlockSpec((size, step), lambda i, *_: (0, i)),
-            ),
-            out_shape=jax.ShapeDtypeStruct((size, width), jnp.bfloat16),
-            compiler_params=params(),
-            name="down",
-        )(info, *operands)
+    quarter = width // 4
+    in_a = pl.BlockSpec((quarter, FF), lambda i, *_: (jnp.minimum(i, 1), 0))
+    in_b = pl.BlockSpec((quarter, FF), lambda i, *_: (jnp.maximum(i, 2) - 2, 0))
 
     def returned(x):
         slots = x.shape[0]
@@ -492,31 +492,54 @@
 
     extra = blk_count * (CAP - FIRST)
     own_hidden, late_hidden = hidden_of(own_kernel, (first, second), first + extra, g_own, u_own)
-    own_out = tied(outputs_of(first, (one,), own_hidden, d_own), u_oth)
+    d_own = tied(d_own, own_hidden)
+    half = width // 2
+    d_oth_a = swapped(d_own[:half])
+    own_out = pl.pallas_call(
+        own_down_kernel,
+        grid=(width // step,),
+        in_specs=[whole((first, FF)), pl.BlockSpec((step, FF), lambda i: (i, 0))],
+        out_specs=pl.BlockSpec((first, step), lambda i: (0, i)),
+        out_shape=jax.ShapeDtypeStruct((first, width), jnp.bfloat16),
+        compiler_params=params(),
+        name="own_down",
+    )(own_hidden, d_own)
+    own_out = tied(own_out, u_oth)
     own_back = returned(own_out)
     (oth_hidden,) = hidden_of(oth_kernel, (second,), second, g_oth, u_oth, own_out)
-    oth_out = outputs_of(second, (one, other), late_hidden, d_own, oth_hidden, d_both)
+    d_oth_b = swapped(tied(d_own[half:], d_oth_a, oth_hidden))
+    oth_out = pl.pallas_call(
+        oth_down_kernel,
+        grid=(4,),
+        in_specs=[
+            whole((second, FF)),
+            pl.BlockSpec((quarter, FF), lambda i: (i, 0)),
+            whole((second, FF)),
+            in_a,
+            in_b,
+        ],
+        out_specs=pl.BlockSpec((second, quarter), lambda i: (0, i)),
+        out_shape=jax.ShapeDtypeStruct((second, width), jnp.bfloat16),
+        compiler_params=params(),
+        name="oth_down",
+    )(late_hidden, d_own, oth_hidden, d_oth_a, d_oth_b)
     oth_back = returned(oth_out)
 
-    part = width // 4
     server = pl.pallas_call(
         place_kernel,
         grid_spec=pltpu.PrefetchScalarGridSpec(
             num_scalar_prefetch=1,
-            grid=(width // part,),
-            in_specs=[pl.BlockSpec((part, FF), lambda i, *_: (i, 0))] * 4
-            + [
-                pl.BlockSpec((2, part, FF), lambda i, *_: (0, i, 0)),
-                pl.BlockSpec(memory_space=pl.ANY),
-            ],
-            out_specs=pl.BlockSpec((3, part, 2 * FF), lambda i, *_: (0, i, 0)),
+            grid=(4,),
+            in_specs=[pl.BlockSpec((quarter, FF), lambda i, *_: (i, 0))] * 5
+            + [in_a, in_b, pl.BlockSpec(memory_space=pl.ANY)],
+            out_specs=pl.BlockSpec((3, quarter, 2 * FF), lambda i, *_: (0, i, 0)),
         ),
         out_shape=jax.ShapeDtypeStruct((3, width, 2 * FF), jnp.bfloat16),
         compiler_params=params(),
         name="place",
-    )(info, g_own, g_oth, u_own, u_oth, d_both, oth_out)
-
-    first_mix, second_mix = pl.pallas_call(
+    )(info, g_own, g_oth, u_own, u_oth, d_own, d_oth_a, d_oth_b, oth_out)
+
+    first_mix, second_mix, last_mix = pl.pallas_call(
         mix_kernel,
         grid_spec=pltpu.PrefetchScalarGridSpec(
             num_scalar_prefetch=1,
@@ -525,11 +548,12 @@
                 pl.BlockSpec((rows, LANES), lambda i, *_: (0, width // LANES)),
                 whole((3 * rows, LANES)),
             ],
-            out_specs=[whole((3 * rows, first)), whole((3 * rows, second))],
+            out_specs=[whole((3 * rows, first)), whole((3 * rows, second)), whole((16, second))],
         ),
         out_shape=[
             jax.ShapeDtypeStruct((3 * rows, first), jnp.bfloat16),
             jax.ShapeDtypeStruct((3 * rows, second), jnp.bfloat16),
+            jax.ShapeDtypeStruct((16, second), jnp.bfloat16),
         ],
         compiler_params=params(),
         name="mix",
@@ -539,27 +563,36 @@
         return [whole((3 * rows, slots)), pl.BlockSpec((slots, step), lambda i, *_: (0, i))]
 
     column = pl.BlockSpec((rows, step), lambda i, *_: (0, i))
-    base = pl.pallas_call(
+    lane_row = pl.BlockSpec((1, step), lambda i, *_: (0, i))
+    base, last_base = pl.pallas_call(
         first_kernel,
-        grid=(width // step,),
-        in_specs=weigh_specs(first) + [column],
-        out_specs=column,
-        out_shape=jax.ShapeDtypeStruct((rows, width), jnp.float32),
-        compiler_params=params(),
-        name="first",
-    )(first_mix, own_back, resid)
-    told = pl.pallas_call(
-        last_kernel,
         grid_spec=pltpu.PrefetchScalarGridSpec(
             num_scalar_prefetch=1,
             grid=(width // step,),
-            in_specs=weigh_specs(second) + [column, pl.BlockSpec(memory_space=pl.ANY)],
-            out_specs=pl.BlockSpec((blk_count, 1, step), lambda i, *_: (0, 0, i)),
+            in_specs=weigh_specs(first) + [column],
+            out_specs=[column, lane_row],
         ),
+        out_shape=[
+            jax.ShapeDtypeStruct((rows, width), jnp.float32),
+            jax.ShapeDtypeStruct((1, width), jnp.float32),
+        ],
+        compiler_params=params(),
+        name="first",
+    )(info, first_mix, own_back, resid)
+    told = pl.pallas_call(
+        last_kernel,
+        grid=(width // step,),
+        in_specs=[
+            whole((16, second)),
+            pl.BlockSpec((second, step), lambda i: (0, i)),
+            lane_row,
+            pl.BlockSpec(memory_space=pl.ANY),
+        ],
+        out_specs=pl.BlockSpec((blk_count, 1, step), lambda i: (0, 0, i)),
         out_shape=jax.ShapeDtypeStruct((blk_count, 1, width), jnp.float32),
         compiler_params=params(),
         name="last",
-    )(info, second_mix, oth_back, base, server)
+    )(last_mix, oth_back, last_base, server)
     out_rows, square = pl.pallas_call(
         combine_kernel,
         grid_spec=pltpu.PrefetchScalarGridSpec(

time: 318 us -> 314 us (0.987)
  waiting for transfers between devices: 152 us -> 147 us
    ppermute x2 -> x4, waiting for transfers between devices: 31.1 us -> 56.3 us  [swapped(): return lax.ppermute(x, 'rep', [(0, 1), (1, 0)])]
    all_gather x1 -> x0, waiting for transfers between devices: 15.8 us -> none  [paired(): d_both = lax.all_gather(d_own, 'rep', axis=0)]
    all_to_all x3, waiting for transfers between devices: 80 us -> 65.9 us  [moved(): own = lax.all_to_all(x, 'blk', split_axis=0, concat_axis=0, tiled=True)]
    all_to_all x2, starting transfers between devices: 18.2 us -> 14.9 us  [returned(): x = lax.all_to_all(x, 'blk', split_axis=0, concat_axis=0, tiled=True)]
  transfers between devices with their start and end apart: 10 -> 11, of which waited for: 8 -> 7; matrix products, arithmetic and copies ran while one was open for 0% -> 1% of each run, Pallas kernels for 19% -> 22%
where the time goes in v8:
time: 314 us; the launch traced here: 313 us
  waiting for transfers between devices  147 us (47%)
  Pallas kernels  74.3 us (24%)
  starting transfers between devices  52.6 us (17%)
  between operations  14.2 us (5%)
  blocking collectives  10.8 us (3%)
  local copies, waits for them, and re-layouts  7.78 us (2%)
  matrix products  4.64 us (1%)
    all_to_all x3, waiting for transfers between devices, moved(): own = lax.all_to_all(x, 'blk', split_axis=0, concat_axis=0, tiled=True)  65.9 us
    ppermute x4, waiting for transfers between devices, swapped(): return lax.ppermute(x, 'rep', [(0, 1), (1, 0)])  56.3 us
    all_to_all x2, waiting for transfers between devices, returned(): x = lax.all_to_all(x, 'blk', split_axis=0, concat_axis=0, tiled=True)  23 us
    all_to_all x3, starting transfers between devices, moved(): own = lax.all_to_all(x, 'blk', split_axis=0, concat_axis=0, tiled=True)  20.9 us
    pallas_call x2, Pallas kernels, hidden_of(): pl.pallas_call(kernel, grid_spec=pltpu.PrefetchScalarGridSpec(num_scalar_...  19.5 us
    pallas_call x3, Pallas kernels, turned(): pl.pallas_call(functools.partial(cast_kernel, blk_count), grid=(shard_row...  16.3 us
    all_to_all x2, starting transfers between devices, returned(): x = lax.all_to_all(x, 'blk', split_axis=0, concat_axis=0, tiled=True)  14.9 us
    all_to_all x1, blocking collectives, everywhere(): lax.all_to_all(copies, 'blk', split_axis=0, concat_axis=0, tiled=True)  10.8 us
  transfers between devices with their start and end apart: 11, of which 7 were waited for; matrix products, arithmetic and copies ran while one was open for 1% of the time, Pallas kernels for 22%

profile of v8, /device:TPU:0, one launch (start us, length us, event | category | flops | bytes accessed | tf_op | source)
XLA Modules:
  0.0 312.6 jit_solution(12035488782357119386)
XLA Ops:
  7.2 0.0 all-gather.2.cloned.1.call-start
  7.2 1.3 dynamic_slice.3.length_ref
  8.5 3.0 prep.1
  11.4 0.0 all-gather.2.cloned.1.call-update
  11.5 5.4 %cast.3 = bf16[16,96,512]{2,1,0:T(8,128)(2,1)} custom-call(f32[4608,512]{1,0:T(8,128)} %bitcast.42, bf16[128,1664]{1,0:T(8,128)(2,1)} %get-tuple-element.14.rank_ref.refs_0_), custom_call_target="tpu_custom_call" | custom-call | tf_op jit(solution)/shard_map/cast/pallas_call | solution.py:408
  16.9 7.4 %all-to-all-start = ((bf16[16,96,512]{2,1,0:T(8,128)(2,1)}), bf16[16,96,512]{2,1,0:T(8,128)(2,1)S(1)}, u32[]{:S(2)}, u32[]{:S(2)}) async-start(bf16[16,96,512]{2,1,0:T(8,128)(2,1)} %cast.3), calls=%async_computation | async-start | bytes 3145728 | tf_op jit(solution)/shard_map/all_to_all | solution.py:420
  24.3 5.5 %cast.4 = bf16[16,96,512]{2,1,0:T(8,128)(2,1)} custom-call(f32[4608,512]{1,0:T(8,128)} %bitcast.43), custom_call_target="tpu_custom_call" | custom-call | tf_op jit(solution)/shard_map/cast/pallas_call | solution.py:408
  29.8 46.5 %all-to-all-done = bf16[16,96,512]{2,1,0:T(8,128)(2,1)S(1)} async-done(((bf16[16,96,512]{2,1,0:T(8,128)(2,1)}), bf16[16,96,512]{2,1,0:T(8,128)(2,1)S(1)}, u32[]{:S(2)}, u32[]{:S(2)}) %all-to-all-start) | async-done | bytes 1572896 | tf_op jit(solution)/shard_map/all_to_all | solution.py:420
  76.3 0.0 copy-start.3
  76.3 6.1 %all-to-all-start.1 = ((bf16[16,96,512]{2,1,0:T(8,128)(2,1)}), bf16[16,96,512]{2,1,0:T(8,128)(2,1)S(1)}, u32[]{:S(2)}, u32[]{:S(2)}) async-start(bf16[16,96,512]{2,1,0:T(8,128)(2,1)} %cast.4), calls=%async_computation.1 | async-start | bytes 3145728 | tf_op jit(solution)/shard_map/all_to_all | solution.py:420
  82.4 0.0 copy-done.3
  82.4 1.6 collective-permute-start
  84.0 5.4 %cast.5.__0_ = bf16[16,96,512]{2,1,0:T(8,128)(2,1)} custom-call(f32[4608,512]{1,0:T(8,128)} %bitcast.44), custom_call_target="tpu_custom_call" | custom-call | tf_op jit(solution)/shard_map/cast/pallas_call | solution.py:408
  89.4 29.9 %collective-permute-done.__1_.g_ref.g_oth = bf16[1536,512]{1,0:T(8,128)(2,1)} collective-permute-done((bf16[1536,512]{1,0:T(8,128)(2,1)S(1)}, bf16[1536,512]{1,0:T(8,128)(2,1)}, u32[]{:S(2)}, u32[]{:S(2)}) %collective-permute-start) | collective-permute-done | bytes 1572896 | tf_op jit(solution)/shard_map/ppermute | solution.py:424
  119.3 0.0 all-to-all-done.1
  119.3 0.0 copy-start.4
  119.3 7.4 %all-to-all-start.2 = ((bf16[16,96,512]{2,1,0:T(8,128)(2,1)}), bf16[16,96,512]{2,1,0:T(8,128)(2,1)S(1)}, u32[]{:S(2)}, u32[]{:S(2)}) async-start(bf16[16,96,512]{2,1,0:T(8,128)(2,1)} %tie.4), calls=%async_computation.2 | async-start | bytes 3145728 | tf_op jit(solution)/shard_map/all_to_all | solution.py:420
  126.7 1.5 collective-permute-start.1
  128.3 1.3 stack.34.info
  129.5 0.0 all-gather.2.cloned.1.call-done.x_ref
  129.5 0.0 copy-done.4
  129.5 9.8 %gate_up.2 = (bf16[512,512]{1,0:T(8,128)(2,1)}, bf16[640,512]{1,0:T(8,128)(2,1)}) custom-call(s32[20]{0:T(128)} %stack.34.info, bf16[2048,1664]{1,0:T(8,128)(2,1)} %all-gather.2.cloned.1.call-done.x_ref, bf16[1536,512]{1,0:T(8,128)(2,1)} %bitcast.51, bf16[1536,512]{1,0:T(8,128)(2,1)} %bitcast.54), custom_call_target="tpu_custom_call" | custom-call | tf_op jit(solution)/shard_map/gate_up/pallas_call | solution.py:465
  139.3 19.4 %all-to-all-done.2 = bf16[16,96,512]{2,1,0:T(8,128)(2,1)S(1)} async-done(((bf16[16,96,512]{2,1,0:T(8,128)(2,1)}), bf16[16,96,512]{2,1,0:T(8,128)(2,1)S(1)}, u32[]{:S(2)}, u32[]{:S(2)}) %all-to-all-start.2) | async-done | bytes 1572896 | tf_op jit(solution)/shard_map/all_to_all | solution.py:420
  158.7 0.0 copy-start
  158.7 1.1 copy-done
  159.9 4.2 %own_down.1.__0_ = bf16[512,1536]{1,0:T(8,128)(2,1)} custom-call(bf16[512,512]{1,0:T(8,128)(2,1)} %get-tuple-element.18.__1_.hidden_ref, bf16[1536,512]{1,0:T(8,128)(2,1)} %tie.5.d_ref.d_own), custom_call_target="tpu_custom_call" | custom-call | tf_op jit(solution)/shard_map/own_down/pallas_call | solution.py:498
  164.0 0.0 collective-permute-done.1.__1_.u_ref.u_oth
  164.0 0.0 copy-start.1
  164.0 9.3 %all-to-all-start.4 = ((bf16[16,32,1536]{2,1,0:T(8,128)(2,1)}), bf16[16,32,1536]{2,1,0:T(8,128)(2,1)}, u32[]{:S(2)}, u32[]{:S(2)}) async-start(bf16[16,32,1536]{2,1,0:T(8,128)(2,1)} %bitcast.46), calls=%async_computation.4 | async-start | bytes 3145728 | tf_op jit(solution)/shard_map/all_to_all | solution.py:490
  173.3 0.0 copy-done.1
  173.4 1.0 fusion.8
  174.4 1.5 collective-permute-start.2
  175.8 9.7 %gate_up.3.__2_.hidden_ref = bf16[640,512]{1,0:T(8,128)(2,1)} custom-call(s32[20]{0:T(128)} %stack.34.info, bf16[2048,1664]{1,0:T(8,128)(2,1)} %all-gather.2.cloned.1.call-done.x_ref, bf16[1536,512]{1,0:T(8,128)(2,1)} %collective-permute-done.__1_.g_ref.g_oth, bf16[1536,512]{1,0:T(8,128)(2,1)} %collective-permute-done.1.__1_.u_ref.u_oth, bf16[512,1536]{1,0:T(8,128)(2,1)} %tie.6._), custom_call_target="tpu_custom_call" | custom-call | tf_op jit(solution)/shard_map/gate_up/pallas_call | solution.py:465
  185.5 8.7 %collective-permute-done.2.__1_.d_a = bf16[768,512]{1,0:T(8,128)(2,1)S(1)} collective-permute-done((bf16[768,512]{1,0:T(8,128)(2,1)S(1)}, bf16[768,512]{1,0:T(8,128)(2,1)S(1)}, u32[]{:S(2)}, u32[]{:S(2)}) %collective-permute-start.2) | collective-permute-done | bytes 786464 | tf_op jit(solution)/shard_map/ppermute | solution.py:424
  194.2 0.0 copy-start.5
  194.2 0.9 copy-done.5
  195.1 1.5 collective-permute-start.3
  196.5 17.7 %collective-permute-done.3.d_b = bf16[768,512]{1,0:T(8,128)(2,1)S(1)} collective-permute-done((bf16[768,512]{1,0:T(8,128)(2,1)}, bf16[768,512]{1,0:T(8,128)(2,1)S(1)}, u32[]{:S(2)}, u32[]{:S(2)}) %collective-permute-start.3) | collective-permute-done | bytes 786464 | tf_op jit(solution)/shard_map/ppermute | solution.py:424
  214.3 0.0 copy-start.6
  214.3 0.9 copy-done.6
  215.1 7.1 %oth_down.1._ = bf16[640,1536]{1,0:T(8,128)(2,1)} custom-call(bf16[640,512]{1,0:T(8,128)(2,1)} %get-tuple-element.17.late_ref, bf16[1536,512]{1,0:T(8,128)(2,1)} %tie.5.d_ref.d_own, bf16[640,512]{1,0:T(8,128)(2,1)} %gate_up.3.__2_.hidden_ref, bf16[768,512]{1,0:T(8,128)(2,1)} %copy-done.5, bf16[768,512]{1,0:T(8,128)(2,1)} %copy-done.6), custom_call_target="tpu_custom_call" | custom-call | tf_op jit(solution)/shard_map/oth_down/pallas_call | solution.py:511
  222.3 0.0 all-to-all-done.4
  222.3 5.6 %all-to-all-start.3 = ((bf16[16,40,1536]{2,1,0:T(8,128)(2,1)}), bf16[16,40,1536]{2,1,0:T(8,128)(2,1)S(1)}, u32[]{:S(2)}, u32[]{:S(2)}) async-start(bf16[16,40,1536]{2,1,0:T(8,128)(2,1)} %bitcast.49), calls=%async_computation.3 | async-start | bytes 3932160 | tf_op jit(solution)/shard_map/all_to_all | solution.py:490
  227.9 3.0 mix.1
  231.0 8.1 %place.1._ = bf16[3,1536,1024]{2,1,0:T(8,128)(2,1)} custom-call(s32[20]{0:T(128)} %stack.34.info, bf16[1536,512]{1,0:T(8,128)(2,1)} %bitcast.52, bf16[1536,512]{1,0:T(8,128)(2,1)} %collective-permute-done.__1_.g_ref.g_oth, bf16[1536,512]{1,0:T(8,128)(2,1)} %bitcast.55, bf16[1536,512]{1,0:T(8,128)(2,1)} %collective-permute-done.1.__1_.u_ref.u_oth, ...), custom_call_target="tpu_custom_call" | custom-call | tf_op jit(solution)/shard_map/place/pallas_call | solution.py:528
  239.1 4.7 %first.1 = (f32[128,1536]{1,0:T(8,128)}, f32[1,1536]{1,0:T(1,128)}) custom-call(s32[20]{0:T(128)} %stack.34.info, bf16[384,512]{1,0:T(8,128)(2,1)} %get-tuple-element.19.mix_ref, bf16[512,1536]{1,0:T(8,128)(2,1)} %bitcast.15.back_ref, bf16[128,1536]{1,0:T(8,128)(2,1)} %bitcast.57), custom_call_target="tpu_custom_call" | custom-call | tf_op jit(solution)/shard_map/first/pallas_call | solution.py:567
  243.8 23.0 %all-to-all-done.3 = bf16[16,40,1536]{2,1,0:T(8,128)(2,1)S(1)} async-done(((bf16[16,40,1536]{2,1,0:T(8,128)(2,1)}), bf16[16,40,1536]{2,1,0:T(8,128)(2,1)S(1)}, u32[]{:S(2)}, u32[]{:S(2)}) %all-to-all-start.3) | async-done | bytes 1966112 | tf_op jit(solution)/shard_map/all_to_all | solution.py:490
  266.8 0.0 copy-start.2
  266.8 1.3 copy-done.2
  268.1 3.3 %last.1._ = f32[16,1,1536]{2,1,0:T(1,128)} custom-call(bf16[16,640]{1,0:T(8,128)(2,1)} %get-tuple-element.21.mix_ref, bf16[640,1536]{1,0:T(8,128)(2,1)} %bitcast.47, f32[1,1536]{1,0:T(1,128)} %get-tuple-element.22.base_ref, bf16[3,1536,1024]{2,1,0:T(8,128)(2,1)} %place.1._), custom_call_target="tpu_custom_call" | custom-call | tf_op jit(solution)/shard_map/last/pallas_call | solution.py:582
  271.3 10.7 %all-to-all-start.5 = ((f32[16,1,1536]{2,1,0:T(1,128)}), f32[16,1,1536]{2,1,0:T(1,128)S(1)}, u32[]{:S(2)}, u32[]{:S(2)}) async-start(f32[16,1,1536]{2,1,0:T(1,128)} %last.1._), calls=%async_computation.5 | async-start | bytes 196608 | tf_op jit(solution)/shard_map/all_to_all | solution.py:614
  282.0 0.0 copy-start.7
  282.0 0.0 copy-start.8
  282.0 5.1 %combine.1 = (bf16[128,1536]{1,0:T(8,128)(2,1)}, f32[1,128]{1,0:T(1,128)}) custom-call(s32[20]{0:T(128)} %stack.34.info, bf16[384,640]{1,0:T(8,128)(2,1)} %get-tuple-element.16.mix_ref, bf16[640,1536]{1,0:T(8,128)(2,1)} %bitcast.48, f32[128,1536]{1,0:T(8,128)} %get-tuple-element.20.base_ref, f32[16,1,1536]{2,1,0:T(1,128)} %last.1._), custom_call_target="tpu_custom_call" | custom-call | tf_op jit(solution)/shard_map/combine/pallas_call | solution.py:596
  287.1 0.7 compare_select_fusion
  287.8 1.6 all-to-all-done.5
  289.4 0.1 fusion
  289.6 0.0 copy-done.7
  289.6 0.0 copy-done.8
  289.6 0.0 copy-start.9
  289.6 4.6 %fusion.7 = (f32[16]{0:T(128)S(1)}, f32[16]{0:T(128)S(1)}) fusion(s32[2048]{0:T(1024)S(1)} %iota_add_fusion, s32[16]{0:T(128)S(1)} %copy-done.8, bf16[2048,1536]{1,0:T(8,128)(2,1)} %param.15, f32[16,1,1536]{2,1,0:T(1,128)S(1)} %all-to-all-done.5, f32[1536]{0:T(1024)S(1)} %copy-done.7, f32[16]{0:T(128)S(1)} %add_rsqrt_fusion), kind=kOutput, calls=%fused_computation.17 | convolution fusion | flops 100868064 | bytes 6404352 | tf_op jit(solution)/shard_map/dot_general | solution.py:622
  294.3 10.8 %all_to_all.35 = f32[16,3,16]{2,1,0:T(4,128)S(1)} all-to-all(f32[16,3,16]{2,1,0:T(4,128)S(1)} %broadcast_in_dim.24), channel_id=1, replica_groups=mesh['blk'=16,'rep'=2] {'blk'}, dimensions={0} | all-to-all | bytes 6144 | tf_op jit(solution)/shard_map/all_to_all | solution.py:614
  305.1 0.0 copy-done.9
  305.2 0.6 pad_maximum_fusion.1
  (13 shorter events, 0.1 us)
Async XLA Ops:
  7.2 122.4 %all-gather.2.cloned.1.call-start = ((), (), s32[]{:S(2)}) async-start(), calls=%async_computation.7 | async-start | bytes 7241728 | tf_op jit(solution)/shard_map/all_gather | solution.py:462
  16.9 59.4 %all-to-all-start = ((bf16[16,96,512]{2,1,0:T(8,128)(2,1)}), bf16[16,96,512]{2,1,0:T(8,128)(2,1)S(1)}, u32[]{:S(2)}, u32[]{:S(2)}) async-start(bf16[16,96,512]{2,1,0:T(8,128)(2,1)} %cast.3), calls=%async_computation | async-start | bytes 3145728 | tf_op jit(solution)/shard_map/all_to_all | solution.py:420
  76.3 6.1 %copy-start.3 = (bf16[16,96,512]{2,1,0:T(8,128)(2,1)}, bf16[16,96,512]{2,1,0:T(8,128)(2,1)S(1)}, u32[]{:S(2)}) copy-start(bf16[16,96,512]{2,1,0:T(8,128)(2,1)S(1)} %all-to-all-done) | copy-start | bytes 4718596
  76.3 43.0 %all-to-all-start.1 = ((bf16[16,96,512]{2,1,0:T(8,128)(2,1)}), bf16[16,96,512]{2,1,0:T(8,128)(2,1)S(1)}, u32[]{:S(2)}, u32[]{:S(2)}) async-start(bf16[16,96,512]{2,1,0:T(8,128)(2,1)} %cast.4), calls=%async_computation.1 | async-start | bytes 3145728 | tf_op jit(solution)/shard_map/all_to_all | solution.py:420
  82.4 36.9 %collective-permute-start = (bf16[1536,512]{1,0:T(8,128)(2,1)S(1)}, bf16[1536,512]{1,0:T(8,128)(2,1)}, u32[]{:S(2)}, u32[]{:S(2)}) collective-permute-start(bf16[1536,512]{1,0:T(8,128)(2,1)S(1)} %bitcast.50), channel_id=1, source_target_pairs={{0,1},{1,0},{2,3},{3,2},{4,5},{5,4},{6,7},{7,6},{8,9},{9,8},{10,11... | collective-permute-start | bytes 4718600 | tf_op jit(solution)/shard_map/ppermute | solution.py:424
  119.3 10.2 %copy-start.4 = (bf16[16,96,512]{2,1,0:T(8,128)(2,1)}, bf16[16,96,512]{2,1,0:T(8,128)(2,1)S(1)}, u32[]{:S(2)}) copy-start(bf16[16,96,512]{2,1,0:T(8,128)(2,1)S(1)} %all-to-all-done.1) | copy-start | bytes 4718596
  119.3 39.4 %all-to-all-start.2 = ((bf16[16,96,512]{2,1,0:T(8,128)(2,1)}), bf16[16,96,512]{2,1,0:T(8,128)(2,1)S(1)}, u32[]{:S(2)}, u32[]{:S(2)}) async-start(bf16[16,96,512]{2,1,0:T(8,128)(2,1)} %tie.4), calls=%async_computation.2 | async-start | bytes 3145728 | tf_op jit(solution)/shard_map/all_to_all | solution.py:420
  126.7 37.3 %collective-permute-start.1 = (bf16[1536,512]{1,0:T(8,128)(2,1)S(1)}, bf16[1536,512]{1,0:T(8,128)(2,1)}, u32[]{:S(2)}, u32[]{:S(2)}) collective-permute-start(bf16[1536,512]{1,0:T(8,128)(2,1)S(1)} %bitcast.53), channel_id=1, source_target_pairs={{0,1},{1,0},{2,3},{3,2},{4,5},{5,4},{6,7},{7,6},{8,9},{9,8},{10,11... | collective-permute-start | bytes 4718600 | tf_op jit(solution)/shard_map/ppermute | solution.py:424
  158.7 1.2 copy-start
  164.0 9.3 %copy-start.1 = (bf16[1536,512]{1,0:T(8,128)(2,1)S(1)}, bf16[1536,512]{1,0:T(8,128)(2,1)}, u32[]{:S(2)}) copy-start(bf16[1536,512]{1,0:T(8,128)(2,1)} %tie.5.d_ref.d_own) | copy-start | bytes 4718596
  164.0 58.2 %all-to-all-start.4 = ((bf16[16,32,1536]{2,1,0:T(8,128)(2,1)}), bf16[16,32,1536]{2,1,0:T(8,128)(2,1)}, u32[]{:S(2)}, u32[]{:S(2)}) async-start(bf16[16,32,1536]{2,1,0:T(8,128)(2,1)} %bitcast.46), calls=%async_computation.4 | async-start | bytes 3145728 | tf_op jit(solution)/shard_map/all_to_all | solution.py:490
  174.4 19.8 %collective-permute-start.2 = (bf16[768,512]{1,0:T(8,128)(2,1)S(1)}, bf16[768,512]{1,0:T(8,128)(2,1)S(1)}, u32[]{:S(2)}, u32[]{:S(2)}) collective-permute-start(bf16[768,512]{1,0:T(8,128)(2,1)S(1)} %get-tuple-element.28), channel_id=1, source_target_pairs={{0,1},{1,0},{2,3},{3,2},{4,5},{5,4},{6,7},{7,6},{8,9},{9,8},{10,11... | collective-permute-start | bytes 2359304 | tf_op jit(solution)/shard_map/ppermute | solution.py:424
  194.2 0.9 copy-start.5
  195.1 19.2 %collective-permute-start.3 = (bf16[768,512]{1,0:T(8,128)(2,1)}, bf16[768,512]{1,0:T(8,128)(2,1)S(1)}, u32[]{:S(2)}, u32[]{:S(2)}) collective-permute-start(bf16[768,512]{1,0:T(8,128)(2,1)} %tie.7), channel_id=1, source_target_pairs={{0,1},{1,0},{2,3},{3,2},{4,5},{5,4},{6,7},{7,6},{8,9},{9,8},{10,11... | collective-permute-start | bytes 2359304 | tf_op jit(solution)/shard_map/ppermute | solution.py:424
  214.3 0.9 copy-start.6
  222.3 44.5 %all-to-all-start.3 = ((bf16[16,40,1536]{2,1,0:T(8,128)(2,1)}), bf16[16,40,1536]{2,1,0:T(8,128)(2,1)S(1)}, u32[]{:S(2)}, u32[]{:S(2)}) async-start(bf16[16,40,1536]{2,1,0:T(8,128)(2,1)} %bitcast.49), calls=%async_computation.3 | async-start | bytes 3932160 | tf_op jit(solution)/shard_map/all_to_all | solution.py:490
  266.8 1.3 copy-start.2
  271.3 18.1 %all-to-all-start.5 = ((f32[16,1,1536]{2,1,0:T(1,128)}), f32[16,1,1536]{2,1,0:T(1,128)S(1)}, u32[]{:S(2)}, u32[]{:S(2)}) async-start(f32[16,1,1536]{2,1,0:T(1,128)} %last.1._), calls=%async_computation.5 | async-start | bytes 196608 | tf_op jit(solution)/shard_map/all_to_all | solution.py:614
  282.0 7.5 %copy-start.7 = (f32[1536]{0:T(1024)S(1)}, f32[1536]{0:T(1024)}, u32[]{:S(2)}) copy-start(f32[1536]{0:T(1024)} %param.16) | copy-start | bytes 18436
  282.0 7.5 %copy-start.8 = (s32[16]{0:T(128)S(1)}, s32[16]{0:T(128)}, u32[]{:S(2)}) copy-start(s32[16]{0:T(128)} %param.17) | copy-start | bytes 196
  289.6 15.5 %copy-start.9 = (s32[16]{0:T(128)S(1)}, s32[16]{0:T(128)}, u32[]{:S(2)}) copy-start(s32[16]{0:T(128)} %param.10) | copy-start | bytes 196
Sparse Core Ops, SparseCore 0:
  11.6 86.3 all-gather.1

commit v9 on v8

--- a/solution.py
+++ b/solution.py
@@ -200,7 +200,7 @@
     return (gate / (1.0 + jnp.exp(-gate)) * up).astype(jnp.bfloat16)
 
 
-def own_kernel(info, x_ref, g_ref, u_ref, out_ref, late_ref, picked):
+def own_kernel(info, x_ref, g_ref, u_ref, out_ref, spot_ref, picked):
     step = pl.program_id(0)
     sources = x_ref.shape[0] // LEN
     more = CAP - FIRST
@@ -221,21 +221,17 @@
 
     @pl.when(step == GROUPS - 1)
     def _():
-        hidden = activ(picked[...], g_ref, u_ref)
-        out_ref[...] = hidden[:all_early]
-        rest = hidden[all_early:]
-        shape = (late_ref.shape[0], rest.shape[0])
-        column = iota(shape, 1)
+        out_ref[...] = activ(picked[...], g_ref, u_ref)
+        column = iota(spot_ref.shape, 1)
+        owner = lax.shift_right_logical(column, more.bit_length() - 1)
         source = jnp.zeros_like(column)
         for k, b in enumerate(RING):
-            source = source + jnp.where(column // more == k, b, 0)
-        one_hot = jnp.where(iota(shape, 0) == source * SECOND + column % more, 1.0, 0.0)
-        late_ref[...] = jnp.dot(
-            one_hot.astype(jnp.bfloat16), rest, preferred_element_type=jnp.float32
-        ).astype(jnp.bfloat16)
-
-
-def oth_kernel(info, x_ref, g_ref, u_ref, _, out_ref, picked):
+            source = source + jnp.where(owner == k, b, 0)
+        spot = source * SECOND + (column & (more - 1))
+        spot_ref[...] = jnp.where(iota(spot_ref.shape, 0) == spot, 1.0, 0.0).astype(jnp.bfloat16)
+
+
+def oth_kernel(info, x_ref, g_ref, u_ref, _, __, out_ref, picked):
     step = pl.program_id(0)
     sources = x_ref.shape[0] // LEN
 
@@ -258,12 +254,15 @@
     )
 
 
-def own_down_kernel(hidden_ref, d_ref, out_ref):
-    out_ref[...] = matmul_nt(hidden_ref, d_ref).astype(jnp.bfloat16)
-
-
-def oth_down_kernel(late_ref, d_ref, hidden_ref, d_a, d_b, out_ref):
-    late = matmul_nt(late_ref, d_ref)
+def own_down_kernel(hidden_ref, d_ref, out_ref, late_ref):
+    out = matmul_nt(hidden_ref, d_ref).astype(jnp.bfloat16)
+    rows = out_ref.shape[0]
+    out_ref[...] = out[:rows]
+    late_ref[...] = out[rows:]
+
+
+def oth_down_kernel(hidden_ref, spot_ref, late_ref, d_a, d_b, out_ref):
+    late = jnp.dot(spot_ref[...], late_ref[...], preferred_element_type=jnp.float32)
     in_a = pl.program_id(0) < pl.num_programs(0) // 2
 
     @pl.when(in_a)
@@ -360,15 +359,17 @@
 
 
 def cast_kernel(blocks, x_ref, *refs):
-    out_ref = refs[-1]
+    out_ref, order = refs[-2:]
     rows = out_ref.shape[1]
-    shape = (blocks * rows, blocks * rows)
-    target = iota(shape, 0)
-    one_hot = jnp.where(iota(shape, 1) == target % rows * blocks + target // rows, 1.0, 0.0)
+
+    @pl.when(pl.program_id(0) == 0)
+    def _():
+        target = iota(order.shape, 0)
+        source = (target & (rows - 1)) * blocks + lax.shift_right_logical(target, 4)
+        order[...] = jnp.where(iota(order.shape, 1) == source, 1.0, 0.0).astype(jnp.bfloat16)
+
     turned = jnp.dot(
-        one_hot.astype(jnp.bfloat16),
-        x_ref[...].astype(jnp.bfloat16),
-        preferred_element_type=jnp.float32,
+        order[...], x_ref[...].astype(jnp.bfloat16), preferred_element_type=jnp.float32
     ).astype(jnp.bfloat16)
     for b in range(blocks):
         out_ref[b] = turned[b * rows : (b + 1) * rows]
@@ -412,6 +413,7 @@
             + [pl.BlockSpec(memory_space=pl.ANY)] * len(after),
             out_specs=pl.BlockSpec((blk_count, 16, FF), lambda i: (0, i, 0)),
             out_shape=jax.ShapeDtypeStruct((blk_count, shard_rows, FF), jnp.bfloat16),
+            scratch_shapes=[pltpu.VMEM((16 * blk_count, 16 * blk_count), jnp.bfloat16)],
             compiler_params=params(),
             name="cast",
         )(flat, *after)
@@ -470,10 +472,10 @@
                 in_specs=[pl.BlockSpec((blk_count // GROUPS * rows, width + LANES), lambda i, *_: (i, 0))]
                 + [whole((width, FF))] * 2
                 + [pl.BlockSpec(memory_space=pl.ANY)] * len(after),
-                out_specs=[whole((size, FF)) for size in sizes],
+                out_specs=[whole(size) for size in sizes],
                 scratch_shapes=[pltpu.VMEM((scratch, width), jnp.float32)],
             ),
-            out_shape=[jax.ShapeDtypeStruct((size, FF), jnp.bfloat16) for size in sizes],
+            out_shape=[jax.ShapeDtypeStruct(size, jnp.bfloat16) for size in sizes],
             compiler_params=params(),
             name="gate_up",
         )(info, tokens, g, u, *after)
@@ -491,30 +493,40 @@
         return x.reshape(slots, width)
 
     extra = blk_count * (CAP - FIRST)
-    own_hidden, late_hidden = hidden_of(own_kernel, (first, second), first + extra, g_own, u_own)
+    own_hidden, spot = hidden_of(
+        own_kernel, ((first + extra, FF), (second, extra)), first + extra, g_own, u_own
+    )
     d_own = tied(d_own, own_hidden)
     half = width // 2
     d_oth_a = swapped(d_own[:half])
-    own_out = pl.pallas_call(
+    d_oth_b = swapped(tied(d_own[half:], d_oth_a))
+    own_out, late_out = pl.pallas_call(
         own_down_kernel,
         grid=(width // step,),
-        in_specs=[whole((first, FF)), pl.BlockSpec((step, FF), lambda i: (i, 0))],
-        out_specs=pl.BlockSpec((first, step), lambda i: (0, i)),
-        out_shape=jax.ShapeDtypeStruct((first, width), jnp.bfloat16),
+        in_specs=[whole((first + extra, FF)), pl.BlockSpec((step, FF), lambda i: (i, 0))],
+        out_specs=[
+            pl.BlockSpec((first, step), lambda i: (0, i)),
+            pl.BlockSpec((extra, step), lambda i: (0, i)),
+        ],
+        out_shape=[
+            jax.ShapeDtypeStruct((first, width), jnp.bfloat16),
+            jax.ShapeDtypeStruct((extra, width), jnp.bfloat16),
+        ],
         compiler_params=params(),
         name="own_down",
     )(own_hidden, d_own)
     own_out = tied(own_out, u_oth)
     own_back = returned(own_out)
-    (oth_hidden,) = hidden_of(oth_kernel, (second,), second, g_oth, u_oth, own_out)
-    d_oth_b = swapped(tied(d_own[half:], d_oth_a, oth_hidden))
+    (oth_hidden,) = hidden_of(
+        oth_kernel, ((second, FF),), second, g_oth, u_oth, own_out, d_oth_a
+    )
     oth_out = pl.pallas_call(
         oth_down_kernel,
         grid=(4,),
         in_specs=[
             whole((second, FF)),
-            pl.BlockSpec((quarter, FF), lambda i: (i, 0)),
-            whole((second, FF)),
+            whole((second, extra)),
+            pl.BlockSpec((extra, quarter), lambda i: (0, i)),
             in_a,
             in_b,
         ],
@@ -522,7 +534,7 @@
         out_shape=jax.ShapeDtypeStruct((second, width), jnp.bfloat16),
         compiler_params=params(),
         name="oth_down",
-    )(late_hidden, d_own, oth_hidden, d_oth_a, d_oth_b)
+    )(oth_hidden, spot, late_out, d_oth_a, d_oth_b)
     oth_back = returned(oth_out)
 
     server = pl.pallas_call(

time: 314 us -> 313 us (level)
  transfers between devices with their start and end apart: 11 -> 11, of which waited for: 7 -> 7; matrix products, arithmetic and copies ran while one was open for 1% -> 1% of each run, Pallas kernels for 22% -> 21%
where the time goes in v9:
time: 313 us; the launch traced here: 312 us
  waiting for transfers between devices  147 us (47%)
  Pallas kernels  73 us (23%)
  starting transfers between devices  52.5 us (17%)
  between operations  14.2 us (5%)
  blocking collectives  10.8 us (3%)
  local copies, waits for them, and re-layouts  7.86 us (3%)
  matrix products  4.64 us (1%)
    all_to_all x3, waiting for transfers between devices, moved(): own = lax.all_to_all(x, 'blk', split_axis=0, concat_axis=0, tiled=True)  66.2 us
    ppermute x4, waiting for transfers between devices, swapped(): return lax.ppermute(x, 'rep', [(0, 1), (1, 0)])  56.3 us
    all_to_all x2, waiting for transfers between devices, returned(): x = lax.all_to_all(x, 'blk', split_axis=0, concat_axis=0, tiled=True)  23 us
    all_to_all x3, starting transfers between devices, moved(): own = lax.all_to_all(x, 'blk', split_axis=0, concat_axis=0, tiled=True)  20.8 us
    pallas_call x2, Pallas kernels, hidden_of(): pl.pallas_call(kernel, grid_spec=pltpu.PrefetchScalarGridSpec(num_scalar_...  19.1 us
    pallas_call x3, Pallas kernels, turned(): pl.pallas_call(functools.partial(cast_kernel, blk_count), grid=(shard_row...  16.5 us
    all_to_all x2, starting transfers between devices, returned(): x = lax.all_to_all(x, 'blk', split_axis=0, concat_axis=0, tiled=True)  14.9 us
    all_to_all x1, blocking collectives, everywhere(): lax.all_to_all(copies, 'blk', split_axis=0, concat_axis=0, tiled=True)  10.8 us
  transfers between devices with their start and end apart: 11, of which 7 were waited for; matrix products, arithmetic and copies ran while one was open for 1% of the time, Pallas kernels for 21%

profile of v9, /device:TPU:0, one launch (start us, length us, event | category | flops | bytes accessed | tf_op | source)
XLA Modules:
  0.0 311.5 jit_solution(17434036359787259386)
XLA Ops:
  7.2 0.0 all-gather.2.cloned.1.call-start
  7.2 1.3 dynamic_slice.3.length_ref
  8.5 3.0 prep.1
  11.5 0.0 all-gather.2.cloned.1.call-update
  11.5 5.5 %cast.3 = bf16[16,96,512]{2,1,0:T(8,128)(2,1)} custom-call(f32[4608,512]{1,0:T(8,128)} %bitcast.42, bf16[128,1664]{1,0:T(8,128)(2,1)} %get-tuple-element.16.rank_ref.refs_0_), custom_call_target="tpu_custom_call" | custom-call | tf_op jit(solution)/shard_map/cast/pallas_call | solution.py:409
  17.0 7.4 %all-to-all-start = ((bf16[16,96,512]{2,1,0:T(8,128)(2,1)}), bf16[16,96,512]{2,1,0:T(8,128)(2,1)S(1)}, u32[]{:S(2)}, u32[]{:S(2)}) async-start(bf16[16,96,512]{2,1,0:T(8,128)(2,1)} %cast.3), calls=%async_computation | async-start | bytes 3145728 | tf_op jit(solution)/shard_map/all_to_all | solution.py:422
  24.4 5.6 %cast.4 = bf16[16,96,512]{2,1,0:T(8,128)(2,1)} custom-call(f32[4608,512]{1,0:T(8,128)} %bitcast.43), custom_call_target="tpu_custom_call" | custom-call | tf_op jit(solution)/shard_map/cast/pallas_call | solution.py:409
  30.0 46.4 %all-to-all-done = bf16[16,96,512]{2,1,0:T(8,128)(2,1)S(1)} async-done(((bf16[16,96,512]{2,1,0:T(8,128)(2,1)}), bf16[16,96,512]{2,1,0:T(8,128)(2,1)S(1)}, u32[]{:S(2)}, u32[]{:S(2)}) %all-to-all-start) | async-done | bytes 1572896 | tf_op jit(solution)/shard_map/all_to_all | solution.py:422
  76.4 0.0 copy-start.3
  76.4 6.1 %all-to-all-start.1 = ((bf16[16,96,512]{2,1,0:T(8,128)(2,1)}), bf16[16,96,512]{2,1,0:T(8,128)(2,1)S(1)}, u32[]{:S(2)}, u32[]{:S(2)}) async-start(bf16[16,96,512]{2,1,0:T(8,128)(2,1)} %cast.4), calls=%async_computation.1 | async-start | bytes 3145728 | tf_op jit(solution)/shard_map/all_to_all | solution.py:422
  82.5 0.0 copy-done.3
  82.5 1.6 collective-permute-start
  84.1 5.4 %cast.5.__0_ = bf16[16,96,512]{2,1,0:T(8,128)(2,1)} custom-call(f32[4608,512]{1,0:T(8,128)} %bitcast.44), custom_call_target="tpu_custom_call" | custom-call | tf_op jit(solution)/shard_map/cast/pallas_call | solution.py:409
  89.5 29.9 %collective-permute-done.__1_.g_ref.g_oth = bf16[1536,512]{1,0:T(8,128)(2,1)} collective-permute-done((bf16[1536,512]{1,0:T(8,128)(2,1)S(1)}, bf16[1536,512]{1,0:T(8,128)(2,1)}, u32[]{:S(2)}, u32[]{:S(2)}) %collective-permute-start) | collective-permute-done | bytes 1572896 | tf_op jit(solution)/shard_map/ppermute | solution.py:426
  119.4 0.0 all-to-all-done.1
  119.4 0.0 copy-start.4
  119.4 7.3 %all-to-all-start.2 = ((bf16[16,96,512]{2,1,0:T(8,128)(2,1)}), bf16[16,96,512]{2,1,0:T(8,128)(2,1)S(1)}, u32[]{:S(2)}, u32[]{:S(2)}) async-start(bf16[16,96,512]{2,1,0:T(8,128)(2,1)} %tie.4), calls=%async_computation.2 | async-start | bytes 3145728 | tf_op jit(solution)/shard_map/all_to_all | solution.py:422
  126.8 1.5 collective-permute-start.1
  128.3 1.3 stack.34.info
  129.6 0.0 all-gather.2.cloned.1.call-done.x_ref
  129.6 0.0 copy-done.4
  129.6 9.4 %gate_up.2 = (bf16[576,512]{1,0:T(8,128)(2,1)}, bf16[640,64]{1,0:T(8,128)(2,1)}) custom-call(s32[20]{0:T(128)} %stack.34.info, bf16[2048,1664]{1,0:T(8,128)(2,1)} %all-gather.2.cloned.1.call-done.x_ref, bf16[1536,512]{1,0:T(8,128)(2,1)} %bitcast.50, bf16[1536,512]{1,0:T(8,128)(2,1)} %bitcast.53), custom_call_target="tpu_custom_call" | custom-call | tf_op jit(solution)/shard_map/gate_up/pallas_call | solution.py:467
  139.0 19.7 %all-to-all-done.2 = bf16[16,96,512]{2,1,0:T(8,128)(2,1)S(1)} async-done(((bf16[16,96,512]{2,1,0:T(8,128)(2,1)}), bf16[16,96,512]{2,1,0:T(8,128)(2,1)S(1)}, u32[]{:S(2)}, u32[]{:S(2)}) %all-to-all-start.2) | async-done | bytes 1572896 | tf_op jit(solution)/shard_map/all_to_all | solution.py:422
  158.7 0.0 copy-start
  158.7 1.1 copy-done
  159.9 4.3 %own_down.1 = (bf16[512,1536]{1,0:T(8,128)(2,1)}, bf16[64,1536]{1,0:T(8,128)(2,1)}) custom-call(bf16[576,512]{1,0:T(8,128)(2,1)} %get-tuple-element.19.__1_.hidden_ref, bf16[1536,512]{1,0:T(8,128)(2,1)} %tie.5.d_ref.d_own), custom_call_target="tpu_custom_call" | custom-call | tf_op jit(solution)/shard_map/own_down/pallas_call | solution.py:503
  164.2 0.0 collective-permute-done.1.__1_.u_ref.u_oth
  164.2 0.0 copy-start.1
  164.2 9.3 %all-to-all-start.4 = ((bf16[16,32,1536]{2,1,0:T(8,128)(2,1)}), bf16[16,32,1536]{2,1,0:T(8,128)(2,1)}, u32[]{:S(2)}, u32[]{:S(2)}) async-start(bf16[16,32,1536]{2,1,0:T(8,128)(2,1)} %bitcast.55), calls=%async_computation.4 | async-start | bytes 3145728 | tf_op jit(solution)/shard_map/all_to_all | solution.py:492
  173.5 0.0 copy-done.1
  173.5 1.0 fusion.8
  174.5 1.5 collective-permute-start.2
  176.0 18.3 %collective-permute-done.2.__.__1_.d_a = bf16[768,512]{1,0:T(8,128)(2,1)S(1)} collective-permute-done((bf16[768,512]{1,0:T(8,128)(2,1)S(1)}, bf16[768,512]{1,0:T(8,128)(2,1)S(1)}, u32[]{:S(2)}, u32[]{:S(2)}) %collective-permute-start.2) | collective-permute-done | bytes 786464 | tf_op jit(solution)/shard_map/ppermute | solution.py:426
  194.3 0.0 copy-start.5
  194.3 0.9 copy-done.5
  195.2 1.5 collective-permute-start.3
  196.6 9.7 %gate_up.3.hidden_ref = bf16[640,512]{1,0:T(8,128)(2,1)} custom-call(s32[20]{0:T(128)} %stack.34.info, bf16[2048,1664]{1,0:T(8,128)(2,1)} %all-gather.2.cloned.1.call-done.x_ref, bf16[1536,512]{1,0:T(8,128)(2,1)} %collective-permute-done.__1_.g_ref.g_oth, bf16[1536,512]{1,0:T(8,128)(2,1)} %collective-permute-done.1.__1_.u_ref.u_oth, ...), custom_call_target="tpu_custom_call" | custom-call | tf_op jit(solution)/shard_map/gate_up/pallas_call | solution.py:467
  206.3 8.1 %collective-permute-done.3.d_b = bf16[768,512]{1,0:T(8,128)(2,1)S(1)} collective-permute-done((bf16[768,512]{1,0:T(8,128)(2,1)}, bf16[768,512]{1,0:T(8,128)(2,1)S(1)}, u32[]{:S(2)}, u32[]{:S(2)}) %collective-permute-start.3) | collective-permute-done | bytes 786464 | tf_op jit(solution)/shard_map/ppermute | solution.py:426
  214.4 0.0 copy-start.6
  214.4 0.9 copy-done.6
  215.3 6.0 %oth_down.1._ = bf16[640,1536]{1,0:T(8,128)(2,1)} custom-call(bf16[640,512]{1,0:T(8,128)(2,1)} %gate_up.3.hidden_ref, bf16[640,64]{1,0:T(8,128)(2,1)} %get-tuple-element.21.spot_ref, bf16[64,1536]{1,0:T(8,128)(2,1)} %get-tuple-element.22.late_ref, bf16[768,512]{1,0:T(8,128)(2,1)} %copy-done.5, bf16[768,512]{1,0:T(8,128)(2,1)} %copy-done.6), custom_call_target="tpu_custom_call" | custom-call | tf_op jit(solution)/shard_map/oth_down/pallas_call | solution.py:523
  221.2 0.0 all-to-all-done.4
  221.2 5.6 %all-to-all-start.3 = ((bf16[16,40,1536]{2,1,0:T(8,128)(2,1)}), bf16[16,40,1536]{2,1,0:T(8,128)(2,1)S(1)}, u32[]{:S(2)}, u32[]{:S(2)}) async-start(bf16[16,40,1536]{2,1,0:T(8,128)(2,1)} %bitcast.48), calls=%async_computation.3 | async-start | bytes 3932160 | tf_op jit(solution)/shard_map/all_to_all | solution.py:492
  226.9 3.0 mix.1
  229.9 8.1 %place.1._ = bf16[3,1536,1024]{2,1,0:T(8,128)(2,1)} custom-call(s32[20]{0:T(128)} %stack.34.info, bf16[1536,512]{1,0:T(8,128)(2,1)} %bitcast.51, bf16[1536,512]{1,0:T(8,128)(2,1)} %collective-permute-done.__1_.g_ref.g_oth, bf16[1536,512]{1,0:T(8,128)(2,1)} %bitcast.54, bf16[1536,512]{1,0:T(8,128)(2,1)} %collective-permute-done.1.__1_.u_ref.u_oth, ...), custom_call_target="tpu_custom_call" | custom-call | tf_op jit(solution)/shard_map/place/pallas_call | solution.py:540
  238.0 4.7 %first.1 = (f32[128,1536]{1,0:T(8,128)}, f32[1,1536]{1,0:T(1,128)}) custom-call(s32[20]{0:T(128)} %stack.34.info, bf16[384,512]{1,0:T(8,128)(2,1)} %get-tuple-element.23.mix_ref, bf16[512,1536]{1,0:T(8,128)(2,1)} %bitcast.15.back_ref, bf16[128,1536]{1,0:T(8,128)(2,1)} %bitcast.57), custom_call_target="tpu_custom_call" | custom-call | tf_op jit(solution)/shard_map/first/pallas_call | solution.py:579
  242.7 23.0 %all-to-all-done.3 = bf16[16,40,1536]{2,1,0:T(8,128)(2,1)S(1)} async-done(((bf16[16,40,1536]{2,1,0:T(8,128)(2,1)}), bf16[16,40,1536]{2,1,0:T(8,128)(2,1)S(1)}, u32[]{:S(2)}, u32[]{:S(2)}) %all-to-all-start.3) | async-done | bytes 1966112 | tf_op jit(solution)/shard_map/all_to_all | solution.py:492
  265.7 0.0 copy-start.2
  265.7 1.3 copy-done.2
  267.0 3.3 %last.1._ = f32[16,1,1536]{2,1,0:T(1,128)} custom-call(bf16[16,640]{1,0:T(8,128)(2,1)} %get-tuple-element.25.mix_ref, bf16[640,1536]{1,0:T(8,128)(2,1)} %bitcast.46, f32[1,1536]{1,0:T(1,128)} %get-tuple-element.26.base_ref, bf16[3,1536,1024]{2,1,0:T(8,128)(2,1)} %place.1._), custom_call_target="tpu_custom_call" | custom-call | tf_op jit(solution)/shard_map/last/pallas_call | solution.py:594
  270.3 10.7 %all-to-all-start.5 = ((f32[16,1,1536]{2,1,0:T(1,128)}), f32[16,1,1536]{2,1,0:T(1,128)S(1)}, u32[]{:S(2)}, u32[]{:S(2)}) async-start(f32[16,1,1536]{2,1,0:T(1,128)} %last.1._), calls=%async_computation.5 | async-start | bytes 196608 | tf_op jit(solution)/shard_map/all_to_all | solution.py:626
  280.9 0.0 copy-start.7
  281.0 0.0 copy-start.8
  281.0 5.1 %combine.1 = (bf16[128,1536]{1,0:T(8,128)(2,1)}, f32[1,128]{1,0:T(1,128)}) custom-call(s32[20]{0:T(128)} %stack.34.info, bf16[384,640]{1,0:T(8,128)(2,1)} %get-tuple-element.18.mix_ref, bf16[640,1536]{1,0:T(8,128)(2,1)} %bitcast.47, f32[128,1536]{1,0:T(8,128)} %get-tuple-element.24.base_ref, f32[16,1,1536]{2,1,0:T(1,128)} %last.1._), custom_call_target="tpu_custom_call" | custom-call | tf_op jit(solution)/shard_map/combine/pallas_call | solution.py:608
  286.1 0.7 compare_select_fusion
  286.7 1.6 all-to-all-done.5
  288.4 0.1 fusion
  288.5 0.0 copy-done.7
  288.5 0.0 copy-done.8
  288.5 0.0 copy-start.9
  288.5 4.6 %fusion.7 = (f32[16]{0:T(128)S(1)}, f32[16]{0:T(128)S(1)}) fusion(s32[2048]{0:T(1024)S(1)} %iota_add_fusion, s32[16]{0:T(128)S(1)} %copy-done.8, bf16[2048,1536]{1,0:T(8,128)(2,1)} %param.15, f32[16,1,1536]{2,1,0:T(1,128)S(1)} %all-to-all-done.5, f32[1536]{0:T(1024)S(1)} %copy-done.7, f32[16]{0:T(128)S(1)} %add_rsqrt_fusion), kind=kOutput, calls=%fused_computation.17 | convolution fusion | flops 100868064 | bytes 6404352 | tf_op jit(solution)/shard_map/dot_general | solution.py:634
  293.2 10.8 %all_to_all.35 = f32[16,3,16]{2,1,0:T(4,128)S(1)} all-to-all(f32[16,3,16]{2,1,0:T(4,128)S(1)} %broadcast_in_dim.24), channel_id=1, replica_groups=mesh['blk'=16,'rep'=2] {'blk'}, dimensions={0} | all-to-all | bytes 6144 | tf_op jit(solution)/shard_map/all_to_all | solution.py:626
  304.0 0.0 copy-done.9
  304.1 0.6 pad_maximum_fusion.1
  (13 shorter events, 0.1 us)
Async XLA Ops:
  7.2 122.4 %all-gather.2.cloned.1.call-start = ((), (), s32[]{:S(2)}) async-start(), calls=%async_computation.7 | async-start | bytes 7241728 | tf_op jit(solution)/shard_map/all_gather | solution.py:464
  17.0 59.4 %all-to-all-start = ((bf16[16,96,512]{2,1,0:T(8,128)(2,1)}), bf16[16,96,512]{2,1,0:T(8,128)(2,1)S(1)}, u32[]{:S(2)}, u32[]{:S(2)}) async-start(bf16[16,96,512]{2,1,0:T(8,128)(2,1)} %cast.3), calls=%async_computation | async-start | bytes 3145728 | tf_op jit(solution)/shard_map/all_to_all | solution.py:422
  76.4 6.1 %copy-start.3 = (bf16[16,96,512]{2,1,0:T(8,128)(2,1)}, bf16[16,96,512]{2,1,0:T(8,128)(2,1)S(1)}, u32[]{:S(2)}) copy-start(bf16[16,96,512]{2,1,0:T(8,128)(2,1)S(1)} %all-to-all-done) | copy-start | bytes 4718596
  76.4 43.0 %all-to-all-start.1 = ((bf16[16,96,512]{2,1,0:T(8,128)(2,1)}), bf16[16,96,512]{2,1,0:T(8,128)(2,1)S(1)}, u32[]{:S(2)}, u32[]{:S(2)}) async-start(bf16[16,96,512]{2,1,0:T(8,128)(2,1)} %cast.4), calls=%async_computation.1 | async-start | bytes 3145728 | tf_op jit(solution)/shard_map/all_to_all | solution.py:422
  82.5 36.9 %collective-permute-start = (bf16[1536,512]{1,0:T(8,128)(2,1)S(1)}, bf16[1536,512]{1,0:T(8,128)(2,1)}, u32[]{:S(2)}, u32[]{:S(2)}) collective-permute-start(bf16[1536,512]{1,0:T(8,128)(2,1)S(1)} %bitcast.49), channel_id=1, source_target_pairs={{0,1},{1,0},{2,3},{3,2},{4,5},{5,4},{6,7},{7,6},{8,9},{9,8},{10,11... | collective-permute-start | bytes 4718600 | tf_op jit(solution)/shard_map/ppermute | solution.py:426
  119.4 10.2 %copy-start.4 = (bf16[16,96,512]{2,1,0:T(8,128)(2,1)}, bf16[16,96,512]{2,1,0:T(8,128)(2,1)S(1)}, u32[]{:S(2)}) copy-start(bf16[16,96,512]{2,1,0:T(8,128)(2,1)S(1)} %all-to-all-done.1) | copy-start | bytes 4718596
  119.4 39.3 %all-to-all-start.2 = ((bf16[16,96,512]{2,1,0:T(8,128)(2,1)}), bf16[16,96,512]{2,1,0:T(8,128)(2,1)S(1)}, u32[]{:S(2)}, u32[]{:S(2)}) async-start(bf16[16,96,512]{2,1,0:T(8,128)(2,1)} %tie.4), calls=%async_computation.2 | async-start | bytes 3145728 | tf_op jit(solution)/shard_map/all_to_all | solution.py:422
  126.8 37.4 %collective-permute-start.1 = (bf16[1536,512]{1,0:T(8,128)(2,1)S(1)}, bf16[1536,512]{1,0:T(8,128)(2,1)}, u32[]{:S(2)}, u32[]{:S(2)}) collective-permute-start(bf16[1536,512]{1,0:T(8,128)(2,1)S(1)} %bitcast.52), channel_id=1, source_target_pairs={{0,1},{1,0},{2,3},{3,2},{4,5},{5,4},{6,7},{7,6},{8,9},{9,8},{10,11... | collective-permute-start | bytes 4718600 | tf_op jit(solution)/shard_map/ppermute | solution.py:426
  158.7 1.1 copy-start
  164.2 9.3 %copy-start.1 = (bf16[1536,512]{1,0:T(8,128)(2,1)S(1)}, bf16[1536,512]{1,0:T(8,128)(2,1)}, u32[]{:S(2)}) copy-start(bf16[1536,512]{1,0:T(8,128)(2,1)} %tie.5.d_ref.d_own) | copy-start | bytes 4718596
  164.2 57.0 %all-to-all-start.4 = ((bf16[16,32,1536]{2,1,0:T(8,128)(2,1)}), bf16[16,32,1536]{2,1,0:T(8,128)(2,1)}, u32[]{:S(2)}, u32[]{:S(2)}) async-start(bf16[16,32,1536]{2,1,0:T(8,128)(2,1)} %bitcast.55), calls=%async_computation.4 | async-start | bytes 3145728 | tf_op jit(solution)/shard_map/all_to_all | solution.py:492
  174.5 19.8 %collective-permute-start.2 = (bf16[768,512]{1,0:T(8,128)(2,1)S(1)}, bf16[768,512]{1,0:T(8,128)(2,1)S(1)}, u32[]{:S(2)}, u32[]{:S(2)}) collective-permute-start(bf16[768,512]{1,0:T(8,128)(2,1)S(1)} %get-tuple-element.32), channel_id=1, source_target_pairs={{0,1},{1,0},{2,3},{3,2},{4,5},{5,4},{6,7},{7,6},{8,9},{9,8},{10,11... | collective-permute-start | bytes 2359304 | tf_op jit(solution)/shard_map/ppermute | solution.py:426
  194.3 0.9 copy-start.5
  195.2 19.2 %collective-permute-start.3 = (bf16[768,512]{1,0:T(8,128)(2,1)}, bf16[768,512]{1,0:T(8,128)(2,1)S(1)}, u32[]{:S(2)}, u32[]{:S(2)}) collective-permute-start(bf16[768,512]{1,0:T(8,128)(2,1)} %tie.7), channel_id=1, source_target_pairs={{0,1},{1,0},{2,3},{3,2},{4,5},{5,4},{6,7},{7,6},{8,9},{9,8},{10,11... | collective-permute-start | bytes 2359304 | tf_op jit(solution)/shard_map/ppermute | solution.py:426
  214.4 0.9 copy-start.6
  221.2 44.5 %all-to-all-start.3 = ((bf16[16,40,1536]{2,1,0:T(8,128)(2,1)}), bf16[16,40,1536]{2,1,0:T(8,128)(2,1)S(1)}, u32[]{:S(2)}, u32[]{:S(2)}) async-start(bf16[16,40,1536]{2,1,0:T(8,128)(2,1)} %bitcast.48), calls=%async_computation.3 | async-start | bytes 3932160 | tf_op jit(solution)/shard_map/all_to_all | solution.py:492
  265.7 1.3 copy-start.2
  270.3 18.1 %all-to-all-start.5 = ((f32[16,1,1536]{2,1,0:T(1,128)}), f32[16,1,1536]{2,1,0:T(1,128)S(1)}, u32[]{:S(2)}, u32[]{:S(2)}) async-start(f32[16,1,1536]{2,1,0:T(1,128)} %last.1._), calls=%async_computation.5 | async-start | bytes 196608 | tf_op jit(solution)/shard_map/all_to_all | solution.py:626
  280.9 7.5 %copy-start.7 = (f32[1536]{0:T(1024)S(1)}, f32[1536]{0:T(1024)}, u32[]{:S(2)}) copy-start(f32[1536]{0:T(1024)} %param.16) | copy-start | bytes 18436
  281.0 7.5 %copy-start.8 = (s32[16]{0:T(128)S(1)}, s32[16]{0:T(128)}, u32[]{:S(2)}) copy-start(s32[16]{0:T(128)} %param.17) | copy-start | bytes 196
  288.5 15.5 %copy-start.9 = (s32[16]{0:T(128)S(1)}, s32[16]{0:T(128)}, u32[]{:S(2)}) copy-start(s32[16]{0:T(128)} %param.10) | copy-start | bytes 196
Sparse Core Ops, SparseCore 0:
  11.6 86.2 all-gather.1

commit v10 on v9

--- a/solution.py
+++ b/solution.py
@@ -16,7 +16,7 @@
 GROUPS = 4
 RING = (0, 1, 4, 5, 8, 9, 12, 13, 14, 15, 10, 11, 6, 7, 2, 3)
 LANES = 128
-VMEM = 56 * 1024 * 1024
+VMEM = 36 * 1024 * 1024
 
 
 def merged(x, axis, combine):
@@ -231,7 +231,7 @@
         spot_ref[...] = jnp.where(iota(spot_ref.shape, 0) == spot, 1.0, 0.0).astype(jnp.bfloat16)
 
 
-def oth_kernel(info, x_ref, g_ref, u_ref, _, __, out_ref, picked):
+def oth_kernel(info, x_ref, g_ref, u_ref, _, out_ref, picked):
     step = pl.program_id(0)
     sources = x_ref.shape[0] // LEN
 
@@ -248,30 +248,46 @@
         out_ref[...] = activ(picked[...], g_ref, u_ref)
 
 
-def matmul_nt(hidden_ref, d_ref):
+def matmul_nt(hidden_ref, d):
     return lax.dot_general(
-        hidden_ref[...], d_ref[...], (((1,), (1,)), ((), ())), preferred_element_type=jnp.float32
-    )
-
-
-def own_down_kernel(hidden_ref, d_ref, out_ref, late_ref):
-    out = matmul_nt(hidden_ref, d_ref).astype(jnp.bfloat16)
+        hidden_ref[...], d, (((1,), (1,)), ((), ())), preferred_element_type=jnp.float32
+    )
+
+
+def fetched(sources, held, sems):
+    step = pl.program_id(0)
+    rows = held.shape[1]
+
+    @pl.when(step == 0)
+    def _():
+        for k, source in enumerate(sources):
+            pltpu.make_async_copy(source, held.at[k], sems.at[k]).start()
+
+    for k, source in enumerate(sources):
+
+        @pl.when(step == k)
+        def _():
+            pltpu.make_async_copy(source, held.at[k], sems.at[k]).wait()
+
+    return held[step]
+
+
+def own_down_kernel(hidden_ref, d_ref, out_ref, late_ref, held, sems):
+    size = held.shape[1]
+    d = fetched([d_ref.at[k * size : (k + 1) * size] for k in range(held.shape[0])], held, sems)
+    out = matmul_nt(hidden_ref, d).astype(jnp.bfloat16)
     rows = out_ref.shape[0]
     out_ref[...] = out[:rows]
     late_ref[...] = out[rows:]
 
 
-def oth_down_kernel(hidden_ref, spot_ref, late_ref, d_a, d_b, out_ref):
+def oth_down_kernel(info, hidden_ref, spot_ref, late_ref, d_a, d_b, out_ref, held, sems):
+    size = held.shape[1]
+    other = 1 - info[2]
+    sources = [d_a.at[other, :size], d_a.at[other, size:], d_b.at[:size], d_b.at[size:]]
+    d = fetched(sources, held, sems)
     late = jnp.dot(spot_ref[...], late_ref[...], preferred_element_type=jnp.float32)
-    in_a = pl.program_id(0) < pl.num_programs(0) // 2
-
-    @pl.when(in_a)
-    def _():
-        out_ref[...] = (late + matmul_nt(hidden_ref, d_a)).astype(jnp.bfloat16)
-
-    @pl.when(jnp.logical_not(in_a))
-    def _():
-        out_ref[...] = (late + matmul_nt(hidden_ref, d_b)).astype(jnp.bfloat16)
+    out_ref[...] = (late + matmul_nt(hidden_ref, d)).astype(jnp.bfloat16)
 
 
 def mix_kernel(info, rank_ref, pieces_ref, first_ref, second_ref, last_ref):
@@ -321,8 +337,20 @@
     last_ref[...] = jnp.sum(jnp.where(is_last, base, 0.0), axis=0, keepdims=True)
 
 
-def last_kernel(mix_ref, back_ref, base_ref, _, told_ref):
-    parts = jnp.dot(mix_ref[...], back_ref[...], preferred_element_type=jnp.float32)
+def last_kernel(mix_ref, base_ref, back_ref, _, told_ref, held, sems):
+    size = held.shape[1]
+    copies = [
+        pltpu.make_async_copy(back_ref.at[k * size : (k + 1) * size], held.at[k], sems.at[k])
+        for k in range(held.shape[0])
+    ]
+    for copy in copies:
+        copy.start()
+    parts = jnp.zeros((mix_ref.shape[0], held.shape[2]), jnp.float32)
+    for k, copy in enumerate(copies):
+        copy.wait()
+        parts = parts + jnp.dot(
+            mix_ref[:, k * size : (k + 1) * size], held[k], preferred_element_type=jnp.float32
+        )
     moe = parts[2:3] + parts[1:2] + parts[0:1]
     out = (base_ref[...] + moe).astype(jnp.bfloat16).astype(jnp.float32)
     told_ref[...] = jnp.broadcast_to(out[None], told_ref.shape)
@@ -360,19 +388,19 @@
 
 def cast_kernel(blocks, x_ref, *refs):
     out_ref, order = refs[-2:]
-    rows = out_ref.shape[1]
 
     @pl.when(pl.program_id(0) == 0)
     def _():
         target = iota(order.shape, 0)
-        source = (target & (rows - 1)) * blocks + lax.shift_right_logical(target, 4)
+        source = (target & 15) * blocks + lax.shift_right_logical(target, 4)
         order[...] = jnp.where(iota(order.shape, 1) == source, 1.0, 0.0).astype(jnp.bfloat16)
 
-    turned = jnp.dot(
-        order[...], x_ref[...].astype(jnp.bfloat16), preferred_element_type=jnp.float32
-    ).astype(jnp.bfloat16)
-    for b in range(blocks):
-        out_ref[b] = turned[b * rows : (b + 1) * rows]
+    size = order.shape[0]
+    for group in range(x_ref.shape[0] // size):
+        x = x_ref[group * size : (group + 1) * size].astype(jnp.bfloat16)
+        turned = jnp.dot(order[...], x, preferred_element_type=jnp.float32).astype(jnp.bfloat16)
+        for b in range(blocks):
+            out_ref[b, group * 16 : (group + 1) * 16] = turned[b * 16 : (b + 1) * 16]
 
 
 def tie_kernel(*_):
@@ -408,10 +436,10 @@
     def turned(k, *after):
         return pl.pallas_call(
             functools.partial(cast_kernel, blk_count),
-            grid=(shard_rows // 16,),
-            in_specs=[pl.BlockSpec((16 * blk_count, FF), lambda i: (k * (shard_rows // 16) + i, 0))]
+            grid=(2,),
+            in_specs=[pl.BlockSpec((shard_rows // 2 * blk_count, FF), lambda i: (2 * k + i, 0))]
             + [pl.BlockSpec(memory_space=pl.ANY)] * len(after),
-            out_specs=pl.BlockSpec((blk_count, 16, FF), lambda i: (0, i, 0)),
+            out_specs=pl.BlockSpec((blk_count, shard_rows // 2, FF), lambda i: (0, i, 0)),
             out_shape=jax.ShapeDtypeStruct((blk_count, shard_rows, FF), jnp.bfloat16),
             scratch_shapes=[pltpu.VMEM((16 * blk_count, 16 * blk_count), jnp.bfloat16)],
             compiler_params=params(),
@@ -483,8 +511,9 @@
     step = 512
 
     quarter = width // 4
-    in_a = pl.BlockSpec((quarter, FF), lambda i, *_: (jnp.minimum(i, 1), 0))
+    in_a = pl.BlockSpec((None, quarter, FF), lambda i, info: (1 - info[2], jnp.minimum(i, 1), 0))
     in_b = pl.BlockSpec((quarter, FF), lambda i, *_: (jnp.maximum(i, 2) - 2, 0))
+    anywhere = pl.BlockSpec(memory_space=pl.ANY)
 
     def returned(x):
         slots = x.shape[0]
@@ -498,12 +527,12 @@
     )
     d_own = tied(d_own, own_hidden)
     half = width // 2
-    d_oth_a = swapped(d_own[:half])
-    d_oth_b = swapped(tied(d_own[half:], d_oth_a))
+    d_oth_a = lax.all_gather(d_own[:half], "rep", axis=0)
+    d_oth_b = swapped(d_own[half:])
     own_out, late_out = pl.pallas_call(
         own_down_kernel,
         grid=(width // step,),
-        in_specs=[whole((first + extra, FF)), pl.BlockSpec((step, FF), lambda i: (i, 0))],
+        in_specs=[whole((first + extra, FF)), anywhere],
         out_specs=[
             pl.BlockSpec((first, step), lambda i: (0, i)),
             pl.BlockSpec((extra, step), lambda i: (0, i)),
@@ -512,29 +541,40 @@
             jax.ShapeDtypeStruct((first, width), jnp.bfloat16),
             jax.ShapeDtypeStruct((extra, width), jnp.bfloat16),
         ],
+        scratch_shapes=[
+            pltpu.VMEM((width // step, step, FF), jnp.bfloat16),
+            pltpu.SemaphoreType.DMA((width // step,)),
+        ],
         compiler_params=params(),
         name="own_down",
     )(own_hidden, d_own)
     own_out = tied(own_out, u_oth)
     own_back = returned(own_out)
     (oth_hidden,) = hidden_of(
-        oth_kernel, ((second, FF),), second, g_oth, u_oth, own_out, d_oth_a
+        oth_kernel, ((second, FF),), second, g_oth, u_oth, own_out
     )
     oth_out = pl.pallas_call(
         oth_down_kernel,
-        grid=(4,),
-        in_specs=[
-            whole((second, FF)),
-            whole((second, extra)),
-            pl.BlockSpec((extra, quarter), lambda i: (0, i)),
-            in_a,
-            in_b,
-        ],
-        out_specs=pl.BlockSpec((second, quarter), lambda i: (0, i)),
+        grid_spec=pltpu.PrefetchScalarGridSpec(
+            num_scalar_prefetch=1,
+            grid=(4,),
+            in_specs=[
+                whole((second, FF)),
+                whole((second, extra)),
+                pl.BlockSpec((extra, quarter), lambda i, *_: (0, i)),
+                anywhere,
+                anywhere,
+            ],
+            out_specs=pl.BlockSpec((second, quarter), lambda i, *_: (0, i)),
+            scratch_shapes=[
+                pltpu.VMEM((4, quarter, FF), jnp.bfloat16),
+                pltpu.SemaphoreType.DMA((4,)),
+            ],
+        ),
         out_shape=jax.ShapeDtypeStruct((second, width), jnp.bfloat16),
         compiler_params=params(),
         name="oth_down",
-    )(oth_hidden, spot, late_out, d_oth_a, d_oth_b)
+    )(info, oth_hidden, spot, late_out, d_oth_a, d_oth_b)
     oth_back = returned(oth_out)
 
     server = pl.pallas_call(
@@ -593,18 +633,17 @@
     )(info, first_mix, own_back, resid)
     told = pl.pallas_call(
         last_kernel,
-        grid=(width // step,),
-        in_specs=[
-            whole((16, second)),
-            pl.BlockSpec((second, step), lambda i: (0, i)),
-            lane_row,
-            pl.BlockSpec(memory_space=pl.ANY),
+        grid=(1,),
+        in_specs=[whole((16, second)), whole((1, width)), anywhere, anywhere],
+        out_specs=whole((blk_count, 1, width)),
+        out_shape=jax.ShapeDtypeStruct((blk_count, 1, width), jnp.float32),
+        scratch_shapes=[
+            pltpu.VMEM((second // LANES, LANES, width), jnp.bfloat16),
+            pltpu.SemaphoreType.DMA((second // LANES,)),
         ],
-        out_specs=pl.BlockSpec((blk_count, 1, step), lambda i: (0, 0, i)),
-        out_shape=jax.ShapeDtypeStruct((blk_count, 1, width), jnp.float32),
         compiler_params=params(),
         name="last",
-    )(last_mix, oth_back, last_base, server)
+    )(last_mix, last_base, oth_back, server)
     out_rows, square = pl.pallas_call(
         combine_kernel,
         grid_spec=pltpu.PrefetchScalarGridSpec(

time: 313 us -> 318 us (1.016)
  local copies, waits for them, and re-layouts: 7.86 us -> 54.1 us
  Pallas kernels: 73 us -> 40.7 us
  waiting for transfers between devices: 147 us -> 140 us
    unnamed x20 -> x86, local copies, waits for them, and re-layouts: 4.25 us -> 50.9 us
    pallas_call x5, Pallas kernels: 25.7 us -> 9.69 us  [the longest x1 4.17 us: paired(): pl.pallas_call(oth_down_kernel, grid_spec=pltpu.PrefetchScalarGridSpec(nu...]
    ppermute x4 -> x3, waiting for transfers between devices: 56.3 us -> 45.2 us  [swapped(): return lax.ppermute(x, 'rep', [(0, 1), (1, 0)])]
    all_gather x0 -> x1, waiting for transfers between devices: none -> 7.91 us  [paired(): d_oth_a = lax.all_gather(d_own[:half], 'rep', axis=0)]
    pallas_call x2, Pallas kernels: 19.1 us -> 12.2 us  [hidden_of(): pl.pallas_call(kernel, grid_spec=pltpu.PrefetchScalarGridSpec(num_scalar_...]
    all_to_all x2, waiting for transfers between devices: 23 us -> 17.6 us  [returned(): x = lax.all_to_all(x, 'blk', split_axis=0, concat_axis=0, tiled=True)]
  transfers between devices with their start and end apart: 11 -> 11, of which waited for: 7 -> 7; matrix products, arithmetic and copies ran while one was open for 1% -> 1% of each run, Pallas kernels for 21% -> 12%
where the time goes in v10:
time: 318 us; the launch traced here: 316 us
  waiting for transfers between devices  140 us (44%)
  local copies, waits for them, and re-layouts  54.1 us (17%)
  starting transfers between devices  51.6 us (16%)
  Pallas kernels  40.7 us (13%)
  between operations  14.4 us (5%)
  blocking collectives  9.2 us (3%)
  matrix products  4.64 us (1%)
    all_to_all x3, waiting for transfers between devices, moved(): own = lax.all_to_all(x, 'blk', split_axis=0, concat_axis=0, tiled=True)  65.5 us
    unnamed x86, local copies, waits for them, and re-layouts  50.9 us
    ppermute x3, waiting for transfers between devices, swapped(): return lax.ppermute(x, 'rep', [(0, 1), (1, 0)])  45.2 us
    all_to_all x3, starting transfers between devices, moved(): own = lax.all_to_all(x, 'blk', split_axis=0, concat_axis=0, tiled=True)  21.1 us
    all_to_all x2, waiting for transfers between devices, returned(): x = lax.all_to_all(x, 'blk', split_axis=0, concat_axis=0, tiled=True)  17.6 us
    all_to_all x2, starting transfers between devices, returned(): x = lax.all_to_all(x, 'blk', split_axis=0, concat_axis=0, tiled=True)  15 us
    pallas_call x2, Pallas kernels, hidden_of(): pl.pallas_call(kernel, grid_spec=pltpu.PrefetchScalarGridSpec(num_scalar_...  12.2 us
    all_to_all x1, starting transfers between devices, everywhere(): lax.all_to_all(copies, 'blk', split_axis=0, concat_axis=0, tiled=True)  10.7 us
  transfers between devices with their start and end apart: 11, of which 7 were waited for; matrix products, arithmetic and copies ran while one was open for 1% of the time, Pallas kernels for 12%

profile of v10, /device:TPU:0, one launch (start us, length us, event | category | flops | bytes accessed | tf_op | source)
XLA Modules:
  0.0 315.9 jit_solution(7912432668270618411)
XLA Ops:
  7.2 1.2 dynamic_slice.3.length_ref
  8.4 1.0 copy-done.29
  9.4 0.7 copy-done.37
  10.1 0.7 copy-done.38
  11.5 1.9 prep.1
  14.1 3.7 %copy-done = f32[3,96,16,512]{3,2,1,0:T(8,128)S(1)} copy-done((f32[3,96,16,512]{3,2,1,0:T(8,128)S(1)}, f32[3,96,16,512]{3,2,1,0:T(8,128)}, u32[]{:S(2)}) %copy-start) | copy-done | bytes 9437208
  17.8 1.7 cast.3
  19.5 7.4 %all-to-all-start = ((bf16[16,96,512]{2,1,0:T(8,128)(2,1)}), bf16[16,96,512]{2,1,0:T(8,128)(2,1)S(1)}, u32[]{:S(2)}, u32[]{:S(2)}) async-start(bf16[16,96,512]{2,1,0:T(8,128)(2,1)} %cast.3), calls=%async_computation | async-start | bytes 3145728 | tf_op jit(solution)/shard_map/all_to_all | solution.py:450
  26.9 3.9 %copy-done.1 = f32[3,96,16,512]{3,2,1,0:T(8,128)S(1)} copy-done((f32[3,96,16,512]{3,2,1,0:T(8,128)S(1)}, f32[3,96,16,512]{3,2,1,0:T(8,128)}, u32[]{:S(2)}) %copy-start.1) | copy-done | bytes 9437208
  30.7 0.9 cast.4
  31.7 1.1 copy-done.21
  32.8 46.0 %all-to-all-done = bf16[16,96,512]{2,1,0:T(8,128)(2,1)S(1)} async-done(((bf16[16,96,512]{2,1,0:T(8,128)(2,1)}), bf16[16,96,512]{2,1,0:T(8,128)(2,1)S(1)}, u32[]{:S(2)}, u32[]{:S(2)}) %all-to-all-start) | async-done | bytes 1572896 | tf_op jit(solution)/shard_map/all_to_all | solution.py:450
  78.7 6.3 %all-to-all-start.1 = ((bf16[16,96,512]{2,1,0:T(8,128)(2,1)}), bf16[16,96,512]{2,1,0:T(8,128)(2,1)S(1)}, u32[]{:S(2)}, u32[]{:S(2)}) async-start(bf16[16,96,512]{2,1,0:T(8,128)(2,1)} %copy-done.21), calls=%async_computation.1 | async-start | bytes 3145728 | tf_op jit(solution)/shard_map/all_to_all | solution.py:450
  85.0 1.6 collective-permute-start
  86.6 3.8 %copy-done.2 = f32[3,96,16,512]{3,2,1,0:T(8,128)S(1)} copy-done((f32[3,96,16,512]{3,2,1,0:T(8,128)S(1)}, f32[3,96,16,512]{3,2,1,0:T(8,128)}, u32[]{:S(2)}) %copy-start.2) | copy-done | bytes 9437208
  90.3 0.9 cast.5.__0_
  91.3 1.2 copy-done.18
  92.5 29.3 %collective-permute-done.__1_.g_ref.g_oth = bf16[1536,512]{1,0:T(8,128)(2,1)} collective-permute-done((bf16[1536,512]{1,0:T(8,128)(2,1)S(1)}, bf16[1536,512]{1,0:T(8,128)(2,1)}, u32[]{:S(2)}, u32[]{:S(2)}) %collective-permute-start) | collective-permute-done | bytes 1572896 | tf_op jit(solution)/shard_map/ppermute | solution.py:454
  121.8 1.1 copy-done.13
  123.0 7.5 %all-to-all-start.2 = ((bf16[16,96,512]{2,1,0:T(8,128)(2,1)}), bf16[16,96,512]{2,1,0:T(8,128)(2,1)S(1)}, u32[]{:S(2)}, u32[]{:S(2)}) async-start(bf16[16,96,512]{2,1,0:T(8,128)(2,1)} %tie.3), calls=%async_computation.2 | async-start | bytes 3145728 | tf_op jit(solution)/shard_map/all_to_all | solution.py:450
  130.5 1.5 collective-permute-start.1
  132.7 2.9 copy-done.7
  135.6 1.4 copy-done.14
  137.1 5.0 %gate_up.2 = (bf16[576,512]{1,0:T(8,128)(2,1)S(1)}, bf16[640,64]{1,0:T(8,128)(2,1)S(1)}) custom-call(s32[20]{0:T(128)S(1)} %stack.34.info, bf16[2048,1664]{1,0:T(8,128)(2,1)S(1)} %copy-done.7, bf16[1536,512]{1,0:T(8,128)(2,1)S(1)} %bitcast.51, bf16[1536,512]{1,0:T(8,128)(2,1)S(1)} %bitcast.54), custom_call_target="tpu_custom_call" | custom-call | tf_op jit(solution)/shard_map/gate_up/pallas_call | solution.py:495
  142.1 0.8 copy-done.27
  142.9 19.6 %all-to-all-done.2 = bf16[16,96,512]{2,1,0:T(8,128)(2,1)S(1)} async-done(((bf16[16,96,512]{2,1,0:T(8,128)(2,1)}), bf16[16,96,512]{2,1,0:T(8,128)(2,1)S(1)}, u32[]{:S(2)}, u32[]{:S(2)}) %all-to-all-start.2) | async-done | bytes 1572896 | tf_op jit(solution)/shard_map/all_to_all | solution.py:450
  162.5 1.1 copy-done.3
  163.6 1.1 copy-done.28
  164.7 1.4 copy-done.4
  166.1 1.8 own_down.1
  167.8 1.1 copy-done.16
  169.0 9.3 %all-to-all-start.4 = ((bf16[16,32,1536]{2,1,0:T(8,128)(2,1)}), bf16[16,32,1536]{2,1,0:T(8,128)(2,1)}, u32[]{:S(2)}, u32[]{:S(2)}) async-start(bf16[16,32,1536]{2,1,0:T(8,128)(2,1)} %bitcast.56), calls=%async_computation.4 | async-start | bytes 3145728 | tf_op jit(solution)/shard_map/all_to_all | solution.py:521
  178.3 1.2 fusion.8
  179.6 1.6 collective-permute-start.2
  181.2 2.9 copy-done.8
  184.1 7.2 %gate_up.3.hidden_ref = bf16[640,512]{1,0:T(8,128)(2,1)S(1)} custom-call(s32[20]{0:T(128)S(1)} %stack.34.info, bf16[2048,1664]{1,0:T(8,128)(2,1)S(1)} %copy-done.8, bf16[1536,512]{1,0:T(8,128)(2,1)} %collective-permute-done.__1_.g_ref.g_oth, bf16[1536,512]{1,0:T(8,128)(2,1)} %collective-permute-done.1.__1_.u_ref.u_oth, bf16[512,1536]{1,0:T(8,128)(2,1)S(1)} %copy-done.17), custom_call_target="tpu_custom_call" | custom-call | tf_op jit(solution)/shard_map/gate_up/pallas_call | solution.py:495
  191.3 0.8 copy-done.25
  192.2 15.8 %collective-permute-done.2.d_b = bf16[768,512]{1,0:T(8,128)(2,1)S(1)} collective-permute-done((bf16[768,512]{1,0:T(8,128)(2,1)}, bf16[768,512]{1,0:T(8,128)(2,1)S(1)}, u32[]{:S(2)}, u32[]{:S(2)}) %collective-permute-start.2) | collective-permute-done | bytes 786464 | tf_op jit(solution)/shard_map/ppermute | solution.py:454
  208.0 0.9 copy-done.22
  208.9 7.9 %all-gather.6.cloned.1.call-done = bf16[1536,512]{1,0:T(8,128)(2,1)} async-done(((bf16[768,512]{1,0:T(8,128)(2,1)}), bf16[1536,512]{1,0:T(8,128)(2,1)}) %all-gather.6.cloned.1.call-update) | async-done | bytes 1572880 | tf_op jit(solution)/shard_map/all_gather | solution.py:530
  216.8 1.4 copy-done.19
  218.2 1.1 copy-done.23
  219.3 1.1 copy-done.26
  220.4 4.2 %oth_down.1._ = bf16[640,1536]{1,0:T(8,128)(2,1)S(1)} custom-call(s32[20]{0:T(128)S(1)} %stack.34.info, bf16[640,512]{1,0:T(8,128)(2,1)S(1)} %copy-done.26, bf16[640,64]{1,0:T(8,128)(2,1)S(1)} %get-tuple-element.21.spot_ref, bf16[64,1536]{1,0:T(8,128)(2,1)S(1)} %get-tuple-element.22.late_ref, bf16[2,768,512]{2,1,0:T(8,128)(2,1)S(1)} %bitcast.57, ...), custom_call_target="tpu_custom_call" | custom-call | tf_op jit(solution)/shard_map/oth_down/pallas_call | solution.py:556
  224.6 1.3 copy-done.9
  225.9 5.8 %all-to-all-start.3 = ((bf16[16,40,1536]{2,1,0:T(8,128)(2,1)}), bf16[16,40,1536]{2,1,0:T(8,128)(2,1)S(1)}, u32[]{:S(2)}, u32[]{:S(2)}) async-start(bf16[16,40,1536]{2,1,0:T(8,128)(2,1)} %bitcast.49), calls=%async_computation.3 | async-start | bytes 3932160 | tf_op jit(solution)/shard_map/all_to_all | solution.py:521
  231.7 0.9 copy-done.34
  232.6 2.1 mix.1
  234.7 0.8 copy-done.31
  236.1 1.5 copy-done.10
  237.6 1.4 copy-done.12
  239.0 1.4 copy-done.15
  240.4 1.4 copy-done.20
  241.8 1.1 copy-done.24
  243.0 6.5 %place.1._ = bf16[3,1536,1024]{2,1,0:T(8,128)(2,1)} custom-call(s32[20]{0:T(128)S(1)} %stack.34.info, bf16[1536,512]{1,0:T(8,128)(2,1)S(1)} %bitcast.52, bf16[1536,512]{1,0:T(8,128)(2,1)} %collective-permute-done.__1_.g_ref.g_oth, bf16[1536,512]{1,0:T(8,128)(2,1)S(1)} %bitcast.55, bf16[1536,512]{1,0:T(8,128)(2,1)} %collective-permute-done.1.__1_.u_ref.u_oth, ...), custom_call_target="tpu_custom_call" | custom-call | tf_op jit(solution)/shard_map/place/pallas_call | solution.py:580
  249.5 3.4 %first.1 = (f32[128,1536]{1,0:T(8,128)S(1)}, f32[1,1536]{1,0:T(1,128)S(1)}) custom-call(s32[20]{0:T(128)S(1)} %stack.34.info, bf16[384,512]{1,0:T(8,128)(2,1)S(1)} %get-tuple-element.23.mix_ref, bf16[512,1536]{1,0:T(8,128)(2,1)} %bitcast.16.back_ref, bf16[128,1536]{1,0:T(8,128)(2,1)S(1)} %bitcast.60), custom_call_target="tpu_custom_call" | custom-call | tf_op jit(solution)/shard_map/first/pallas_call | solution.py:619
  252.9 17.5 %all-to-all-done.3 = bf16[16,40,1536]{2,1,0:T(8,128)(2,1)S(1)} async-done(((bf16[16,40,1536]{2,1,0:T(8,128)(2,1)}), bf16[16,40,1536]{2,1,0:T(8,128)(2,1)S(1)}, u32[]{:S(2)}, u32[]{:S(2)}) %all-to-all-start.3) | async-done | bytes 1966112 | tf_op jit(solution)/shard_map/all_to_all | solution.py:521
  270.5 3.7 %copy-done.6 = bf16[3,1536,1024]{2,1,0:T(8,128)(2,1)S(1)} copy-done((bf16[3,1536,1024]{2,1,0:T(8,128)(2,1)S(1)}, bf16[3,1536,1024]{2,1,0:T(8,128)(2,1)}, u32[]{:S(2)}) %copy-start.6) | copy-done | bytes 9437208
  274.2 2.0 last.1._
  276.2 10.7 %all-to-all-start.5 = ((f32[16,1,1536]{2,1,0:T(1,128)}), f32[16,1,1536]{2,1,0:T(1,128)S(1)}, u32[]{:S(2)}, u32[]{:S(2)}) async-start(f32[16,1,1536]{2,1,0:T(1,128)} %last.1._), calls=%async_computation.5 | async-start | bytes 196608 | tf_op jit(solution)/shard_map/all_to_all | solution.py:665
  287.0 3.1 combine.1
  290.1 4.3 %all-to-all-done.5 = f32[16,1,1536]{2,1,0:T(1,128)S(1)} async-done(((f32[16,1,1536]{2,1,0:T(1,128)}), f32[16,1,1536]{2,1,0:T(1,128)S(1)}, u32[]{:S(2)}, u32[]{:S(2)}) %all-to-all-start.5) | async-done | bytes 98336 | tf_op jit(solution)/shard_map/all_to_all | solution.py:665
  294.5 4.6 %fusion.7 = (f32[16]{0:T(128)S(1)}, f32[16]{0:T(128)S(1)}) fusion(s32[2048]{0:T(1024)S(1)} %iota_add_fusion, s32[16]{0:T(128)S(1)} %copy-done.41, bf16[2048,1536]{1,0:T(8,128)(2,1)} %param.15, f32[16,1,1536]{2,1,0:T(1,128)S(1)} %all-to-all-done.5, f32[1536]{0:T(1024)S(1)} %copy-done.40, f32[16]{0:T(128)S(1)} %add_rsqrt_fusion), kind=kOutput, calls=%fused_computation.17 | convolution fusion | flops 100868064 | bytes 6404352 | tf_op jit(solution)/shard_map/dot_general | solution.py:673
  299.2 9.2 %all_to_all.35 = f32[16,3,16]{2,1,0:T(4,128)S(1)} all-to-all(f32[16,3,16]{2,1,0:T(4,128)S(1)} %broadcast_in_dim.24), channel_id=1, replica_groups=mesh['blk'=16,'rep'=2] {'blk'}, dimensions={0} | all-to-all | bytes 6144 | tf_op jit(solution)/shard_map/all_to_all | solution.py:665
  (79 shorter events, 3.6 us)
Async XLA Ops:
  7.2 125.5 %all-gather.4.cloned.1.call-start = ((), (), s32[]{:S(2)}) async-start(), calls=%async_computation.7 | async-start | bytes 7241728 | tf_op jit(solution)/shard_map/all_gather | solution.py:492
  8.4 1.0 copy-start.29
  9.4 0.7 copy-start.37
  10.1 0.7 copy-start.38
  10.8 0.7 copy-start.39
  13.4 0.6 copy-start.33
  14.1 3.7 %copy-start = (f32[3,96,16,512]{3,2,1,0:T(8,128)S(1)}, f32[3,96,16,512]{3,2,1,0:T(8,128)}, u32[]{:S(2)}) copy-start(f32[3,96,16,512]{3,2,1,0:T(8,128)} %param.14) | copy-start | bytes 28311556
  19.5 59.2 %all-to-all-start = ((bf16[16,96,512]{2,1,0:T(8,128)(2,1)}), bf16[16,96,512]{2,1,0:T(8,128)(2,1)S(1)}, u32[]{:S(2)}, u32[]{:S(2)}) async-start(bf16[16,96,512]{2,1,0:T(8,128)(2,1)} %cast.3), calls=%async_computation | async-start | bytes 3145728 | tf_op jit(solution)/shard_map/all_to_all | solution.py:450
  26.9 3.9 %copy-start.1 = (f32[3,96,16,512]{3,2,1,0:T(8,128)S(1)}, f32[3,96,16,512]{3,2,1,0:T(8,128)}, u32[]{:S(2)}) copy-start(f32[3,96,16,512]{3,2,1,0:T(8,128)} %param.14) | copy-start | bytes 28311556
  31.6 1.1 copy-start.21
  78.7 54.0 %copy-start.11 = (bf16[16,96,512]{2,1,0:T(8,128)(2,1)}, bf16[16,96,512]{2,1,0:T(8,128)(2,1)S(1)}, u32[]{:S(2)}) copy-start(bf16[16,96,512]{2,1,0:T(8,128)(2,1)S(1)} %all-to-all-done) | copy-start | bytes 4718596
  78.7 43.1 %all-to-all-start.1 = ((bf16[16,96,512]{2,1,0:T(8,128)(2,1)}), bf16[16,96,512]{2,1,0:T(8,128)(2,1)S(1)}, u32[]{:S(2)}, u32[]{:S(2)}) async-start(bf16[16,96,512]{2,1,0:T(8,128)(2,1)} %copy-done.21), calls=%async_computation.1 | async-start | bytes 3145728 | tf_op jit(solution)/shard_map/all_to_all | solution.py:450
  85.0 36.8 %collective-permute-start = (bf16[1536,512]{1,0:T(8,128)(2,1)S(1)}, bf16[1536,512]{1,0:T(8,128)(2,1)}, u32[]{:S(2)}, u32[]{:S(2)}) collective-permute-start(bf16[1536,512]{1,0:T(8,128)(2,1)S(1)} %bitcast.50), channel_id=1, source_target_pairs={{0,1},{1,0},{2,3},{3,2},{4,5},{5,4},{6,7},{7,6},{8,9},{9,8},{10,11... | collective-permute-start | bytes 4718600 | tf_op jit(solution)/shard_map/ppermute | solution.py:454
  86.6 3.8 %copy-start.2 = (f32[3,96,16,512]{3,2,1,0:T(8,128)S(1)}, f32[3,96,16,512]{3,2,1,0:T(8,128)}, u32[]{:S(2)}) copy-start(f32[3,96,16,512]{3,2,1,0:T(8,128)} %param.14) | copy-start | bytes 28311556
  91.2 1.2 copy-start.18
  121.8 1.1 copy-start.13
  123.0 39.5 %all-to-all-start.2 = ((bf16[16,96,512]{2,1,0:T(8,128)(2,1)}), bf16[16,96,512]{2,1,0:T(8,128)(2,1)S(1)}, u32[]{:S(2)}, u32[]{:S(2)}) async-start(bf16[16,96,512]{2,1,0:T(8,128)(2,1)} %tie.3), calls=%async_computation.2 | async-start | bytes 3145728 | tf_op jit(solution)/shard_map/all_to_all | solution.py:450
  130.5 38.5 %collective-permute-start.1 = (bf16[1536,512]{1,0:T(8,128)(2,1)}, bf16[1536,512]{1,0:T(8,128)(2,1)}, u32[]{:S(2)}, u32[]{:S(2)}) collective-permute-start(bf16[1536,512]{1,0:T(8,128)(2,1)} %bitcast.53), channel_id=1, source_target_pairs={{0,1},{1,0},{2,3},{3,2},{4,5},{5,4},{6,7},{7,6},{8,9},{9,8},{10,11... | collective-permute-start | bytes 4718600 | tf_op jit(solution)/shard_map/ppermute | solution.py:454
  132.7 2.9 copy-start.7
  135.6 1.4 copy-start.14
  142.1 0.8 copy-start.27
  162.4 1.1 copy-start.3
  163.6 1.1 copy-start.28
  164.7 1.4 copy-start.4
  167.8 1.2 copy-start.16
  169.0 9.4 %copy-start.5 = (bf16[1536,512]{1,0:T(8,128)(2,1)S(1)}, bf16[1536,512]{1,0:T(8,128)(2,1)}, u32[]{:S(2)}) copy-start(bf16[1536,512]{1,0:T(8,128)(2,1)} %tie.4.d_ref.d_own) | copy-start | bytes 4718596
  169.0 56.9 %all-to-all-start.4 = ((bf16[16,32,1536]{2,1,0:T(8,128)(2,1)}), bf16[16,32,1536]{2,1,0:T(8,128)(2,1)}, u32[]{:S(2)}, u32[]{:S(2)}) async-start(bf16[16,32,1536]{2,1,0:T(8,128)(2,1)} %bitcast.56), calls=%async_computation.4 | async-start | bytes 3145728 | tf_op jit(solution)/shard_map/all_to_all | solution.py:521
  178.3 2.9 copy-start.17
  178.3 38.5 %all-gather.6.cloned.1.call-start = ((), (), s32[]{:S(2)}) async-start(), calls=%async_computation.8 | async-start | bytes 2359296 | tf_op jit(solution)/shard_map/all_gather | solution.py:530
  179.6 28.4 %collective-permute-start.2 = (bf16[768,512]{1,0:T(8,128)(2,1)}, bf16[768,512]{1,0:T(8,128)(2,1)S(1)}, u32[]{:S(2)}, u32[]{:S(2)}) collective-permute-start(bf16[768,512]{1,0:T(8,128)(2,1)} %get-tuple-element.31), channel_id=1, source_target_pairs={{0,1},{1,0},{2,3},{3,2},{4,5},{5,4},{6,7},{7,6},{8,9},{9,8},{10,11... | collective-permute-start | bytes 2359304 | tf_op jit(solution)/shard_map/ppermute | solution.py:454
  181.2 2.9 copy-start.8
  191.3 0.9 copy-start.25
  208.0 0.9 copy-start.22
  216.8 1.4 copy-start.19
  218.2 1.1 copy-start.23
  219.3 1.1 copy-start.26
  224.6 1.3 copy-start.9
  225.9 44.6 %all-to-all-start.3 = ((bf16[16,40,1536]{2,1,0:T(8,128)(2,1)}), bf16[16,40,1536]{2,1,0:T(8,128)(2,1)S(1)}, u32[]{:S(2)}, u32[]{:S(2)}) async-start(bf16[16,40,1536]{2,1,0:T(8,128)(2,1)} %bitcast.49), calls=%async_computation.3 | async-start | bytes 3932160 | tf_op jit(solution)/shard_map/all_to_all | solution.py:521
  231.7 0.9 copy-start.34
  234.7 0.8 copy-start.31
  235.5 0.6 copy-start.35
  236.1 1.5 copy-start.10
  237.6 1.4 copy-start.12
  239.0 1.4 copy-start.15
  240.4 1.4 copy-start.20
  241.8 1.1 copy-start.24
  243.0 6.5 %copy-start.30 = (bf16[1,128,1536]{2,1,0:T(8,128)(2,1)S(1)}, bf16[1,128,1536]{2,1,0:T(8,128)(2,1)}, u32[]{:S(2)}) copy-start(bf16[1,128,1536]{2,1,0:T(8,128)(2,1)} %param.9) | copy-start | bytes 1179652
  249.5 21.0 %copy-start.36 = (bf16[16,640]{1,0:T(8,128)(2,1)S(1)}, bf16[16,640]{1,0:T(8,128)(2,1)}, u32[]{:S(2)}) copy-start(bf16[16,640]{1,0:T(8,128)(2,1)} %copy-done.35) | copy-start | bytes 61444
  270.5 3.7 %copy-start.6 = (bf16[3,1536,1024]{2,1,0:T(8,128)(2,1)S(1)}, bf16[3,1536,1024]{2,1,0:T(8,128)(2,1)}, u32[]{:S(2)}) copy-start(bf16[3,1536,1024]{2,1,0:T(8,128)(2,1)} %place.1._) | copy-start | bytes 28311556
  274.2 12.8 %copy-start.32 = (bf16[384,640]{1,0:T(8,128)(2,1)S(1)}, bf16[384,640]{1,0:T(8,128)(2,1)}, u32[]{:S(2)}) copy-start(bf16[384,640]{1,0:T(8,128)(2,1)} %copy-done.31) | copy-start | bytes 1474564
  276.2 18.1 %all-to-all-start.5 = ((f32[16,1,1536]{2,1,0:T(1,128)}), f32[16,1,1536]{2,1,0:T(1,128)S(1)}, u32[]{:S(2)}, u32[]{:S(2)}) async-start(f32[16,1,1536]{2,1,0:T(1,128)} %last.1._), calls=%async_computation.5 | async-start | bytes 196608 | tf_op jit(solution)/shard_map/all_to_all | solution.py:665
  286.9 7.5 %copy-start.40 = (f32[1536]{0:T(1024)S(1)}, f32[1536]{0:T(1024)}, u32[]{:S(2)}) copy-start(f32[1536]{0:T(1024)} %param.16) | copy-start | bytes 18436
  287.0 7.5 %copy-start.41 = (s32[16]{0:T(128)S(1)}, s32[16]{0:T(128)}, u32[]{:S(2)}) copy-start(s32[16]{0:T(128)} %param.17) | copy-start | bytes 196
  294.5 13.9 %copy-start.42 = (s32[16]{0:T(128)S(1)}, s32[16]{0:T(128)}, u32[]{:S(2)}) copy-start(s32[16]{0:T(128)} %param.10) | copy-start | bytes 196
Sparse Core Ops, SparseCore 0:
  14.2 86.3 all-gather.3
  180.7 36.0 all-gather.5

commit v11 on v10

--- a/solution.py
+++ b/solution.py
@@ -16,7 +16,7 @@
 GROUPS = 4
 RING = (0, 1, 4, 5, 8, 9, 12, 13, 14, 15, 10, 11, 6, 7, 2, 3)
 LANES = 128
-VMEM = 36 * 1024 * 1024
+VMEM = 56 * 1024 * 1024
 
 
 def merged(x, axis, combine):
@@ -281,10 +281,10 @@
     late_ref[...] = out[rows:]
 
 
-def oth_down_kernel(info, hidden_ref, spot_ref, late_ref, d_a, d_b, out_ref, held, sems):
+def oth_down_kernel(info, hidden_ref, spot_ref, late_ref, d_ref, out_ref, held, sems):
     size = held.shape[1]
     other = 1 - info[2]
-    sources = [d_a.at[other, :size], d_a.at[other, size:], d_b.at[:size], d_b.at[size:]]
+    sources = [d_ref.at[other, k * size : (k + 1) * size] for k in range(held.shape[0])]
     d = fetched(sources, held, sems)
     late = jnp.dot(spot_ref[...], late_ref[...], preferred_element_type=jnp.float32)
     out_ref[...] = (late + matmul_nt(hidden_ref, d)).astype(jnp.bfloat16)
@@ -375,32 +375,36 @@
         square_ref[...] = jnp.broadcast_to(total, square_ref.shape)
 
 
-def place_kernel(info, g_own, g_oth, u_own, u_oth, d_own, d_a, d_b, _, out_ref):
-    second_half = pl.program_id(0) >= pl.num_programs(0) // 2
-    d_oth = jnp.where(second_half, d_b[...], d_a[...])
-    for k, (own, oth) in enumerate(
-        ((g_own[...], g_oth[...]), (u_own[...], u_oth[...]), (d_own[...], d_oth))
-    ):
-        left = info[2] == 0
+def place_kernel(info, g_own, g_oth, u_own, u_oth, d_both, _, out_ref):
+    left = info[2] == 0
+    for k, (own, oth) in enumerate(((g_own[...], g_oth[...]), (u_own[...], u_oth[...]))):
         out_ref[k, :, :FF] = jnp.where(left, own, oth)
         out_ref[k, :, FF:] = jnp.where(left, oth, own)
-
-
-def cast_kernel(blocks, x_ref, *refs):
-    out_ref, order = refs[-2:]
-
-    @pl.when(pl.program_id(0) == 0)
-    def _():
-        target = iota(order.shape, 0)
-        source = (target & 15) * blocks + lax.shift_right_logical(target, 4)
-        order[...] = jnp.where(iota(order.shape, 1) == source, 1.0, 0.0).astype(jnp.bfloat16)
-
-    size = order.shape[0]
-    for group in range(x_ref.shape[0] // size):
-        x = x_ref[group * size : (group + 1) * size].astype(jnp.bfloat16)
-        turned = jnp.dot(order[...], x, preferred_element_type=jnp.float32).astype(jnp.bfloat16)
-        for b in range(blocks):
-            out_ref[b, group * 16 : (group + 1) * 16] = turned[b * 16 : (b + 1) * 16]
+    out_ref[2, :, :FF] = d_both[0]
+    out_ref[2, :, FF:] = d_both[1]
+
+
+def cast_kernel(first_row, blocks, x_ref, *refs):
+    out_ref, held, turned, sems_in, sems_out = refs[-5:]
+    groups, size = held.shape[:2]
+    fetches, stores = [], []
+    for g in range(groups):
+        rows = pl.ds(first_row + g * size, size)
+        fetches.append(pltpu.make_async_copy(x_ref.at[rows], held.at[g], sems_in.at[g]))
+        target = out_ref.at[:, g * 16 : (g + 1) * 16]
+        stores.append(pltpu.make_async_copy(turned.at[g], target, sems_out.at[g]))
+    for fetch in fetches:
+        fetch.start()
+    target = iota((size, size), 0)
+    source = (target & 15) * blocks + lax.shift_right_logical(target, 4)
+    order = jnp.where(iota((size, size), 1) == source, 1.0, 0.0).astype(jnp.bfloat16)
+    for g in range(groups):
+        fetches[g].wait()
+        rows = jnp.dot(order, held[g].astype(jnp.bfloat16), preferred_element_type=jnp.float32)
+        turned[g] = rows.astype(jnp.bfloat16).reshape(turned.shape[1:])
+        stores[g].start()
+    for store in stores:
+        store.wait()
 
 
 def tie_kernel(*_):
@@ -433,16 +437,21 @@
     shard_rows = master.shape[1]
     flat = master.reshape(3 * shard_rows * blk_count, FF)
 
+    groups = shard_rows // 16
+
     def turned(k, *after):
         return pl.pallas_call(
-            functools.partial(cast_kernel, blk_count),
-            grid=(2,),
-            in_specs=[pl.BlockSpec((shard_rows // 2 * blk_count, FF), lambda i: (2 * k + i, 0))]
-            + [pl.BlockSpec(memory_space=pl.ANY)] * len(after),
-            out_specs=pl.BlockSpec((blk_count, shard_rows // 2, FF), lambda i: (0, i, 0)),
+            functools.partial(cast_kernel, k * shard_rows * blk_count, blk_count),
+            in_specs=[pl.BlockSpec(memory_space=pl.ANY)] * (1 + len(after)),
+            out_specs=pl.BlockSpec(memory_space=pl.ANY),
             out_shape=jax.ShapeDtypeStruct((blk_count, shard_rows, FF), jnp.bfloat16),
-            scratch_shapes=[pltpu.VMEM((16 * blk_count, 16 * blk_count), jnp.bfloat16)],
-            compiler_params=params(),
+            scratch_shapes=[
+                pltpu.VMEM((groups, 16 * blk_count, FF), jnp.float32),
+                pltpu.VMEM((groups, blk_count, 16, FF), jnp.bfloat16),
+                pltpu.SemaphoreType.DMA((groups,)),
+                pltpu.SemaphoreType.DMA((groups,)),
+            ],
+            compiler_params=pltpu.CompilerParams(vmem_limit_bytes=VMEM),
             name="cast",
         )(flat, *after)
 
@@ -511,8 +520,6 @@
     step = 512
 
     quarter = width // 4
-    in_a = pl.BlockSpec((None, quarter, FF), lambda i, info: (1 - info[2], jnp.minimum(i, 1), 0))
-    in_b = pl.BlockSpec((quarter, FF), lambda i, *_: (jnp.maximum(i, 2) - 2, 0))
     anywhere = pl.BlockSpec(memory_space=pl.ANY)
 
     def returned(x):
@@ -526,9 +533,7 @@
         own_kernel, ((first + extra, FF), (second, extra)), first + extra, g_own, u_own
     )
     d_own = tied(d_own, own_hidden)
-    half = width // 2
-    d_oth_a = lax.all_gather(d_own[:half], "rep", axis=0)
-    d_oth_b = swapped(d_own[half:])
+    d_both = lax.all_gather(d_own, "rep", axis=0)
     own_out, late_out = pl.pallas_call(
         own_down_kernel,
         grid=(width // step,),
@@ -563,7 +568,6 @@
                 whole((second, extra)),
                 pl.BlockSpec((extra, quarter), lambda i, *_: (0, i)),
                 anywhere,
-                anywhere,
             ],
             out_specs=pl.BlockSpec((second, quarter), lambda i, *_: (0, i)),
             scratch_shapes=[
@@ -574,7 +578,7 @@
         out_shape=jax.ShapeDtypeStruct((second, width), jnp.bfloat16),
         compiler_params=params(),
         name="oth_down",
-    )(info, oth_hidden, spot, late_out, d_oth_a, d_oth_b)
+    )(info, oth_hidden, spot, late_out, d_both)
     oth_back = returned(oth_out)
 
     server = pl.pallas_call(
@@ -582,14 +586,14 @@
         grid_spec=pltpu.PrefetchScalarGridSpec(
             num_scalar_prefetch=1,
             grid=(4,),
-            in_specs=[pl.BlockSpec((quarter, FF), lambda i, *_: (i, 0))] * 5
-            + [in_a, in_b, pl.BlockSpec(memory_space=pl.ANY)],
+            in_specs=[pl.BlockSpec((quarter, FF), lambda i, *_: (i, 0))] * 4
+            + [pl.BlockSpec((2, quarter, FF), lambda i, *_: (0, i, 0)), anywhere],
             out_specs=pl.BlockSpec((3, quarter, 2 * FF), lambda i, *_: (0, i, 0)),
         ),
         out_shape=jax.ShapeDtypeStruct((3, width, 2 * FF), jnp.bfloat16),
         compiler_params=params(),
         name="place",
-    )(info, g_own, g_oth, u_own, u_oth, d_own, d_oth_a, d_oth_b, oth_out)
+    )(info, g_own, g_oth, u_own, u_oth, d_both, oth_out)
 
     first_mix, second_mix, last_mix = pl.pallas_call(
         mix_kernel,

time: 318 us -> 309 us (0.972)
  local copies, waits for them, and re-layouts: 54.1 us -> 6.2 us
  Pallas kernels: 40.7 us -> 67.7 us
  waiting for transfers between devices: 140 us -> 151 us
    unnamed x86 -> x16, local copies, waits for them, and re-layouts: 50.9 us -> 3.6 us
    all_gather x1, waiting for transfers between devices: 7.91 us -> 25.6 us  [paired(): d_both = lax.all_gather(d_own, 'rep', axis=0)]
    ppermute x3 -> x2, waiting for transfers between devices: 45.2 us -> 32.1 us  [swapped(): return lax.ppermute(x, 'rep', [(0, 1), (1, 0)])]
    pallas_call x2, Pallas kernels: 12.2 us -> 19.3 us  [hidden_of(): pl.pallas_call(kernel, grid_spec=pltpu.PrefetchScalarGridSpec(num_scalar_...]
    pallas_call x3, Pallas kernels: 3.48 us -> 9.74 us  [turned(): pl.pallas_call(functools.partial(cast_kernel, k * shard_rows * blk_count,...]
    all_to_all x2, waiting for transfers between devices: 17.6 us -> 22.8 us  [returned(): x = lax.all_to_all(x, 'blk', split_axis=0, concat_axis=0, tiled=True)]
    all_to_all x3, waiting for transfers between devices: 65.5 us -> 68.9 us  [moved(): own = lax.all_to_all(x, 'blk', split_axis=0, concat_axis=0, tiled=True)]
  transfers between devices with their start and end apart: 11 -> 10, of which waited for: 7 -> 7; matrix products, arithmetic and copies ran while one was open for 1% -> 1% of each run, Pallas kernels for 12% -> 20%
where the time goes in v11:
time: 309 us; the launch traced here: 307 us
  waiting for transfers between devices  151 us (49%)
  Pallas kernels  67.7 us (22%)
  starting transfers between devices  51.2 us (17%)
  between operations  14.3 us (5%)
  blocking collectives  10.8 us (3%)
  local copies, waits for them, and re-layouts  6.2 us (2%)
  matrix products  4.64 us (2%)
    all_to_all x3, waiting for transfers between devices, moved(): own = lax.all_to_all(x, 'blk', split_axis=0, concat_axis=0, tiled=True)  68.9 us
    ppermute x2, waiting for transfers between devices, swapped(): return lax.ppermute(x, 'rep', [(0, 1), (1, 0)])  32.1 us
    all_gather x1, waiting for transfers between devices, paired(): d_both = lax.all_gather(d_own, 'rep', axis=0)  25.6 us
    all_to_all x2, waiting for transfers between devices, returned(): x = lax.all_to_all(x, 'blk', split_axis=0, concat_axis=0, tiled=True)  22.8 us
    all_to_all x3, starting transfers between devices, moved(): own = lax.all_to_all(x, 'blk', split_axis=0, concat_axis=0, tiled=True)  22.6 us
    pallas_call x2, Pallas kernels, hidden_of(): pl.pallas_call(kernel, grid_spec=pltpu.PrefetchScalarGridSpec(num_scalar_...  19.3 us
    all_to_all x2, starting transfers between devices, returned(): x = lax.all_to_all(x, 'blk', split_axis=0, concat_axis=0, tiled=True)  14.7 us
    all_to_all x1, blocking collectives, everywhere(): lax.all_to_all(copies, 'blk', split_axis=0, concat_axis=0, tiled=True)  10.8 us
  transfers between devices with their start and end apart: 10, of which 7 were waited for; matrix products, arithmetic and copies ran while one was open for 1% of the time, Pallas kernels for 20%

profile of v11, /device:TPU:0, one launch (start us, length us, event | category | flops | bytes accessed | tf_op | source)
XLA Modules:
  0.0 307.4 jit_solution(12254194917792571869)
XLA Ops:
  7.2 0.0 all-gather.4.cloned.1.call-start
  7.2 1.3 dynamic_slice.3.length_ref
  8.5 3.0 prep.1
  11.5 0.0 all-gather.4.cloned.1.call-update
  11.5 3.2 %cast.3 = bf16[16,96,512]{2,1,0:T(8,128)(2,1)} custom-call(f32[4608,512]{1,0:T(8,128)} %bitcast.43, bf16[128,1664]{1,0:T(8,128)(2,1)} %get-tuple-element.16.rank_ref.refs_0_), custom_call_target="tpu_custom_call" | custom-call | tf_op jit(solution)/shard_map/cast/pallas_call | solution.py:443
  14.8 7.4 %all-to-all-start = ((bf16[16,96,512]{2,1,0:T(8,128)(2,1)}), bf16[16,96,512]{2,1,0:T(8,128)(2,1)S(1)}, u32[]{:S(2)}, u32[]{:S(2)}) async-start(bf16[16,96,512]{2,1,0:T(8,128)(2,1)} %cast.3), calls=%async_computation | async-start | bytes 3145728 | tf_op jit(solution)/shard_map/all_to_all | solution.py:459
  22.2 3.3 %cast.4 = bf16[16,96,512]{2,1,0:T(8,128)(2,1)} custom-call(f32[4608,512]{1,0:T(8,128)} %bitcast.44), custom_call_target="tpu_custom_call" | custom-call | tf_op jit(solution)/shard_map/cast/pallas_call | solution.py:443
  25.4 48.8 %all-to-all-done = bf16[16,96,512]{2,1,0:T(8,128)(2,1)S(1)} async-done(((bf16[16,96,512]{2,1,0:T(8,128)(2,1)}), bf16[16,96,512]{2,1,0:T(8,128)(2,1)S(1)}, u32[]{:S(2)}, u32[]{:S(2)}) %all-to-all-start) | async-done | bytes 1572896 | tf_op jit(solution)/shard_map/all_to_all | solution.py:459
  74.2 0.0 copy-start.2
  74.2 6.0 %all-to-all-start.1 = ((bf16[16,96,512]{2,1,0:T(8,128)(2,1)}), bf16[16,96,512]{2,1,0:T(8,128)(2,1)S(1)}, u32[]{:S(2)}, u32[]{:S(2)}) async-start(bf16[16,96,512]{2,1,0:T(8,128)(2,1)} %cast.4), calls=%async_computation.1 | async-start | bytes 3145728 | tf_op jit(solution)/shard_map/all_to_all | solution.py:459
  80.3 0.0 copy-done.2
  80.3 1.6 collective-permute-start
  81.9 3.2 %cast.5.__0_ = bf16[16,96,512]{2,1,0:T(8,128)(2,1)} custom-call(f32[4608,512]{1,0:T(8,128)} %bitcast.45), custom_call_target="tpu_custom_call" | custom-call | tf_op jit(solution)/shard_map/cast/pallas_call | solution.py:443
  85.1 32.1 %collective-permute-done.__1_.g_ref.g_oth = bf16[1536,512]{1,0:T(8,128)(2,1)} collective-permute-done((bf16[1536,512]{1,0:T(8,128)(2,1)S(1)}, bf16[1536,512]{1,0:T(8,128)(2,1)}, u32[]{:S(2)}, u32[]{:S(2)}) %collective-permute-start) | collective-permute-done | bytes 1572896 | tf_op jit(solution)/shard_map/ppermute | solution.py:463
  117.2 0.4 all-to-all-done.1
  117.6 0.0 copy-start.3
  117.6 9.1 %all-to-all-start.2 = ((bf16[16,96,512]{2,1,0:T(8,128)(2,1)}), bf16[16,96,512]{2,1,0:T(8,128)(2,1)S(1)}, u32[]{:S(2)}, u32[]{:S(2)}) async-start(bf16[16,96,512]{2,1,0:T(8,128)(2,1)} %tie.3), calls=%async_computation.2 | async-start | bytes 3145728 | tf_op jit(solution)/shard_map/all_to_all | solution.py:459
  126.8 0.0 all-gather.6.cloned.1.call-start
  126.8 1.5 collective-permute-start.1
  128.3 1.3 stack.34.info
  129.7 0.0 all-gather.4.cloned.1.call-done.x_ref
  129.7 0.0 copy-done.3
  129.7 9.4 %gate_up.2 = (bf16[576,512]{1,0:T(8,128)(2,1)}, bf16[640,64]{1,0:T(8,128)(2,1)}) custom-call(s32[20]{0:T(128)} %stack.34.info, bf16[2048,1664]{1,0:T(8,128)(2,1)} %all-gather.4.cloned.1.call-done.x_ref, bf16[1536,512]{1,0:T(8,128)(2,1)} %bitcast.51, bf16[1536,512]{1,0:T(8,128)(2,1)} %bitcast.54), custom_call_target="tpu_custom_call" | custom-call | tf_op jit(solution)/shard_map/gate_up/pallas_call | solution.py:504
  139.1 19.7 %all-to-all-done.2 = bf16[16,96,512]{2,1,0:T(8,128)(2,1)S(1)} async-done(((bf16[16,96,512]{2,1,0:T(8,128)(2,1)}), bf16[16,96,512]{2,1,0:T(8,128)(2,1)S(1)}, u32[]{:S(2)}, u32[]{:S(2)}) %all-to-all-start.2) | async-done | bytes 1572896 | tf_op jit(solution)/shard_map/all_to_all | solution.py:459
  158.7 0.0 copy-start
  158.7 1.1 copy-done
  159.9 0.0 all-gather.6.cloned.1.call-update
  159.9 4.8 %own_down.1 = (bf16[512,1536]{1,0:T(8,128)(2,1)}, bf16[64,1536]{1,0:T(8,128)(2,1)}) custom-call(bf16[576,512]{1,0:T(8,128)(2,1)} %get-tuple-element.19.__1_.hidden_ref, bf16[1536,512]{1,0:T(8,128)(2,1)} %tie.4.d_ref), custom_call_target="tpu_custom_call" | custom-call | tf_op jit(solution)/shard_map/own_down/pallas_call | solution.py:537
  164.7 0.0 collective-permute-done.1.__1_.u_ref.u_oth
  164.7 9.1 %all-to-all-start.4 = ((bf16[16,32,1536]{2,1,0:T(8,128)(2,1)}), bf16[16,32,1536]{2,1,0:T(8,128)(2,1)S(1)}, u32[]{:S(2)}, u32[]{:S(2)}) async-start(bf16[16,32,1536]{2,1,0:T(8,128)(2,1)} %bitcast.56), calls=%async_computation.4 | async-start | bytes 3145728 | tf_op jit(solution)/shard_map/all_to_all | solution.py:528
  173.9 9.9 %gate_up.3.hidden_ref = bf16[640,512]{1,0:T(8,128)(2,1)} custom-call(s32[20]{0:T(128)} %stack.34.info, bf16[2048,1664]{1,0:T(8,128)(2,1)} %all-gather.4.cloned.1.call-done.x_ref, bf16[1536,512]{1,0:T(8,128)(2,1)} %collective-permute-done.__1_.g_ref.g_oth, bf16[1536,512]{1,0:T(8,128)(2,1)} %collective-permute-done.1.__1_.u_ref.u_oth, bf16[512,1536]{1,0:T(8,128)(2,1)} %tie.5._), custom_call_target="tpu_custom_call" | custom-call | tf_op jit(solution)/shard_map/gate_up/pallas_call | solution.py:504
  183.8 25.6 %all-gather.6.cloned.1.call-done = bf16[3072,512]{1,0:T(8,128)(2,1)} async-done(((bf16[1536,512]{1,0:T(8,128)(2,1)}), bf16[3072,512]{1,0:T(8,128)(2,1)}) %all-gather.6.cloned.1.call-update) | async-done | bytes 3145744 | tf_op jit(solution)/shard_map/all_gather | solution.py:536
  209.4 6.7 %oth_down.1._ = bf16[640,1536]{1,0:T(8,128)(2,1)} custom-call(s32[20]{0:T(128)} %stack.34.info, bf16[640,512]{1,0:T(8,128)(2,1)} %gate_up.3.hidden_ref, bf16[640,64]{1,0:T(8,128)(2,1)} %get-tuple-element.21.spot_ref, bf16[64,1536]{1,0:T(8,128)(2,1)} %get-tuple-element.22.late_ref, bf16[2,1536,512]{2,1,0:T(8,128)(2,1)} %bitcast.57), custom_call_target="tpu_custom_call" | custom-call | tf_op jit(solution)/shard_map/oth_down/pallas_call | solution.py:561
  216.1 0.0 all-to-all-done.4
  216.1 0.0 copy-start.4
  216.1 1.1 copy-done.4
  217.2 5.6 %all-to-all-start.3 = ((bf16[16,40,1536]{2,1,0:T(8,128)(2,1)}), bf16[16,40,1536]{2,1,0:T(8,128)(2,1)S(1)}, u32[]{:S(2)}, u32[]{:S(2)}) async-start(bf16[16,40,1536]{2,1,0:T(8,128)(2,1)} %bitcast.49), calls=%async_computation.3 | async-start | bytes 3932160 | tf_op jit(solution)/shard_map/all_to_all | solution.py:528
  222.9 3.0 mix.1
  225.9 4.7 %first.1 = (f32[128,1536]{1,0:T(8,128)}, f32[1,1536]{1,0:T(1,128)}) custom-call(s32[20]{0:T(128)} %stack.34.info, bf16[384,512]{1,0:T(8,128)(2,1)} %get-tuple-element.23.mix_ref, bf16[512,1536]{1,0:T(8,128)(2,1)} %bitcast.59, bf16[128,1536]{1,0:T(8,128)(2,1)} %bitcast.61), custom_call_target="tpu_custom_call" | custom-call | tf_op jit(solution)/shard_map/first/pallas_call | solution.py:623
  230.6 8.3 %place.1._ = bf16[3,1536,1024]{2,1,0:T(8,128)(2,1)} custom-call(s32[20]{0:T(128)} %stack.34.info, bf16[1536,512]{1,0:T(8,128)(2,1)} %bitcast.52, bf16[1536,512]{1,0:T(8,128)(2,1)} %collective-permute-done.__1_.g_ref.g_oth, bf16[1536,512]{1,0:T(8,128)(2,1)} %bitcast.55, bf16[1536,512]{1,0:T(8,128)(2,1)} %collective-permute-done.1.__1_.u_ref.u_oth, ...), custom_call_target="tpu_custom_call" | custom-call | tf_op jit(solution)/shard_map/place/pallas_call | solution.py:584
  238.9 22.8 %all-to-all-done.3 = bf16[16,40,1536]{2,1,0:T(8,128)(2,1)S(1)} async-done(((bf16[16,40,1536]{2,1,0:T(8,128)(2,1)}), bf16[16,40,1536]{2,1,0:T(8,128)(2,1)S(1)}, u32[]{:S(2)}, u32[]{:S(2)}) %all-to-all-start.3) | async-done | bytes 1966112 | tf_op jit(solution)/shard_map/all_to_all | solution.py:528
  261.7 0.0 copy-start.1
  261.7 1.3 copy-done.1
  263.0 3.1 last.1._
  266.0 10.7 %all-to-all-start.5 = ((f32[16,1,1536]{2,1,0:T(1,128)}), f32[16,1,1536]{2,1,0:T(1,128)S(1)}, u32[]{:S(2)}, u32[]{:S(2)}) async-start(f32[16,1,1536]{2,1,0:T(1,128)} %last.1._), calls=%async_computation.5 | async-start | bytes 196608 | tf_op jit(solution)/shard_map/all_to_all | solution.py:669
  276.8 0.0 copy-start.5
  276.8 0.0 copy-start.6
  276.8 5.1 %combine.1 = (bf16[128,1536]{1,0:T(8,128)(2,1)}, f32[1,128]{1,0:T(1,128)}) custom-call(s32[20]{0:T(128)} %stack.34.info, bf16[384,640]{1,0:T(8,128)(2,1)} %get-tuple-element.18.mix_ref, bf16[640,1536]{1,0:T(8,128)(2,1)} %bitcast.48, f32[128,1536]{1,0:T(8,128)} %get-tuple-element.24.base_ref, f32[16,1,1536]{2,1,0:T(1,128)} %last.1._), custom_call_target="tpu_custom_call" | custom-call | tf_op jit(solution)/shard_map/combine/pallas_call | solution.py:651
  281.9 0.7 compare_select_fusion
  282.5 1.6 all-to-all-done.5
  284.2 0.1 fusion
  284.3 0.0 copy-done.5
  284.3 0.0 copy-done.6
  284.3 0.0 copy-start.7
  284.3 4.6 %fusion.7 = (f32[16]{0:T(128)S(1)}, f32[16]{0:T(128)S(1)}) fusion(s32[2048]{0:T(1024)S(1)} %iota_add_fusion, s32[16]{0:T(128)S(1)} %copy-done.6, bf16[2048,1536]{1,0:T(8,128)(2,1)} %param.15, f32[16,1,1536]{2,1,0:T(1,128)S(1)} %all-to-all-done.5, f32[1536]{0:T(1024)S(1)} %copy-done.5, f32[16]{0:T(128)S(1)} %add_rsqrt_fusion), kind=kOutput, calls=%fused_computation.17 | convolution fusion | flops 100868064 | bytes 6404352 | tf_op jit(solution)/shard_map/dot_general | solution.py:677
  289.0 10.8 %all_to_all.35 = f32[16,3,16]{2,1,0:T(4,128)S(1)} all-to-all(f32[16,3,16]{2,1,0:T(4,128)S(1)} %broadcast_in_dim.24), channel_id=1, replica_groups=mesh['blk'=16,'rep'=2] {'blk'}, dimensions={0} | all-to-all | bytes 6144 | tf_op jit(solution)/shard_map/all_to_all | solution.py:669
  299.9 0.0 copy-done.7
  299.9 0.6 pad_maximum_fusion.1
  (12 shorter events, 0.1 us)
Async XLA Ops:
  7.2 122.5 %all-gather.4.cloned.1.call-start = ((), (), s32[]{:S(2)}) async-start(), calls=%async_computation.7 | async-start | bytes 7241728 | tf_op jit(solution)/shard_map/all_gather | solution.py:501
  14.8 59.5 %all-to-all-start = ((bf16[16,96,512]{2,1,0:T(8,128)(2,1)}), bf16[16,96,512]{2,1,0:T(8,128)(2,1)S(1)}, u32[]{:S(2)}, u32[]{:S(2)}) async-start(bf16[16,96,512]{2,1,0:T(8,128)(2,1)} %cast.3), calls=%async_computation | async-start | bytes 3145728 | tf_op jit(solution)/shard_map/all_to_all | solution.py:459
  74.2 6.1 %copy-start.2 = (bf16[16,96,512]{2,1,0:T(8,128)(2,1)}, bf16[16,96,512]{2,1,0:T(8,128)(2,1)S(1)}, u32[]{:S(2)}) copy-start(bf16[16,96,512]{2,1,0:T(8,128)(2,1)S(1)} %all-to-all-done) | copy-start | bytes 4718596
  74.2 43.4 %all-to-all-start.1 = ((bf16[16,96,512]{2,1,0:T(8,128)(2,1)}), bf16[16,96,512]{2,1,0:T(8,128)(2,1)S(1)}, u32[]{:S(2)}, u32[]{:S(2)}) async-start(bf16[16,96,512]{2,1,0:T(8,128)(2,1)} %cast.4), calls=%async_computation.1 | async-start | bytes 3145728 | tf_op jit(solution)/shard_map/all_to_all | solution.py:459
  80.3 36.9 %collective-permute-start = (bf16[1536,512]{1,0:T(8,128)(2,1)S(1)}, bf16[1536,512]{1,0:T(8,128)(2,1)}, u32[]{:S(2)}, u32[]{:S(2)}) collective-permute-start(bf16[1536,512]{1,0:T(8,128)(2,1)S(1)} %bitcast.50), channel_id=1, source_target_pairs={{0,1},{1,0},{2,3},{3,2},{4,5},{5,4},{6,7},{7,6},{8,9},{9,8},{10,11... | collective-permute-start | bytes 4718600 | tf_op jit(solution)/shard_map/ppermute | solution.py:463
  117.6 12.0 %copy-start.3 = (bf16[16,96,512]{2,1,0:T(8,128)(2,1)}, bf16[16,96,512]{2,1,0:T(8,128)(2,1)S(1)}, u32[]{:S(2)}) copy-start(bf16[16,96,512]{2,1,0:T(8,128)(2,1)S(1)} %all-to-all-done.1) | copy-start | bytes 4718596
  117.6 41.1 %all-to-all-start.2 = ((bf16[16,96,512]{2,1,0:T(8,128)(2,1)}), bf16[16,96,512]{2,1,0:T(8,128)(2,1)S(1)}, u32[]{:S(2)}, u32[]{:S(2)}) async-start(bf16[16,96,512]{2,1,0:T(8,128)(2,1)} %tie.3), calls=%async_computation.2 | async-start | bytes 3145728 | tf_op jit(solution)/shard_map/all_to_all | solution.py:459
  126.8 82.6 %all-gather.6.cloned.1.call-start = ((), (), s32[]{:S(2)}) async-start(), calls=%async_computation.8 | async-start | bytes 4718592 | tf_op jit(solution)/shard_map/all_gather | solution.py:536
  126.8 37.9 %collective-permute-start.1 = (bf16[1536,512]{1,0:T(8,128)(2,1)S(1)}, bf16[1536,512]{1,0:T(8,128)(2,1)}, u32[]{:S(2)}, u32[]{:S(2)}) collective-permute-start(bf16[1536,512]{1,0:T(8,128)(2,1)S(1)} %bitcast.53), channel_id=1, source_target_pairs={{0,1},{1,0},{2,3},{3,2},{4,5},{5,4},{6,7},{7,6},{8,9},{9,8},{10,11... | collective-permute-start | bytes 4718600 | tf_op jit(solution)/shard_map/ppermute | solution.py:463
  158.7 1.1 copy-start
  164.7 51.3 %all-to-all-start.4 = ((bf16[16,32,1536]{2,1,0:T(8,128)(2,1)}), bf16[16,32,1536]{2,1,0:T(8,128)(2,1)S(1)}, u32[]{:S(2)}, u32[]{:S(2)}) async-start(bf16[16,32,1536]{2,1,0:T(8,128)(2,1)} %bitcast.56), calls=%async_computation.4 | async-start | bytes 3145728 | tf_op jit(solution)/shard_map/all_to_all | solution.py:528
  216.1 1.1 copy-start.4
  217.2 44.5 %all-to-all-start.3 = ((bf16[16,40,1536]{2,1,0:T(8,128)(2,1)}), bf16[16,40,1536]{2,1,0:T(8,128)(2,1)S(1)}, u32[]{:S(2)}, u32[]{:S(2)}) async-start(bf16[16,40,1536]{2,1,0:T(8,128)(2,1)} %bitcast.49), calls=%async_computation.3 | async-start | bytes 3932160 | tf_op jit(solution)/shard_map/all_to_all | solution.py:528
  261.7 1.3 copy-start.1
  266.0 18.1 %all-to-all-start.5 = ((f32[16,1,1536]{2,1,0:T(1,128)}), f32[16,1,1536]{2,1,0:T(1,128)S(1)}, u32[]{:S(2)}, u32[]{:S(2)}) async-start(f32[16,1,1536]{2,1,0:T(1,128)} %last.1._), calls=%async_computation.5 | async-start | bytes 196608 | tf_op jit(solution)/shard_map/all_to_all | solution.py:669
  276.8 7.5 %copy-start.5 = (f32[1536]{0:T(1024)S(1)}, f32[1536]{0:T(1024)}, u32[]{:S(2)}) copy-start(f32[1536]{0:T(1024)} %param.16) | copy-start | bytes 18436
  276.8 7.5 %copy-start.6 = (s32[16]{0:T(128)S(1)}, s32[16]{0:T(128)}, u32[]{:S(2)}) copy-start(s32[16]{0:T(128)} %param.17) | copy-start | bytes 196
  284.3 15.5 %copy-start.7 = (s32[16]{0:T(128)S(1)}, s32[16]{0:T(128)}, u32[]{:S(2)}) copy-start(s32[16]{0:T(128)} %param.10) | copy-start | bytes 196
Sparse Core Ops, SparseCore 0:
  11.6 95.2 all-gather.3
  160.0 49.3 all-gather.5

commit v12 on v11

--- a/solution.py
+++ b/solution.py
@@ -149,9 +149,9 @@
     return lax.broadcasted_iota(jnp.int32, shape, dim)
 
 
-def prep_kernel(length_ref, hidden_ref, routes_ref, weights_ref, gain_ref, rows_ref, pieces_ref):
+def prep_kernel(lengths_ref, blk_ref, hidden_ref, routes_ref, weights_ref, gain_ref, rows_ref, pieces_ref):
     rows, width = hidden_ref.shape
-    length = length_ref[0]
+    length = lengths_ref[blk_ref[0]]
     x = hidden_ref[...].astype(jnp.float32)
     scale = lax.rsqrt(jnp.mean(x * x, axis=-1, keepdims=True) + 1e-05)
     rows_ref[:, :width] = (x * scale * gain_ref[...][None]).astype(jnp.bfloat16)
@@ -272,19 +272,29 @@
     return held[step]
 
 
-def own_down_kernel(hidden_ref, d_ref, out_ref, late_ref, held, sems):
+def own_down_kernel(hidden_ref, d_ref, out_ref, late_ref, a_ref, b_ref, held, sems):
+    step = pl.program_id(0)
     size = held.shape[1]
     d = fetched([d_ref.at[k * size : (k + 1) * size] for k in range(held.shape[0])], held, sems)
+
+    @pl.when(step < held.shape[0] // 2)
+    def _():
+        a_ref[...] = d
+
+    @pl.when(step >= held.shape[0] // 2)
+    def _():
+        b_ref[...] = d
+
     out = matmul_nt(hidden_ref, d).astype(jnp.bfloat16)
     rows = out_ref.shape[0]
     out_ref[...] = out[:rows]
     late_ref[...] = out[rows:]
 
 
-def oth_down_kernel(info, hidden_ref, spot_ref, late_ref, d_ref, out_ref, held, sems):
+def oth_down_kernel(info, hidden_ref, spot_ref, late_ref, d_a, d_b, out_ref, held, sems):
     size = held.shape[1]
     other = 1 - info[2]
-    sources = [d_ref.at[other, k * size : (k + 1) * size] for k in range(held.shape[0])]
+    sources = [d_a.at[other, :size], d_a.at[other, size:], d_b.at[:size], d_b.at[size:]]
     d = fetched(sources, held, sems)
     late = jnp.dot(spot_ref[...], late_ref[...], preferred_element_type=jnp.float32)
     out_ref[...] = (late + matmul_nt(hidden_ref, d)).astype(jnp.bfloat16)
@@ -324,14 +334,20 @@
     ).astype(jnp.bfloat16)
 
 
-def weigh(mix_ref, back_ref):
+def weigh(mix_ref, back):
     rows = mix_ref.shape[0] // 3
-    parts = jnp.dot(mix_ref[...], back_ref[...], preferred_element_type=jnp.float32)
+    parts = jnp.dot(mix_ref[...], back, preferred_element_type=jnp.float32)
     return parts[2 * rows :] + parts[rows : 2 * rows] + parts[:rows]
 
 
-def first_kernel(info, mix_ref, back_ref, resid_ref, base_ref, last_ref):
-    base = resid_ref[...].astype(jnp.float32) + weigh(mix_ref, back_ref)
+def columns(ref, held):
+    size = held.shape[2]
+    return [ref.at[:, k * size : (k + 1) * size] for k in range(held.shape[0])]
+
+
+def first_kernel(info, mix_ref, back_ref, resid_ref, base_ref, last_ref, held, sems):
+    back = fetched(columns(back_ref, held), held, sems)
+    base = resid_ref[...].astype(jnp.float32) + weigh(mix_ref, back)
     base_ref[...] = base
     is_last = iota(base.shape, 0) == info[3] - 1
     last_ref[...] = jnp.sum(jnp.where(is_last, base, 0.0), axis=0, keepdims=True)
@@ -356,14 +372,15 @@
     told_ref[...] = jnp.broadcast_to(out[None], told_ref.shape)
 
 
-def combine_kernel(info, mix_ref, back_ref, base_ref, _, out_ref, square_ref, squares):
+def combine_kernel(info, mix_ref, back_ref, base_ref, _, out_ref, square_ref, squares, held, sems):
     step = pl.program_id(0)
 
     @pl.when(step == 0)
     def _():
         squares[...] = jnp.zeros_like(squares)
 
-    out = (base_ref[...] + weigh(mix_ref, back_ref)).astype(jnp.bfloat16)
+    back = fetched(columns(back_ref, held), held, sems)
+    out = (base_ref[...] + weigh(mix_ref, back)).astype(jnp.bfloat16)
     out_ref[...] = out
     out_f = out.astype(jnp.float32)
     row = iota(out_f.shape, 0)
@@ -375,13 +392,14 @@
         square_ref[...] = jnp.broadcast_to(total, square_ref.shape)
 
 
-def place_kernel(info, g_own, g_oth, u_own, u_oth, d_both, _, out_ref):
+def place_kernel(info, g_own, g_oth, u_own, u_oth, d_a, b_own, b_oth, _, out_ref):
     left = info[2] == 0
     for k, (own, oth) in enumerate(((g_own[...], g_oth[...]), (u_own[...], u_oth[...]))):
         out_ref[k, :, :FF] = jnp.where(left, own, oth)
         out_ref[k, :, FF:] = jnp.where(left, oth, own)
-    out_ref[2, :, :FF] = d_both[0]
-    out_ref[2, :, FF:] = d_both[1]
+    in_a = pl.program_id(0) < pl.num_programs(0) // 2
+    out_ref[2, :, :FF] = jnp.where(in_a, d_a[0], jnp.where(left, b_own[...], b_oth[...]))
+    out_ref[2, :, FF:] = jnp.where(in_a, d_a[1], jnp.where(left, b_oth[...], b_own[...]))
 
 
 def cast_kernel(first_row, blocks, x_ref, *refs):
@@ -430,8 +448,7 @@
     first = blk_count * FIRST
     second = blk_count * SECOND
     resid = hidden_in[0]
-    length = lax.dynamic_slice(lengths, (blk,), (1,))
-    info = jnp.stack([2 * blk + rep, 2 * blk + 1 - rep, rep, length[0]] + list(RING))
+    info = jnp.stack([2 * blk + rep, 2 * blk + 1 - rep, rep, lengths[blk]] + list(RING))
     info = info.astype(jnp.int32)
 
     shard_rows = master.shape[1]
@@ -475,7 +492,7 @@
     row_ext, pieces = pl.pallas_call(
         prep_kernel,
         grid_spec=pltpu.PrefetchScalarGridSpec(
-            num_scalar_prefetch=1,
+            num_scalar_prefetch=2,
             grid=(1,),
             in_specs=[
                 whole((rows, width)),
@@ -491,7 +508,7 @@
         ],
         compiler_params=params(),
         name="prep",
-    )(length, resid, routes[0].T, route_weights[0].T, norm_gain)
+    )(lengths, blk[None].astype(jnp.int32), resid, routes[0].T, route_weights[0].T, norm_gain)
     g_own = moved(turned(0, row_ext))
     g_oth = swapped(g_own)
     u_own = moved(turned(1))
@@ -532,27 +549,34 @@
     own_hidden, spot = hidden_of(
         own_kernel, ((first + extra, FF), (second, extra)), first + extra, g_own, u_own
     )
-    d_own = tied(d_own, own_hidden)
-    d_both = lax.all_gather(d_own, "rep", axis=0)
-    own_out, late_out = pl.pallas_call(
+    half = width // 2
+    in_a = pl.BlockSpec((quarter, FF), lambda i, *_: (jnp.minimum(i, 1), 0))
+    in_b = pl.BlockSpec((quarter, FF), lambda i, *_: (jnp.maximum(i, 2) - 2, 0))
+    own_out, late_out, d_a, d_b = pl.pallas_call(
         own_down_kernel,
-        grid=(width // step,),
+        grid=(4,),
         in_specs=[whole((first + extra, FF)), anywhere],
         out_specs=[
-            pl.BlockSpec((first, step), lambda i: (0, i)),
-            pl.BlockSpec((extra, step), lambda i: (0, i)),
+            pl.BlockSpec((first, quarter), lambda i: (0, i)),
+            pl.BlockSpec((extra, quarter), lambda i: (0, i)),
+            in_a,
+            in_b,
         ],
         out_shape=[
             jax.ShapeDtypeStruct((first, width), jnp.bfloat16),
             jax.ShapeDtypeStruct((extra, width), jnp.bfloat16),
+            jax.ShapeDtypeStruct((half, FF), jnp.bfloat16),
+            jax.ShapeDtypeStruct((half, FF), jnp.bfloat16),
         ],
         scratch_shapes=[
-            pltpu.VMEM((width // step, step, FF), jnp.bfloat16),
-            pltpu.SemaphoreType.DMA((width // step,)),
+            pltpu.VMEM((4, quarter, FF), jnp.bfloat16),
+            pltpu.SemaphoreType.DMA((4,)),
         ],
         compiler_params=params(),
         name="own_down",
     )(own_hidden, d_own)
+    both_a = lax.all_gather(d_a, "rep", axis=0)
+    oth_b = swapped(d_b)
     own_out = tied(own_out, u_oth)
     own_back = returned(own_out)
     (oth_hidden,) = hidden_of(
@@ -567,6 +591,7 @@
                 whole((second, FF)),
                 whole((second, extra)),
                 pl.BlockSpec((extra, quarter), lambda i, *_: (0, i)),
+                anywhere,
                 anywhere,
             ],
             out_specs=pl.BlockSpec((second, quarter), lambda i, *_: (0, i)),
@@ -578,7 +603,7 @@
         out_shape=jax.ShapeDtypeStruct((second, width), jnp.bfloat16),
         compiler_params=params(),
         name="oth_down",
-    )(info, oth_hidden, spot, late_out, d_both)
+    )(info, oth_hidden, spot, late_out, both_a, oth_b)
     oth_back = returned(oth_out)
 
     server = pl.pallas_call(
@@ -587,13 +612,18 @@
             num_scalar_prefetch=1,
             grid=(4,),
             in_specs=[pl.BlockSpec((quarter, FF), lambda i, *_: (i, 0))] * 4
-            + [pl.BlockSpec((2, quarter, FF), lambda i, *_: (0, i, 0)), anywhere],
+            + [
+                pl.BlockSpec((2, quarter, FF), lambda i, *_: (0, jnp.minimum(i, 1), 0)),
+                in_b,
+                in_b,
+                anywhere,
+            ],
             out_specs=pl.BlockSpec((3, quarter, 2 * FF), lambda i, *_: (0, i, 0)),
         ),
         out_shape=jax.ShapeDtypeStruct((3, width, 2 * FF), jnp.bfloat16),
         compiler_params=params(),
         name="place",
-    )(info, g_own, g_oth, u_own, u_oth, d_both, oth_out)
+    )(info, g_own, g_oth, u_own, u_oth, both_a, d_b, oth_b, oth_out)
 
     first_mix, second_mix, last_mix = pl.pallas_call(
         mix_kernel,
@@ -616,7 +646,13 @@
     )(info, row_ext, pieces)
 
     def weigh_specs(slots):
-        return [whole((3 * rows, slots)), pl.BlockSpec((slots, step), lambda i, *_: (0, i))]
+        return [whole((3 * rows, slots)), anywhere]
+
+    def hold(slots):
+        return [
+            pltpu.VMEM((width // step, slots, step), jnp.bfloat16),
+            pltpu.SemaphoreType.DMA((width // step,)),
+        ]
 
     column = pl.BlockSpec((rows, step), lambda i, *_: (0, i))
     lane_row = pl.BlockSpec((1, step), lambda i, *_: (0, i))
@@ -627,6 +663,7 @@
             grid=(width // step,),
             in_specs=weigh_specs(first) + [column],
             out_specs=[column, lane_row],
+            scratch_shapes=hold(first),
         ),
         out_shape=[
             jax.ShapeDtypeStruct((rows, width), jnp.float32),
@@ -655,7 +692,7 @@
             grid=(width // step,),
             in_specs=weigh_specs(second) + [column, pl.BlockSpec(memory_space=pl.ANY)],
             out_specs=[column, whole((1, LANES))],
-            scratch_shapes=[pltpu.VMEM((1, step), jnp.float32)],
+            scratch_shapes=[pltpu.VMEM((1, step), jnp.float32)] + hold(second),
         ),
         out_shape=[
             jax.ShapeDtypeStruct((rows, width), jnp.bfloat16),

time: 309 us -> 311 us (level)
    ppermute x2 -> x3, waiting for transfers between devices: 32.1 us -> 48.2 us  [swapped(): return lax.ppermute(x, 'rep', [(0, 1), (1, 0)])]
    all_gather x1, waiting for transfers between devices: 25.6 us -> 9.74 us  [paired(): both_a = lax.all_gather(d_a, 'rep', axis=0)]
  transfers between devices with their start and end apart: 10 -> 11, of which waited for: 7 -> 8; matrix products, arithmetic and copies ran while one was open for 1% -> 1% of each run, Pallas kernels for 20% -> 20%
where the time goes in v12:
time: 311 us; the launch traced here: 310 us
  waiting for transfers between devices  150 us (48%)
  Pallas kernels  69.5 us (22%)
  starting transfers between devices  53 us (17%)
  between operations  14.3 us (5%)
  blocking collectives  11.6 us (4%)
  local copies, waits for them, and re-layouts  5.36 us (2%)
  matrix products  4.63 us (1%)
    all_to_all x3, waiting for transfers between devices, moved(): own = lax.all_to_all(x, 'blk', split_axis=0, concat_axis=0, tiled=True)  68.5 us
    ppermute x3, waiting for transfers between devices, swapped(): return lax.ppermute(x, 'rep', [(0, 1), (1, 0)])  48.2 us
    all_to_all x3, starting transfers between devices, moved(): own = lax.all_to_all(x, 'blk', split_axis=0, concat_axis=0, tiled=True)  22.6 us
    all_to_all x2, waiting for transfers between devices, returned(): x = lax.all_to_all(x, 'blk', split_axis=0, concat_axis=0, tiled=True)  22.3 us
    pallas_call x2, Pallas kernels, hidden_of(): pl.pallas_call(kernel, grid_spec=pltpu.PrefetchScalarGridSpec(num_scalar_...  19.1 us
    all_to_all x2, starting transfers between devices, returned(): x = lax.all_to_all(x, 'blk', split_axis=0, concat_axis=0, tiled=True)  15 us
    all_to_all x1, blocking collectives, everywhere(): lax.all_to_all(copies, 'blk', split_axis=0, concat_axis=0, tiled=True)  11.6 us
    all_to_all x1, starting transfers between devices, everywhere(): lax.all_to_all(copies, 'blk', split_axis=0, concat_axis=0, tiled=True)  10.7 us
  transfers between devices with their start and end apart: 11, of which 8 were waited for; matrix products, arithmetic and copies ran while one was open for 1% of the time, Pallas kernels for 20%

profile of v12, /device:TPU:0, one launch (start us, length us, event | category | flops | bytes accessed | tf_op | source)
XLA Modules:
  0.0 310.1 jit_solution(5630981965237634799)
XLA Ops:
  7.2 0.0 all-gather.4.cloned.1.call-start
  7.2 3.0 prep.1
  10.2 0.0 all-gather.4.cloned.1.call-update
  10.3 3.3 %cast.3 = bf16[16,96,512]{2,1,0:T(8,128)(2,1)} custom-call(f32[4608,512]{1,0:T(8,128)} %bitcast.44, bf16[128,1664]{1,0:T(8,128)(2,1)} %get-tuple-element.18.rank_ref.refs_0_), custom_call_target="tpu_custom_call" | custom-call | tf_op jit(solution)/shard_map/cast/pallas_call | solution.py:460
  13.5 7.4 %all-to-all-start = ((bf16[16,96,512]{2,1,0:T(8,128)(2,1)}), bf16[16,96,512]{2,1,0:T(8,128)(2,1)S(1)}, u32[]{:S(2)}, u32[]{:S(2)}) async-start(bf16[16,96,512]{2,1,0:T(8,128)(2,1)} %cast.3), calls=%async_computation | async-start | bytes 3145728 | tf_op jit(solution)/shard_map/all_to_all | solution.py:476
  20.9 3.3 %cast.4 = bf16[16,96,512]{2,1,0:T(8,128)(2,1)} custom-call(f32[4608,512]{1,0:T(8,128)} %bitcast.45), custom_call_target="tpu_custom_call" | custom-call | tf_op jit(solution)/shard_map/cast/pallas_call | solution.py:460
  24.2 48.8 %all-to-all-done = bf16[16,96,512]{2,1,0:T(8,128)(2,1)S(1)} async-done(((bf16[16,96,512]{2,1,0:T(8,128)(2,1)}), bf16[16,96,512]{2,1,0:T(8,128)(2,1)S(1)}, u32[]{:S(2)}, u32[]{:S(2)}) %all-to-all-start) | async-done | bytes 1572896 | tf_op jit(solution)/shard_map/all_to_all | solution.py:476
  73.0 0.0 copy-start.1
  73.0 6.1 %all-to-all-start.1 = ((bf16[16,96,512]{2,1,0:T(8,128)(2,1)}), bf16[16,96,512]{2,1,0:T(8,128)(2,1)S(1)}, u32[]{:S(2)}, u32[]{:S(2)}) async-start(bf16[16,96,512]{2,1,0:T(8,128)(2,1)} %cast.4), calls=%async_computation.1 | async-start | bytes 3145728 | tf_op jit(solution)/shard_map/all_to_all | solution.py:476
  79.1 0.0 copy-done.1
  79.1 1.5 collective-permute-start
  80.6 3.2 %cast.5.__0_ = bf16[16,96,512]{2,1,0:T(8,128)(2,1)} custom-call(f32[4608,512]{1,0:T(8,128)} %bitcast.46), custom_call_target="tpu_custom_call" | custom-call | tf_op jit(solution)/shard_map/cast/pallas_call | solution.py:460
  83.8 32.1 %collective-permute-done.__1_.g_ref.g_oth = bf16[1536,512]{1,0:T(8,128)(2,1)} collective-permute-done((bf16[1536,512]{1,0:T(8,128)(2,1)S(1)}, bf16[1536,512]{1,0:T(8,128)(2,1)}, u32[]{:S(2)}, u32[]{:S(2)}) %collective-permute-start) | collective-permute-done | bytes 1572896 | tf_op jit(solution)/shard_map/ppermute | solution.py:480
  116.0 0.0 copy-start.9
  116.0 0.4 all-to-all-done.1
  116.3 0.0 copy-start.2
  116.3 9.2 %all-to-all-start.2 = ((bf16[16,96,512]{2,1,0:T(8,128)(2,1)}), bf16[16,96,512]{2,1,0:T(8,128)(2,1)}, u32[]{:S(2)}, u32[]{:S(2)}) async-start(bf16[16,96,512]{2,1,0:T(8,128)(2,1)} %tie.2), calls=%async_computation.2 | async-start | bytes 3145728 | tf_op jit(solution)/shard_map/all_to_all | solution.py:476
  125.5 0.0 copy-done.2
  125.5 1.5 collective-permute-start.1
  127.1 0.0 copy-done.9
  127.1 0.5 dynamic_slice.3
  127.6 1.2 stack.34.info
  128.8 0.0 all-gather.4.cloned.1.call-done.x_ref
  128.8 9.4 %gate_up.2 = (bf16[576,512]{1,0:T(8,128)(2,1)}, bf16[640,64]{1,0:T(8,128)(2,1)}) custom-call(s32[20]{0:T(128)} %stack.34.info, bf16[2048,1664]{1,0:T(8,128)(2,1)} %all-gather.4.cloned.1.call-done.x_ref, bf16[1536,512]{1,0:T(8,128)(2,1)} %bitcast.51, bf16[1536,512]{1,0:T(8,128)(2,1)} %bitcast.54), custom_call_target="tpu_custom_call" | custom-call | tf_op jit(solution)/shard_map/gate_up/pallas_call | solution.py:521
  138.2 19.4 %all-to-all-done.2 = bf16[16,96,512]{2,1,0:T(8,128)(2,1)} async-done(((bf16[16,96,512]{2,1,0:T(8,128)(2,1)}), bf16[16,96,512]{2,1,0:T(8,128)(2,1)}, u32[]{:S(2)}, u32[]{:S(2)}) %all-to-all-start.2) | async-done | bytes 1572896 | tf_op jit(solution)/shard_map/all_to_all | solution.py:476
  157.6 5.5 %own_down.1 = (bf16[512,1536]{1,0:T(8,128)(2,1)}, bf16[64,1536]{1,0:T(8,128)(2,1)}, bf16[768,512]{1,0:T(8,128)(2,1)}, bf16[768,512]{1,0:T(8,128)(2,1)}) custom-call(bf16[576,512]{1,0:T(8,128)(2,1)} %get-tuple-element.21.hidden_ref, bf16[1536,512]{1,0:T(8,128)(2,1)} %bitcast.12.d_ref), custom_call_target="tpu_custom_call" | custom-call | tf_op jit(solution)/shard_map/own_down/pallas_call | solution.py:555
  163.1 0.0 collective-permute-done.1.__1_.u_ref.u_oth
  163.1 0.0 copy-start.3
  163.1 1.1 copy-done.3
  164.3 0.0 copy-start.6
  164.3 9.2 %all-to-all-start.4 = ((bf16[16,32,1536]{2,1,0:T(8,128)(2,1)}), bf16[16,32,1536]{2,1,0:T(8,128)(2,1)S(1)}, u32[]{:S(2)}, u32[]{:S(2)}) async-start(bf16[16,32,1536]{2,1,0:T(8,128)(2,1)} %bitcast.56), calls=%async_computation.4 | async-start | bytes 3145728 | tf_op jit(solution)/shard_map/all_to_all | solution.py:545
  173.5 0.0 all-gather.6.cloned.1.call-start
  173.6 0.7 all-gather.6.cloned.1.call-update
  174.3 0.0 copy-done.6
  174.3 1.5 collective-permute-start.2
  175.8 9.7 %gate_up.3.hidden_ref = bf16[640,512]{1,0:T(8,128)(2,1)} custom-call(s32[20]{0:T(128)} %stack.34.info, bf16[2048,1664]{1,0:T(8,128)(2,1)} %all-gather.4.cloned.1.call-done.x_ref, bf16[1536,512]{1,0:T(8,128)(2,1)} %collective-permute-done.__1_.g_ref.g_oth, bf16[1536,512]{1,0:T(8,128)(2,1)} %copy-done.3, bf16[512,1536]{1,0:T(8,128)(2,1)} %tie.3._), custom_call_target="tpu_custom_call" | custom-call | tf_op jit(solution)/shard_map/gate_up/pallas_call | solution.py:521
  185.5 16.1 %collective-permute-done.2.d_b.b_oth = bf16[768,512]{1,0:T(8,128)(2,1)S(1)} collective-permute-done((bf16[768,512]{1,0:T(8,128)(2,1)S(1)}, bf16[768,512]{1,0:T(8,128)(2,1)S(1)}, u32[]{:S(2)}, u32[]{:S(2)}) %collective-permute-start.2) | collective-permute-done | bytes 786464 | tf_op jit(solution)/shard_map/ppermute | solution.py:480
  201.6 0.0 copy-start.5
  201.6 9.7 %all-gather.6.cloned.1.call-done = bf16[1536,512]{1,0:T(8,128)(2,1)} async-done(((bf16[768,512]{1,0:T(8,128)(2,1)}), bf16[1536,512]{1,0:T(8,128)(2,1)}) %all-gather.6.cloned.1.call-update) | async-done | bytes 1572880 | tf_op jit(solution)/shard_map/all_gather | solution.py:578
  211.3 0.0 copy-done.5
  211.3 6.7 %oth_down.1._ = bf16[640,1536]{1,0:T(8,128)(2,1)} custom-call(s32[20]{0:T(128)} %stack.34.info, bf16[640,512]{1,0:T(8,128)(2,1)} %gate_up.3.hidden_ref, bf16[640,64]{1,0:T(8,128)(2,1)} %get-tuple-element.23.spot_ref, bf16[64,1536]{1,0:T(8,128)(2,1)} %get-tuple-element.24.late_ref, bf16[2,768,512]{2,1,0:T(8,128)(2,1)} %bitcast.58, bf16[768,512]{1,0:T(8,128)(2,1)} %copy-done.5), custom_call_target="tpu_custom_call" | custom-call | tf_op jit(solution)/shard_map/oth_down/pallas_call | solution.py:585
  218.0 0.0 all-to-all-done.4
  218.0 0.0 copy-start.4
  218.0 1.2 copy-done.4
  219.2 5.7 %all-to-all-start.3 = ((bf16[16,40,1536]{2,1,0:T(8,128)(2,1)}), bf16[16,40,1536]{2,1,0:T(8,128)(2,1)S(1)}, u32[]{:S(2)}, u32[]{:S(2)}) async-start(bf16[16,40,1536]{2,1,0:T(8,128)(2,1)} %bitcast.49), calls=%async_computation.3 | async-start | bytes 3932160 | tf_op jit(solution)/shard_map/all_to_all | solution.py:545
  224.9 3.1 mix.1
  228.0 8.2 %place.1._ = bf16[3,1536,1024]{2,1,0:T(8,128)(2,1)} custom-call(s32[20]{0:T(128)} %stack.34.info, bf16[1536,512]{1,0:T(8,128)(2,1)} %bitcast.52, bf16[1536,512]{1,0:T(8,128)(2,1)} %collective-permute-done.__1_.g_ref.g_oth, bf16[1536,512]{1,0:T(8,128)(2,1)} %bitcast.55, bf16[1536,512]{1,0:T(8,128)(2,1)} %copy-done.3, bf16[2,768,512]{2,1,0:T(8,128)(2,1)} %bitcast.59, ...), custom_call_target="tpu_custom_call" | custom-call | tf_op jit(solution)/shard_map/place/pallas_call | solution.py:609
  236.2 5.3 %first.1 = (f32[128,1536]{1,0:T(8,128)}, f32[1,1536]{1,0:T(1,128)}) custom-call(s32[20]{0:T(128)} %stack.34.info, bf16[384,512]{1,0:T(8,128)(2,1)} %get-tuple-element.27.mix_ref, bf16[512,1536]{1,0:T(8,128)(2,1)} %bitcast.57, bf16[128,1536]{1,0:T(8,128)(2,1)} %bitcast.61), custom_call_target="tpu_custom_call" | custom-call | tf_op jit(solution)/shard_map/first/pallas_call | solution.py:659
  241.5 22.3 %all-to-all-done.3 = bf16[16,40,1536]{2,1,0:T(8,128)(2,1)S(1)} async-done(((bf16[16,40,1536]{2,1,0:T(8,128)(2,1)}), bf16[16,40,1536]{2,1,0:T(8,128)(2,1)S(1)}, u32[]{:S(2)}, u32[]{:S(2)}) %all-to-all-start.3) | async-done | bytes 1966112 | tf_op jit(solution)/shard_map/all_to_all | solution.py:545
  263.7 0.0 copy-start
  263.7 1.3 copy-done
  265.0 3.1 last.1._
  268.1 10.7 %all-to-all-start.5 = ((f32[16,1,1536]{2,1,0:T(1,128)}), f32[16,1,1536]{2,1,0:T(1,128)S(1)}, u32[]{:S(2)}, u32[]{:S(2)}) async-start(f32[16,1,1536]{2,1,0:T(1,128)} %last.1._), calls=%async_computation.5 | async-start | bytes 196608 | tf_op jit(solution)/shard_map/all_to_all | solution.py:706
  278.8 0.0 copy-start.7
  278.8 0.0 copy-start.8
  278.8 5.8 %combine.1 = (bf16[128,1536]{1,0:T(8,128)(2,1)}, f32[1,128]{1,0:T(1,128)}) custom-call(s32[20]{0:T(128)} %stack.34.info, bf16[384,640]{1,0:T(8,128)(2,1)} %get-tuple-element.20.mix_ref, bf16[640,1536]{1,0:T(8,128)(2,1)} %bitcast.48, f32[128,1536]{1,0:T(8,128)} %get-tuple-element.28.base_ref, f32[16,1,1536]{2,1,0:T(1,128)} %last.1._), custom_call_target="tpu_custom_call" | custom-call | tf_op jit(solution)/shard_map/combine/pallas_call | solution.py:688
  284.7 0.7 compare_select_fusion
  285.3 0.9 all-to-all-done.5
  286.2 0.1 fusion
  286.3 0.0 copy-done.7
  286.3 0.0 copy-done.8
  286.3 4.6 %fusion.7 = (f32[16]{0:T(128)S(1)}, f32[16]{0:T(128)S(1)}) fusion(s32[2048]{0:T(1024)S(1)} %iota_add_fusion, s32[16]{0:T(128)S(1)} %copy-done.8, bf16[2048,1536]{1,0:T(8,128)(2,1)} %param.15, f32[16,1,1536]{2,1,0:T(1,128)S(1)} %all-to-all-done.5, f32[1536]{0:T(1024)S(1)} %copy-done.7, f32[16]{0:T(128)S(1)} %add_rsqrt_fusion), kind=kOutput, calls=%fused_computation.17 | convolution fusion | flops 100868064 | bytes 6404352 | tf_op jit(solution)/shard_map/dot_general | solution.py:714
  291.0 11.6 %all_to_all.35 = f32[16,3,16]{2,1,0:T(4,128)S(1)} all-to-all(f32[16,3,16]{2,1,0:T(4,128)S(1)} %broadcast_in_dim.28), channel_id=1, replica_groups=mesh['blk'=16,'rep'=2] {'blk'}, dimensions={0} | all-to-all | bytes 6144 | tf_op jit(solution)/shard_map/all_to_all | solution.py:706
  302.7 0.6 pad_maximum_fusion.1
  (11 shorter events, 0.1 us)
Async XLA Ops:
  7.2 121.6 %all-gather.4.cloned.1.call-start = ((), (), s32[]{:S(2)}) async-start(), calls=%async_computation.7 | async-start | bytes 7241728 | tf_op jit(solution)/shard_map/all_gather | solution.py:518
  13.5 59.5 %all-to-all-start = ((bf16[16,96,512]{2,1,0:T(8,128)(2,1)}), bf16[16,96,512]{2,1,0:T(8,128)(2,1)S(1)}, u32[]{:S(2)}, u32[]{:S(2)}) async-start(bf16[16,96,512]{2,1,0:T(8,128)(2,1)} %cast.3), calls=%async_computation | async-start | bytes 3145728 | tf_op jit(solution)/shard_map/all_to_all | solution.py:476
  73.0 6.1 %copy-start.1 = (bf16[16,96,512]{2,1,0:T(8,128)(2,1)}, bf16[16,96,512]{2,1,0:T(8,128)(2,1)S(1)}, u32[]{:S(2)}) copy-start(bf16[16,96,512]{2,1,0:T(8,128)(2,1)S(1)} %all-to-all-done) | copy-start | bytes 4718596
  73.0 43.4 %all-to-all-start.1 = ((bf16[16,96,512]{2,1,0:T(8,128)(2,1)}), bf16[16,96,512]{2,1,0:T(8,128)(2,1)S(1)}, u32[]{:S(2)}, u32[]{:S(2)}) async-start(bf16[16,96,512]{2,1,0:T(8,128)(2,1)} %cast.4), calls=%async_computation.1 | async-start | bytes 3145728 | tf_op jit(solution)/shard_map/all_to_all | solution.py:476
  79.1 36.9 %collective-permute-start = (bf16[1536,512]{1,0:T(8,128)(2,1)S(1)}, bf16[1536,512]{1,0:T(8,128)(2,1)}, u32[]{:S(2)}, u32[]{:S(2)}) collective-permute-start(bf16[1536,512]{1,0:T(8,128)(2,1)S(1)} %bitcast.50), channel_id=1, source_target_pairs={{0,1},{1,0},{2,3},{3,2},{4,5},{5,4},{6,7},{7,6},{8,9},{9,8},{10,11... | collective-permute-start | bytes 4718600 | tf_op jit(solution)/shard_map/ppermute | solution.py:480
  116.0 11.1 %copy-start.9 = (s32[16]{0:T(128)S(1)}, s32[16]{0:T(128)}, u32[]{:S(2)}) copy-start(s32[16]{0:T(128)} %lengths_ref.1) | copy-start | bytes 196
  116.3 9.2 %copy-start.2 = (bf16[16,96,512]{2,1,0:T(8,128)(2,1)}, bf16[16,96,512]{2,1,0:T(8,128)(2,1)S(1)}, u32[]{:S(2)}) copy-start(bf16[16,96,512]{2,1,0:T(8,128)(2,1)S(1)} %all-to-all-done.1) | copy-start | bytes 4718596
  116.3 41.2 %all-to-all-start.2 = ((bf16[16,96,512]{2,1,0:T(8,128)(2,1)}), bf16[16,96,512]{2,1,0:T(8,128)(2,1)}, u32[]{:S(2)}, u32[]{:S(2)}) async-start(bf16[16,96,512]{2,1,0:T(8,128)(2,1)} %tie.2), calls=%async_computation.2 | async-start | bytes 3145728 | tf_op jit(solution)/shard_map/all_to_all | solution.py:476
  125.5 37.6 %collective-permute-start.1 = (bf16[1536,512]{1,0:T(8,128)(2,1)S(1)}, bf16[1536,512]{1,0:T(8,128)(2,1)S(1)}, u32[]{:S(2)}, u32[]{:S(2)}) collective-permute-start(bf16[1536,512]{1,0:T(8,128)(2,1)S(1)} %bitcast.53), channel_id=1, source_target_pairs={{0,1},{1,0},{2,3},{3,2},{4,5},{5,4},{6,7},{7,6},{8,9},{9,8},{10,11... | collective-permute-start | bytes 4718600 | tf_op jit(solution)/shard_map/ppermute | solution.py:480
  163.1 1.2 copy-start.3
  164.3 10.0 %copy-start.6 = (bf16[768,512]{1,0:T(8,128)(2,1)S(1)}, bf16[768,512]{1,0:T(8,128)(2,1)}, u32[]{:S(2)}) copy-start(bf16[768,512]{1,0:T(8,128)(2,1)} %get-tuple-element.26.b_own) | copy-start | bytes 2359300
  164.3 53.7 %all-to-all-start.4 = ((bf16[16,32,1536]{2,1,0:T(8,128)(2,1)}), bf16[16,32,1536]{2,1,0:T(8,128)(2,1)S(1)}, u32[]{:S(2)}, u32[]{:S(2)}) async-start(bf16[16,32,1536]{2,1,0:T(8,128)(2,1)} %bitcast.56), calls=%async_computation.4 | async-start | bytes 3145728 | tf_op jit(solution)/shard_map/all_to_all | solution.py:545
  173.5 37.8 %all-gather.6.cloned.1.call-start = ((), (), s32[]{:S(2)}) async-start(), calls=%async_computation.8 | async-start | bytes 2359296 | tf_op jit(solution)/shard_map/all_gather | solution.py:578
  174.3 27.3 %collective-permute-start.2 = (bf16[768,512]{1,0:T(8,128)(2,1)S(1)}, bf16[768,512]{1,0:T(8,128)(2,1)S(1)}, u32[]{:S(2)}, u32[]{:S(2)}) collective-permute-start(bf16[768,512]{1,0:T(8,128)(2,1)S(1)} %copy-done.6), channel_id=1, source_target_pairs={{0,1},{1,0},{2,3},{3,2},{4,5},{5,4},{6,7},{7,6},{8,9},{9,8},{10,11... | collective-permute-start | bytes 2359304 | tf_op jit(solution)/shard_map/ppermute | solution.py:480
  201.6 9.7 %copy-start.5 = (bf16[768,512]{1,0:T(8,128)(2,1)}, bf16[768,512]{1,0:T(8,128)(2,1)S(1)}, u32[]{:S(2)}) copy-start(bf16[768,512]{1,0:T(8,128)(2,1)S(1)} %collective-permute-done.2.d_b.b_oth) | copy-start | bytes 2359300
  218.0 1.2 copy-start.4
  219.2 44.6 %all-to-all-start.3 = ((bf16[16,40,1536]{2,1,0:T(8,128)(2,1)}), bf16[16,40,1536]{2,1,0:T(8,128)(2,1)S(1)}, u32[]{:S(2)}, u32[]{:S(2)}) async-start(bf16[16,40,1536]{2,1,0:T(8,128)(2,1)} %bitcast.49), calls=%async_computation.3 | async-start | bytes 3932160 | tf_op jit(solution)/shard_map/all_to_all | solution.py:545
  263.7 1.3 copy-start
  268.1 18.1 %all-to-all-start.5 = ((f32[16,1,1536]{2,1,0:T(1,128)}), f32[16,1,1536]{2,1,0:T(1,128)S(1)}, u32[]{:S(2)}, u32[]{:S(2)}) async-start(f32[16,1,1536]{2,1,0:T(1,128)} %last.1._), calls=%async_computation.5 | async-start | bytes 196608 | tf_op jit(solution)/shard_map/all_to_all | solution.py:706
  278.8 7.5 %copy-start.7 = (f32[1536]{0:T(1024)S(1)}, f32[1536]{0:T(1024)}, u32[]{:S(2)}) copy-start(f32[1536]{0:T(1024)} %param.16) | copy-start | bytes 18436
  278.8 7.5 %copy-start.8 = (s32[16]{0:T(128)S(1)}, s32[16]{0:T(128)}, u32[]{:S(2)}) copy-start(s32[16]{0:T(128)} %param.17) | copy-start | bytes 196
Sparse Core Ops, SparseCore 0:
  10.4 95.2 all-gather.3
  175.9 35.3 all-gather.5

commit v13 on v11

--- a/solution.py
+++ b/solution.py
@@ -149,13 +149,14 @@
     return lax.broadcasted_iota(jnp.int32, shape, dim)
 
 
-def prep_kernel(length_ref, hidden_ref, routes_ref, weights_ref, gain_ref, rows_ref, pieces_ref):
+def prep_kernel(lengths_ref, blk_ref, hidden_ref, routes_ref, weights_ref, gain_ref, rows_ref, pieces_ref):
     rows, width = hidden_ref.shape
-    length = length_ref[0]
+    length = lengths_ref[blk_ref[0]]
     x = hidden_ref[...].astype(jnp.float32)
     scale = lax.rsqrt(jnp.mean(x * x, axis=-1, keepdims=True) + 1e-05)
     rows_ref[:, :width] = (x * scale * gain_ref[...][None]).astype(jnp.bfloat16)
-    lane = iota((rows, LANES), 1)
+    column = iota((rows, LANES), 1)
+    lane = column & (EXPERTS - 1)
     row = iota((rows, LANES), 0)
     hit = jnp.zeros((rows, LANES), jnp.float32)
     weight = jnp.zeros((rows, LANES), jnp.float32)
@@ -172,24 +173,58 @@
     rank = jnp.dot(
         before.astype(jnp.bfloat16), hit.astype(jnp.bfloat16), preferred_element_type=jnp.float32
     )
-    rows_ref[:, width:] = jnp.where(hit > 0.0, rank, -1.0).astype(jnp.bfloat16)
+    told = jnp.where(hit > 0.0, rank, -1.0)
     for k in range(3):
         piece = weight.astype(jnp.bfloat16)
         pieces_ref[k * rows : (k + 1) * rows, :] = piece
-        weight = weight - piece.astype(jnp.float32)
-
-
-def pick(info, which, x_ref, width, place, slots):
+        value = piece.astype(jnp.float32)
+        told = jnp.where(column >= (k + 1) * EXPERTS, value, told)
+        weight = weight - value
+    rows_ref[:, width:] = told.astype(jnp.bfloat16)
+
+
+def pick(info, lengths_ref, ring_ref, which, x_ref, width, place, slots, lasts):
+    step = pl.program_id(0)
     rows = x_ref.shape[0]
+    sources = rows // LEN
     ranks = x_ref[:, width:].astype(jnp.float32)
     lane = iota((rows, LANES), 1)
-    source = (iota((rows, 1), 0) // LEN).astype(jnp.float32)
+    row = iota((rows, 1), 0)
+    source = row // LEN
     rank = jnp.sum(jnp.where(lane == info[which], ranks, 0.0), axis=1, keepdims=True)
-    slot = jnp.where(rank >= 0.0, place(source, rank), -1.0)
+    slot = jnp.where(rank >= 0.0, place(source.astype(jnp.float32), rank), -1.0)
     slot_lane = iota((rows, slots), 1).astype(jnp.float32)
     one_hot = jnp.where(slot == slot_lane, 1.0, 0.0).astype(jnp.bfloat16)
-    return lax.dot_general(
-        one_hot, x_ref[:, :width], (((0,), (0,)), ((), ())), preferred_element_type=jnp.float32
+    dims = (((0,), (0,)), ((), ()))
+    chosen = lax.dot_general(
+        one_hot, x_ref[:, :width], dims, preferred_element_type=jnp.float32
+    )
+    home = jnp.full_like(row, -1)
+    for s in range(sources):
+        owner = ring_ref[step * sources + s]
+        home = jnp.where(row == s * LEN + lengths_ref[owner] - 1, owner, home)
+    home = jnp.where(rank >= 0.0, home, -1)
+    count = lasts.shape[0]
+    one_hot = jnp.where(home == iota((rows, count), 1), 1.0, 0.0).astype(jnp.bfloat16)
+    last = lax.dot_general(one_hot, x_ref[...], dims, preferred_element_type=jnp.float32)
+
+    @pl.when(step == 0)
+    def _():
+        lasts[...] = last
+
+    @pl.when(step != 0)
+    def _():
+        lasts[...] += last
+
+    return chosen
+
+
+def share_of(info, which, lasts, width):
+    ext = lasts[:, width:]
+    lane = iota(ext.shape, 1)
+    is_own = (lane >= EXPERTS) & ((lane & (EXPERTS - 1)) == info[which])
+    return jnp.broadcast_to(
+        jnp.sum(jnp.where(is_own, ext, 0.0), axis=1, keepdims=True), ext.shape
     )
 
 
@@ -200,52 +235,82 @@
     return (gate / (1.0 + jnp.exp(-gate)) * up).astype(jnp.bfloat16)
 
 
-def own_kernel(info, x_ref, g_ref, u_ref, out_ref, spot_ref, picked):
+def own_kernel(
+    info, lengths_ref, ring_ref, x_ref, g_ref, u_ref, out_ref, spot_ref, share_ref, picked, lasts
+):
     step = pl.program_id(0)
     sources = x_ref.shape[0] // LEN
+    width = g_ref.shape[0]
     more = CAP - FIRST
     early = sources * FIRST
     all_early = GROUPS * early
+    all_rows = all_early + GROUPS * sources * more
 
     def place(source, rank):
         return jnp.where(
             rank < FIRST, source * FIRST + rank, early + source * more + (rank - FIRST)
         )
 
-    chosen = pick(info, 0, x_ref, g_ref.shape[0], place, early + sources * more)
+    chosen = pick(
+        info, lengths_ref, ring_ref, 0, x_ref, width, place, early + sources * more, lasts
+    )
     for s in range(sources):
-        start = pl.multiple_of(info[4 + step * sources + s] * FIRST, FIRST)
+        start = pl.multiple_of(ring_ref[step * sources + s] * FIRST, FIRST)
         picked[pl.ds(start, FIRST), :] = chosen[s * FIRST : (s + 1) * FIRST]
     start = pl.multiple_of(all_early + step * sources * more, sources * more)
     picked[pl.ds(start, sources * more), :] = chosen[early:]
 
     @pl.when(step == GROUPS - 1)
     def _():
+        picked[all_rows:, :] = lasts[:, :width]
         out_ref[...] = activ(picked[...], g_ref, u_ref)
+        share_ref[...] = share_of(info, 0, lasts, width)
         column = iota(spot_ref.shape, 1)
         owner = lax.shift_right_logical(column, more.bit_length() - 1)
-        source = jnp.zeros_like(column)
+        source = jnp.full_like(column, -1)
         for k, b in enumerate(RING):
-            source = source + jnp.where(owner == k, b, 0)
-        spot = source * SECOND + (column & (more - 1))
+            source = jnp.where(owner == k, b, source)
+        spot = jnp.where(source >= 0, source * SECOND + (column & (more - 1)), -1)
         spot_ref[...] = jnp.where(iota(spot_ref.shape, 0) == spot, 1.0, 0.0).astype(jnp.bfloat16)
 
 
-def oth_kernel(info, x_ref, g_ref, u_ref, _, out_ref, picked):
+def oth_kernel(
+    info,
+    lengths_ref,
+    ring_ref,
+    x_ref,
+    g_ref,
+    u_ref,
+    resid_ref,
+    _,
+    out_ref,
+    share_ref,
+    base_ref,
+    picked,
+    lasts,
+):
     step = pl.program_id(0)
     sources = x_ref.shape[0] // LEN
+    width = g_ref.shape[0]
+    all_rows = GROUPS * sources * SECOND
 
     def place(source, rank):
         return source * SECOND + (SECOND - CAP) + rank
 
-    chosen = pick(info, 1, x_ref, g_ref.shape[0], place, sources * SECOND)
+    chosen = pick(info, lengths_ref, ring_ref, 1, x_ref, width, place, sources * SECOND, lasts)
     for s in range(sources):
-        start = pl.multiple_of(info[4 + step * sources + s] * SECOND, SECOND)
+        start = pl.multiple_of(ring_ref[step * sources + s] * SECOND, SECOND)
         picked[pl.ds(start, SECOND), :] = chosen[s * SECOND : (s + 1) * SECOND]
 
     @pl.when(step == GROUPS - 1)
     def _():
+        picked[all_rows:, :] = lasts[:, :width]
         out_ref[...] = activ(picked[...], g_ref, u_ref)
+        share_ref[...] = share_of(info, 1, lasts, width)
+        resid = resid_ref[...].astype(jnp.float32)
+        is_last = iota(resid.shape, 0) == info[3] - 1
+        last = jnp.sum(jnp.where(is_last, resid, 0.0), axis=0, keepdims=True)
+        base_ref[...] = jnp.where(iota(base_ref.shape, 0) == info[4], last, 0.0)
 
 
 def matmul_nt(hidden_ref, d):
@@ -272,25 +337,44 @@
     return held[step]
 
 
-def own_down_kernel(hidden_ref, d_ref, out_ref, late_ref, held, sems):
+def own_down_kernel(hidden_ref, share_ref, d_ref, out_ref, late_ref, part_ref, held, sems):
     size = held.shape[1]
     d = fetched([d_ref.at[k * size : (k + 1) * size] for k in range(held.shape[0])], held, sems)
     out = matmul_nt(hidden_ref, d).astype(jnp.bfloat16)
     rows = out_ref.shape[0]
     out_ref[...] = out[:rows]
     late_ref[...] = out[rows:]
-
-
-def oth_down_kernel(info, hidden_ref, spot_ref, late_ref, d_ref, out_ref, held, sems):
+    count = part_ref.shape[0]
+    part_ref[...] = share_ref[:, :1] * out[-count:].astype(jnp.float32)
+
+
+def oth_down_kernel(
+    info,
+    hidden_ref,
+    share_ref,
+    spot_ref,
+    late_ref,
+    base_ref,
+    part_ref,
+    d_ref,
+    out_ref,
+    sum_ref,
+    held,
+    sems,
+):
     size = held.shape[1]
     other = 1 - info[2]
     sources = [d_ref.at[other, k * size : (k + 1) * size] for k in range(held.shape[0])]
     d = fetched(sources, held, sems)
     late = jnp.dot(spot_ref[...], late_ref[...], preferred_element_type=jnp.float32)
-    out_ref[...] = (late + matmul_nt(hidden_ref, d)).astype(jnp.bfloat16)
-
-
-def mix_kernel(info, rank_ref, pieces_ref, first_ref, second_ref, last_ref):
+    out = matmul_nt(hidden_ref, d)
+    rows = out_ref.shape[0]
+    out_ref[...] = (late + out[:rows]).astype(jnp.bfloat16)
+    last = out[rows:].astype(jnp.bfloat16).astype(jnp.float32)
+    sum_ref[...] = base_ref[...] + part_ref[...] + share_ref[:, :1] * last
+
+
+def mix_kernel(info, rank_ref, pieces_ref, first_ref, second_ref):
     rows = rank_ref.shape[0]
     late = SECOND - CAP
     own, oth = info[2], 1 - info[2]
@@ -317,11 +401,6 @@
                 pieces_ref[k * rows : (k + 1) * rows, :], spread, preferred_element_type=jnp.float32
             )
             mix_ref[k * rows : (k + 1) * rows, :] = jnp.where(match, part, 0.0).astype(jnp.bfloat16)
-    shape = (last_ref.shape[0], 3 * rows)
-    one_hot = jnp.where(iota(shape, 1) == iota(shape, 0) * rows + info[3] - 1, 1.0, 0.0)
-    last_ref[...] = jnp.dot(
-        one_hot.astype(jnp.bfloat16), second_ref[...], preferred_element_type=jnp.float32
-    ).astype(jnp.bfloat16)
 
 
 def weigh(mix_ref, back_ref):
@@ -330,33 +409,11 @@
     return parts[2 * rows :] + parts[rows : 2 * rows] + parts[:rows]
 
 
-def first_kernel(info, mix_ref, back_ref, resid_ref, base_ref, last_ref):
-    base = resid_ref[...].astype(jnp.float32) + weigh(mix_ref, back_ref)
-    base_ref[...] = base
-    is_last = iota(base.shape, 0) == info[3] - 1
-    last_ref[...] = jnp.sum(jnp.where(is_last, base, 0.0), axis=0, keepdims=True)
-
-
-def last_kernel(mix_ref, base_ref, back_ref, _, told_ref, held, sems):
-    size = held.shape[1]
-    copies = [
-        pltpu.make_async_copy(back_ref.at[k * size : (k + 1) * size], held.at[k], sems.at[k])
-        for k in range(held.shape[0])
-    ]
-    for copy in copies:
-        copy.start()
-    parts = jnp.zeros((mix_ref.shape[0], held.shape[2]), jnp.float32)
-    for k, copy in enumerate(copies):
-        copy.wait()
-        parts = parts + jnp.dot(
-            mix_ref[:, k * size : (k + 1) * size], held[k], preferred_element_type=jnp.float32
-        )
-    moe = parts[2:3] + parts[1:2] + parts[0:1]
-    out = (base_ref[...] + moe).astype(jnp.bfloat16).astype(jnp.float32)
-    told_ref[...] = jnp.broadcast_to(out[None], told_ref.shape)
-
-
-def combine_kernel(info, mix_ref, back_ref, base_ref, _, out_ref, square_ref, squares):
+def first_kernel(mix_ref, back_ref, resid_ref, base_ref):
+    base_ref[...] = resid_ref[...].astype(jnp.float32) + weigh(mix_ref, back_ref)
+
+
+def combine_kernel(info, mix_ref, back_ref, base_ref, _, __, out_ref, square_ref, squares):
     step = pl.program_id(0)
 
     @pl.when(step == 0)
@@ -430,8 +487,7 @@
     first = blk_count * FIRST
     second = blk_count * SECOND
     resid = hidden_in[0]
-    length = lax.dynamic_slice(lengths, (blk,), (1,))
-    info = jnp.stack([2 * blk + rep, 2 * blk + 1 - rep, rep, length[0]] + list(RING))
+    info = jnp.stack([2 * blk + rep, 2 * blk + 1 - rep, rep, lengths[blk], blk])
     info = info.astype(jnp.int32)
 
     shard_rows = master.shape[1]
@@ -475,7 +531,7 @@
     row_ext, pieces = pl.pallas_call(
         prep_kernel,
         grid_spec=pltpu.PrefetchScalarGridSpec(
-            num_scalar_prefetch=1,
+            num_scalar_prefetch=2,
             grid=(1,),
             in_specs=[
                 whole((rows, width)),
@@ -491,7 +547,7 @@
         ],
         compiler_params=params(),
         name="prep",
-    )(length, resid, routes[0].T, route_weights[0].T, norm_gain)
+    )(lengths, blk[None].astype(jnp.int32), resid, routes[0].T, route_weights[0].T, norm_gain)
     g_own = moved(turned(0, row_ext))
     g_oth = swapped(g_own)
     u_own = moved(turned(1))
@@ -500,25 +556,29 @@
 
     tokens = lax.all_gather(row_ext, "blk", axis_index_groups=[list(RING)], axis=0, tiled=True)
 
-    def hidden_of(kernel, sizes, scratch, g, u, *after):
+    ring = jnp.array(RING, jnp.int32)
+
+    def hidden_of(kernel, outs, picked, operands, specs):
         return pl.pallas_call(
             kernel,
             grid_spec=pltpu.PrefetchScalarGridSpec(
-                num_scalar_prefetch=1,
+                num_scalar_prefetch=3,
                 grid=(GROUPS,),
                 in_specs=[pl.BlockSpec((blk_count // GROUPS * rows, width + LANES), lambda i, *_: (i, 0))]
                 + [whole((width, FF))] * 2
-                + [pl.BlockSpec(memory_space=pl.ANY)] * len(after),
-                out_specs=[whole(size) for size in sizes],
-                scratch_shapes=[pltpu.VMEM((scratch, width), jnp.float32)],
+                + specs,
+                out_specs=[whole(out.shape) for out in outs],
+                scratch_shapes=[
+                    pltpu.VMEM((picked, width), jnp.float32),
+                    pltpu.VMEM((blk_count, width + LANES), jnp.float32),
+                ],
             ),
-            out_shape=[jax.ShapeDtypeStruct(size, jnp.bfloat16) for size in sizes],
+            out_shape=outs,
             compiler_params=params(),
             name="gate_up",
-        )(info, tokens, g, u, *after)
+        )(info, lengths, ring, tokens, *operands)
 
     step = 512
-
     quarter = width // 4
     anywhere = pl.BlockSpec(memory_space=pl.ANY)
 
@@ -528,57 +588,74 @@
         x = lax.all_to_all(x, "blk", split_axis=0, concat_axis=0, tiled=True)
         return x.reshape(slots, width)
 
-    extra = blk_count * (CAP - FIRST)
-    own_hidden, spot = hidden_of(
-        own_kernel, ((first + extra, FF), (second, extra)), first + extra, g_own, u_own
+    def bf16(*shape):
+        return jax.ShapeDtypeStruct(shape, jnp.bfloat16)
+
+    def f32(*shape):
+        return jax.ShapeDtypeStruct(shape, jnp.float32)
+
+    extra = blk_count * (CAP - FIRST) + blk_count
+    own_hidden, spot, own_share = hidden_of(
+        own_kernel,
+        [bf16(first + extra, FF), bf16(second, extra), f32(blk_count, LANES)],
+        first + extra,
+        (g_own, u_own),
+        [],
     )
     d_own = tied(d_own, own_hidden)
     d_both = lax.all_gather(d_own, "rep", axis=0)
-    own_out, late_out = pl.pallas_call(
+    own_out, late_out, own_part = pl.pallas_call(
         own_down_kernel,
         grid=(width // step,),
-        in_specs=[whole((first + extra, FF)), anywhere],
+        in_specs=[whole((first + extra, FF)), whole((blk_count, LANES)), anywhere],
         out_specs=[
             pl.BlockSpec((first, step), lambda i: (0, i)),
             pl.BlockSpec((extra, step), lambda i: (0, i)),
+            pl.BlockSpec((blk_count, step), lambda i: (0, i)),
         ],
-        out_shape=[
-            jax.ShapeDtypeStruct((first, width), jnp.bfloat16),
-            jax.ShapeDtypeStruct((extra, width), jnp.bfloat16),
-        ],
+        out_shape=[bf16(first, width), bf16(extra, width), f32(blk_count, width)],
         scratch_shapes=[
             pltpu.VMEM((width // step, step, FF), jnp.bfloat16),
             pltpu.SemaphoreType.DMA((width // step,)),
         ],
         compiler_params=params(),
         name="own_down",
-    )(own_hidden, d_own)
+    )(own_hidden, own_share, d_own)
     own_out = tied(own_out, u_oth)
     own_back = returned(own_out)
-    (oth_hidden,) = hidden_of(
-        oth_kernel, ((second, FF),), second, g_oth, u_oth, own_out
-    )
-    oth_out = pl.pallas_call(
+    oth_hidden, oth_share, base_part = hidden_of(
+        oth_kernel,
+        [bf16(second + blk_count, FF), f32(blk_count, LANES), f32(blk_count, width)],
+        second + blk_count,
+        (g_oth, u_oth, resid, own_out),
+        [whole((rows, width)), anywhere],
+    )
+    part_spec = pl.BlockSpec((blk_count, quarter), lambda i, *_: (0, i))
+    oth_out, last_part = pl.pallas_call(
         oth_down_kernel,
         grid_spec=pltpu.PrefetchScalarGridSpec(
             num_scalar_prefetch=1,
             grid=(4,),
             in_specs=[
-                whole((second, FF)),
+                whole((second + blk_count, FF)),
+                whole((blk_count, LANES)),
                 whole((second, extra)),
                 pl.BlockSpec((extra, quarter), lambda i, *_: (0, i)),
+                part_spec,
+                part_spec,
                 anywhere,
             ],
-            out_specs=pl.BlockSpec((second, quarter), lambda i, *_: (0, i)),
+            out_specs=[pl.BlockSpec((second, quarter), lambda i, *_: (0, i)), part_spec],
             scratch_shapes=[
                 pltpu.VMEM((4, quarter, FF), jnp.bfloat16),
                 pltpu.SemaphoreType.DMA((4,)),
             ],
         ),
-        out_shape=jax.ShapeDtypeStruct((second, width), jnp.bfloat16),
+        out_shape=[bf16(second, width), f32(blk_count, width)],
         compiler_params=params(),
         name="oth_down",
-    )(info, oth_hidden, spot, late_out, d_both)
+    )(info, oth_hidden, oth_share, spot, late_out, base_part, own_part, d_both)
+    last_parts = lax.all_gather(last_part, "blk", axis_index_groups=[list(RING)], axis=0)
     oth_back = returned(oth_out)
 
     server = pl.pallas_call(
@@ -595,7 +672,7 @@
         name="place",
     )(info, g_own, g_oth, u_own, u_oth, d_both, oth_out)
 
-    first_mix, second_mix, last_mix = pl.pallas_call(
+    first_mix, second_mix = pl.pallas_call(
         mix_kernel,
         grid_spec=pltpu.PrefetchScalarGridSpec(
             num_scalar_prefetch=1,
@@ -604,12 +681,11 @@
                 pl.BlockSpec((rows, LANES), lambda i, *_: (0, width // LANES)),
                 whole((3 * rows, LANES)),
             ],
-            out_specs=[whole((3 * rows, first)), whole((3 * rows, second)), whole((16, second))],
+            out_specs=[whole((3 * rows, first)), whole((3 * rows, second))],
         ),
         out_shape=[
             jax.ShapeDtypeStruct((3 * rows, first), jnp.bfloat16),
             jax.ShapeDtypeStruct((3 * rows, second), jnp.bfloat16),
-            jax.ShapeDtypeStruct((16, second), jnp.bfloat16),
         ],
         compiler_params=params(),
         name="mix",
@@ -619,41 +695,37 @@
         return [whole((3 * rows, slots)), pl.BlockSpec((slots, step), lambda i, *_: (0, i))]
 
     column = pl.BlockSpec((rows, step), lambda i, *_: (0, i))
-    lane_row = pl.BlockSpec((1, step), lambda i, *_: (0, i))
-    base, last_base = pl.pallas_call(
+    base = pl.pallas_call(
         first_kernel,
-        grid_spec=pltpu.PrefetchScalarGridSpec(
-            num_scalar_prefetch=1,
-            grid=(width // step,),
-            in_specs=weigh_specs(first) + [column],
-            out_specs=[column, lane_row],
-        ),
-        out_shape=[
-            jax.ShapeDtypeStruct((rows, width), jnp.float32),
-            jax.ShapeDtypeStruct((1, width), jnp.float32),
-        ],
+        grid=(width // step,),
+        in_specs=weigh_specs(first) + [column],
+        out_specs=column,
+        out_shape=f32(rows, width),
         compiler_params=params(),
         name="first",
-    )(info, first_mix, own_back, resid)
-    told = pl.pallas_call(
-        last_kernel,
-        grid=(1,),
-        in_specs=[whole((16, second)), whole((1, width)), anywhere, anywhere],
-        out_specs=whole((blk_count, 1, width)),
-        out_shape=jax.ShapeDtypeStruct((blk_count, 1, width), jnp.float32),
-        scratch_shapes=[
-            pltpu.VMEM((second // LANES, LANES, width), jnp.bfloat16),
-            pltpu.SemaphoreType.DMA((second // LANES,)),
-        ],
-        compiler_params=params(),
-        name="last",
-    )(last_mix, last_base, oth_back, server)
+    )(first_mix, own_back, resid)
+    last_rows = lax.reduce_precision(jnp.sum(last_parts, axis=0), 8, 7)
+    final = (
+        last_rows
+        * lax.rsqrt(jnp.mean(last_rows * last_rows, axis=-1, keepdims=True) + 1e-05)
+        * final_gain
+    ).astype(jnp.bfloat16)
+    logits = lax.dot_general(
+        final, unembed, (((1,), (1,)), ((), ())), preferred_element_type=jnp.float32
+    )
+    vocab_base = blk * unembed.shape[0]
+    target_hit = (
+        target_ids[:, None] == vocab_base + jnp.arange(unembed.shape[0], dtype=jnp.int32)[None, :]
+    )
+    target_part = jnp.sum(jnp.where(target_hit, logits, 0.0), axis=1)
+    top_part = jnp.max(logits, axis=1)
+
     out_rows, square = pl.pallas_call(
         combine_kernel,
         grid_spec=pltpu.PrefetchScalarGridSpec(
             num_scalar_prefetch=1,
             grid=(width // step,),
-            in_specs=weigh_specs(second) + [column, pl.BlockSpec(memory_space=pl.ANY)],
+            in_specs=weigh_specs(second) + [column, anywhere, anywhere],
             out_specs=[column, whole((1, LANES))],
             scratch_shapes=[pltpu.VMEM((1, step), jnp.float32)],
         ),
@@ -663,26 +735,11 @@
         ],
         compiler_params=params(),
         name="combine",
-    )(info, second_mix, oth_back, base, told)
+    )(info, second_mix, oth_back, base, server, top_part[None])
 
     def everywhere(copies):
         return lax.all_to_all(copies, "blk", split_axis=0, concat_axis=0, tiled=True)
 
-    last_rows = everywhere(told)[:, 0]
-    final = (
-        last_rows
-        * lax.rsqrt(jnp.mean(last_rows * last_rows, axis=-1, keepdims=True) + 1e-05)
-        * final_gain
-    ).astype(jnp.bfloat16)
-    logits = lax.dot_general(
-        final, unembed, (((1,), (1,)), ((), ())), preferred_element_type=jnp.float32
-    )
-    vocab_base = blk * unembed.shape[0]
-    target_hit = (
-        target_ids[:, None] == vocab_base + jnp.arange(unembed.shape[0], dtype=jnp.int32)[None, :]
-    )
-    target_part = jnp.sum(jnp.where(target_hit, logits, 0.0), axis=1)
-    top_part = jnp.max(logits, axis=1)
     prompt = jnp.arange(blk_count, dtype=jnp.int32)
     square_part = jnp.where(prompt == blk, square[0, :blk_count], 0.0)
     stats = jnp.stack([top_part, target_part, square_part])

time: 309 us -> 301 us (0.974)
  starting transfers between devices: 51.2 us -> 40 us
    all_gather x0 -> x1, waiting for transfers between devices: none -> 30.4 us  [paired(): lax.all_gather(last_part, 'blk', axis_index_groups=[list(RING)], axis=0)]
    all_to_all x2, waiting for transfers between devices: 22.8 us -> 0.01 us  [returned(): x = lax.all_to_all(x, 'blk', split_axis=0, concat_axis=0, tiled=True)]
    all_to_all x1 -> x0, starting transfers between devices: 10.7 us -> none  [everywhere(): lax.all_to_all(copies, 'blk', split_axis=0, concat_axis=0, tiled=True)]
    pallas_call x2 -> x1, Pallas kernels: 7.79 us -> 4.08 us  [paired(): pl.pallas_call(first_kernel, grid=(width // step,), in_specs=weigh_specs(...]
  transfers between devices with their start and end apart: 10 -> 10, of which waited for: 7 -> 5; matrix products, arithmetic and copies ran while one was open for 1% -> 3% of each run, Pallas kernels for 20% -> 19%
where the time goes in v13:
time: 301 us; the launch traced here: 298 us
  waiting for transfers between devices  153 us (51%)
  Pallas kernels  66.2 us (22%)
  starting transfers between devices  40 us (13%)
  between operations  13.9 us (5%)
  blocking collectives  9.71 us (3%)
  local copies, waits for them, and re-layouts  7.9 us (3%)
  matrix products  5.18 us (2%)
    all_to_all x3, waiting for transfers between devices, moved(): own = lax.all_to_all(x, 'blk', split_axis=0, concat_axis=0, tiled=True)  66.8 us
    ppermute x2, waiting for transfers between devices, swapped(): return lax.ppermute(x, 'rep', [(0, 1), (1, 0)])  31.9 us
    all_gather x1, waiting for transfers between devices, paired(): lax.all_gather(last_part, 'blk', axis_index_groups=[list(RING)], axis=0)  30.4 us
    all_gather x1, waiting for transfers between devices, paired(): d_both = lax.all_gather(d_own, 'rep', axis=0)  23.5 us
    all_to_all x3, starting transfers between devices, moved(): own = lax.all_to_all(x, 'blk', split_axis=0, concat_axis=0, tiled=True)  22 us
    pallas_call x2, Pallas kernels, hidden_of(): pl.pallas_call(kernel, grid_spec=pltpu.PrefetchScalarGridSpec(num_scalar_...  21.3 us
    all_to_all x2, starting transfers between devices, returned(): x = lax.all_to_all(x, 'blk', split_axis=0, concat_axis=0, tiled=True)  14.7 us
    pallas_call x3, Pallas kernels, turned(): pl.pallas_call(functools.partial(cast_kernel, k * shard_rows * blk_count,...  9.79 us
  transfers between devices with their start and end apart: 10, of which 5 were waited for; matrix products, arithmetic and copies ran while one was open for 3% of the time, Pallas kernels for 19%

profile of v13, /device:TPU:0, one launch (start us, length us, event | category | flops | bytes accessed | tf_op | source)
XLA Modules:
  0.0 298.4 jit_solution(16268214523491531889)
XLA Ops:
  7.2 0.0 all-gather.6.cloned.1.call-start
  7.2 3.0 %prep.1 = (bf16[128,1664]{1,0:T(8,128)(2,1)}, bf16[384,128]{1,0:T(8,128)(2,1)}) custom-call(s32[16]{0:T(128)} %lengths_ref.5, s32[1]{0:T(128)} %bitcast.3.blk_ref, bf16[128,1536]{1,0:T(8,128)(2,1)} %bitcast.46, s32[8,128]{1,0:T(8,128)} %bitcast.53, f32[8,128]{1,0:T(8,128)} %bitcast.54, f32[1536]{0:T(1024)} %gain_ref.1), custom_call_target="tpu_custom_call" | custom-call | tf_op jit(solution)/shard_map/prep/pallas_call | solution.py:531
  10.2 0.0 all-gather.6.cloned.1.call-update
  10.2 3.3 %cast.3 = bf16[16,96,512]{2,1,0:T(8,128)(2,1)} custom-call(f32[4608,512]{1,0:T(8,128)} %bitcast.33, bf16[128,1664]{1,0:T(8,128)(2,1)} %get-tuple-element.20.rank_ref.refs_0_), custom_call_target="tpu_custom_call" | custom-call | tf_op jit(solution)/shard_map/cast/pallas_call | solution.py:499
  13.5 7.4 %all-to-all-start = ((bf16[16,96,512]{2,1,0:T(8,128)(2,1)}), bf16[16,96,512]{2,1,0:T(8,128)(2,1)S(1)}, u32[]{:S(2)}, u32[]{:S(2)}) async-start(bf16[16,96,512]{2,1,0:T(8,128)(2,1)} %cast.3), calls=%async_computation | async-start | bytes 3145728 | tf_op jit(solution)/shard_map/all_to_all | solution.py:515
  20.9 3.3 %cast.4 = bf16[16,96,512]{2,1,0:T(8,128)(2,1)} custom-call(f32[4608,512]{1,0:T(8,128)} %bitcast.34), custom_call_target="tpu_custom_call" | custom-call | tf_op jit(solution)/shard_map/cast/pallas_call | solution.py:499
  24.2 48.8 %all-to-all-done = bf16[16,96,512]{2,1,0:T(8,128)(2,1)S(1)} async-done(((bf16[16,96,512]{2,1,0:T(8,128)(2,1)}), bf16[16,96,512]{2,1,0:T(8,128)(2,1)S(1)}, u32[]{:S(2)}, u32[]{:S(2)}) %all-to-all-start) | async-done | bytes 1572896 | tf_op jit(solution)/shard_map/all_to_all | solution.py:515
  73.0 0.0 copy-start.3
  73.0 6.1 %all-to-all-start.1 = ((bf16[16,96,512]{2,1,0:T(8,128)(2,1)}), bf16[16,96,512]{2,1,0:T(8,128)(2,1)}, u32[]{:S(2)}, u32[]{:S(2)}) async-start(bf16[16,96,512]{2,1,0:T(8,128)(2,1)} %cast.4), calls=%async_computation.1 | async-start | bytes 3145728 | tf_op jit(solution)/shard_map/all_to_all | solution.py:515
  79.1 0.0 copy-done.3
  79.1 1.6 collective-permute-start
  80.7 3.2 %cast.5.__0_ = bf16[16,96,512]{2,1,0:T(8,128)(2,1)} custom-call(f32[4608,512]{1,0:T(8,128)} %bitcast.35), custom_call_target="tpu_custom_call" | custom-call | tf_op jit(solution)/shard_map/cast/pallas_call | solution.py:499
  83.9 31.9 %collective-permute-done.__1_.g_ref.g_oth = bf16[1536,512]{1,0:T(8,128)(2,1)S(1)} collective-permute-done((bf16[1536,512]{1,0:T(8,128)(2,1)S(1)}, bf16[1536,512]{1,0:T(8,128)(2,1)S(1)}, u32[]{:S(2)}, u32[]{:S(2)}) %collective-permute-start) | collective-permute-done | bytes 1572896 | tf_op jit(solution)/shard_map/ppermute | solution.py:519
  115.8 0.0 copy-start.1
  115.8 1.2 copy-done.1
  117.1 0.0 copy-start.8
  117.1 0.0 all-to-all-done.1
  117.1 8.5 %all-to-all-start.2 = ((bf16[16,96,512]{2,1,0:T(8,128)(2,1)}), bf16[16,96,512]{2,1,0:T(8,128)(2,1)S(1)}, u32[]{:S(2)}, u32[]{:S(2)}) async-start(bf16[16,96,512]{2,1,0:T(8,128)(2,1)} %tie.3), calls=%async_computation.2 | async-start | bytes 3145728 | tf_op jit(solution)/shard_map/all_to_all | solution.py:515
  125.6 0.0 all-gather.8.cloned.1.call-start
  125.6 1.5 collective-permute-start.1
  127.2 0.0 copy-done.8
  127.2 0.6 dynamic_slice.3
  127.8 1.3 stack.36.info
  129.1 0.0 all-gather.6.cloned.1.call-done.x_ref
  129.1 10.5 %gate_up.2 = (bf16[592,512]{1,0:T(8,128)(2,1)}, bf16[640,80]{1,0:T(8,128)(2,1)}, f32[16,128]{1,0:T(8,128)}) custom-call(s32[5]{0:T(128)} %stack.36.info, s32[16]{0:T(128)} %lengths_ref.5, s32[16]{0:T(128)} %constant.33.clone.ring_ref, bf16[2048,1664]{1,0:T(8,128)(2,1)} %all-gather.6.cloned.1.call-done.x_ref, bf16[1536,512]{1,0:T(8,128)(2,1)} %bitcast.39, ...), custom_call_target="tpu_custom_call" | custom-call | tf_op jit(solution)/shard_map/gate_up/pallas_call | solution.py:562
  139.5 18.0 %all-to-all-done.2 = bf16[16,96,512]{2,1,0:T(8,128)(2,1)S(1)} async-done(((bf16[16,96,512]{2,1,0:T(8,128)(2,1)}), bf16[16,96,512]{2,1,0:T(8,128)(2,1)S(1)}, u32[]{:S(2)}, u32[]{:S(2)}) %all-to-all-start.2) | async-done | bytes 1572896 | tf_op jit(solution)/shard_map/all_to_all | solution.py:515
  157.6 0.0 copy-start
  157.6 1.1 copy-done
  158.7 0.0 all-gather.8.cloned.1.call-update
  158.7 4.9 %own_down.1 = (bf16[512,1536]{1,0:T(8,128)(2,1)}, bf16[80,1536]{1,0:T(8,128)(2,1)}, f32[16,1536]{1,0:T(8,128)}) custom-call(bf16[592,512]{1,0:T(8,128)(2,1)} %get-tuple-element.23.__1_.hidden_ref, f32[16,128]{1,0:T(8,128)} %get-tuple-element.24.share_ref, bf16[1536,512]{1,0:T(8,128)(2,1)} %tie.4.d_ref), custom_call_target="tpu_custom_call" | custom-call | tf_op jit(solution)/shard_map/own_down/pallas_call | solution.py:607
  163.6 0.0 collective-permute-done.1.__1_.u_ref.u_oth
  163.6 0.0 copy-start.2
  163.6 1.1 copy-done.2
  164.8 9.1 %all-to-all-start.4 = ((bf16[16,32,1536]{2,1,0:T(8,128)(2,1)}), bf16[16,32,1536]{2,1,0:T(8,128)(2,1)S(1)}, u32[]{:S(2)}, u32[]{:S(2)}) async-start(bf16[16,32,1536]{2,1,0:T(8,128)(2,1)} %bitcast.37), calls=%async_computation.4 | async-start | bytes 3145728 | tf_op jit(solution)/shard_map/all_to_all | solution.py:588
  173.9 0.0 all-gather.10.cloned.1.call-start
  173.9 10.8 %gate_up.3 = (bf16[656,512]{1,0:T(8,128)(2,1)}, f32[16,128]{1,0:T(8,128)}, f32[16,1536]{1,0:T(8,128)}) custom-call(s32[5]{0:T(128)} %stack.36.info, s32[16]{0:T(128)} %lengths_ref.5, s32[16]{0:T(128)} %constant.33.clone.ring_ref, bf16[2048,1664]{1,0:T(8,128)(2,1)} %all-gather.6.cloned.1.call-done.x_ref, bf16[1536,512]{1,0:T(8,128)(2,1)} %copy-done.1, ...), custom_call_target="tpu_custom_call" | custom-call | tf_op jit(solution)/shard_map/gate_up/pallas_call | solution.py:562
  184.7 23.5 %all-gather.8.cloned.1.call-done = bf16[3072,512]{1,0:T(8,128)(2,1)} async-done(((bf16[1536,512]{1,0:T(8,128)(2,1)}), bf16[3072,512]{1,0:T(8,128)(2,1)}) %all-gather.8.cloned.1.call-update) | async-done | bytes 3145744 | tf_op jit(solution)/shard_map/all_gather | solution.py:606
  208.2 6.8 %oth_down.1 = (bf16[640,1536]{1,0:T(8,128)(2,1)}, f32[16,1536]{1,0:T(8,128)}) custom-call(s32[5]{0:T(128)} %stack.36.info, bf16[656,512]{1,0:T(8,128)(2,1)} %get-tuple-element.26.hidden_ref, f32[16,128]{1,0:T(8,128)} %get-tuple-element.27.share_ref, bf16[640,80]{1,0:T(8,128)(2,1)} %get-tuple-element.28.spot_ref, ...), custom_call_target="tpu_custom_call" | custom-call | tf_op jit(solution)/shard_map/oth_down/pallas_call | solution.py:634
  215.0 0.0 all-gather.10.cloned.1.call-update
  215.0 0.0 all-to-all-done.4
  215.0 0.0 copy-start.5
  215.1 1.1 copy-done.5
  216.2 5.6 %all-to-all-start.3 = ((bf16[16,40,1536]{2,1,0:T(8,128)(2,1)}), bf16[16,40,1536]{2,1,0:T(8,128)(2,1)S(1)}, u32[]{:S(2)}, u32[]{:S(2)}) async-start(bf16[16,40,1536]{2,1,0:T(8,128)(2,1)} %bitcast.44), calls=%async_computation.3 | async-start | bytes 3932160 | tf_op jit(solution)/shard_map/all_to_all | solution.py:588
  221.8 3.1 %mix.1 = (bf16[384,512]{1,0:T(8,128)(2,1)}, bf16[384,640]{1,0:T(8,128)(2,1)}) custom-call(s32[5]{0:T(128)} %stack.36.info, bf16[128,1664]{1,0:T(8,128)(2,1)} %get-tuple-element.20.rank_ref.refs_0_, bf16[384,128]{1,0:T(8,128)(2,1)} %get-tuple-element.21.pieces_ref), custom_call_target="tpu_custom_call" | custom-call | tf_op jit(solution)/shard_map/mix/pallas_call | solution.py:675
  224.9 4.1 %first.1.base_ref = f32[128,1536]{1,0:T(8,128)} custom-call(bf16[384,512]{1,0:T(8,128)(2,1)} %get-tuple-element.33.mix_ref, bf16[512,1536]{1,0:T(8,128)(2,1)} %bitcast.45, bf16[128,1536]{1,0:T(8,128)(2,1)} %bitcast.48), custom_call_target="tpu_custom_call" | custom-call | tf_op jit(solution)/shard_map/first/pallas_call | solution.py:698
  229.0 8.3 %place.1._ = bf16[3,1536,1024]{2,1,0:T(8,128)(2,1)} custom-call(s32[5]{0:T(128)} %stack.36.info, bf16[1536,512]{1,0:T(8,128)(2,1)} %bitcast.40, bf16[1536,512]{1,0:T(8,128)(2,1)} %copy-done.1, bf16[1536,512]{1,0:T(8,128)(2,1)} %bitcast.11.u_ref.u_own, bf16[1536,512]{1,0:T(8,128)(2,1)} %copy-done.2, bf16[2,1536,512]{2,1,0:T(8,128)(2,1)} %bitcast.42, ...), custom_call_target="tpu_custom_call" | custom-call | tf_op jit(solution)/shard_map/place/pallas_call | solution.py:661
  237.2 0.0 copy-start.6
  237.2 0.0 copy-start.10
  237.2 30.4 %all-gather.10.cloned.1.call-done = f32[256,1536]{1,0:T(8,128)} async-done(((f32[16,1536]{1,0:T(8,128)}), f32[256,1536]{1,0:T(8,128)}) %all-gather.10.cloned.1.call-update) | async-done | bytes 1572880 | tf_op jit(solution)/shard_map/all_gather | solution.py:658
  267.6 1.5 reduce_sum.36
  269.1 0.1 multiply_reduce_fusion
  269.3 0.0 copy-done.6
  269.3 0.0 copy-done.10
  269.3 5.2 %select_reduce_fusion = (f32[16]{0:T(128)S(1)}, f32[16]{0:T(128)}) fusion(s32[2048]{0:T(1024)S(1)} %iota_add_fusion, s32[16]{0:T(128)S(1)} %copy-done.10, bf16[2048,1536]{1,0:T(8,128)(2,1)} %param.16, f32[16,1536]{1,0:T(8,128)S(1)} %reduce_sum.36, f32[1536]{0:T(1024)S(1)} %copy-done.6, f32[16]{0:T(128)S(1)} %add_rsqrt_fusion), kind=kOutput, calls=%fused_computation | convolution fusion | flops 100892640 | bytes 6404352 | tf_op jit(solution)/shard_map/dot_general | solution.py:713
  274.5 0.0 all-to-all-done.3
  274.5 0.0 copy-start.4
  274.5 1.3 copy-done.4
  275.8 0.0 copy-start.7
  275.8 5.1 %combine.1 = (bf16[128,1536]{1,0:T(8,128)(2,1)}, f32[1,128]{1,0:T(1,128)}) custom-call(s32[5]{0:T(128)} %stack.36.info, bf16[384,640]{1,0:T(8,128)(2,1)} %get-tuple-element.22.mix_ref, bf16[640,1536]{1,0:T(8,128)(2,1)} %bitcast.43, f32[128,1536]{1,0:T(8,128)} %first.1.base_ref, bf16[3,1536,1024]{2,1,0:T(8,128)(2,1)} %place.1._, f32[1,16]{1,0:T(1,128)} %bitcast.51), custom_call_target="tpu_custom_call" | custom-call | tf_op jit(solution)/shard_map/combine/pallas_call | solution.py:723
  280.9 0.6 compare_select_fusion
  281.5 0.0 copy-done.7
  281.5 9.7 %all_to_all.30 = f32[16,3,16]{2,1,0:T(4,128)S(1)} all-to-all(f32[16,3,16]{2,1,0:T(4,128)S(1)} %broadcast_in_dim.29), channel_id=1, replica_groups=mesh['blk'=16,'rep'=2] {'blk'}, dimensions={0} | all-to-all | bytes 6144 | tf_op jit(solution)/shard_map/all_to_all | solution.py:741
  291.2 0.0 copy-done.9
  291.3 0.6 pad_maximum_fusion.1
  (13 shorter events, 0.1 us)
Async XLA Ops:
  7.2 121.9 %all-gather.6.cloned.1.call-start = ((), (), s32[]{:S(2)}) async-start(), calls=%async_computation.6 | async-start | bytes 7241728 | tf_op jit(solution)/shard_map/all_gather | solution.py:557
  13.5 59.5 %all-to-all-start = ((bf16[16,96,512]{2,1,0:T(8,128)(2,1)}), bf16[16,96,512]{2,1,0:T(8,128)(2,1)S(1)}, u32[]{:S(2)}, u32[]{:S(2)}) async-start(bf16[16,96,512]{2,1,0:T(8,128)(2,1)} %cast.3), calls=%async_computation | async-start | bytes 3145728 | tf_op jit(solution)/shard_map/all_to_all | solution.py:515
  73.0 6.1 %copy-start.3 = (bf16[16,96,512]{2,1,0:T(8,128)(2,1)}, bf16[16,96,512]{2,1,0:T(8,128)(2,1)S(1)}, u32[]{:S(2)}) copy-start(bf16[16,96,512]{2,1,0:T(8,128)(2,1)S(1)} %all-to-all-done) | copy-start | bytes 4718596
  73.0 44.1 %all-to-all-start.1 = ((bf16[16,96,512]{2,1,0:T(8,128)(2,1)}), bf16[16,96,512]{2,1,0:T(8,128)(2,1)}, u32[]{:S(2)}, u32[]{:S(2)}) async-start(bf16[16,96,512]{2,1,0:T(8,128)(2,1)} %cast.4), calls=%async_computation.1 | async-start | bytes 3145728 | tf_op jit(solution)/shard_map/all_to_all | solution.py:515
  79.1 36.7 %collective-permute-start = (bf16[1536,512]{1,0:T(8,128)(2,1)S(1)}, bf16[1536,512]{1,0:T(8,128)(2,1)S(1)}, u32[]{:S(2)}, u32[]{:S(2)}) collective-permute-start(bf16[1536,512]{1,0:T(8,128)(2,1)S(1)} %bitcast.38), channel_id=1, source_target_pairs={{0,1},{1,0},{2,3},{3,2},{4,5},{5,4},{6,7},{7,6},{8,9},{9,8},{10,11... | collective-permute-start | bytes 4718600 | tf_op jit(solution)/shard_map/ppermute | solution.py:519
  115.8 1.3 copy-start.1
  117.1 10.1 %copy-start.8 = (s32[16]{0:T(128)S(1)}, s32[16]{0:T(128)}, u32[]{:S(2)}) copy-start(s32[16]{0:T(128)} %lengths_ref.5) | copy-start | bytes 196
  117.1 40.5 %all-to-all-start.2 = ((bf16[16,96,512]{2,1,0:T(8,128)(2,1)}), bf16[16,96,512]{2,1,0:T(8,128)(2,1)S(1)}, u32[]{:S(2)}, u32[]{:S(2)}) async-start(bf16[16,96,512]{2,1,0:T(8,128)(2,1)} %tie.3), calls=%async_computation.2 | async-start | bytes 3145728 | tf_op jit(solution)/shard_map/all_to_all | solution.py:515
  125.6 82.6 %all-gather.8.cloned.1.call-start = ((), (), s32[]{:S(2)}) async-start(), calls=%async_computation.7 | async-start | bytes 4718592 | tf_op jit(solution)/shard_map/all_gather | solution.py:606
  125.6 38.0 %collective-permute-start.1 = (bf16[1536,512]{1,0:T(8,128)(2,1)}, bf16[1536,512]{1,0:T(8,128)(2,1)S(1)}, u32[]{:S(2)}, u32[]{:S(2)}) collective-permute-start(bf16[1536,512]{1,0:T(8,128)(2,1)} %bitcast.11.u_ref.u_own), channel_id=1, source_target_pairs={{0,1},{1,0},{2,3},{3,2},{4,5},{5,4},{6,7},{7,6},{8,9},{9,8},{10,11... | collective-permute-start | bytes 4718600 | tf_op jit(solution)/shard_map/ppermute | solution.py:519
  157.6 1.1 copy-start
  163.6 1.1 copy-start.2
  164.8 50.3 %all-to-all-start.4 = ((bf16[16,32,1536]{2,1,0:T(8,128)(2,1)}), bf16[16,32,1536]{2,1,0:T(8,128)(2,1)S(1)}, u32[]{:S(2)}, u32[]{:S(2)}) async-start(bf16[16,32,1536]{2,1,0:T(8,128)(2,1)} %bitcast.37), calls=%async_computation.4 | async-start | bytes 3145728 | tf_op jit(solution)/shard_map/all_to_all | solution.py:588
  173.9 93.8 %all-gather.10.cloned.1.call-start = ((), (), s32[]{:S(2)}) async-start(), calls=%async_computation.8 | async-start | bytes 1671168 | tf_op jit(solution)/shard_map/all_gather | solution.py:658
  215.0 1.1 copy-start.5
  216.2 58.3 %all-to-all-start.3 = ((bf16[16,40,1536]{2,1,0:T(8,128)(2,1)}), bf16[16,40,1536]{2,1,0:T(8,128)(2,1)S(1)}, u32[]{:S(2)}, u32[]{:S(2)}) async-start(bf16[16,40,1536]{2,1,0:T(8,128)(2,1)} %bitcast.44), calls=%async_computation.3 | async-start | bytes 3932160 | tf_op jit(solution)/shard_map/all_to_all | solution.py:588
  237.2 32.1 %copy-start.6 = (f32[1536]{0:T(1024)S(1)}, f32[1536]{0:T(1024)}, u32[]{:S(2)}) copy-start(f32[1536]{0:T(1024)} %param.17) | copy-start | bytes 18436
  237.2 32.1 %copy-start.10 = (s32[16]{0:T(128)S(1)}, s32[16]{0:T(128)}, u32[]{:S(2)}) copy-start(s32[16]{0:T(128)} %param.18) | copy-start | bytes 196
  274.5 1.3 copy-start.4
  275.8 5.7 %copy-start.7 = (f32[16]{0:T(128)S(1)}, f32[16]{0:T(128)}, u32[]{:S(2)}) copy-start(f32[16]{0:T(128)} %get-tuple-element.38) | copy-start | bytes 196
  275.8 15.5 %copy-start.9 = (s32[16]{0:T(128)S(1)}, s32[16]{0:T(128)}, u32[]{:S(2)}) copy-start(s32[16]{0:T(128)} %lengths_ref.5) | copy-start | bytes 196
Sparse Core Ops, SparseCore 0:
  10.4 95.2 all-gather.5
  158.9 49.3 all-gather.7
  215.1 52.4 all-gather.9

commit v14 on v13

--- a/solution.py
+++ b/solution.py
@@ -16,7 +16,7 @@
 GROUPS = 4
 RING = (0, 1, 4, 5, 8, 9, 12, 13, 14, 15, 10, 11, 6, 7, 2, 3)
 LANES = 128
-VMEM = 56 * 1024 * 1024
+VMEM = 62 * 1024 * 1024
 
 
 def merged(x, axis, combine):
@@ -371,7 +371,14 @@
     rows = out_ref.shape[0]
     out_ref[...] = (late + out[:rows]).astype(jnp.bfloat16)
     last = out[rows:].astype(jnp.bfloat16).astype(jnp.float32)
-    sum_ref[...] = base_ref[...] + part_ref[...] + share_ref[:, :1] * last
+    total = base_ref[...] + part_ref[...] + share_ref[:, :1] * last
+    high = total.astype(jnp.bfloat16)
+    low = jnp.where(iota(total.shape, 0) == info[4], total - high.astype(jnp.float32), 0.0)
+    low = jnp.sum(low, axis=0, keepdims=True)
+    count = total.shape[0]
+    sum_ref[:count, :] = high
+    rest = (sum_ref.shape[0] - count, total.shape[1])
+    sum_ref[count:, :] = jnp.where(iota(rest, 0) == 0, low, 0.0).astype(jnp.bfloat16)
 
 
 def mix_kernel(info, rank_ref, pieces_ref, first_ref, second_ref):
@@ -645,17 +652,21 @@
                 part_spec,
                 anywhere,
             ],
-            out_specs=[pl.BlockSpec((second, quarter), lambda i, *_: (0, i)), part_spec],
+            out_specs=[
+                pl.BlockSpec((second, quarter), lambda i, *_: (0, i)),
+                pl.BlockSpec((blk_count + 8, quarter), lambda i, *_: (0, i)),
+            ],
             scratch_shapes=[
                 pltpu.VMEM((4, quarter, FF), jnp.bfloat16),
                 pltpu.SemaphoreType.DMA((4,)),
             ],
         ),
-        out_shape=[bf16(second, width), f32(blk_count, width)],
+        out_shape=[bf16(second, width), bf16(blk_count + 8, width)],
         compiler_params=params(),
         name="oth_down",
     )(info, oth_hidden, oth_share, spot, late_out, base_part, own_part, d_both)
-    last_parts = lax.all_gather(last_part, "blk", axis_index_groups=[list(RING)], axis=0)
+    last_parts = lax.all_gather(last_part, "blk", axis=0).astype(jnp.float32)
+    last_total = jnp.sum(last_parts[:, :blk_count], axis=0) + last_parts[:, blk_count]
     oth_back = returned(oth_out)
 
     server = pl.pallas_call(
@@ -704,7 +715,7 @@
         compiler_params=params(),
         name="first",
     )(first_mix, own_back, resid)
-    last_rows = lax.reduce_precision(jnp.sum(last_parts, axis=0), 8, 7)
+    last_rows = lax.reduce_precision(last_total, 8, 7)
     final = (
         last_rows
         * lax.rsqrt(jnp.mean(last_rows * last_rows, axis=-1, keepdims=True) + 1e-05)

time: 301 us -> 312 us (1.037)
  waiting for transfers between devices: 153 us -> 164 us
    all_gather x1, waiting for transfers between devices: 30.4 us -> 40.1 us  [paired(): last_parts = lax.all_gather(last_part, 'blk', axis=0).astype(jnp.float32)]
    unnamed x22 -> x20, local copies, waits for them, and re-layouts: 5.99 us -> 6.44 us
where the time goes in v14:
time: 312 us; the launch traced here: 311 us
  waiting for transfers between devices  164 us (53%)
  Pallas kernels  66.5 us (21%)
  starting transfers between devices  38.8 us (12%)
  between operations  13.9 us (4%)
  blocking collectives  10.1 us (3%)
  local copies, waits for them, and re-layouts  9.34 us (3%)
  matrix products  5.18 us (2%)
    all_to_all x3, waiting for transfers between devices, moved(): own = lax.all_to_all(x, 'blk', split_axis=0, concat_axis=0, tiled=True)  66.8 us
    all_gather x1, waiting for transfers between devices, paired(): last_parts = lax.all_gather(last_part, 'blk', axis=0).astype(jnp.float32)  40.1 us
    ppermute x2, waiting for transfers between devices, swapped(): return lax.ppermute(x, 'rep', [(0, 1), (1, 0)])  32.1 us
    all_gather x1, waiting for transfers between devices, paired(): d_both = lax.all_gather(d_own, 'rep', axis=0)  24.4 us
    pallas_call x2, Pallas kernels, hidden_of(): pl.pallas_call(kernel, grid_spec=pltpu.PrefetchScalarGridSpec(num_scalar_...  21.5 us
    all_to_all x3, starting transfers between devices, moved(): own = lax.all_to_all(x, 'blk', split_axis=0, concat_axis=0, tiled=True)  20.7 us
    all_to_all x2, starting transfers between devices, returned(): x = lax.all_to_all(x, 'blk', split_axis=0, concat_axis=0, tiled=True)  14.7 us
    all_to_all x1, blocking collectives, everywhere(): lax.all_to_all(copies, 'blk', split_axis=0, concat_axis=0, tiled=True)  10.1 us
  transfers between devices with their start and end apart: 10, of which 5 were waited for; matrix products, arithmetic and copies ran while one was open for 3% of the time, Pallas kernels for 19%

profile of v14, /device:TPU:0, one launch (start us, length us, event | category | flops | bytes accessed | tf_op | source)
XLA Modules:
  0.0 310.9 jit_solution(1616866247633532778)
XLA Ops:
  7.2 0.0 all-gather.6.cloned.1.call-start
  7.2 3.0 prep.1
  10.2 0.0 all-gather.6.cloned.1.call-update
  10.3 3.2 %cast.3 = bf16[16,96,512]{2,1,0:T(8,128)(2,1)} custom-call(f32[4608,512]{1,0:T(8,128)} %bitcast.45, bf16[128,1664]{1,0:T(8,128)(2,1)} %get-tuple-element.20.rank_ref.refs_0_), custom_call_target="tpu_custom_call" | custom-call | tf_op jit(solution)/shard_map/cast/pallas_call | solution.py:506
  13.5 7.4 %all-to-all-start = ((bf16[16,96,512]{2,1,0:T(8,128)(2,1)}), bf16[16,96,512]{2,1,0:T(8,128)(2,1)S(1)}, u32[]{:S(2)}, u32[]{:S(2)}) async-start(bf16[16,96,512]{2,1,0:T(8,128)(2,1)} %cast.3), calls=%async_computation | async-start | bytes 3145728 | tf_op jit(solution)/shard_map/all_to_all | solution.py:522
  20.9 3.3 %cast.4 = bf16[16,96,512]{2,1,0:T(8,128)(2,1)} custom-call(f32[4608,512]{1,0:T(8,128)} %bitcast.46), custom_call_target="tpu_custom_call" | custom-call | tf_op jit(solution)/shard_map/cast/pallas_call | solution.py:506
  24.2 48.8 %all-to-all-done = bf16[16,96,512]{2,1,0:T(8,128)(2,1)S(1)} async-done(((bf16[16,96,512]{2,1,0:T(8,128)(2,1)}), bf16[16,96,512]{2,1,0:T(8,128)(2,1)S(1)}, u32[]{:S(2)}, u32[]{:S(2)}) %all-to-all-start) | async-done | bytes 1572896 | tf_op jit(solution)/shard_map/all_to_all | solution.py:522
  73.0 0.0 copy-start.2
  73.0 1.3 copy-done.2
  74.3 6.1 %all-to-all-start.1 = ((bf16[16,96,512]{2,1,0:T(8,128)(2,1)}), bf16[16,96,512]{2,1,0:T(8,128)(2,1)}, u32[]{:S(2)}, u32[]{:S(2)}) async-start(bf16[16,96,512]{2,1,0:T(8,128)(2,1)} %cast.4), calls=%async_computation.1 | async-start | bytes 3145728 | tf_op jit(solution)/shard_map/all_to_all | solution.py:522
  80.4 1.5 collective-permute-start
  81.9 3.2 %cast.5.__0_ = bf16[16,96,512]{2,1,0:T(8,128)(2,1)} custom-call(f32[4608,512]{1,0:T(8,128)} %bitcast.47), custom_call_target="tpu_custom_call" | custom-call | tf_op jit(solution)/shard_map/cast/pallas_call | solution.py:506
  85.2 32.1 %collective-permute-done.__1_.g_ref.g_oth = bf16[1536,512]{1,0:T(8,128)(2,1)S(1)} collective-permute-done((bf16[1536,512]{1,0:T(8,128)(2,1)}, bf16[1536,512]{1,0:T(8,128)(2,1)S(1)}, u32[]{:S(2)}, u32[]{:S(2)}) %collective-permute-start) | collective-permute-done | bytes 1572896 | tf_op jit(solution)/shard_map/ppermute | solution.py:526
  117.2 0.0 copy-start.1
  117.2 1.1 copy-done.1
  118.4 0.0 copy-start.7
  118.4 0.0 all-to-all-done.1
  118.4 7.2 %all-to-all-start.2 = ((bf16[16,96,512]{2,1,0:T(8,128)(2,1)}), bf16[16,96,512]{2,1,0:T(8,128)(2,1)S(1)}, u32[]{:S(2)}, u32[]{:S(2)}) async-start(bf16[16,96,512]{2,1,0:T(8,128)(2,1)} %tie.3), calls=%async_computation.2 | async-start | bytes 3145728 | tf_op jit(solution)/shard_map/all_to_all | solution.py:522
  125.6 0.0 all-gather.8.cloned.1.call-start
  125.7 1.5 collective-permute-start.1
  127.2 0.0 copy-done.7
  127.2 0.6 dynamic_slice.3
  127.8 1.2 stack.36.info
  129.0 0.0 all-gather.6.cloned.1.call-done.x_ref
  129.0 10.5 %gate_up.2 = (bf16[592,512]{1,0:T(8,128)(2,1)}, bf16[640,80]{1,0:T(8,128)(2,1)}, f32[16,128]{1,0:T(8,128)}) custom-call(s32[5]{0:T(128)} %stack.36.info, s32[16]{0:T(128)} %lengths_ref.5, s32[16]{0:T(128)} %constant.33.clone.ring_ref, bf16[2048,1664]{1,0:T(8,128)(2,1)} %all-gather.6.cloned.1.call-done.x_ref, bf16[1536,512]{1,0:T(8,128)(2,1)} %bitcast.51, ...), custom_call_target="tpu_custom_call" | custom-call | tf_op jit(solution)/shard_map/gate_up/pallas_call | solution.py:569
  139.5 18.1 %all-to-all-done.2 = bf16[16,96,512]{2,1,0:T(8,128)(2,1)S(1)} async-done(((bf16[16,96,512]{2,1,0:T(8,128)(2,1)}), bf16[16,96,512]{2,1,0:T(8,128)(2,1)S(1)}, u32[]{:S(2)}, u32[]{:S(2)}) %all-to-all-start.2) | async-done | bytes 1572896 | tf_op jit(solution)/shard_map/all_to_all | solution.py:522
  157.6 0.0 copy-start
  157.6 1.1 copy-done
  158.7 0.0 all-gather.8.cloned.1.call-update
  158.8 4.9 %own_down.1 = (bf16[512,1536]{1,0:T(8,128)(2,1)}, bf16[80,1536]{1,0:T(8,128)(2,1)}, f32[16,1536]{1,0:T(8,128)}) custom-call(bf16[592,512]{1,0:T(8,128)(2,1)} %get-tuple-element.23.__1_.hidden_ref, f32[16,128]{1,0:T(8,128)} %get-tuple-element.24.share_ref, bf16[1536,512]{1,0:T(8,128)(2,1)} %tie.4.d_ref), custom_call_target="tpu_custom_call" | custom-call | tf_op jit(solution)/shard_map/own_down/pallas_call | solution.py:614
  163.6 0.0 collective-permute-done.1.__1_.u_ref.u_oth
  163.7 9.1 %all-to-all-start.4 = ((bf16[16,32,1536]{2,1,0:T(8,128)(2,1)}), bf16[16,32,1536]{2,1,0:T(8,128)(2,1)S(1)}, u32[]{:S(2)}, u32[]{:S(2)}) async-start(bf16[16,32,1536]{2,1,0:T(8,128)(2,1)} %bitcast.49), calls=%async_computation.4 | async-start | bytes 3145728 | tf_op jit(solution)/shard_map/all_to_all | solution.py:595
  172.8 11.0 %gate_up.3 = (bf16[656,512]{1,0:T(8,128)(2,1)}, f32[16,128]{1,0:T(8,128)}, f32[16,1536]{1,0:T(8,128)}) custom-call(s32[5]{0:T(128)} %stack.36.info, s32[16]{0:T(128)} %lengths_ref.5, s32[16]{0:T(128)} %constant.33.clone.ring_ref, bf16[2048,1664]{1,0:T(8,128)(2,1)} %all-gather.6.cloned.1.call-done.x_ref, bf16[1536,512]{1,0:T(8,128)(2,1)} %copy-done.1, ...), custom_call_target="tpu_custom_call" | custom-call | tf_op jit(solution)/shard_map/gate_up/pallas_call | solution.py:569
  183.8 24.4 %all-gather.8.cloned.1.call-done = bf16[3072,512]{1,0:T(8,128)(2,1)} async-done(((bf16[1536,512]{1,0:T(8,128)(2,1)}), bf16[3072,512]{1,0:T(8,128)(2,1)}) %all-gather.8.cloned.1.call-update) | async-done | bytes 3145744 | tf_op jit(solution)/shard_map/all_gather | solution.py:613
  208.2 6.8 %oth_down.1 = (bf16[640,1536]{1,0:T(8,128)(2,1)}, bf16[24,1536]{1,0:T(8,128)(2,1)}) custom-call(s32[5]{0:T(128)} %stack.36.info, bf16[656,512]{1,0:T(8,128)(2,1)} %get-tuple-element.26.hidden_ref, f32[16,128]{1,0:T(8,128)} %get-tuple-element.27.share_ref, bf16[640,80]{1,0:T(8,128)(2,1)} %get-tuple-element.28.spot_ref, ...), custom_call_target="tpu_custom_call" | custom-call | tf_op jit(solution)/shard_map/oth_down/pallas_call | solution.py:641
  215.1 0.0 all-to-all-done.4
  215.1 0.0 copy-start.4
  215.1 1.1 copy-done.4
  216.2 5.6 %all-to-all-start.3 = ((bf16[16,40,1536]{2,1,0:T(8,128)(2,1)}), bf16[16,40,1536]{2,1,0:T(8,128)(2,1)S(1)}, u32[]{:S(2)}, u32[]{:S(2)}) async-start(bf16[16,40,1536]{2,1,0:T(8,128)(2,1)} %bitcast.56), calls=%async_computation.3 | async-start | bytes 3932160 | tf_op jit(solution)/shard_map/all_to_all | solution.py:595
  221.9 0.2 all-gather.10.cloned.1.call-start
  222.1 0.5 all-gather.10.cloned.1.call-update
  222.6 3.0 mix.1
  225.6 4.1 %first.1.base_ref = f32[128,1536]{1,0:T(8,128)} custom-call(bf16[384,512]{1,0:T(8,128)(2,1)} %get-tuple-element.33.mix_ref, bf16[512,1536]{1,0:T(8,128)(2,1)} %bitcast.57, bf16[128,1536]{1,0:T(8,128)(2,1)} %bitcast.60), custom_call_target="tpu_custom_call" | custom-call | tf_op jit(solution)/shard_map/first/pallas_call | solution.py:709
  229.7 8.3 %place.1._ = bf16[3,1536,1024]{2,1,0:T(8,128)(2,1)} custom-call(s32[5]{0:T(128)} %stack.36.info, bf16[1536,512]{1,0:T(8,128)(2,1)} %bitcast.52, bf16[1536,512]{1,0:T(8,128)(2,1)} %copy-done.1, bf16[1536,512]{1,0:T(8,128)(2,1)} %bitcast.11.u_ref.u_own, bf16[1536,512]{1,0:T(8,128)(2,1)} %collective-permute-done.1.__1_.u_ref.u_oth, ...), custom_call_target="tpu_custom_call" | custom-call | tf_op jit(solution)/shard_map/place/pallas_call | solution.py:672
  238.0 40.1 %all-gather.10.cloned.1.call-done = bf16[384,1536]{1,0:T(8,128)(2,1)} async-done(((bf16[24,1536]{1,0:T(8,128)(2,1)}), bf16[384,1536]{1,0:T(8,128)(2,1)}) %all-gather.10.cloned.1.call-update) | async-done | bytes 1179664 | tf_op jit(solution)/shard_map/all_gather | solution.py:668
  278.1 1.0 slice.29
  279.1 1.5 convert
  280.7 0.0 copy-start.5
  280.7 0.0 copy-start.9
  280.7 0.1 slice_reduce_fusion
  280.8 0.1 multiply_reduce_fusion
  280.9 0.5 copy-done.5
  281.4 0.0 copy-done.9
  281.4 5.2 %select_reduce_fusion = (f32[16]{0:T(128)S(1)}, f32[16]{0:T(128)}) fusion(s32[2048]{0:T(1024)S(1)} %iota_add_fusion, s32[16]{0:T(128)S(1)} %copy-done.9, bf16[2048,1536]{1,0:T(8,128)(2,1)} %param.16, f32[1536]{0:T(1024)S(1)} %copy-done.5, f32[16]{0:T(128)S(1)} %add_rsqrt_fusion, f32[16,1536]{1,0:T(8,128)S(1)} %slice_reduce_fusion, f32[16,1,1536]{2,1,0:T(1,128)S(1)} %slice.29), kind=kOutput, calls=%fused_computation.1 | convolution fusion | flops 100917216 | bytes 6502656 | tf_op jit(solution)/shard_map/dot_general | solution.py:724
  286.5 0.0 all-to-all-done.3
  286.5 0.0 copy-start.3
  286.5 1.3 copy-done.3
  287.8 0.0 copy-start.6
  287.8 5.1 %combine.1 = (bf16[128,1536]{1,0:T(8,128)(2,1)}, f32[1,128]{1,0:T(1,128)}) custom-call(s32[5]{0:T(128)} %stack.36.info, bf16[384,640]{1,0:T(8,128)(2,1)} %get-tuple-element.22.mix_ref, bf16[640,1536]{1,0:T(8,128)(2,1)} %bitcast.55, f32[128,1536]{1,0:T(8,128)} %first.1.base_ref, bf16[3,1536,1024]{2,1,0:T(8,128)(2,1)} %place.1._, f32[1,16]{1,0:T(1,128)} %bitcast.64), custom_call_target="tpu_custom_call" | custom-call | tf_op jit(solution)/shard_map/combine/pallas_call | solution.py:734
  292.9 0.6 compare_select_fusion
  293.6 0.0 copy-done.6
  293.6 10.1 %all_to_all.30 = f32[16,3,16]{2,1,0:T(4,128)S(1)} all-to-all(f32[16,3,16]{2,1,0:T(4,128)S(1)} %broadcast_in_dim.29), channel_id=1, replica_groups=mesh['blk'=16,'rep'=2] {'blk'}, dimensions={0} | all-to-all | bytes 6144 | tf_op jit(solution)/shard_map/all_to_all | solution.py:752
  303.7 0.0 copy-done.8
  303.8 0.6 pad_maximum_fusion.1
  (13 shorter events, 0.1 us)
Async XLA Ops:
  7.2 121.9 %all-gather.6.cloned.1.call-start = ((), (), s32[]{:S(2)}) async-start(), calls=%async_computation.6 | async-start | bytes 7241728 | tf_op jit(solution)/shard_map/all_gather | solution.py:564
  13.5 59.5 %all-to-all-start = ((bf16[16,96,512]{2,1,0:T(8,128)(2,1)}), bf16[16,96,512]{2,1,0:T(8,128)(2,1)S(1)}, u32[]{:S(2)}, u32[]{:S(2)}) async-start(bf16[16,96,512]{2,1,0:T(8,128)(2,1)} %cast.3), calls=%async_computation | async-start | bytes 3145728 | tf_op jit(solution)/shard_map/all_to_all | solution.py:522
  73.0 1.3 copy-start.2
  74.3 44.1 %all-to-all-start.1 = ((bf16[16,96,512]{2,1,0:T(8,128)(2,1)}), bf16[16,96,512]{2,1,0:T(8,128)(2,1)}, u32[]{:S(2)}, u32[]{:S(2)}) async-start(bf16[16,96,512]{2,1,0:T(8,128)(2,1)} %cast.4), calls=%async_computation.1 | async-start | bytes 3145728 | tf_op jit(solution)/shard_map/all_to_all | solution.py:522
  80.4 36.9 %collective-permute-start = (bf16[1536,512]{1,0:T(8,128)(2,1)}, bf16[1536,512]{1,0:T(8,128)(2,1)S(1)}, u32[]{:S(2)}, u32[]{:S(2)}) collective-permute-start(bf16[1536,512]{1,0:T(8,128)(2,1)} %bitcast.50), channel_id=1, source_target_pairs={{0,1},{1,0},{2,3},{3,2},{4,5},{5,4},{6,7},{7,6},{8,9},{9,8},{10,11... | collective-permute-start | bytes 4718600 | tf_op jit(solution)/shard_map/ppermute | solution.py:526
  117.2 1.1 copy-start.1
  118.4 8.8 %copy-start.7 = (s32[16]{0:T(128)S(1)}, s32[16]{0:T(128)}, u32[]{:S(2)}) copy-start(s32[16]{0:T(128)} %lengths_ref.5) | copy-start | bytes 196
  118.4 39.2 %all-to-all-start.2 = ((bf16[16,96,512]{2,1,0:T(8,128)(2,1)}), bf16[16,96,512]{2,1,0:T(8,128)(2,1)S(1)}, u32[]{:S(2)}, u32[]{:S(2)}) async-start(bf16[16,96,512]{2,1,0:T(8,128)(2,1)} %tie.3), calls=%async_computation.2 | async-start | bytes 3145728 | tf_op jit(solution)/shard_map/all_to_all | solution.py:522
  125.6 82.6 %all-gather.8.cloned.1.call-start = ((), (), s32[]{:S(2)}) async-start(), calls=%async_computation.7 | async-start | bytes 4718592 | tf_op jit(solution)/shard_map/all_gather | solution.py:613
  125.7 38.0 %collective-permute-start.1 = (bf16[1536,512]{1,0:T(8,128)(2,1)}, bf16[1536,512]{1,0:T(8,128)(2,1)}, u32[]{:S(2)}, u32[]{:S(2)}) collective-permute-start(bf16[1536,512]{1,0:T(8,128)(2,1)} %bitcast.11.u_ref.u_own), channel_id=1, source_target_pairs={{0,1},{1,0},{2,3},{3,2},{4,5},{5,4},{6,7},{7,6},{8,9},{9,8},{10,11... | collective-permute-start | bytes 4718600 | tf_op jit(solution)/shard_map/ppermute | solution.py:526
  157.6 1.1 copy-start
  163.7 51.4 %all-to-all-start.4 = ((bf16[16,32,1536]{2,1,0:T(8,128)(2,1)}), bf16[16,32,1536]{2,1,0:T(8,128)(2,1)S(1)}, u32[]{:S(2)}, u32[]{:S(2)}) async-start(bf16[16,32,1536]{2,1,0:T(8,128)(2,1)} %bitcast.49), calls=%async_computation.4 | async-start | bytes 3145728 | tf_op jit(solution)/shard_map/all_to_all | solution.py:595
  215.1 1.1 copy-start.4
  216.2 70.3 %all-to-all-start.3 = ((bf16[16,40,1536]{2,1,0:T(8,128)(2,1)}), bf16[16,40,1536]{2,1,0:T(8,128)(2,1)S(1)}, u32[]{:S(2)}, u32[]{:S(2)}) async-start(bf16[16,40,1536]{2,1,0:T(8,128)(2,1)} %bitcast.56), calls=%async_computation.3 | async-start | bytes 3932160 | tf_op jit(solution)/shard_map/all_to_all | solution.py:595
  221.9 56.2 %all-gather.10.cloned.1.call-start = ((), (), s32[]{:S(2)}) async-start(), calls=%async_computation.8 | async-start | bytes 1253376 | tf_op jit(solution)/shard_map/all_gather | solution.py:668
  280.7 0.7 copy-start.5
  280.7 0.7 copy-start.9
  286.5 1.3 copy-start.3
  287.8 5.7 %copy-start.6 = (f32[16]{0:T(128)S(1)}, f32[16]{0:T(128)}, u32[]{:S(2)}) copy-start(f32[16]{0:T(128)} %get-tuple-element.38) | copy-start | bytes 196
  287.8 15.9 %copy-start.8 = (s32[16]{0:T(128)S(1)}, s32[16]{0:T(128)}, u32[]{:S(2)}) copy-start(s32[16]{0:T(128)} %lengths_ref.5) | copy-start | bytes 196
Sparse Core Ops, SparseCore 0:
  10.4 89.0 all-gather.5
  158.9 49.3 all-gather.7
  225.0 53.0 all-gather.9

commit v15 on v13

--- a/solution.py
+++ b/solution.py
@@ -262,7 +262,10 @@
 
     @pl.when(step == GROUPS - 1)
     def _():
-        picked[all_rows:, :] = lasts[:, :width]
+        count = lasts.shape[0]
+        picked[all_rows : all_rows + count, :] = lasts[:, :width]
+        blank = picked.shape[0] - all_rows - count
+        picked[all_rows + count :, :] = jnp.zeros((blank, width), jnp.float32)
         out_ref[...] = activ(picked[...], g_ref, u_ref)
         share_ref[...] = share_of(info, 0, lasts, width)
         column = iota(spot_ref.shape, 1)
@@ -319,59 +322,102 @@
     )
 
 
-def fetched(sources, held, sems):
-    step = pl.program_id(0)
-    rows = held.shape[1]
-
-    @pl.when(step == 0)
-    def _():
-        for k, source in enumerate(sources):
-            pltpu.make_async_copy(source, held.at[k], sems.at[k]).start()
-
-    for k, source in enumerate(sources):
-
-        @pl.when(step == k)
-        def _():
-            pltpu.make_async_copy(source, held.at[k], sems.at[k]).wait()
-
-    return held[step]
-
-
-def own_down_kernel(hidden_ref, share_ref, d_ref, out_ref, late_ref, part_ref, held, sems):
-    size = held.shape[1]
-    d = fetched([d_ref.at[k * size : (k + 1) * size] for k in range(held.shape[0])], held, sems)
-    out = matmul_nt(hidden_ref, d).astype(jnp.bfloat16)
-    rows = out_ref.shape[0]
-    out_ref[...] = out[:rows]
-    late_ref[...] = out[rows:]
-    count = part_ref.shape[0]
-    part_ref[...] = share_ref[:, :1] * out[-count:].astype(jnp.float32)
+def started(copies):
+    for copy in copies:
+        copy.start()
+    return copies
+
+
+def waited(copies):
+    for copy in copies:
+        copy.wait()
+
+
+def own_down_kernel(
+    hidden_any, share_any, d_any, out_any, late_any, part_any, hidden, share, d, out, part, sems
+):
+    chunks, size = d.shape[:2]
+    rows, count = out_any.shape[0], part.shape[1]
+    at = rows + count * (CAP - FIRST)
+    copy = pltpu.make_async_copy
+    first = started(
+        [copy(hidden_any, hidden, sems.at[0, 0]), copy(share_any, share, sems.at[0, 1])]
+    )
+    downs = started(
+        [
+            copy(d_any.at[k * size : (k + 1) * size], d.at[k], sems.at[1, k])
+            for k in range(chunks)
+        ]
+    )
+    waited(first)
+    stores = []
+    for k in range(chunks):
+        downs[k].wait()
+        out[k] = matmul_nt(hidden, d[k]).astype(jnp.bfloat16)
+        part[k] = share[:, :1] * out[k, at : at + count].astype(jnp.float32)
+        columns = slice(k * size, (k + 1) * size)
+        stores += started(
+            [
+                copy(out.at[k, :rows], out_any.at[:, columns], sems.at[2, k]),
+                copy(out.at[k, rows:], late_any.at[:, columns], sems.at[3, k]),
+                copy(part.at[k], part_any.at[:, columns], sems.at[4, k]),
+            ]
+        )
+    waited(stores)
 
 
 def oth_down_kernel(
     info,
-    hidden_ref,
-    share_ref,
-    spot_ref,
-    late_ref,
-    base_ref,
-    part_ref,
-    d_ref,
-    out_ref,
-    sum_ref,
-    held,
+    hidden_any,
+    share_any,
+    spot_any,
+    late_any,
+    base_any,
+    part_any,
+    d_any,
+    out_any,
+    sum_any,
+    hidden,
+    share,
+    spot,
+    late,
+    base,
+    part,
+    d,
+    out,
+    total,
     sems,
 ):
-    size = held.shape[1]
+    chunks, size = d.shape[:2]
+    rows = out_any.shape[0]
+    copy = pltpu.make_async_copy
     other = 1 - info[2]
-    sources = [d_ref.at[other, k * size : (k + 1) * size] for k in range(held.shape[0])]
-    d = fetched(sources, held, sems)
-    late = jnp.dot(spot_ref[...], late_ref[...], preferred_element_type=jnp.float32)
-    out = matmul_nt(hidden_ref, d)
-    rows = out_ref.shape[0]
-    out_ref[...] = (late + out[:rows]).astype(jnp.bfloat16)
-    last = out[rows:].astype(jnp.bfloat16).astype(jnp.float32)
-    sum_ref[...] = base_ref[...] + part_ref[...] + share_ref[:, :1] * last
+    sources = (hidden_any, share_any, spot_any, late_any, base_any, part_any)
+    targets = (hidden, share, spot, late, base, part)
+    downs = started(
+        [
+            copy(d_any.at[other, k * size : (k + 1) * size], d.at[k], sems.at[1, k])
+            for k in range(chunks)
+        ]
+    )
+    first = started([copy(x, y, sems.at[0, k]) for k, (x, y) in enumerate(zip(sources, targets))])
+    waited(first)
+    stores = []
+    for k in range(chunks):
+        downs[k].wait()
+        columns = slice(k * size, (k + 1) * size)
+        placed = jnp.dot(spot[...], late[:, columns], preferred_element_type=jnp.float32)
+        value = matmul_nt(hidden, d[k])
+        out[k] = (placed + value[:rows]).astype(jnp.bfloat16)
+        last = value[rows:].astype(jnp.bfloat16).astype(jnp.float32)
+        total[k] = base[:, columns] + part[:, columns] + share[:, :1] * last
+        stores += started(
+            [
+                copy(total.at[k], sum_any.at[:, columns], sems.at[3, k]),
+                copy(out.at[k], out_any.at[:, columns], sems.at[2, k]),
+            ]
+        )
+    waited(stores)
 
 
 def mix_kernel(info, rank_ref, pieces_ref, first_ref, second_ref):
@@ -413,23 +459,34 @@
     base_ref[...] = resid_ref[...].astype(jnp.float32) + weigh(mix_ref, back_ref)
 
 
-def combine_kernel(info, mix_ref, back_ref, base_ref, _, __, out_ref, square_ref, squares):
-    step = pl.program_id(0)
-
-    @pl.when(step == 0)
-    def _():
-        squares[...] = jnp.zeros_like(squares)
-
-    out = (base_ref[...] + weigh(mix_ref, back_ref)).astype(jnp.bfloat16)
+def combine_kernel(
+    info, mix_any, back_any, base_any, _, __, out_ref, square_ref, mix, back, base, sems
+):
+    chunks, size = back.shape[:2]
+    rows = base.shape[0]
+    copy = pltpu.make_async_copy
+    first = started([copy(mix_any, mix, sems.at[chunks])])
+    backs = started(
+        [copy(back_any.at[k * size : (k + 1) * size], back.at[k], sems.at[k]) for k in range(chunks)]
+    )
+    late = started([copy(base_any, base, sems.at[chunks + 1])])
+    waited(first)
+    parts = jnp.zeros((mix.shape[0], base.shape[1]), jnp.float32)
+    for k in range(chunks):
+        backs[k].wait()
+        parts = parts + jnp.dot(
+            mix[:, k * size : (k + 1) * size], back[k], preferred_element_type=jnp.float32
+        )
+    waited(late)
+    moe = parts[2 * rows :] + parts[rows : 2 * rows] + parts[:rows]
+    out = (base[...] + moe).astype(jnp.bfloat16)
     out_ref[...] = out
     out_f = out.astype(jnp.float32)
     row = iota(out_f.shape, 0)
-    squares[...] += jnp.sum(jnp.where(row < info[3], out_f * out_f, 0.0), axis=0, keepdims=True)
-
-    @pl.when(step == pl.num_programs(0) - 1)
-    def _():
-        total = jnp.sum(squares[...], axis=1, keepdims=True)
-        square_ref[...] = jnp.broadcast_to(total, square_ref.shape)
+    total = jnp.sum(jnp.where(row < info[3], out_f * out_f, 0.0), axis=0, keepdims=True)
+    square_ref[...] = jnp.broadcast_to(
+        jnp.sum(total, axis=1, keepdims=True), square_ref.shape
+    )
 
 
 def place_kernel(info, g_own, g_oth, u_own, u_oth, d_both, _, out_ref):
@@ -594,7 +651,7 @@
     def f32(*shape):
         return jax.ShapeDtypeStruct(shape, jnp.float32)
 
-    extra = blk_count * (CAP - FIRST) + blk_count
+    extra = LANES
     own_hidden, spot, own_share = hidden_of(
         own_kernel,
         [bf16(first + extra, FF), bf16(second, extra), f32(blk_count, LANES)],
@@ -606,19 +663,18 @@
     d_both = lax.all_gather(d_own, "rep", axis=0)
     own_out, late_out, own_part = pl.pallas_call(
         own_down_kernel,
-        grid=(width // step,),
-        in_specs=[whole((first + extra, FF)), whole((blk_count, LANES)), anywhere],
-        out_specs=[
-            pl.BlockSpec((first, step), lambda i: (0, i)),
-            pl.BlockSpec((extra, step), lambda i: (0, i)),
-            pl.BlockSpec((blk_count, step), lambda i: (0, i)),
-        ],
+        in_specs=[anywhere] * 3,
+        out_specs=[anywhere] * 3,
         out_shape=[bf16(first, width), bf16(extra, width), f32(blk_count, width)],
         scratch_shapes=[
-            pltpu.VMEM((width // step, step, FF), jnp.bfloat16),
-            pltpu.SemaphoreType.DMA((width // step,)),
+            pltpu.VMEM((first + extra, FF), jnp.bfloat16),
+            pltpu.VMEM((blk_count, LANES), jnp.float32),
+            pltpu.VMEM((4, quarter, FF), jnp.bfloat16),
+            pltpu.VMEM((4, first + extra, quarter), jnp.bfloat16),
+            pltpu.VMEM((4, blk_count, quarter), jnp.float32),
+            pltpu.SemaphoreType.DMA((5, 4)),
         ],
-        compiler_params=params(),
+        compiler_params=pltpu.CompilerParams(vmem_limit_bytes=VMEM),
         name="own_down",
     )(own_hidden, own_share, d_own)
     own_out = tied(own_out, u_oth)
@@ -630,25 +686,24 @@
         (g_oth, u_oth, resid, own_out),
         [whole((rows, width)), anywhere],
     )
-    part_spec = pl.BlockSpec((blk_count, quarter), lambda i, *_: (0, i))
     oth_out, last_part = pl.pallas_call(
         oth_down_kernel,
         grid_spec=pltpu.PrefetchScalarGridSpec(
             num_scalar_prefetch=1,
-            grid=(4,),
-            in_specs=[
-                whole((second + blk_count, FF)),
-                whole((blk_count, LANES)),
-                whole((second, extra)),
-                pl.BlockSpec((extra, quarter), lambda i, *_: (0, i)),
-                part_spec,
-                part_spec,
-                anywhere,
-            ],
-            out_specs=[pl.BlockSpec((second, quarter), lambda i, *_: (0, i)), part_spec],
+            grid=(1,),
+            in_specs=[anywhere] * 7,
+            out_specs=[anywhere] * 2,
             scratch_shapes=[
+                pltpu.VMEM((second + blk_count, FF), jnp.bfloat16),
+                pltpu.VMEM((blk_count, LANES), jnp.float32),
+                pltpu.VMEM((second, extra), jnp.bfloat16),
+                pltpu.VMEM((extra, width), jnp.bfloat16),
+                pltpu.VMEM((blk_count, width), jnp.float32),
+                pltpu.VMEM((blk_count, width), jnp.float32),
                 pltpu.VMEM((4, quarter, FF), jnp.bfloat16),
-                pltpu.SemaphoreType.DMA((4,)),
+                pltpu.VMEM((4, second, quarter), jnp.bfloat16),
+                pltpu.VMEM((4, blk_count, quarter), jnp.float32),
+                pltpu.SemaphoreType.DMA((4, 6)),
             ],
         ),
         out_shape=[bf16(second, width), f32(blk_count, width)],
@@ -724,15 +779,17 @@
         combine_kernel,
         grid_spec=pltpu.PrefetchScalarGridSpec(
             num_scalar_prefetch=1,
-            grid=(width // step,),
-            in_specs=weigh_specs(second) + [column, anywhere, anywhere],
-            out_specs=[column, whole((1, LANES))],
-            scratch_shapes=[pltpu.VMEM((1, step), jnp.float32)],
+            grid=(1,),
+            in_specs=[anywhere] * 5,
+            out_specs=[whole((rows, width)), whole((1, LANES))],
+            scratch_shapes=[
+                pltpu.VMEM((3 * rows, second), jnp.bfloat16),
+                pltpu.VMEM((second // LANES, LANES, width), jnp.bfloat16),
+                pltpu.VMEM((rows, width), jnp.float32),
+                pltpu.SemaphoreType.DMA((second // LANES + 2,)),
+            ],
         ),
-        out_shape=[
-            jax.ShapeDtypeStruct((rows, width), jnp.bfloat16),
-            jax.ShapeDtypeStruct((1, LANES), jnp.float32),
-        ],
+        out_shape=[bf16(rows, width), f32(1, LANES)],
         compiler_params=params(),
         name="combine",
     )(info, second_mix, oth_back, base, server, top_part[None])

time: 301 us -> 299 us (level)
  no operation moved by 1% of the time
where the time goes in v15:
time: 299 us; the launch traced here: 298 us
  waiting for transfers between devices  153 us (51%)
  Pallas kernels  65 us (22%)
  starting transfers between devices  40.1 us (13%)
  between operations  13.9 us (5%)
  blocking collectives  9.9 us (3%)
  local copies, waits for them, and re-layouts  7.9 us (3%)
  matrix products  5.18 us (2%)
    all_to_all x3, waiting for transfers between devices, moved(): own = lax.all_to_all(x, 'blk', split_axis=0, concat_axis=0, tiled=True)  66.7 us
    ppermute x2, waiting for transfers between devices, swapped(): return lax.ppermute(x, 'rep', [(0, 1), (1, 0)])  31.9 us
    all_gather x1, waiting for transfers between devices, paired(): lax.all_gather(last_part, 'blk', axis_index_groups=[list(RING)], axis=0)  30.2 us
    all_gather x1, waiting for transfers between devices, paired(): d_both = lax.all_gather(d_own, 'rep', axis=0)  23.8 us
    all_to_all x3, starting transfers between devices, moved(): own = lax.all_to_all(x, 'blk', split_axis=0, concat_axis=0, tiled=True)  22 us
    pallas_call x2, Pallas kernels, hidden_of(): pl.pallas_call(kernel, grid_spec=pltpu.PrefetchScalarGridSpec(num_scalar_...  21.5 us
    all_to_all x2, starting transfers between devices, returned(): x = lax.all_to_all(x, 'blk', split_axis=0, concat_axis=0, tiled=True)  14.7 us
    all_to_all x1, blocking collectives, everywhere(): lax.all_to_all(copies, 'blk', split_axis=0, concat_axis=0, tiled=True)  9.9 us
  transfers between devices with their start and end apart: 10, of which 5 were waited for; matrix products, arithmetic and copies ran while one was open for 3% of the time, Pallas kernels for 19%

profile of v15, /device:TPU:0, one launch (start us, length us, event | category | flops | bytes accessed | tf_op | source)
XLA Modules:
  0.0 297.5 jit_solution(6644273838554207278)
XLA Ops:
  7.2 0.0 all-gather.6.cloned.1.call-start
  7.2 3.0 %prep.1 = (bf16[128,1664]{1,0:T(8,128)(2,1)}, bf16[384,128]{1,0:T(8,128)(2,1)}) custom-call(s32[16]{0:T(128)} %lengths_ref.5, s32[1]{0:T(128)} %bitcast.3.blk_ref, bf16[128,1536]{1,0:T(8,128)(2,1)} %bitcast.46, s32[8,128]{1,0:T(8,128)} %bitcast.53, f32[8,128]{1,0:T(8,128)} %bitcast.54, f32[1536]{0:T(1024)} %gain_ref.1), custom_call_target="tpu_custom_call" | custom-call | tf_op jit(solution)/shard_map/prep/pallas_call | solution.py:588
  10.2 0.0 all-gather.6.cloned.1.call-update
  10.2 3.3 %cast.3 = bf16[16,96,512]{2,1,0:T(8,128)(2,1)} custom-call(f32[4608,512]{1,0:T(8,128)} %bitcast.33, bf16[128,1664]{1,0:T(8,128)(2,1)} %get-tuple-element.20.rank_ref.refs_0_), custom_call_target="tpu_custom_call" | custom-call | tf_op jit(solution)/shard_map/cast/pallas_call | solution.py:556
  13.5 7.4 %all-to-all-start = ((bf16[16,96,512]{2,1,0:T(8,128)(2,1)}), bf16[16,96,512]{2,1,0:T(8,128)(2,1)S(1)}, u32[]{:S(2)}, u32[]{:S(2)}) async-start(bf16[16,96,512]{2,1,0:T(8,128)(2,1)} %cast.3), calls=%async_computation | async-start | bytes 3145728 | tf_op jit(solution)/shard_map/all_to_all | solution.py:572
  20.9 3.3 %cast.4 = bf16[16,96,512]{2,1,0:T(8,128)(2,1)} custom-call(f32[4608,512]{1,0:T(8,128)} %bitcast.34), custom_call_target="tpu_custom_call" | custom-call | tf_op jit(solution)/shard_map/cast/pallas_call | solution.py:556
  24.2 48.8 %all-to-all-done = bf16[16,96,512]{2,1,0:T(8,128)(2,1)S(1)} async-done(((bf16[16,96,512]{2,1,0:T(8,128)(2,1)}), bf16[16,96,512]{2,1,0:T(8,128)(2,1)S(1)}, u32[]{:S(2)}, u32[]{:S(2)}) %all-to-all-start) | async-done | bytes 1572896 | tf_op jit(solution)/shard_map/all_to_all | solution.py:572
  73.0 0.0 copy-start.3
  73.0 6.1 %all-to-all-start.1 = ((bf16[16,96,512]{2,1,0:T(8,128)(2,1)}), bf16[16,96,512]{2,1,0:T(8,128)(2,1)}, u32[]{:S(2)}, u32[]{:S(2)}) async-start(bf16[16,96,512]{2,1,0:T(8,128)(2,1)} %cast.4), calls=%async_computation.1 | async-start | bytes 3145728 | tf_op jit(solution)/shard_map/all_to_all | solution.py:572
  79.1 0.0 copy-done.3
  79.1 1.6 collective-permute-start
  80.7 3.2 %cast.5.__0_ = bf16[16,96,512]{2,1,0:T(8,128)(2,1)} custom-call(f32[4608,512]{1,0:T(8,128)} %bitcast.35), custom_call_target="tpu_custom_call" | custom-call | tf_op jit(solution)/shard_map/cast/pallas_call | solution.py:556
  83.9 31.9 %collective-permute-done.__1_.g_ref.g_oth = bf16[1536,512]{1,0:T(8,128)(2,1)S(1)} collective-permute-done((bf16[1536,512]{1,0:T(8,128)(2,1)S(1)}, bf16[1536,512]{1,0:T(8,128)(2,1)S(1)}, u32[]{:S(2)}, u32[]{:S(2)}) %collective-permute-start) | collective-permute-done | bytes 1572896 | tf_op jit(solution)/shard_map/ppermute | solution.py:576
  115.8 0.0 copy-start.1
  115.8 1.2 copy-done.1
  117.1 0.0 copy-start.8
  117.1 0.0 all-to-all-done.1
  117.1 8.5 %all-to-all-start.2 = ((bf16[16,96,512]{2,1,0:T(8,128)(2,1)}), bf16[16,96,512]{2,1,0:T(8,128)(2,1)S(1)}, u32[]{:S(2)}, u32[]{:S(2)}) async-start(bf16[16,96,512]{2,1,0:T(8,128)(2,1)} %tie.3), calls=%async_computation.2 | async-start | bytes 3145728 | tf_op jit(solution)/shard_map/all_to_all | solution.py:572
  125.6 0.0 all-gather.8.cloned.1.call-start
  125.6 1.5 collective-permute-start.1
  127.2 0.0 copy-done.8
  127.2 0.6 dynamic_slice.3
  127.8 1.3 stack.36.info
  129.1 0.0 all-gather.6.cloned.1.call-done.x_ref
  129.1 10.6 %gate_up.2 = (bf16[640,512]{1,0:T(8,128)(2,1)}, bf16[640,128]{1,0:T(8,128)(2,1)}, f32[16,128]{1,0:T(8,128)}) custom-call(s32[5]{0:T(128)} %stack.36.info, s32[16]{0:T(128)} %lengths_ref.5, s32[16]{0:T(128)} %constant.33.clone.ring_ref, bf16[2048,1664]{1,0:T(8,128)(2,1)} %all-gather.6.cloned.1.call-done.x_ref, bf16[1536,512]{1,0:T(8,128)(2,1)} %bitcast.39, ...), custom_call_target="tpu_custom_call" | custom-call | tf_op jit(solution)/shard_map/gate_up/pallas_call | solution.py:619
  139.7 17.9 %all-to-all-done.2 = bf16[16,96,512]{2,1,0:T(8,128)(2,1)S(1)} async-done(((bf16[16,96,512]{2,1,0:T(8,128)(2,1)}), bf16[16,96,512]{2,1,0:T(8,128)(2,1)S(1)}, u32[]{:S(2)}, u32[]{:S(2)}) %all-to-all-start.2) | async-done | bytes 1572896 | tf_op jit(solution)/shard_map/all_to_all | solution.py:572
  157.6 0.0 copy-start
  157.6 1.1 copy-done
  158.7 0.0 all-gather.8.cloned.1.call-update
  158.7 4.3 %own_down.1 = (bf16[512,1536]{1,0:T(8,128)(2,1)}, bf16[128,1536]{1,0:T(8,128)(2,1)}, f32[16,1536]{1,0:T(8,128)}) custom-call(bf16[640,512]{1,0:T(8,128)(2,1)} %get-tuple-element.23.__1_.hidden_any, f32[16,128]{1,0:T(8,128)} %get-tuple-element.24.share_any, bf16[1536,512]{1,0:T(8,128)(2,1)} %tie.4.d_any), custom_call_target="tpu_custom_call" | custom-call | tf_op jit(solution)/shard_map/own_down/pallas_call | solution.py:664
  163.1 0.0 collective-permute-done.1.__1_.u_ref.u_oth
  163.1 0.0 copy-start.2
  163.1 1.1 copy-done.2
  164.2 9.1 %all-to-all-start.4 = ((bf16[16,32,1536]{2,1,0:T(8,128)(2,1)}), bf16[16,32,1536]{2,1,0:T(8,128)(2,1)S(1)}, u32[]{:S(2)}, u32[]{:S(2)}) async-start(bf16[16,32,1536]{2,1,0:T(8,128)(2,1)} %bitcast.37), calls=%async_computation.4 | async-start | bytes 3145728 | tf_op jit(solution)/shard_map/all_to_all | solution.py:645
  173.3 0.2 all-gather.10.cloned.1.call-start
  173.6 10.9 %gate_up.3 = (bf16[656,512]{1,0:T(8,128)(2,1)}, f32[16,128]{1,0:T(8,128)}, f32[16,1536]{1,0:T(8,128)}) custom-call(s32[5]{0:T(128)} %stack.36.info, s32[16]{0:T(128)} %lengths_ref.5, s32[16]{0:T(128)} %constant.33.clone.ring_ref, bf16[2048,1664]{1,0:T(8,128)(2,1)} %all-gather.6.cloned.1.call-done.x_ref, bf16[1536,512]{1,0:T(8,128)(2,1)} %copy-done.1, ...), custom_call_target="tpu_custom_call" | custom-call | tf_op jit(solution)/shard_map/gate_up/pallas_call | solution.py:619
  184.5 23.8 %all-gather.8.cloned.1.call-done = bf16[3072,512]{1,0:T(8,128)(2,1)} async-done(((bf16[1536,512]{1,0:T(8,128)(2,1)}), bf16[3072,512]{1,0:T(8,128)(2,1)}) %all-gather.8.cloned.1.call-update) | async-done | bytes 3145744 | tf_op jit(solution)/shard_map/all_gather | solution.py:663
  208.2 6.3 %oth_down.1 = (bf16[640,1536]{1,0:T(8,128)(2,1)}, f32[16,1536]{1,0:T(8,128)}) custom-call(s32[5]{0:T(128)} %stack.36.info, bf16[656,512]{1,0:T(8,128)(2,1)} %get-tuple-element.26.hidden_any, f32[16,128]{1,0:T(8,128)} %get-tuple-element.27.share_any, bf16[640,128]{1,0:T(8,128)(2,1)} %get-tuple-element.28.spot_any, ...), custom_call_target="tpu_custom_call" | custom-call | tf_op jit(solution)/shard_map/oth_down/pallas_call | solution.py:689
  214.5 0.0 all-gather.10.cloned.1.call-update
  214.5 0.0 all-to-all-done.4
  214.5 0.0 copy-start.5
  214.5 1.1 copy-done.5
  215.7 5.6 %all-to-all-start.3 = ((bf16[16,40,1536]{2,1,0:T(8,128)(2,1)}), bf16[16,40,1536]{2,1,0:T(8,128)(2,1)S(1)}, u32[]{:S(2)}, u32[]{:S(2)}) async-start(bf16[16,40,1536]{2,1,0:T(8,128)(2,1)} %bitcast.44), calls=%async_computation.3 | async-start | bytes 3932160 | tf_op jit(solution)/shard_map/all_to_all | solution.py:645
  221.3 3.1 %mix.1 = (bf16[384,512]{1,0:T(8,128)(2,1)}, bf16[384,640]{1,0:T(8,128)(2,1)}) custom-call(s32[5]{0:T(128)} %stack.36.info, bf16[128,1664]{1,0:T(8,128)(2,1)} %get-tuple-element.20.rank_ref.refs_0_, bf16[384,128]{1,0:T(8,128)(2,1)} %get-tuple-element.21.pieces_ref), custom_call_target="tpu_custom_call" | custom-call | tf_op jit(solution)/shard_map/mix/pallas_call | solution.py:730
  224.4 4.1 %first.1.base_any = f32[128,1536]{1,0:T(8,128)} custom-call(bf16[384,512]{1,0:T(8,128)(2,1)} %get-tuple-element.33.mix_ref, bf16[512,1536]{1,0:T(8,128)(2,1)} %bitcast.45, bf16[128,1536]{1,0:T(8,128)(2,1)} %bitcast.48), custom_call_target="tpu_custom_call" | custom-call | tf_op jit(solution)/shard_map/first/pallas_call | solution.py:753
  228.4 8.3 %place.1._ = bf16[3,1536,1024]{2,1,0:T(8,128)(2,1)} custom-call(s32[5]{0:T(128)} %stack.36.info, bf16[1536,512]{1,0:T(8,128)(2,1)} %bitcast.40, bf16[1536,512]{1,0:T(8,128)(2,1)} %copy-done.1, bf16[1536,512]{1,0:T(8,128)(2,1)} %bitcast.11.u_ref.u_own, bf16[1536,512]{1,0:T(8,128)(2,1)} %copy-done.2, bf16[2,1536,512]{2,1,0:T(8,128)(2,1)} %bitcast.42, ...), custom_call_target="tpu_custom_call" | custom-call | tf_op jit(solution)/shard_map/place/pallas_call | solution.py:716
  236.7 0.0 copy-start.6
  236.7 0.0 copy-start.10
  236.7 30.2 %all-gather.10.cloned.1.call-done = f32[256,1536]{1,0:T(8,128)} async-done(((f32[16,1536]{1,0:T(8,128)}), f32[256,1536]{1,0:T(8,128)}) %all-gather.10.cloned.1.call-update) | async-done | bytes 1572880 | tf_op jit(solution)/shard_map/all_gather | solution.py:713
  266.9 1.5 reduce_sum.36
  268.4 0.1 multiply_reduce_fusion
  268.6 0.0 copy-done.6
  268.6 0.0 copy-done.10
  268.6 5.2 %select_reduce_fusion = (f32[16]{0:T(128)S(1)}, f32[16]{0:T(128)}) fusion(s32[2048]{0:T(1024)S(1)} %iota_add_fusion, s32[16]{0:T(128)S(1)} %copy-done.10, bf16[2048,1536]{1,0:T(8,128)(2,1)} %param.16, f32[16,1536]{1,0:T(8,128)S(1)} %reduce_sum.36, f32[1536]{0:T(1024)S(1)} %copy-done.6, f32[16]{0:T(128)S(1)} %add_rsqrt_fusion), kind=kOutput, calls=%fused_computation | convolution fusion | flops 100892640 | bytes 6404352 | tf_op jit(solution)/shard_map/dot_general | solution.py:768
  273.8 0.0 all-to-all-done.3
  273.8 0.0 copy-start.4
  273.8 1.3 copy-done.4
  275.1 0.0 copy-start.9
  275.1 4.7 %combine.1 = (bf16[128,1536]{1,0:T(8,128)(2,1)}, f32[1,128]{1,0:T(1,128)}) custom-call(s32[5]{0:T(128)} %stack.36.info, bf16[384,640]{1,0:T(8,128)(2,1)} %get-tuple-element.22.mix_any, bf16[640,1536]{1,0:T(8,128)(2,1)} %bitcast.43, f32[128,1536]{1,0:T(8,128)} %first.1.base_any, bf16[3,1536,1024]{2,1,0:T(8,128)(2,1)} %place.1._, f32[1,16]{1,0:T(1,128)} %bitcast.51), custom_call_target="tpu_custom_call" | custom-call | tf_op jit(solution)/shard_map/combine/pallas_call | solution.py:778
  279.8 0.6 compare_select_fusion
  280.4 0.0 copy-done.7
  280.4 9.9 %all_to_all.30 = f32[16,3,16]{2,1,0:T(4,128)S(1)} all-to-all(f32[16,3,16]{2,1,0:T(4,128)S(1)} %broadcast_in_dim.29), channel_id=1, replica_groups=mesh['blk'=16,'rep'=2] {'blk'}, dimensions={0} | all-to-all | bytes 6144 | tf_op jit(solution)/shard_map/all_to_all | solution.py:798
  290.3 0.0 copy-done.9
  290.4 0.6 pad_maximum_fusion.1
  (13 shorter events, 0.1 us)
Async XLA Ops:
  7.2 121.9 %all-gather.6.cloned.1.call-start = ((), (), s32[]{:S(2)}) async-start(), calls=%async_computation.6 | async-start | bytes 7241728 | tf_op jit(solution)/shard_map/all_gather | solution.py:614
  13.5 59.5 %all-to-all-start = ((bf16[16,96,512]{2,1,0:T(8,128)(2,1)}), bf16[16,96,512]{2,1,0:T(8,128)(2,1)S(1)}, u32[]{:S(2)}, u32[]{:S(2)}) async-start(bf16[16,96,512]{2,1,0:T(8,128)(2,1)} %cast.3), calls=%async_computation | async-start | bytes 3145728 | tf_op jit(solution)/shard_map/all_to_all | solution.py:572
  73.0 6.1 %copy-start.3 = (bf16[16,96,512]{2,1,0:T(8,128)(2,1)}, bf16[16,96,512]{2,1,0:T(8,128)(2,1)S(1)}, u32[]{:S(2)}) copy-start(bf16[16,96,512]{2,1,0:T(8,128)(2,1)S(1)} %all-to-all-done) | copy-start | bytes 4718596
  73.0 44.1 %all-to-all-start.1 = ((bf16[16,96,512]{2,1,0:T(8,128)(2,1)}), bf16[16,96,512]{2,1,0:T(8,128)(2,1)}, u32[]{:S(2)}, u32[]{:S(2)}) async-start(bf16[16,96,512]{2,1,0:T(8,128)(2,1)} %cast.4), calls=%async_computation.1 | async-start | bytes 3145728 | tf_op jit(solution)/shard_map/all_to_all | solution.py:572
  79.1 36.7 %collective-permute-start = (bf16[1536,512]{1,0:T(8,128)(2,1)S(1)}, bf16[1536,512]{1,0:T(8,128)(2,1)S(1)}, u32[]{:S(2)}, u32[]{:S(2)}) collective-permute-start(bf16[1536,512]{1,0:T(8,128)(2,1)S(1)} %bitcast.38), channel_id=1, source_target_pairs={{0,1},{1,0},{2,3},{3,2},{4,5},{5,4},{6,7},{7,6},{8,9},{9,8},{10,11... | collective-permute-start | bytes 4718600 | tf_op jit(solution)/shard_map/ppermute | solution.py:576
  115.8 1.3 copy-start.1
  117.1 10.1 %copy-start.8 = (s32[16]{0:T(128)S(1)}, s32[16]{0:T(128)}, u32[]{:S(2)}) copy-start(s32[16]{0:T(128)} %lengths_ref.5) | copy-start | bytes 196
  117.1 40.5 %all-to-all-start.2 = ((bf16[16,96,512]{2,1,0:T(8,128)(2,1)}), bf16[16,96,512]{2,1,0:T(8,128)(2,1)S(1)}, u32[]{:S(2)}, u32[]{:S(2)}) async-start(bf16[16,96,512]{2,1,0:T(8,128)(2,1)} %tie.3), calls=%async_computation.2 | async-start | bytes 3145728 | tf_op jit(solution)/shard_map/all_to_all | solution.py:572
  125.6 82.6 %all-gather.8.cloned.1.call-start = ((), (), s32[]{:S(2)}) async-start(), calls=%async_computation.7 | async-start | bytes 4718592 | tf_op jit(solution)/shard_map/all_gather | solution.py:663
  125.6 37.4 %collective-permute-start.1 = (bf16[1536,512]{1,0:T(8,128)(2,1)}, bf16[1536,512]{1,0:T(8,128)(2,1)S(1)}, u32[]{:S(2)}, u32[]{:S(2)}) collective-permute-start(bf16[1536,512]{1,0:T(8,128)(2,1)} %bitcast.11.u_ref.u_own), channel_id=1, source_target_pairs={{0,1},{1,0},{2,3},{3,2},{4,5},{5,4},{6,7},{7,6},{8,9},{9,8},{10,11... | collective-permute-start | bytes 4718600 | tf_op jit(solution)/shard_map/ppermute | solution.py:576
  157.6 1.1 copy-start
  163.1 1.1 copy-start.2
  164.2 50.3 %all-to-all-start.4 = ((bf16[16,32,1536]{2,1,0:T(8,128)(2,1)}), bf16[16,32,1536]{2,1,0:T(8,128)(2,1)S(1)}, u32[]{:S(2)}, u32[]{:S(2)}) async-start(bf16[16,32,1536]{2,1,0:T(8,128)(2,1)} %bitcast.37), calls=%async_computation.4 | async-start | bytes 3145728 | tf_op jit(solution)/shard_map/all_to_all | solution.py:645
  173.3 93.6 %all-gather.10.cloned.1.call-start = ((), (), s32[]{:S(2)}) async-start(), calls=%async_computation.8 | async-start | bytes 1671168 | tf_op jit(solution)/shard_map/all_gather | solution.py:713
  214.5 1.1 copy-start.5
  215.7 58.1 %all-to-all-start.3 = ((bf16[16,40,1536]{2,1,0:T(8,128)(2,1)}), bf16[16,40,1536]{2,1,0:T(8,128)(2,1)S(1)}, u32[]{:S(2)}, u32[]{:S(2)}) async-start(bf16[16,40,1536]{2,1,0:T(8,128)(2,1)} %bitcast.44), calls=%async_computation.3 | async-start | bytes 3932160 | tf_op jit(solution)/shard_map/all_to_all | solution.py:645
  236.7 31.9 %copy-start.6 = (f32[1536]{0:T(1024)S(1)}, f32[1536]{0:T(1024)}, u32[]{:S(2)}) copy-start(f32[1536]{0:T(1024)} %param.17) | copy-start | bytes 18436
  236.7 31.9 %copy-start.10 = (s32[16]{0:T(128)S(1)}, s32[16]{0:T(128)}, u32[]{:S(2)}) copy-start(s32[16]{0:T(128)} %param.18) | copy-start | bytes 196
  273.8 1.3 copy-start.4
  275.1 5.3 %copy-start.7 = (f32[16]{0:T(128)S(1)}, f32[16]{0:T(128)}, u32[]{:S(2)}) copy-start(f32[16]{0:T(128)} %get-tuple-element.38) | copy-start | bytes 196
  275.1 15.3 %copy-start.9 = (s32[16]{0:T(128)S(1)}, s32[16]{0:T(128)}, u32[]{:S(2)}) copy-start(s32[16]{0:T(128)} %lengths_ref.5) | copy-start | bytes 196
Sparse Core Ops, SparseCore 0:
  10.4 95.2 all-gather.5
  158.9 49.3 all-gather.7
  214.6 52.2 all-gather.9

commit v16 on v15

--- a/solution.py
+++ b/solution.py
@@ -316,9 +316,9 @@
         base_ref[...] = jnp.where(iota(base_ref.shape, 0) == info[4], last, 0.0)
 
 
-def matmul_nt(hidden_ref, d):
+def matmul_nt(hidden, d):
     return lax.dot_general(
-        hidden_ref[...], d, (((1,), (1,)), ((), ())), preferred_element_type=jnp.float32
+        hidden[...], d, (((1,), (1,)), ((), ())), preferred_element_type=jnp.float32
     )
 
 
@@ -410,7 +410,14 @@
         value = matmul_nt(hidden, d[k])
         out[k] = (placed + value[:rows]).astype(jnp.bfloat16)
         last = value[rows:].astype(jnp.bfloat16).astype(jnp.float32)
-        total[k] = base[:, columns] + part[:, columns] + share[:, :1] * last
+        value = base[:, columns] + part[:, columns] + share[:, :1] * last
+        high = value.astype(jnp.bfloat16)
+        low = jnp.where(iota(value.shape, 0) == info[4], value - high.astype(jnp.float32), 0.0)
+        count = value.shape[0]
+        total[k, :count] = high
+        low = jnp.sum(low, axis=0, keepdims=True)
+        rest = (total.shape[1] - count, size)
+        total[k, count:] = jnp.where(iota(rest, 0) == 0, low, 0.0).astype(jnp.bfloat16)
         stores += started(
             [
                 copy(total.at[k], sum_any.at[:, columns], sems.at[3, k]),
@@ -484,9 +491,44 @@
     out_f = out.astype(jnp.float32)
     row = iota(out_f.shape, 0)
     total = jnp.sum(jnp.where(row < info[3], out_f * out_f, 0.0), axis=0, keepdims=True)
-    square_ref[...] = jnp.broadcast_to(
-        jnp.sum(total, axis=1, keepdims=True), square_ref.shape
-    )
+    total = jnp.sum(total, axis=1, keepdims=True)
+    square_ref[...] = jnp.where(iota(square_ref.shape, 1) == info[4], total, 0.0)
+
+
+def logits_kernel(info, parts_any, gain_ref, target_ref, unembed_any, out_ref, parts, unembed, sems):
+    chunks, size = unembed.shape[:2]
+    copy = pltpu.make_async_copy
+    first = copy(parts_any, parts, sems.at[chunks])
+    first.start()
+    rows = started(
+        [
+            copy(unembed_any.at[k * size : (k + 1) * size], unembed.at[k], sems.at[k])
+            for k in range(chunks)
+        ]
+    )
+    first.wait()
+    count = out_ref.shape[0]
+    shares = parts[...].astype(jnp.float32)
+    last = jnp.zeros((count, parts.shape[1]), jnp.float32)
+    place = iota(last.shape, 0)
+    for k, owner in enumerate(RING):
+        at = k * (count + 8)
+        last = last + shares[at : at + count]
+        last = last + jnp.where(place == owner, shares[at + count : at + count + 1], 0.0)
+    last = last.astype(jnp.bfloat16).astype(jnp.float32)
+    scale = lax.rsqrt(jnp.mean(last * last, axis=-1, keepdims=True) + 1e-05)
+    final = (last * scale * gain_ref[...][None]).astype(jnp.bfloat16)
+    lane = iota((count, size), 1)
+    top = jnp.full((count, 1), -jnp.inf, jnp.float32)
+    target = jnp.zeros((count, 1), jnp.float32)
+    for k in range(chunks):
+        rows[k].wait()
+        logits = matmul_nt(final, unembed[k])
+        top = jnp.maximum(top, jnp.max(logits, axis=1, keepdims=True))
+        place = target_ref[...] - info[4] * (chunks * size) - k * size
+        target = target + jnp.sum(jnp.where(lane == place, logits, 0.0), axis=1, keepdims=True)
+    column = iota(out_ref.shape, 1)
+    out_ref[...] = jnp.where(column == 0, top, jnp.where(column == 1, target, 0.0))
 
 
 def place_kernel(info, g_own, g_oth, u_own, u_oth, d_both, _, out_ref):
@@ -702,15 +744,17 @@
                 pltpu.VMEM((blk_count, width), jnp.float32),
                 pltpu.VMEM((4, quarter, FF), jnp.bfloat16),
                 pltpu.VMEM((4, second, quarter), jnp.bfloat16),
-                pltpu.VMEM((4, blk_count, quarter), jnp.float32),
+                pltpu.VMEM((4, 2 * blk_count, quarter), jnp.bfloat16),
                 pltpu.SemaphoreType.DMA((4, 6)),
             ],
         ),
-        out_shape=[bf16(second, width), f32(blk_count, width)],
+        out_shape=[bf16(second, width), bf16(2 * blk_count, width)],
         compiler_params=params(),
         name="oth_down",
     )(info, oth_hidden, oth_share, spot, late_out, base_part, own_part, d_both)
-    last_parts = lax.all_gather(last_part, "blk", axis_index_groups=[list(RING)], axis=0)
+    last_parts = lax.all_gather(
+        last_part[: blk_count + 8], "blk", axis_index_groups=[list(RING)], axis=0, tiled=True
+    )
     oth_back = returned(oth_out)
 
     server = pl.pallas_call(
@@ -759,21 +803,24 @@
         compiler_params=params(),
         name="first",
     )(first_mix, own_back, resid)
-    last_rows = lax.reduce_precision(jnp.sum(last_parts, axis=0), 8, 7)
-    final = (
-        last_rows
-        * lax.rsqrt(jnp.mean(last_rows * last_rows, axis=-1, keepdims=True) + 1e-05)
-        * final_gain
-    ).astype(jnp.bfloat16)
-    logits = lax.dot_general(
-        final, unembed, (((1,), (1,)), ((), ())), preferred_element_type=jnp.float32
-    )
-    vocab_base = blk * unembed.shape[0]
-    target_hit = (
-        target_ids[:, None] == vocab_base + jnp.arange(unembed.shape[0], dtype=jnp.int32)[None, :]
-    )
-    target_part = jnp.sum(jnp.where(target_hit, logits, 0.0), axis=1)
-    top_part = jnp.max(logits, axis=1)
+    vocab = unembed.shape[0] // 8
+    tops = pl.pallas_call(
+        logits_kernel,
+        grid_spec=pltpu.PrefetchScalarGridSpec(
+            num_scalar_prefetch=1,
+            grid=(1,),
+            in_specs=[anywhere, whole((width,)), whole((blk_count, 1)), anywhere],
+            out_specs=whole((blk_count, LANES)),
+            scratch_shapes=[
+                pltpu.VMEM((blk_count * (blk_count + 8), width), jnp.bfloat16),
+                pltpu.VMEM((8, vocab, width), jnp.bfloat16),
+                pltpu.SemaphoreType.DMA((9,)),
+            ],
+        ),
+        out_shape=f32(blk_count, LANES),
+        compiler_params=params(),
+        name="logits",
+    )(info, last_parts, final_gain, target_ids[:, None], unembed)
 
     out_rows, square = pl.pallas_call(
         combine_kernel,
@@ -792,14 +839,12 @@
         out_shape=[bf16(rows, width), f32(1, LANES)],
         compiler_params=params(),
         name="combine",
-    )(info, second_mix, oth_back, base, server, top_part[None])
+    )(info, second_mix, oth_back, base, server, tops)
 
     def everywhere(copies):
         return lax.all_to_all(copies, "blk", split_axis=0, concat_axis=0, tiled=True)
 
-    prompt = jnp.arange(blk_count, dtype=jnp.int32)
-    square_part = jnp.where(prompt == blk, square[0, :blk_count], 0.0)
-    stats = jnp.stack([top_part, target_part, square_part])
+    stats = jnp.concatenate([tops[:, :2].T, square[:, :blk_count]], axis=0)
     parts = everywhere(jnp.broadcast_to(stats[None], (blk_count,) + stats.shape))
     sums = jnp.sum(parts[:, 1:], axis=0)
     norms = jnp.sqrt(sums[1] / (lengths.astype(jnp.float32) * width) + 1e-06)

time: 299 us -> 308 us (1.030)
  Pallas kernels: 65 us -> 73.4 us
  matrix products: 5.18 us -> 0 us
    pallas_call x0 -> x1, Pallas kernels: none -> 8.49 us  [paired(): pl.pallas_call(logits_kernel, grid_spec=pltpu.PrefetchScalarGridSpec(num_...]
    dot_general x1 -> x0, matrix products: 5.18 us -> none  [paired(): lax.dot_general(final, unembed, (((1,), (1,)), ((), ())), preferred_eleme...]
    all_gather x1, waiting for transfers between devices: 30.2 us -> 33.4 us  [paired(): lax.all_gather(last_part[:blk_count + 8], 'blk', axis_index_groups=[list(...]
  transfers between devices with their start and end apart: 10 -> 10, of which waited for: 5 -> 5; matrix products, arithmetic and copies ran while one was open for 3% -> 2% of each run, Pallas kernels for 19% -> 21%
where the time goes in v16:
time: 308 us; the launch traced here: 307 us
  waiting for transfers between devices  156 us (51%)
  Pallas kernels  73.4 us (24%)
  starting transfers between devices  40 us (13%)
  between operations  13.9 us (5%)
  blocking collectives  11.8 us (4%)
  local copies, waits for them, and re-layouts  10.9 us (4%)
    all_to_all x3, waiting for transfers between devices, moved(): own = lax.all_to_all(x, 'blk', split_axis=0, concat_axis=0, tiled=True)  66.6 us
    all_gather x1, waiting for transfers between devices, paired(): lax.all_gather(last_part[:blk_count + 8], 'blk', axis_index_groups=[list(...  33.4 us
    ppermute x2, waiting for transfers between devices, swapped(): return lax.ppermute(x, 'rep', [(0, 1), (1, 0)])  31.9 us
    all_gather x1, waiting for transfers between devices, paired(): d_both = lax.all_gather(d_own, 'rep', axis=0)  24 us
    all_to_all x3, starting transfers between devices, moved(): own = lax.all_to_all(x, 'blk', split_axis=0, concat_axis=0, tiled=True)  22 us
    pallas_call x2, Pallas kernels, hidden_of(): pl.pallas_call(kernel, grid_spec=pltpu.PrefetchScalarGridSpec(num_scalar_...  21.5 us
    all_to_all x2, starting transfers between devices, returned(): x = lax.all_to_all(x, 'blk', split_axis=0, concat_axis=0, tiled=True)  14.7 us
    all_to_all x1, blocking collectives, everywhere(): lax.all_to_all(copies, 'blk', split_axis=0, concat_axis=0, tiled=True)  11.8 us
  transfers between devices with their start and end apart: 10, of which 5 were waited for; matrix products, arithmetic and copies ran while one was open for 2% of the time, Pallas kernels for 21%

profile of v16, /device:TPU:0, one launch (start us, length us, event | category | flops | bytes accessed | tf_op | source)
XLA Modules:
  0.0 307.3 jit_solution(3475985292108092423)
XLA Ops:
  7.2 0.0 all-gather.5.cloned.1.call-start
  7.2 3.0 prep.1
  10.2 0.0 all-gather.5.cloned.1.call-update
  10.3 3.2 %cast.3 = bf16[16,96,512]{2,1,0:T(8,128)(2,1)} custom-call(f32[4608,512]{1,0:T(8,128)} %bitcast.33, bf16[128,1664]{1,0:T(8,128)(2,1)} %get-tuple-element.20.rank_ref.refs_0_), custom_call_target="tpu_custom_call" | custom-call | tf_op jit(solution)/shard_map/cast/pallas_call | solution.py:598
  13.5 7.4 %all-to-all-start = ((bf16[16,96,512]{2,1,0:T(8,128)(2,1)}), bf16[16,96,512]{2,1,0:T(8,128)(2,1)S(1)}, u32[]{:S(2)}, u32[]{:S(2)}) async-start(bf16[16,96,512]{2,1,0:T(8,128)(2,1)} %cast.3), calls=%async_computation | async-start | bytes 3145728 | tf_op jit(solution)/shard_map/all_to_all | solution.py:614
  20.9 3.3 %cast.4 = bf16[16,96,512]{2,1,0:T(8,128)(2,1)} custom-call(f32[4608,512]{1,0:T(8,128)} %bitcast.34), custom_call_target="tpu_custom_call" | custom-call | tf_op jit(solution)/shard_map/cast/pallas_call | solution.py:598
  24.2 48.8 %all-to-all-done = bf16[16,96,512]{2,1,0:T(8,128)(2,1)S(1)} async-done(((bf16[16,96,512]{2,1,0:T(8,128)(2,1)}), bf16[16,96,512]{2,1,0:T(8,128)(2,1)S(1)}, u32[]{:S(2)}, u32[]{:S(2)}) %all-to-all-start) | async-done | bytes 1572896 | tf_op jit(solution)/shard_map/all_to_all | solution.py:614
  73.0 0.0 copy-start.3
  73.0 6.1 %all-to-all-start.1 = ((bf16[16,96,512]{2,1,0:T(8,128)(2,1)}), bf16[16,96,512]{2,1,0:T(8,128)(2,1)}, u32[]{:S(2)}, u32[]{:S(2)}) async-start(bf16[16,96,512]{2,1,0:T(8,128)(2,1)} %cast.4), calls=%async_computation.1 | async-start | bytes 3145728 | tf_op jit(solution)/shard_map/all_to_all | solution.py:614
  79.1 0.0 copy-done.3
  79.1 1.5 collective-permute-start
  80.7 3.2 %cast.5.__0_ = bf16[16,96,512]{2,1,0:T(8,128)(2,1)} custom-call(f32[4608,512]{1,0:T(8,128)} %bitcast.35), custom_call_target="tpu_custom_call" | custom-call | tf_op jit(solution)/shard_map/cast/pallas_call | solution.py:598
  83.9 31.9 %collective-permute-done.__1_.g_ref.g_oth = bf16[1536,512]{1,0:T(8,128)(2,1)S(1)} collective-permute-done((bf16[1536,512]{1,0:T(8,128)(2,1)S(1)}, bf16[1536,512]{1,0:T(8,128)(2,1)S(1)}, u32[]{:S(2)}, u32[]{:S(2)}) %collective-permute-start) | collective-permute-done | bytes 1572896 | tf_op jit(solution)/shard_map/ppermute | solution.py:618
  115.8 0.0 copy-start.1
  115.8 1.2 copy-done.1
  117.1 0.0 copy-start.6
  117.1 0.0 all-to-all-done.1
  117.1 8.5 %all-to-all-start.2 = ((bf16[16,96,512]{2,1,0:T(8,128)(2,1)}), bf16[16,96,512]{2,1,0:T(8,128)(2,1)S(1)}, u32[]{:S(2)}, u32[]{:S(2)}) async-start(bf16[16,96,512]{2,1,0:T(8,128)(2,1)} %tie.3), calls=%async_computation.2 | async-start | bytes 3145728 | tf_op jit(solution)/shard_map/all_to_all | solution.py:614
  125.6 0.0 all-gather.9.cloned.1.call-start
  125.7 1.5 collective-permute-start.1
  127.2 0.0 copy-done.6
  127.2 0.7 dynamic_slice.3
  127.8 1.3 stack.28.info
  129.1 0.0 all-gather.5.cloned.1.call-done.x_ref
  129.1 10.7 %gate_up.2 = (bf16[640,512]{1,0:T(8,128)(2,1)}, bf16[640,128]{1,0:T(8,128)(2,1)}, f32[16,128]{1,0:T(8,128)}) custom-call(s32[5]{0:T(128)} %stack.28.info, s32[16]{0:T(128)} %lengths_ref.5, s32[16]{0:T(128)} %constant.26.clone.ring_ref, bf16[2048,1664]{1,0:T(8,128)(2,1)} %all-gather.5.cloned.1.call-done.x_ref, bf16[1536,512]{1,0:T(8,128)(2,1)} %bitcast.39, ...), custom_call_target="tpu_custom_call" | custom-call | tf_op jit(solution)/shard_map/gate_up/pallas_call | solution.py:661
  139.8 17.8 %all-to-all-done.2 = bf16[16,96,512]{2,1,0:T(8,128)(2,1)S(1)} async-done(((bf16[16,96,512]{2,1,0:T(8,128)(2,1)}), bf16[16,96,512]{2,1,0:T(8,128)(2,1)S(1)}, u32[]{:S(2)}, u32[]{:S(2)}) %all-to-all-start.2) | async-done | bytes 1572896 | tf_op jit(solution)/shard_map/all_to_all | solution.py:614
  157.6 0.0 copy-start
  157.6 1.1 copy-done
  158.7 0.0 all-gather.9.cloned.1.call-update
  158.8 4.3 %own_down.1 = (bf16[512,1536]{1,0:T(8,128)(2,1)}, bf16[128,1536]{1,0:T(8,128)(2,1)}, f32[16,1536]{1,0:T(8,128)}) custom-call(bf16[640,512]{1,0:T(8,128)(2,1)} %get-tuple-element.23.__1_.hidden_any, f32[16,128]{1,0:T(8,128)} %get-tuple-element.24.share_any, bf16[1536,512]{1,0:T(8,128)(2,1)} %tie.4.d_any), custom_call_target="tpu_custom_call" | custom-call | tf_op jit(solution)/shard_map/own_down/pallas_call | solution.py:706
  163.1 0.0 collective-permute-done.1.__1_.u_ref.u_oth
  163.1 0.0 copy-start.2
  163.1 1.2 copy-done.2
  164.3 9.1 %all-to-all-start.4 = ((bf16[16,32,1536]{2,1,0:T(8,128)(2,1)}), bf16[16,32,1536]{2,1,0:T(8,128)(2,1)S(1)}, u32[]{:S(2)}, u32[]{:S(2)}) async-start(bf16[16,32,1536]{2,1,0:T(8,128)(2,1)} %bitcast.37), calls=%async_computation.4 | async-start | bytes 3145728 | tf_op jit(solution)/shard_map/all_to_all | solution.py:687
  173.4 10.9 %gate_up.3 = (bf16[656,512]{1,0:T(8,128)(2,1)}, f32[16,128]{1,0:T(8,128)}, f32[16,1536]{1,0:T(8,128)}) custom-call(s32[5]{0:T(128)} %stack.28.info, s32[16]{0:T(128)} %lengths_ref.5, s32[16]{0:T(128)} %constant.26.clone.ring_ref, bf16[2048,1664]{1,0:T(8,128)(2,1)} %all-gather.5.cloned.1.call-done.x_ref, bf16[1536,512]{1,0:T(8,128)(2,1)} %copy-done.1, ...), custom_call_target="tpu_custom_call" | custom-call | tf_op jit(solution)/shard_map/gate_up/pallas_call | solution.py:661
  184.3 24.0 %all-gather.9.cloned.1.call-done = bf16[3072,512]{1,0:T(8,128)(2,1)} async-done(((bf16[1536,512]{1,0:T(8,128)(2,1)}), bf16[3072,512]{1,0:T(8,128)(2,1)}) %all-gather.9.cloned.1.call-update) | async-done | bytes 3145744 | tf_op jit(solution)/shard_map/all_gather | solution.py:705
  208.2 6.3 %oth_down.1 = (bf16[640,1536]{1,0:T(8,128)(2,1)}, bf16[32,1536]{1,0:T(8,128)(2,1)}) custom-call(s32[5]{0:T(128)} %stack.28.info, bf16[656,512]{1,0:T(8,128)(2,1)} %get-tuple-element.26.hidden_any, f32[16,128]{1,0:T(8,128)} %get-tuple-element.27.share_any, bf16[640,128]{1,0:T(8,128)(2,1)} %get-tuple-element.28.spot_any, ...), custom_call_target="tpu_custom_call" | custom-call | tf_op jit(solution)/shard_map/oth_down/pallas_call | solution.py:731
  214.5 0.0 all-to-all-done.4
  214.5 0.0 copy-start.5
  214.5 0.0 copy-start.8
  214.5 1.1 copy-done.5
  215.7 5.6 %all-to-all-start.3 = ((bf16[16,40,1536]{2,1,0:T(8,128)(2,1)}), bf16[16,40,1536]{2,1,0:T(8,128)(2,1)S(1)}, u32[]{:S(2)}, u32[]{:S(2)}) async-start(bf16[16,40,1536]{2,1,0:T(8,128)(2,1)} %bitcast.43), calls=%async_computation.3 | async-start | bytes 3932160 | tf_op jit(solution)/shard_map/all_to_all | solution.py:687
  221.3 0.0 all-gather.7.cloned.1.call-start
  221.3 1.5 slice.21
  222.8 0.0 all-gather.7.cloned.1.call-update
  222.9 0.0 copy-done.8
  222.9 0.7 copy.23.target_ref
  223.6 3.0 mix.1
  226.6 4.0 %first.1.base_any = f32[128,1536]{1,0:T(8,128)} custom-call(bf16[384,512]{1,0:T(8,128)(2,1)} %get-tuple-element.33.mix_ref, bf16[512,1536]{1,0:T(8,128)(2,1)} %bitcast.45, bf16[128,1536]{1,0:T(8,128)(2,1)} %bitcast.48), custom_call_target="tpu_custom_call" | custom-call | tf_op jit(solution)/shard_map/first/pallas_call | solution.py:797
  230.6 8.3 %place.1._ = bf16[3,1536,1024]{2,1,0:T(8,128)(2,1)} custom-call(s32[5]{0:T(128)} %stack.28.info, bf16[1536,512]{1,0:T(8,128)(2,1)} %bitcast.40, bf16[1536,512]{1,0:T(8,128)(2,1)} %copy-done.1, bf16[1536,512]{1,0:T(8,128)(2,1)} %bitcast.11.u_ref.u_own, bf16[1536,512]{1,0:T(8,128)(2,1)} %copy-done.2, bf16[2,1536,512]{2,1,0:T(8,128)(2,1)} %bitcast.42, ...), custom_call_target="tpu_custom_call" | custom-call | tf_op jit(solution)/shard_map/place/pallas_call | solution.py:760
  238.9 33.4 %all-gather.7.cloned.1.call-done.parts_any = bf16[384,1536]{1,0:T(8,128)(2,1)} async-done(((bf16[24,1536]{1,0:T(8,128)(2,1)}), bf16[384,1536]{1,0:T(8,128)(2,1)}) %all-gather.7.cloned.1.call-update) | async-done | bytes 1179664 | tf_op jit(solution)/shard_map/all_gather | solution.py:755
  272.3 8.5 %logits.1.__ = f32[16,128]{1,0:T(8,128)} custom-call(s32[5]{0:T(128)} %stack.28.info, bf16[384,1536]{1,0:T(8,128)(2,1)} %all-gather.7.cloned.1.call-done.parts_any, f32[1536]{0:T(1024)} %gain_ref.3, s32[16,1]{1,0:T(8,128)} %copy.23.target_ref, bf16[2048,1536]{1,0:T(8,128)(2,1)} %unembed_any.1), custom_call_target="tpu_custom_call" | custom-call | tf_op jit(solution)/shard_map/logits/pallas_call | solution.py:807
  280.8 0.7 slice_bitcast_fusion
  281.5 0.1 copy.24
  281.6 0.0 all-to-all-done.3
  281.6 0.0 copy-start.4
  281.6 1.3 copy-done.4
  282.9 0.0 copy-start.7
  282.9 4.7 %combine.1 = (bf16[128,1536]{1,0:T(8,128)(2,1)}, f32[1,128]{1,0:T(1,128)}) custom-call(s32[5]{0:T(128)} %stack.28.info, bf16[384,640]{1,0:T(8,128)(2,1)} %get-tuple-element.22.mix_any, bf16[640,1536]{1,0:T(8,128)(2,1)} %bitcast.44, f32[128,1536]{1,0:T(8,128)} %first.1.base_any, bf16[3,1536,1024]{2,1,0:T(8,128)(2,1)} %place.1._, f32[16,128]{1,0:T(8,128)} %logits.1.__), custom_call_target="tpu_custom_call" | custom-call | tf_op jit(solution)/shard_map/combine/pallas_call | solution.py:825
  287.6 0.7 pad_maximum_fusion
  288.3 11.8 %all_to_all.30 = f32[16,3,16]{2,1,0:T(4,128)S(1)} all-to-all(f32[16,3,16]{2,1,0:T(4,128)S(1)} %broadcast_in_dim.15), channel_id=1, replica_groups=mesh['blk'=16,'rep'=2] {'blk'}, dimensions={0} | all-to-all | bytes 6144 | tf_op jit(solution)/shard_map/all_to_all | solution.py:845
  300.1 0.0 copy-done.7
  300.2 0.6 pad_maximum_fusion.1
  (9 shorter events, 0.1 us)
Async XLA Ops:
  7.2 122.0 %all-gather.5.cloned.1.call-start = ((), (), s32[]{:S(2)}) async-start(), calls=%async_computation.6 | async-start | bytes 7241728 | tf_op jit(solution)/shard_map/all_gather | solution.py:656
  13.5 59.5 %all-to-all-start = ((bf16[16,96,512]{2,1,0:T(8,128)(2,1)}), bf16[16,96,512]{2,1,0:T(8,128)(2,1)S(1)}, u32[]{:S(2)}, u32[]{:S(2)}) async-start(bf16[16,96,512]{2,1,0:T(8,128)(2,1)} %cast.3), calls=%async_computation | async-start | bytes 3145728 | tf_op jit(solution)/shard_map/all_to_all | solution.py:614
  73.0 6.1 %copy-start.3 = (bf16[16,96,512]{2,1,0:T(8,128)(2,1)}, bf16[16,96,512]{2,1,0:T(8,128)(2,1)S(1)}, u32[]{:S(2)}) copy-start(bf16[16,96,512]{2,1,0:T(8,128)(2,1)S(1)} %all-to-all-done) | copy-start | bytes 4718596
  73.0 44.1 %all-to-all-start.1 = ((bf16[16,96,512]{2,1,0:T(8,128)(2,1)}), bf16[16,96,512]{2,1,0:T(8,128)(2,1)}, u32[]{:S(2)}, u32[]{:S(2)}) async-start(bf16[16,96,512]{2,1,0:T(8,128)(2,1)} %cast.4), calls=%async_computation.1 | async-start | bytes 3145728 | tf_op jit(solution)/shard_map/all_to_all | solution.py:614
  79.1 36.7 %collective-permute-start = (bf16[1536,512]{1,0:T(8,128)(2,1)S(1)}, bf16[1536,512]{1,0:T(8,128)(2,1)S(1)}, u32[]{:S(2)}, u32[]{:S(2)}) collective-permute-start(bf16[1536,512]{1,0:T(8,128)(2,1)S(1)} %bitcast.38), channel_id=1, source_target_pairs={{0,1},{1,0},{2,3},{3,2},{4,5},{5,4},{6,7},{7,6},{8,9},{9,8},{10,11... | collective-permute-start | bytes 4718600 | tf_op jit(solution)/shard_map/ppermute | solution.py:618
  115.8 1.2 copy-start.1
  117.1 10.1 %copy-start.6 = (s32[16]{0:T(128)S(1)}, s32[16]{0:T(128)}, u32[]{:S(2)}) copy-start(s32[16]{0:T(128)} %lengths_ref.5) | copy-start | bytes 196
  117.1 40.5 %all-to-all-start.2 = ((bf16[16,96,512]{2,1,0:T(8,128)(2,1)}), bf16[16,96,512]{2,1,0:T(8,128)(2,1)S(1)}, u32[]{:S(2)}, u32[]{:S(2)}) async-start(bf16[16,96,512]{2,1,0:T(8,128)(2,1)} %tie.3), calls=%async_computation.2 | async-start | bytes 3145728 | tf_op jit(solution)/shard_map/all_to_all | solution.py:614
  125.6 82.6 %all-gather.9.cloned.1.call-start = ((), (), s32[]{:S(2)}) async-start(), calls=%async_computation.8 | async-start | bytes 4718592 | tf_op jit(solution)/shard_map/all_gather | solution.py:705
  125.7 37.5 %collective-permute-start.1 = (bf16[1536,512]{1,0:T(8,128)(2,1)}, bf16[1536,512]{1,0:T(8,128)(2,1)S(1)}, u32[]{:S(2)}, u32[]{:S(2)}) collective-permute-start(bf16[1536,512]{1,0:T(8,128)(2,1)} %bitcast.11.u_ref.u_own), channel_id=1, source_target_pairs={{0,1},{1,0},{2,3},{3,2},{4,5},{5,4},{6,7},{7,6},{8,9},{9,8},{10,11... | collective-permute-start | bytes 4718600 | tf_op jit(solution)/shard_map/ppermute | solution.py:618
  157.6 1.1 copy-start
  163.1 1.2 copy-start.2
  164.3 50.2 %all-to-all-start.4 = ((bf16[16,32,1536]{2,1,0:T(8,128)(2,1)}), bf16[16,32,1536]{2,1,0:T(8,128)(2,1)S(1)}, u32[]{:S(2)}, u32[]{:S(2)}) async-start(bf16[16,32,1536]{2,1,0:T(8,128)(2,1)} %bitcast.37), calls=%async_computation.4 | async-start | bytes 3145728 | tf_op jit(solution)/shard_map/all_to_all | solution.py:687
  214.5 1.1 copy-start.5
  214.5 8.4 %copy-start.8 = (s32[16]{0:T(128)S(1)}, s32[16]{0:T(128)}, u32[]{:S(2)}) copy-start(s32[16]{0:T(128)} %param.18) | copy-start | bytes 196
  215.7 65.9 %all-to-all-start.3 = ((bf16[16,40,1536]{2,1,0:T(8,128)(2,1)}), bf16[16,40,1536]{2,1,0:T(8,128)(2,1)S(1)}, u32[]{:S(2)}, u32[]{:S(2)}) async-start(bf16[16,40,1536]{2,1,0:T(8,128)(2,1)} %bitcast.43), calls=%async_computation.3 | async-start | bytes 3932160 | tf_op jit(solution)/shard_map/all_to_all | solution.py:687
  221.3 51.0 %all-gather.7.cloned.1.call-start = ((), (), s32[]{:S(2)}) async-start(), calls=%async_computation.7 | async-start | bytes 1253376 | tf_op jit(solution)/shard_map/all_gather | solution.py:755
  281.6 1.3 copy-start.4
  282.9 17.2 %copy-start.7 = (s32[16]{0:T(128)S(1)}, s32[16]{0:T(128)}, u32[]{:S(2)}) copy-start(s32[16]{0:T(128)} %lengths_ref.5) | copy-start | bytes 196
Sparse Core Ops, SparseCore 0:
  10.4 95.2 all-gather.4
  158.9 49.3 all-gather.8
  223.7 48.5 all-gather.6

commit v17 on v15

--- a/solution.py
+++ b/solution.py
@@ -16,7 +16,7 @@
 GROUPS = 4
 RING = (0, 1, 4, 5, 8, 9, 12, 13, 14, 15, 10, 11, 6, 7, 2, 3)
 LANES = 128
-VMEM = 56 * 1024 * 1024
+VMEM = 63 * 1024 * 1024
 
 
 def merged(x, axis, combine):

time: 299 us -> 299 us (level)
  local copies, waits for them, and re-layouts: 7.9 us -> 1.9 us
  waiting for transfers between devices: 153 us -> 156 us
    unnamed x22 -> x10, local copies, waits for them, and re-layouts: 5.99 us -> 0.02 us
  transfers between devices with their start and end apart: 10 -> 10, of which waited for: 5 -> 7; matrix products, arithmetic and copies ran while one was open for 3% -> 3% of each run, Pallas kernels for 19% -> 19%
where the time goes in v17:
time: 299 us; the launch traced here: 298 us
  waiting for transfers between devices  156 us (52%)
  Pallas kernels  65.2 us (22%)
  starting transfers between devices  40.3 us (13%)
  between operations  13.9 us (5%)
  blocking collectives  12.3 us (4%)
  matrix products  5.19 us (2%)
    all_to_all x3, waiting for transfers between devices, moved(): own = lax.all_to_all(x, 'blk', split_axis=0, concat_axis=0, tiled=True)  67 us
    ppermute x2, waiting for transfers between devices, swapped(): return lax.ppermute(x, 'rep', [(0, 1), (1, 0)])  32.9 us
    all_gather x1, waiting for transfers between devices, paired(): lax.all_gather(last_part, 'blk', axis_index_groups=[list(RING)], axis=0)  31.6 us
    all_gather x1, waiting for transfers between devices, paired(): d_both = lax.all_gather(d_own, 'rep', axis=0)  24.7 us
    all_to_all x3, starting transfers between devices, moved(): own = lax.all_to_all(x, 'blk', split_axis=0, concat_axis=0, tiled=True)  22.8 us
    pallas_call x2, Pallas kernels, hidden_of(): pl.pallas_call(kernel, grid_spec=pltpu.PrefetchScalarGridSpec(num_scalar_...  21.7 us
    all_to_all x2, starting transfers between devices, returned(): x = lax.all_to_all(x, 'blk', split_axis=0, concat_axis=0, tiled=True)  14.2 us
    all_to_all x1, blocking collectives, everywhere(): lax.all_to_all(copies, 'blk', split_axis=0, concat_axis=0, tiled=True)  12.3 us
  transfers between devices with their start and end apart: 10, of which 7 were waited for; matrix products, arithmetic and copies ran while one was open for 3% of the time, Pallas kernels for 19%

profile of v17, /device:TPU:0, one launch (start us, length us, event | category | flops | bytes accessed | tf_op | source)
XLA Modules:
  0.0 298.0 jit_solution(17343325773362465860)
XLA Ops:
  7.2 0.0 all-gather.6.cloned.1.call-start
  7.2 3.0 %prep.1 = (bf16[128,1664]{1,0:T(8,128)(2,1)}, bf16[384,128]{1,0:T(8,128)(2,1)}) custom-call(s32[16]{0:T(128)} %lengths_ref.5, s32[1]{0:T(128)} %bitcast.3.blk_ref, bf16[128,1536]{1,0:T(8,128)(2,1)} %bitcast.40, s32[8,128]{1,0:T(8,128)} %bitcast.47, f32[8,128]{1,0:T(8,128)} %bitcast.48, f32[1536]{0:T(1024)} %gain_ref.1), custom_call_target="tpu_custom_call" | custom-call | tf_op jit(solution)/shard_map/prep/pallas_call | solution.py:588
  10.2 0.0 all-gather.6.cloned.1.call-update
  10.2 3.3 %cast.3 = bf16[16,96,512]{2,1,0:T(8,128)(2,1)} custom-call(f32[4608,512]{1,0:T(8,128)} %bitcast.33, bf16[128,1664]{1,0:T(8,128)(2,1)} %get-tuple-element.20.rank_ref.refs_0_), custom_call_target="tpu_custom_call" | custom-call | tf_op jit(solution)/shard_map/cast/pallas_call | solution.py:556
  13.5 7.4 %all-to-all-start = ((bf16[16,96,512]{2,1,0:T(8,128)(2,1)}), bf16[16,96,512]{2,1,0:T(8,128)(2,1)}, u32[]{:S(2)}, u32[]{:S(2)}) async-start(bf16[16,96,512]{2,1,0:T(8,128)(2,1)} %cast.3), calls=%async_computation | async-start | bytes 3145728 | tf_op jit(solution)/shard_map/all_to_all | solution.py:572
  21.0 3.3 %cast.4 = bf16[16,96,512]{2,1,0:T(8,128)(2,1)} custom-call(f32[4608,512]{1,0:T(8,128)} %bitcast.34), custom_call_target="tpu_custom_call" | custom-call | tf_op jit(solution)/shard_map/cast/pallas_call | solution.py:556
  24.2 48.8 %all-to-all-done = bf16[16,96,512]{2,1,0:T(8,128)(2,1)} async-done(((bf16[16,96,512]{2,1,0:T(8,128)(2,1)}), bf16[16,96,512]{2,1,0:T(8,128)(2,1)}, u32[]{:S(2)}, u32[]{:S(2)}) %all-to-all-start) | async-done | bytes 1572896 | tf_op jit(solution)/shard_map/all_to_all | solution.py:572
  73.0 6.1 %all-to-all-start.1 = ((bf16[16,96,512]{2,1,0:T(8,128)(2,1)}), bf16[16,96,512]{2,1,0:T(8,128)(2,1)}, u32[]{:S(2)}, u32[]{:S(2)}) async-start(bf16[16,96,512]{2,1,0:T(8,128)(2,1)} %cast.4), calls=%async_computation.1 | async-start | bytes 3145728 | tf_op jit(solution)/shard_map/all_to_all | solution.py:572
  79.2 1.6 collective-permute-start
  80.7 3.2 %cast.5.__0_ = bf16[16,96,512]{2,1,0:T(8,128)(2,1)} custom-call(f32[4608,512]{1,0:T(8,128)} %bitcast.35), custom_call_target="tpu_custom_call" | custom-call | tf_op jit(solution)/shard_map/cast/pallas_call | solution.py:556
  84.0 32.2 %collective-permute-done.__1_.g_ref.g_oth = bf16[1536,512]{1,0:T(8,128)(2,1)} collective-permute-done((bf16[1536,512]{1,0:T(8,128)(2,1)}, bf16[1536,512]{1,0:T(8,128)(2,1)}, u32[]{:S(2)}, u32[]{:S(2)}) %collective-permute-start) | collective-permute-done | bytes 1572896 | tf_op jit(solution)/shard_map/ppermute | solution.py:576
  116.2 0.0 copy-start.2
  116.2 0.3 all-to-all-done.1
  116.4 9.2 %all-to-all-start.2 = ((bf16[16,96,512]{2,1,0:T(8,128)(2,1)}), bf16[16,96,512]{2,1,0:T(8,128)(2,1)}, u32[]{:S(2)}, u32[]{:S(2)}) async-start(bf16[16,96,512]{2,1,0:T(8,128)(2,1)} %tie.3), calls=%async_computation.2 | async-start | bytes 3145728 | tf_op jit(solution)/shard_map/all_to_all | solution.py:572
  125.6 0.0 all-gather.8.cloned.1.call-start
  125.7 1.5 collective-permute-start.1
  127.2 0.0 copy-done.2
  127.2 0.6 dynamic_slice.3
  127.9 1.2 stack.36.info
  129.1 0.0 all-gather.6.cloned.1.call-done.x_ref
  129.1 10.6 %gate_up.2 = (bf16[640,512]{1,0:T(8,128)(2,1)}, bf16[640,128]{1,0:T(8,128)(2,1)}, f32[16,128]{1,0:T(8,128)}) custom-call(s32[5]{0:T(128)} %stack.36.info, s32[16]{0:T(128)} %lengths_ref.5, s32[16]{0:T(128)} %constant.33.clone.ring_ref, bf16[2048,1664]{1,0:T(8,128)(2,1)} %all-gather.6.cloned.1.call-done.x_ref, bf16[1536,512]{1,0:T(8,128)(2,1)} %bitcast.10.g_ref.g_own, ...), custom_call_target="tpu_custom_call" | custom-call | tf_op jit(solution)/shard_map/gate_up/pallas_call | solution.py:619
  139.7 17.9 %all-to-all-done.2 = bf16[16,96,512]{2,1,0:T(8,128)(2,1)} async-done(((bf16[16,96,512]{2,1,0:T(8,128)(2,1)}), bf16[16,96,512]{2,1,0:T(8,128)(2,1)}, u32[]{:S(2)}, u32[]{:S(2)}) %all-to-all-start.2) | async-done | bytes 1572896 | tf_op jit(solution)/shard_map/all_to_all | solution.py:572
  157.7 0.0 all-gather.8.cloned.1.call-update
  157.7 4.3 %own_down.1 = (bf16[512,1536]{1,0:T(8,128)(2,1)}, bf16[128,1536]{1,0:T(8,128)(2,1)}, f32[16,1536]{1,0:T(8,128)}) custom-call(bf16[640,512]{1,0:T(8,128)(2,1)} %get-tuple-element.23.__1_.hidden_any, f32[16,128]{1,0:T(8,128)} %get-tuple-element.24.share_any, bf16[1536,512]{1,0:T(8,128)(2,1)} %tie.4.d_any), custom_call_target="tpu_custom_call" | custom-call | tf_op jit(solution)/shard_map/own_down/pallas_call | solution.py:664
  162.0 0.7 collective-permute-done.1.__1_.u_ref.u_oth
  162.7 8.5 %all-to-all-start.4 = ((bf16[16,32,1536]{2,1,0:T(8,128)(2,1)}), bf16[16,32,1536]{2,1,0:T(8,128)(2,1)}, u32[]{:S(2)}, u32[]{:S(2)}) async-start(bf16[16,32,1536]{2,1,0:T(8,128)(2,1)} %bitcast.36), calls=%async_computation.4 | async-start | bytes 3145728 | tf_op jit(solution)/shard_map/all_to_all | solution.py:645
  171.2 0.2 all-gather.10.cloned.1.call-start
  171.4 11.1 %gate_up.3 = (bf16[656,512]{1,0:T(8,128)(2,1)}, f32[16,128]{1,0:T(8,128)}, f32[16,1536]{1,0:T(8,128)}) custom-call(s32[5]{0:T(128)} %stack.36.info, s32[16]{0:T(128)} %lengths_ref.5, s32[16]{0:T(128)} %constant.33.clone.ring_ref, bf16[2048,1664]{1,0:T(8,128)(2,1)} %all-gather.6.cloned.1.call-done.x_ref, ...), custom_call_target="tpu_custom_call" | custom-call | tf_op jit(solution)/shard_map/gate_up/pallas_call | solution.py:619
  182.5 24.7 %all-gather.8.cloned.1.call-done = bf16[3072,512]{1,0:T(8,128)(2,1)} async-done(((bf16[1536,512]{1,0:T(8,128)(2,1)}), bf16[3072,512]{1,0:T(8,128)(2,1)}) %all-gather.8.cloned.1.call-update) | async-done | bytes 3145744 | tf_op jit(solution)/shard_map/all_gather | solution.py:663
  207.2 6.3 %oth_down.1 = (bf16[640,1536]{1,0:T(8,128)(2,1)}, f32[16,1536]{1,0:T(8,128)}) custom-call(s32[5]{0:T(128)} %stack.36.info, bf16[656,512]{1,0:T(8,128)(2,1)} %get-tuple-element.26.hidden_any, f32[16,128]{1,0:T(8,128)} %get-tuple-element.27.share_any, bf16[640,128]{1,0:T(8,128)(2,1)} %get-tuple-element.28.spot_any, ...), custom_call_target="tpu_custom_call" | custom-call | tf_op jit(solution)/shard_map/oth_down/pallas_call | solution.py:689
  213.4 0.0 all-gather.10.cloned.1.call-update
  213.5 0.0 all-to-all-done.4
  213.5 5.7 %all-to-all-start.3 = ((bf16[16,40,1536]{2,1,0:T(8,128)(2,1)}), bf16[16,40,1536]{2,1,0:T(8,128)(2,1)}, u32[]{:S(2)}, u32[]{:S(2)}) async-start(bf16[16,40,1536]{2,1,0:T(8,128)(2,1)} %bitcast.39), calls=%async_computation.3 | async-start | bytes 3932160 | tf_op jit(solution)/shard_map/all_to_all | solution.py:645
  219.2 3.0 %mix.1 = (bf16[384,512]{1,0:T(8,128)(2,1)}, bf16[384,640]{1,0:T(8,128)(2,1)}) custom-call(s32[5]{0:T(128)} %stack.36.info, bf16[128,1664]{1,0:T(8,128)(2,1)} %get-tuple-element.20.rank_ref.refs_0_, bf16[384,128]{1,0:T(8,128)(2,1)} %get-tuple-element.21.pieces_ref), custom_call_target="tpu_custom_call" | custom-call | tf_op jit(solution)/shard_map/mix/pallas_call | solution.py:730
  222.2 4.0 %first.1.base_any = f32[128,1536]{1,0:T(8,128)} custom-call(bf16[384,512]{1,0:T(8,128)(2,1)} %get-tuple-element.33.mix_ref, bf16[512,1536]{1,0:T(8,128)(2,1)} %bitcast.17.back_ref, bf16[128,1536]{1,0:T(8,128)(2,1)} %bitcast.42), custom_call_target="tpu_custom_call" | custom-call | tf_op jit(solution)/shard_map/first/pallas_call | solution.py:753
  226.3 8.3 %place.1._ = bf16[3,1536,1024]{2,1,0:T(8,128)(2,1)} custom-call(s32[5]{0:T(128)} %stack.36.info, bf16[1536,512]{1,0:T(8,128)(2,1)} %bitcast.10.g_ref.g_own, bf16[1536,512]{1,0:T(8,128)(2,1)} %collective-permute-done.__1_.g_ref.g_oth, bf16[1536,512]{1,0:T(8,128)(2,1)} %bitcast.11.u_ref.u_own, bf16[1536,512]{1,0:T(8,128)(2,1)} %collective-permute-done.1.__1_.u_ref.u_oth, ...), custom_call_target="tpu_custom_call" | custom-call | tf_op jit(solution)/shard_map/place/pallas_call | solution.py:716
  234.5 0.0 copy-start
  234.5 0.0 copy-start.4
  234.5 31.6 %all-gather.10.cloned.1.call-done = f32[256,1536]{1,0:T(8,128)} async-done(((f32[16,1536]{1,0:T(8,128)}), f32[256,1536]{1,0:T(8,128)}) %all-gather.10.cloned.1.call-update) | async-done | bytes 1572880 | tf_op jit(solution)/shard_map/all_gather | solution.py:713
  266.1 1.5 reduce_sum.36
  267.6 0.1 multiply_reduce_fusion
  267.7 0.0 copy-done
  267.7 0.0 copy-done.4
  267.7 5.2 %select_reduce_fusion = (f32[16]{0:T(128)S(1)}, f32[16]{0:T(128)}) fusion(s32[2048]{0:T(1024)S(1)} %iota_add_fusion, s32[16]{0:T(128)S(1)} %copy-done.4, bf16[2048,1536]{1,0:T(8,128)(2,1)} %param.16, f32[16,1536]{1,0:T(8,128)S(1)} %reduce_sum.36, f32[1536]{0:T(1024)S(1)} %copy-done, f32[16]{0:T(128)S(1)} %add_rsqrt_fusion), kind=kOutput, calls=%fused_computation | convolution fusion | flops 100892640 | bytes 6404352 | tf_op jit(solution)/shard_map/dot_general | solution.py:768
  272.9 0.0 all-to-all-done.3
  272.9 0.0 copy-start.1
  272.9 0.0 copy-start.3
  272.9 4.8 %combine.1 = (bf16[128,1536]{1,0:T(8,128)(2,1)}, f32[1,128]{1,0:T(1,128)}) custom-call(s32[5]{0:T(128)} %stack.36.info, bf16[384,640]{1,0:T(8,128)(2,1)} %get-tuple-element.22.mix_any, bf16[640,1536]{1,0:T(8,128)(2,1)} %bitcast.15.back_any, f32[128,1536]{1,0:T(8,128)} %first.1.base_any, bf16[3,1536,1024]{2,1,0:T(8,128)(2,1)} %place.1._, f32[1,16]{1,0:T(1,128)} %bitcast.45), custom_call_target="tpu_custom_call" | custom-call | tf_op jit(solution)/shard_map/combine/pallas_call | solution.py:778
  277.7 0.7 compare_select_fusion
  278.4 0.0 copy-done.1
  278.4 12.3 %all_to_all.30 = f32[16,3,16]{2,1,0:T(4,128)S(1)} all-to-all(f32[16,3,16]{2,1,0:T(4,128)S(1)} %broadcast_in_dim.29), channel_id=1, replica_groups=mesh['blk'=16,'rep'=2] {'blk'}, dimensions={0} | all-to-all | bytes 6144 | tf_op jit(solution)/shard_map/all_to_all | solution.py:798
  290.8 0.0 copy-done.3
  290.9 0.6 pad_maximum_fusion.1
  (12 shorter events, 0.1 us)
Async XLA Ops:
  7.2 121.9 %all-gather.6.cloned.1.call-start = ((), (), s32[]{:S(2)}) async-start(), calls=%async_computation.6 | async-start | bytes 7241728 | tf_op jit(solution)/shard_map/all_gather | solution.py:614
  13.5 59.5 %all-to-all-start = ((bf16[16,96,512]{2,1,0:T(8,128)(2,1)}), bf16[16,96,512]{2,1,0:T(8,128)(2,1)}, u32[]{:S(2)}, u32[]{:S(2)}) async-start(bf16[16,96,512]{2,1,0:T(8,128)(2,1)} %cast.3), calls=%async_computation | async-start | bytes 3145728 | tf_op jit(solution)/shard_map/all_to_all | solution.py:572
  73.0 43.4 %all-to-all-start.1 = ((bf16[16,96,512]{2,1,0:T(8,128)(2,1)}), bf16[16,96,512]{2,1,0:T(8,128)(2,1)}, u32[]{:S(2)}, u32[]{:S(2)}) async-start(bf16[16,96,512]{2,1,0:T(8,128)(2,1)} %cast.4), calls=%async_computation.1 | async-start | bytes 3145728 | tf_op jit(solution)/shard_map/all_to_all | solution.py:572
  79.2 37.0 %collective-permute-start = (bf16[1536,512]{1,0:T(8,128)(2,1)}, bf16[1536,512]{1,0:T(8,128)(2,1)}, u32[]{:S(2)}, u32[]{:S(2)}) collective-permute-start(bf16[1536,512]{1,0:T(8,128)(2,1)} %bitcast.10.g_ref.g_own), channel_id=1, source_target_pairs={{0,1},{1,0},{2,3},{3,2},{4,5},{5,4},{6,7},{7,6},{8,9},{9,8},{10,11... | collective-permute-start | bytes 4718600 | tf_op jit(solution)/shard_map/ppermute | solution.py:576
  116.2 11.1 %copy-start.2 = (s32[16]{0:T(128)S(1)}, s32[16]{0:T(128)}, u32[]{:S(2)}) copy-start(s32[16]{0:T(128)} %lengths_ref.5) | copy-start | bytes 196
  116.4 41.2 %all-to-all-start.2 = ((bf16[16,96,512]{2,1,0:T(8,128)(2,1)}), bf16[16,96,512]{2,1,0:T(8,128)(2,1)}, u32[]{:S(2)}, u32[]{:S(2)}) async-start(bf16[16,96,512]{2,1,0:T(8,128)(2,1)} %tie.3), calls=%async_computation.2 | async-start | bytes 3145728 | tf_op jit(solution)/shard_map/all_to_all | solution.py:572
  125.6 81.5 %all-gather.8.cloned.1.call-start = ((), (), s32[]{:S(2)}) async-start(), calls=%async_computation.7 | async-start | bytes 4718592 | tf_op jit(solution)/shard_map/all_gather | solution.py:663
  125.7 37.0 %collective-permute-start.1 = (bf16[1536,512]{1,0:T(8,128)(2,1)}, bf16[1536,512]{1,0:T(8,128)(2,1)}, u32[]{:S(2)}, u32[]{:S(2)}) collective-permute-start(bf16[1536,512]{1,0:T(8,128)(2,1)} %bitcast.11.u_ref.u_own), channel_id=1, source_target_pairs={{0,1},{1,0},{2,3},{3,2},{4,5},{5,4},{6,7},{7,6},{8,9},{9,8},{10,11... | collective-permute-start | bytes 4718600 | tf_op jit(solution)/shard_map/ppermute | solution.py:576
  162.7 50.8 %all-to-all-start.4 = ((bf16[16,32,1536]{2,1,0:T(8,128)(2,1)}), bf16[16,32,1536]{2,1,0:T(8,128)(2,1)}, u32[]{:S(2)}, u32[]{:S(2)}) async-start(bf16[16,32,1536]{2,1,0:T(8,128)(2,1)} %bitcast.36), calls=%async_computation.4 | async-start | bytes 3145728 | tf_op jit(solution)/shard_map/all_to_all | solution.py:645
  171.2 94.9 %all-gather.10.cloned.1.call-start = ((), (), s32[]{:S(2)}) async-start(), calls=%async_computation.8 | async-start | bytes 1671168 | tf_op jit(solution)/shard_map/all_gather | solution.py:713
  213.5 59.4 %all-to-all-start.3 = ((bf16[16,40,1536]{2,1,0:T(8,128)(2,1)}), bf16[16,40,1536]{2,1,0:T(8,128)(2,1)}, u32[]{:S(2)}, u32[]{:S(2)}) async-start(bf16[16,40,1536]{2,1,0:T(8,128)(2,1)} %bitcast.39), calls=%async_computation.3 | async-start | bytes 3932160 | tf_op jit(solution)/shard_map/all_to_all | solution.py:645
  234.5 33.2 %copy-start = (f32[1536]{0:T(1024)S(1)}, f32[1536]{0:T(1024)}, u32[]{:S(2)}) copy-start(f32[1536]{0:T(1024)} %param.17) | copy-start | bytes 18436
  234.5 33.2 %copy-start.4 = (s32[16]{0:T(128)S(1)}, s32[16]{0:T(128)}, u32[]{:S(2)}) copy-start(s32[16]{0:T(128)} %param.18) | copy-start | bytes 196
  272.9 5.5 %copy-start.1 = (f32[16]{0:T(128)S(1)}, f32[16]{0:T(128)}, u32[]{:S(2)}) copy-start(f32[16]{0:T(128)} %get-tuple-element.38) | copy-start | bytes 196
  272.9 17.9 %copy-start.3 = (s32[16]{0:T(128)S(1)}, s32[16]{0:T(128)}, u32[]{:S(2)}) copy-start(s32[16]{0:T(128)} %lengths_ref.5) | copy-start | bytes 196
Sparse Core Ops, SparseCore 0:
  10.4 95.0 all-gather.5
  157.8 49.3 all-gather.7
  213.6 52.4 all-gather.9

commit v18 on v17

--- a/solution.py
+++ b/solution.py
@@ -180,6 +180,14 @@
         value = piece.astype(jnp.float32)
         told = jnp.where(column >= (k + 1) * EXPERTS, value, told)
         weight = weight - value
+    is_last = iota(x.shape, 0) == length - 1
+    last = jnp.sum(jnp.where(is_last, x, 0.0), axis=0, keepdims=True)
+    place = iota((EXPERTS, LANES), 0)
+    packed = jnp.zeros((EXPERTS, LANES), jnp.float32)
+    for k in range(width // LANES):
+        packed = jnp.where(place == k, last[:, k * LANES : (k + 1) * LANES], packed)
+    packed = jnp.concatenate([jnp.zeros((3 * EXPERTS, LANES), jnp.float32), packed], axis=0)
+    told = jnp.where(column >= 3 * EXPERTS, jnp.transpose(packed), told)
     rows_ref[:, width:] = told.astype(jnp.bfloat16)
 
 
@@ -222,7 +230,7 @@
 def share_of(info, which, lasts, width):
     ext = lasts[:, width:]
     lane = iota(ext.shape, 1)
-    is_own = (lane >= EXPERTS) & ((lane & (EXPERTS - 1)) == info[which])
+    is_own = (lane == EXPERTS + info[which]) | (lane == 2 * EXPERTS + info[which])
     return jnp.broadcast_to(
         jnp.sum(jnp.where(is_own, ext, 0.0), axis=1, keepdims=True), ext.shape
     )
@@ -284,7 +292,6 @@
     x_ref,
     g_ref,
     u_ref,
-    resid_ref,
     _,
     out_ref,
     share_ref,
@@ -300,20 +307,26 @@
     def place(source, rank):
         return source * SECOND + (SECOND - CAP) + rank
 
+    @pl.when(step == 0)
+    def _():
+        base_ref[...] = jnp.zeros_like(base_ref)
+
     chosen = pick(info, lengths_ref, ring_ref, 1, x_ref, width, place, sources * SECOND, lasts)
     for s in range(sources):
         start = pl.multiple_of(ring_ref[step * sources + s] * SECOND, SECOND)
         picked[pl.ds(start, SECOND), :] = chosen[s * SECOND : (s + 1) * SECOND]
+        ext = x_ref[s * LEN : (s + 1) * LEN, width:].astype(jnp.float32)
+        packed = jnp.transpose(ext)[3 * EXPERTS :]
+        mine = iota((base_ref.shape[0], LANES), 0) == ring_ref[step * sources + s]
+        for k in range(width // LANES):
+            lanes = slice(k * LANES, (k + 1) * LANES)
+            base_ref[:, lanes] = jnp.where(mine, packed[k : k + 1], base_ref[:, lanes])
 
     @pl.when(step == GROUPS - 1)
     def _():
         picked[all_rows:, :] = lasts[:, :width]
         out_ref[...] = activ(picked[...], g_ref, u_ref)
         share_ref[...] = share_of(info, 1, lasts, width)
-        resid = resid_ref[...].astype(jnp.float32)
-        is_last = iota(resid.shape, 0) == info[3] - 1
-        last = jnp.sum(jnp.where(is_last, resid, 0.0), axis=0, keepdims=True)
-        base_ref[...] = jnp.where(iota(base_ref.shape, 0) == info[4], last, 0.0)
 
 
 def matmul_nt(hidden_ref, d):
@@ -372,7 +385,6 @@
     share_any,
     spot_any,
     late_any,
-    base_any,
     part_any,
     d_any,
     out_any,
@@ -381,7 +393,6 @@
     share,
     spot,
     late,
-    base,
     part,
     d,
     out,
@@ -392,8 +403,8 @@
     rows = out_any.shape[0]
     copy = pltpu.make_async_copy
     other = 1 - info[2]
-    sources = (hidden_any, share_any, spot_any, late_any, base_any, part_any)
-    targets = (hidden, share, spot, late, base, part)
+    sources = (hidden_any, share_any, spot_any, late_any, part_any)
+    targets = (hidden, share, spot, late, part)
     downs = started(
         [
             copy(d_any.at[other, k * size : (k + 1) * size], d.at[k], sems.at[1, k])
@@ -410,7 +421,7 @@
         value = matmul_nt(hidden, d[k])
         out[k] = (placed + value[:rows]).astype(jnp.bfloat16)
         last = value[rows:].astype(jnp.bfloat16).astype(jnp.float32)
-        total[k] = base[:, columns] + part[:, columns] + share[:, :1] * last
+        total[k] = (part[:, columns] + share[:, :1] * last).astype(jnp.bfloat16)
         stores += started(
             [
                 copy(total.at[k], sum_any.at[:, columns], sems.at[3, k]),
@@ -679,19 +690,19 @@
     )(own_hidden, own_share, d_own)
     own_out = tied(own_out, u_oth)
     own_back = returned(own_out)
-    oth_hidden, oth_share, base_part = hidden_of(
+    oth_hidden, oth_share, resid_last = hidden_of(
         oth_kernel,
         [bf16(second + blk_count, FF), f32(blk_count, LANES), f32(blk_count, width)],
         second + blk_count,
-        (g_oth, u_oth, resid, own_out),
-        [whole((rows, width)), anywhere],
+        (g_oth, u_oth, own_out),
+        [anywhere],
     )
     oth_out, last_part = pl.pallas_call(
         oth_down_kernel,
         grid_spec=pltpu.PrefetchScalarGridSpec(
             num_scalar_prefetch=1,
             grid=(1,),
-            in_specs=[anywhere] * 7,
+            in_specs=[anywhere] * 6,
             out_specs=[anywhere] * 2,
             scratch_shapes=[
                 pltpu.VMEM((second + blk_count, FF), jnp.bfloat16),
@@ -699,17 +710,16 @@
                 pltpu.VMEM((second, extra), jnp.bfloat16),
                 pltpu.VMEM((extra, width), jnp.bfloat16),
                 pltpu.VMEM((blk_count, width), jnp.float32),
-                pltpu.VMEM((blk_count, width), jnp.float32),
                 pltpu.VMEM((4, quarter, FF), jnp.bfloat16),
                 pltpu.VMEM((4, second, quarter), jnp.bfloat16),
-                pltpu.VMEM((4, blk_count, quarter), jnp.float32),
+                pltpu.VMEM((4, blk_count, quarter), jnp.bfloat16),
                 pltpu.SemaphoreType.DMA((4, 6)),
             ],
         ),
-        out_shape=[bf16(second, width), f32(blk_count, width)],
+        out_shape=[bf16(second, width), bf16(blk_count, width)],
         compiler_params=params(),
         name="oth_down",
-    )(info, oth_hidden, oth_share, spot, late_out, base_part, own_part, d_both)
+    )(info, oth_hidden, oth_share, spot, late_out, own_part, d_both)
     last_parts = lax.all_gather(last_part, "blk", axis_index_groups=[list(RING)], axis=0)
     oth_back = returned(oth_out)
 
@@ -759,7 +769,9 @@
         compiler_params=params(),
         name="first",
     )(first_mix, own_back, resid)
-    last_rows = lax.reduce_precision(jnp.sum(last_parts, axis=0), 8, 7)
+    last_rows = lax.reduce_precision(
+        resid_last + jnp.sum(last_parts.astype(jnp.float32), axis=0), 8, 7
+    )
     final = (
         last_rows
         * lax.rsqrt(jnp.mean(last_rows * last_rows, axis=-1, keepdims=True) + 1e-05)

time: 299 us -> 306 us (1.023)
  blocking collectives: 12.3 us -> 51.7 us
  waiting for transfers between devices: 156 us -> 125 us
    all_gather x0 -> x1, blocking collectives: none -> 41.5 us  [paired(): lax.all_gather(last_part, 'blk', axis_index_groups=[list(RING)], axis=0)]
    all_gather x1 -> x0, waiting for transfers between devices: 31.6 us -> none  [paired(): lax.all_gather(last_part, 'blk', axis_index_groups=[list(RING)], axis=0)]
  transfers between devices with their start and end apart: 10 -> 9, of which waited for: 7 -> 6; matrix products, arithmetic and copies ran while one was open for 3% -> 2% of each run, Pallas kernels for 19% -> 19%
where the time goes in v18:
time: 306 us; the launch traced here: 305 us
  waiting for transfers between devices  125 us (41%)
  Pallas kernels  65.3 us (21%)
  blocking collectives  51.7 us (17%)
  starting transfers between devices  40.1 us (13%)
  between operations  14.2 us (5%)
  matrix products  5.18 us (2%)
    all_to_all x3, waiting for transfers between devices, moved(): own = lax.all_to_all(x, 'blk', split_axis=0, concat_axis=0, tiled=True)  67 us
    all_gather x1, blocking collectives, paired(): lax.all_gather(last_part, 'blk', axis_index_groups=[list(RING)], axis=0)  41.5 us
    ppermute x2, waiting for transfers between devices, swapped(): return lax.ppermute(x, 'rep', [(0, 1), (1, 0)])  32.9 us
    all_gather x1, waiting for transfers between devices, paired(): d_both = lax.all_gather(d_own, 'rep', axis=0)  24.9 us
    all_to_all x3, starting transfers between devices, moved(): own = lax.all_to_all(x, 'blk', split_axis=0, concat_axis=0, tiled=True)  22.8 us
    pallas_call x2, Pallas kernels, hidden_of(): pl.pallas_call(kernel, grid_spec=pltpu.PrefetchScalarGridSpec(num_scalar_...  21.8 us
    all_to_all x2, starting transfers between devices, returned(): x = lax.all_to_all(x, 'blk', split_axis=0, concat_axis=0, tiled=True)  14.1 us
    all_to_all x1, blocking collectives, everywhere(): lax.all_to_all(copies, 'blk', split_axis=0, concat_axis=0, tiled=True)  10.2 us
  transfers between devices with their start and end apart: 9, of which 6 were waited for; matrix products, arithmetic and copies ran while one was open for 2% of the time, Pallas kernels for 19%

profile of v18, /device:TPU:0, one launch (start us, length us, event | category | flops | bytes accessed | tf_op | source)
XLA Modules:
  0.0 304.9 jit_solution(14182401091966671396)
XLA Ops:
  7.2 0.0 all-gather.5.cloned.1.call-start
  7.2 3.1 %prep.1 = (bf16[128,1664]{1,0:T(8,128)(2,1)}, bf16[384,128]{1,0:T(8,128)(2,1)}) custom-call(s32[16]{0:T(128)} %lengths_ref.5, s32[1]{0:T(128)} %bitcast.3.blk_ref, bf16[128,1536]{1,0:T(8,128)(2,1)} %bitcast.42, s32[8,128]{1,0:T(8,128)} %bitcast.47, f32[8,128]{1,0:T(8,128)} %bitcast.48, f32[1536]{0:T(1024)} %gain_ref.1), custom_call_target="tpu_custom_call" | custom-call | tf_op jit(solution)/shard_map/prep/pallas_call | solution.py:599
  10.3 0.0 all-gather.5.cloned.1.call-update
  10.3 3.2 %cast.3 = bf16[16,96,512]{2,1,0:T(8,128)(2,1)} custom-call(f32[4608,512]{1,0:T(8,128)} %bitcast.34, bf16[128,1664]{1,0:T(8,128)(2,1)} %get-tuple-element.20.rank_ref.refs_0_), custom_call_target="tpu_custom_call" | custom-call | tf_op jit(solution)/shard_map/cast/pallas_call | solution.py:567
  13.6 7.4 %all-to-all-start = ((bf16[16,96,512]{2,1,0:T(8,128)(2,1)}), bf16[16,96,512]{2,1,0:T(8,128)(2,1)}, u32[]{:S(2)}, u32[]{:S(2)}) async-start(bf16[16,96,512]{2,1,0:T(8,128)(2,1)} %cast.3), calls=%async_computation | async-start | bytes 3145728 | tf_op jit(solution)/shard_map/all_to_all | solution.py:583
  21.0 3.3 %cast.4 = bf16[16,96,512]{2,1,0:T(8,128)(2,1)} custom-call(f32[4608,512]{1,0:T(8,128)} %bitcast.35), custom_call_target="tpu_custom_call" | custom-call | tf_op jit(solution)/shard_map/cast/pallas_call | solution.py:567
  24.3 48.8 %all-to-all-done = bf16[16,96,512]{2,1,0:T(8,128)(2,1)} async-done(((bf16[16,96,512]{2,1,0:T(8,128)(2,1)}), bf16[16,96,512]{2,1,0:T(8,128)(2,1)}, u32[]{:S(2)}, u32[]{:S(2)}) %all-to-all-start) | async-done | bytes 1572896 | tf_op jit(solution)/shard_map/all_to_all | solution.py:583
  73.1 6.2 %all-to-all-start.1 = ((bf16[16,96,512]{2,1,0:T(8,128)(2,1)}), bf16[16,96,512]{2,1,0:T(8,128)(2,1)}, u32[]{:S(2)}, u32[]{:S(2)}) async-start(bf16[16,96,512]{2,1,0:T(8,128)(2,1)} %cast.4), calls=%async_computation.1 | async-start | bytes 3145728 | tf_op jit(solution)/shard_map/all_to_all | solution.py:583
  79.3 1.5 collective-permute-start
  80.8 3.2 %cast.5.__0_ = bf16[16,96,512]{2,1,0:T(8,128)(2,1)} custom-call(f32[4608,512]{1,0:T(8,128)} %bitcast.36), custom_call_target="tpu_custom_call" | custom-call | tf_op jit(solution)/shard_map/cast/pallas_call | solution.py:567
  84.1 32.2 %collective-permute-done.__1_.g_ref.g_oth = bf16[1536,512]{1,0:T(8,128)(2,1)} collective-permute-done((bf16[1536,512]{1,0:T(8,128)(2,1)}, bf16[1536,512]{1,0:T(8,128)(2,1)}, u32[]{:S(2)}, u32[]{:S(2)}) %collective-permute-start) | collective-permute-done | bytes 1572896 | tf_op jit(solution)/shard_map/ppermute | solution.py:587
  116.3 0.0 copy-start.4
  116.3 0.3 all-to-all-done.1
  116.5 9.2 %all-to-all-start.2 = ((bf16[16,96,512]{2,1,0:T(8,128)(2,1)}), bf16[16,96,512]{2,1,0:T(8,128)(2,1)}, u32[]{:S(2)}, u32[]{:S(2)}) async-start(bf16[16,96,512]{2,1,0:T(8,128)(2,1)} %tie.3), calls=%async_computation.2 | async-start | bytes 3145728 | tf_op jit(solution)/shard_map/all_to_all | solution.py:583
  125.7 0.0 all-gather.7.cloned.1.call-start
  125.8 1.5 collective-permute-start.1
  127.3 0.0 copy-done.4
  127.3 0.6 dynamic_slice.3
  127.9 1.2 stack.36.info
  129.1 0.0 all-gather.5.cloned.1.call-done.x_ref
  129.1 10.6 %gate_up.2 = (bf16[640,512]{1,0:T(8,128)(2,1)}, bf16[640,128]{1,0:T(8,128)(2,1)}, f32[16,128]{1,0:T(8,128)}) custom-call(s32[5]{0:T(128)} %stack.36.info, s32[16]{0:T(128)} %lengths_ref.5, s32[16]{0:T(128)} %constant.33.clone.ring_ref, bf16[2048,1664]{1,0:T(8,128)(2,1)} %all-gather.5.cloned.1.call-done.x_ref, bf16[1536,512]{1,0:T(8,128)(2,1)} %bitcast.10.g_ref.g_own, ...), custom_call_target="tpu_custom_call" | custom-call | tf_op jit(solution)/shard_map/gate_up/pallas_call | solution.py:630
  139.8 18.0 %all-to-all-done.2 = bf16[16,96,512]{2,1,0:T(8,128)(2,1)} async-done(((bf16[16,96,512]{2,1,0:T(8,128)(2,1)}), bf16[16,96,512]{2,1,0:T(8,128)(2,1)}, u32[]{:S(2)}, u32[]{:S(2)}) %all-to-all-start.2) | async-done | bytes 1572896 | tf_op jit(solution)/shard_map/all_to_all | solution.py:583
  157.8 0.0 all-gather.7.cloned.1.call-update
  157.8 4.3 %own_down.1 = (bf16[512,1536]{1,0:T(8,128)(2,1)}, bf16[128,1536]{1,0:T(8,128)(2,1)}, f32[16,1536]{1,0:T(8,128)}) custom-call(bf16[640,512]{1,0:T(8,128)(2,1)} %get-tuple-element.23.__1_.hidden_any, f32[16,128]{1,0:T(8,128)} %get-tuple-element.24.share_any, bf16[1536,512]{1,0:T(8,128)(2,1)} %tie.4.d_any), custom_call_target="tpu_custom_call" | custom-call | tf_op jit(solution)/shard_map/own_down/pallas_call | solution.py:675
  162.1 0.7 collective-permute-done.1.__1_.u_ref.u_oth
  162.8 8.5 %all-to-all-start.4 = ((bf16[16,32,1536]{2,1,0:T(8,128)(2,1)}), bf16[16,32,1536]{2,1,0:T(8,128)(2,1)}, u32[]{:S(2)}, u32[]{:S(2)}) async-start(bf16[16,32,1536]{2,1,0:T(8,128)(2,1)} %bitcast.37), calls=%async_computation.4 | async-start | bytes 3145728 | tf_op jit(solution)/shard_map/all_to_all | solution.py:656
  171.3 11.1 %gate_up.3 = (bf16[656,512]{1,0:T(8,128)(2,1)}, f32[16,128]{1,0:T(8,128)}, f32[16,1536]{1,0:T(8,128)}) custom-call(s32[5]{0:T(128)} %stack.36.info, s32[16]{0:T(128)} %lengths_ref.5, s32[16]{0:T(128)} %constant.33.clone.ring_ref, bf16[2048,1664]{1,0:T(8,128)(2,1)} %all-gather.5.cloned.1.call-done.x_ref, ...), custom_call_target="tpu_custom_call" | custom-call | tf_op jit(solution)/shard_map/gate_up/pallas_call | solution.py:630
  182.4 24.9 %all-gather.7.cloned.1.call-done = bf16[3072,512]{1,0:T(8,128)(2,1)} async-done(((bf16[1536,512]{1,0:T(8,128)(2,1)}), bf16[3072,512]{1,0:T(8,128)(2,1)}) %all-gather.7.cloned.1.call-update) | async-done | bytes 3145744 | tf_op jit(solution)/shard_map/all_gather | solution.py:674
  207.3 6.3 %oth_down.1 = (bf16[640,1536]{1,0:T(8,128)(2,1)}, bf16[16,1536]{1,0:T(8,128)(2,1)}) custom-call(s32[5]{0:T(128)} %stack.36.info, bf16[656,512]{1,0:T(8,128)(2,1)} %get-tuple-element.26.hidden_any, f32[16,128]{1,0:T(8,128)} %get-tuple-element.27.share_any, bf16[640,128]{1,0:T(8,128)(2,1)} %get-tuple-element.28.spot_any, ...), custom_call_target="tpu_custom_call" | custom-call | tf_op jit(solution)/shard_map/oth_down/pallas_call | solution.py:700
  213.6 0.0 all-to-all-done.4
  213.6 5.7 %all-to-all-start.3 = ((bf16[16,40,1536]{2,1,0:T(8,128)(2,1)}), bf16[16,40,1536]{2,1,0:T(8,128)(2,1)}, u32[]{:S(2)}, u32[]{:S(2)}) async-start(bf16[16,40,1536]{2,1,0:T(8,128)(2,1)} %bitcast.40), calls=%async_computation.3 | async-start | bytes 3932160 | tf_op jit(solution)/shard_map/all_to_all | solution.py:656
  219.3 3.0 mix.1
  222.3 4.0 %first.1.base_any = f32[128,1536]{1,0:T(8,128)} custom-call(bf16[384,512]{1,0:T(8,128)(2,1)} %get-tuple-element.32.mix_ref, bf16[512,1536]{1,0:T(8,128)(2,1)} %bitcast.17.back_ref, bf16[128,1536]{1,0:T(8,128)(2,1)} %bitcast.43), custom_call_target="tpu_custom_call" | custom-call | tf_op jit(solution)/shard_map/first/pallas_call | solution.py:763
  226.3 0.0 copy-start.1
  226.3 8.4 %place.1._ = bf16[3,1536,1024]{2,1,0:T(8,128)(2,1)} custom-call(s32[5]{0:T(128)} %stack.36.info, bf16[1536,512]{1,0:T(8,128)(2,1)} %bitcast.10.g_ref.g_own, bf16[1536,512]{1,0:T(8,128)(2,1)} %collective-permute-done.__1_.g_ref.g_oth, bf16[1536,512]{1,0:T(8,128)(2,1)} %bitcast.11.u_ref.u_own, bf16[1536,512]{1,0:T(8,128)(2,1)} %collective-permute-done.1.__1_.u_ref.u_oth, ...), custom_call_target="tpu_custom_call" | custom-call | tf_op jit(solution)/shard_map/place/pallas_call | solution.py:726
  234.7 0.0 copy-start
  234.7 0.0 copy-start.2
  234.7 0.0 copy-start.6
  234.7 0.0 copy-done.1
  234.7 41.5 %all-gather.1 = bf16[256,1536]{1,0:T(8,128)(2,1)S(1)} all-gather(bf16[16,1536]{1,0:T(8,128)(2,1)S(1)} %copy-done.1), channel_id=3, replica_groups={{0,2,8,10,16,18,24,26,28,30,20,22,12,14,4,6},{1,3,9,11,17,19,25,27,29,3..., dimensions={0}, use_global_device_ids=true | all-gather | bytes 835584 | tf_op jit(solution)/shard_map/all_gather | solution.py:723
  276.2 0.1 convert_reduce_fusion
  276.3 0.0 copy-done
  276.3 0.1 multiply_reduce_fusion
  276.5 0.0 copy-done.2
  276.5 0.0 copy-done.6
  276.5 5.2 %select_reduce_fusion = (f32[16]{0:T(128)S(1)}, f32[16]{0:T(128)}) fusion(s32[2048]{0:T(1024)S(1)} %iota_add_fusion, s32[16]{0:T(128)S(1)} %copy-done.6, bf16[2048,1536]{1,0:T(8,128)(2,1)} %param.16, f32[1536]{0:T(1024)S(1)} %copy-done.2, f32[16]{0:T(128)S(1)} %add_rsqrt_fusion, f32[16,1536]{1,0:T(8,128)S(1)} %copy-done, f32[16,1536]{1,0:T(8,128)S(1)} %convert_reduce_fusion), kind=kOutput, calls=%fused_computation.1 | convolution fusion | flops 100917216 | bytes 6502656 | tf_op jit(solution)/shard_map/dot_general | solution.py:780
  281.7 0.0 all-to-all-done.3
  281.7 0.0 copy-start.3
  281.7 0.0 copy-start.5
  281.7 4.8 %combine.1 = (bf16[128,1536]{1,0:T(8,128)(2,1)}, f32[1,128]{1,0:T(1,128)}) custom-call(s32[5]{0:T(128)} %stack.36.info, bf16[384,640]{1,0:T(8,128)(2,1)} %get-tuple-element.22.mix_any, bf16[640,1536]{1,0:T(8,128)(2,1)} %bitcast.15.back_any, f32[128,1536]{1,0:T(8,128)} %first.1.base_any, bf16[3,1536,1024]{2,1,0:T(8,128)(2,1)} %place.1._, f32[1,16]{1,0:T(1,128)} %bitcast.45), custom_call_target="tpu_custom_call" | custom-call | tf_op jit(solution)/shard_map/combine/pallas_call | solution.py:790
  286.4 0.7 compare_select_fusion
  287.1 0.0 copy-done.3
  287.1 10.2 %all_to_all.30 = f32[16,3,16]{2,1,0:T(4,128)S(1)} all-to-all(f32[16,3,16]{2,1,0:T(4,128)S(1)} %broadcast_in_dim.29), channel_id=1, replica_groups=mesh['blk'=16,'rep'=2] {'blk'}, dimensions={0} | all-to-all | bytes 6144 | tf_op jit(solution)/shard_map/all_to_all | solution.py:810
  297.4 0.0 copy-done.5
  297.4 0.6 pad_maximum_fusion.1
  (12 shorter events, 0.1 us)
Async XLA Ops:
  7.2 122.0 %all-gather.5.cloned.1.call-start = ((), (), s32[]{:S(2)}) async-start(), calls=%async_computation.6 | async-start | bytes 7241728 | tf_op jit(solution)/shard_map/all_gather | solution.py:625
  13.6 59.5 %all-to-all-start = ((bf16[16,96,512]{2,1,0:T(8,128)(2,1)}), bf16[16,96,512]{2,1,0:T(8,128)(2,1)}, u32[]{:S(2)}, u32[]{:S(2)}) async-start(bf16[16,96,512]{2,1,0:T(8,128)(2,1)} %cast.3), calls=%async_computation | async-start | bytes 3145728 | tf_op jit(solution)/shard_map/all_to_all | solution.py:583
  73.1 43.4 %all-to-all-start.1 = ((bf16[16,96,512]{2,1,0:T(8,128)(2,1)}), bf16[16,96,512]{2,1,0:T(8,128)(2,1)}, u32[]{:S(2)}, u32[]{:S(2)}) async-start(bf16[16,96,512]{2,1,0:T(8,128)(2,1)} %cast.4), calls=%async_computation.1 | async-start | bytes 3145728 | tf_op jit(solution)/shard_map/all_to_all | solution.py:583
  79.3 37.0 %collective-permute-start = (bf16[1536,512]{1,0:T(8,128)(2,1)}, bf16[1536,512]{1,0:T(8,128)(2,1)}, u32[]{:S(2)}, u32[]{:S(2)}) collective-permute-start(bf16[1536,512]{1,0:T(8,128)(2,1)} %bitcast.10.g_ref.g_own), channel_id=1, source_target_pairs={{0,1},{1,0},{2,3},{3,2},{4,5},{5,4},{6,7},{7,6},{8,9},{9,8},{10,11... | collective-permute-start | bytes 4718600 | tf_op jit(solution)/shard_map/ppermute | solution.py:587
  116.3 11.1 %copy-start.4 = (s32[16]{0:T(128)S(1)}, s32[16]{0:T(128)}, u32[]{:S(2)}) copy-start(s32[16]{0:T(128)} %lengths_ref.5) | copy-start | bytes 196
  116.5 41.2 %all-to-all-start.2 = ((bf16[16,96,512]{2,1,0:T(8,128)(2,1)}), bf16[16,96,512]{2,1,0:T(8,128)(2,1)}, u32[]{:S(2)}, u32[]{:S(2)}) async-start(bf16[16,96,512]{2,1,0:T(8,128)(2,1)} %tie.3), calls=%async_computation.2 | async-start | bytes 3145728 | tf_op jit(solution)/shard_map/all_to_all | solution.py:583
  125.7 81.5 %all-gather.7.cloned.1.call-start = ((), (), s32[]{:S(2)}) async-start(), calls=%async_computation.7 | async-start | bytes 4718592 | tf_op jit(solution)/shard_map/all_gather | solution.py:674
  125.8 37.0 %collective-permute-start.1 = (bf16[1536,512]{1,0:T(8,128)(2,1)}, bf16[1536,512]{1,0:T(8,128)(2,1)}, u32[]{:S(2)}, u32[]{:S(2)}) collective-permute-start(bf16[1536,512]{1,0:T(8,128)(2,1)} %bitcast.11.u_ref.u_own), channel_id=1, source_target_pairs={{0,1},{1,0},{2,3},{3,2},{4,5},{5,4},{6,7},{7,6},{8,9},{9,8},{10,11... | collective-permute-start | bytes 4718600 | tf_op jit(solution)/shard_map/ppermute | solution.py:587
  162.8 50.8 %all-to-all-start.4 = ((bf16[16,32,1536]{2,1,0:T(8,128)(2,1)}), bf16[16,32,1536]{2,1,0:T(8,128)(2,1)}, u32[]{:S(2)}, u32[]{:S(2)}) async-start(bf16[16,32,1536]{2,1,0:T(8,128)(2,1)} %bitcast.37), calls=%async_computation.4 | async-start | bytes 3145728 | tf_op jit(solution)/shard_map/all_to_all | solution.py:656
  213.6 68.1 %all-to-all-start.3 = ((bf16[16,40,1536]{2,1,0:T(8,128)(2,1)}), bf16[16,40,1536]{2,1,0:T(8,128)(2,1)}, u32[]{:S(2)}, u32[]{:S(2)}) async-start(bf16[16,40,1536]{2,1,0:T(8,128)(2,1)} %bitcast.40), calls=%async_computation.3 | async-start | bytes 3932160 | tf_op jit(solution)/shard_map/all_to_all | solution.py:656
  226.3 8.4 %copy-start.1 = (bf16[16,1536]{1,0:T(8,128)(2,1)S(1)}, bf16[16,1536]{1,0:T(8,128)(2,1)}, u32[]{:S(2)}) copy-start(bf16[16,1536]{1,0:T(8,128)(2,1)} %get-tuple-element.34) | copy-start | bytes 147460
  234.7 41.6 %copy-start = (f32[16,1536]{1,0:T(8,128)S(1)}, f32[16,1536]{1,0:T(8,128)}, u32[]{:S(2)}) copy-start(f32[16,1536]{1,0:T(8,128)} %get-tuple-element.33) | copy-start | bytes 294916
  234.7 41.8 %copy-start.2 = (f32[1536]{0:T(1024)S(1)}, f32[1536]{0:T(1024)}, u32[]{:S(2)}) copy-start(f32[1536]{0:T(1024)} %param.17) | copy-start | bytes 18436
  234.7 41.8 %copy-start.6 = (s32[16]{0:T(128)S(1)}, s32[16]{0:T(128)}, u32[]{:S(2)}) copy-start(s32[16]{0:T(128)} %param.18) | copy-start | bytes 196
  281.7 5.4 %copy-start.3 = (f32[16]{0:T(128)S(1)}, f32[16]{0:T(128)}, u32[]{:S(2)}) copy-start(f32[16]{0:T(128)} %get-tuple-element.38) | copy-start | bytes 196
  281.7 15.7 %copy-start.5 = (s32[16]{0:T(128)S(1)}, s32[16]{0:T(128)}, u32[]{:S(2)}) copy-start(s32[16]{0:T(128)} %lengths_ref.5) | copy-start | bytes 196
Sparse Core Ops, SparseCore 0:
  10.4 95.0 all-gather.4
  157.9 49.3 all-gather.6

commit v19 on v18

--- a/solution.py
+++ b/solution.py
@@ -397,6 +397,7 @@
     d,
     out,
     total,
+    blank,
     sems,
 ):
     chunks, size = d.shape[:2]
@@ -413,7 +414,8 @@
     )
     first = started([copy(x, y, sems.at[0, k]) for k, (x, y) in enumerate(zip(sources, targets))])
     waited(first)
-    stores = []
+    blank[...] = jnp.zeros_like(blank)
+    stores = started([copy(blank, sum_any.at[:, chunks * size :], sems.at[2, chunks])])
     for k in range(chunks):
         downs[k].wait()
         columns = slice(k * size, (k + 1) * size)
@@ -713,10 +715,11 @@
                 pltpu.VMEM((4, quarter, FF), jnp.bfloat16),
                 pltpu.VMEM((4, second, quarter), jnp.bfloat16),
                 pltpu.VMEM((4, blk_count, quarter), jnp.bfloat16),
+                pltpu.VMEM((blk_count, width // 2), jnp.bfloat16),
                 pltpu.SemaphoreType.DMA((4, 6)),
             ],
         ),
-        out_shape=[bf16(second, width), bf16(blk_count, width)],
+        out_shape=[bf16(second, width), bf16(blk_count, width + width // 2)],
         compiler_params=params(),
         name="oth_down",
     )(info, oth_hidden, oth_share, spot, late_out, own_part, d_both)
@@ -770,7 +773,7 @@
         name="first",
     )(first_mix, own_back, resid)
     last_rows = lax.reduce_precision(
-        resid_last + jnp.sum(last_parts.astype(jnp.float32), axis=0), 8, 7
+        resid_last + jnp.sum(last_parts[:, :, :width].astype(jnp.float32), axis=0), 8, 7
     )
     final = (
         last_rows

time: 306 us -> 302 us (0.987)
  blocking collectives: 51.7 us -> 11.7 us
  waiting for transfers between devices: 125 us -> 160 us
    all_gather x1 -> x0, blocking collectives: 41.5 us -> none  [paired(): lax.all_gather(last_part, 'blk', axis_index_groups=[list(RING)], axis=0)]
    all_gather x0 -> x1, waiting for transfers between devices: none -> 34.7 us  [paired(): lax.all_gather(last_part, 'blk', axis_index_groups=[list(RING)], axis=0)]
  transfers between devices with their start and end apart: 9 -> 10, of which waited for: 6 -> 7; matrix products, arithmetic and copies ran while one was open for 2% -> 3% of each run, Pallas kernels for 19% -> 19%
where the time goes in v19:
time: 302 us; the launch traced here: 301 us
  waiting for transfers between devices  160 us (53%)
  Pallas kernels  65.4 us (22%)
  starting transfers between devices  40.1 us (13%)
  between operations  13.9 us (5%)
  blocking collectives  11.7 us (4%)
  matrix products  5.24 us (2%)
    all_to_all x3, waiting for transfers between devices, moved(): own = lax.all_to_all(x, 'blk', split_axis=0, concat_axis=0, tiled=True)  67 us
    all_gather x1, waiting for transfers between devices, paired(): lax.all_gather(last_part, 'blk', axis_index_groups=[list(RING)], axis=0)  34.7 us
    ppermute x2, waiting for transfers between devices, swapped(): return lax.ppermute(x, 'rep', [(0, 1), (1, 0)])  32.9 us
    all_gather x1, waiting for transfers between devices, paired(): d_both = lax.all_gather(d_own, 'rep', axis=0)  24.8 us
    all_to_all x3, starting transfers between devices, moved(): own = lax.all_to_all(x, 'blk', split_axis=0, concat_axis=0, tiled=True)  22.8 us
    pallas_call x2, Pallas kernels, hidden_of(): pl.pallas_call(kernel, grid_spec=pltpu.PrefetchScalarGridSpec(num_scalar_...  21.8 us
    all_to_all x2, starting transfers between devices, returned(): x = lax.all_to_all(x, 'blk', split_axis=0, concat_axis=0, tiled=True)  14.2 us
    all_to_all x1, blocking collectives, everywhere(): lax.all_to_all(copies, 'blk', split_axis=0, concat_axis=0, tiled=True)  11.7 us
  transfers between devices with their start and end apart: 10, of which 7 were waited for; matrix products, arithmetic and copies ran while one was open for 3% of the time, Pallas kernels for 19%

profile of v19, /device:TPU:0, one launch (start us, length us, event | category | flops | bytes accessed | tf_op | source)
XLA Modules:
  0.0 301.1 jit_solution(7602270795671632326)
XLA Ops:
  7.2 0.0 all-gather.6.cloned.1.call-start
  7.2 3.1 %prep.1 = (bf16[128,1664]{1,0:T(8,128)(2,1)}, bf16[384,128]{1,0:T(8,128)(2,1)}) custom-call(s32[16]{0:T(128)} %lengths_ref.5, s32[1]{0:T(128)} %bitcast.3.blk_ref, bf16[128,1536]{1,0:T(8,128)(2,1)} %bitcast.40, s32[8,128]{1,0:T(8,128)} %bitcast.46, f32[8,128]{1,0:T(8,128)} %bitcast.47, f32[1536]{0:T(1024)} %gain_ref.1), custom_call_target="tpu_custom_call" | custom-call | tf_op jit(solution)/shard_map/prep/pallas_call | solution.py:601
  10.3 0.0 all-gather.6.cloned.1.call-update
  10.3 3.2 %cast.3 = bf16[16,96,512]{2,1,0:T(8,128)(2,1)} custom-call(f32[4608,512]{1,0:T(8,128)} %bitcast.33, bf16[128,1664]{1,0:T(8,128)(2,1)} %get-tuple-element.20.rank_ref.refs_0_), custom_call_target="tpu_custom_call" | custom-call | tf_op jit(solution)/shard_map/cast/pallas_call | solution.py:569
  13.6 7.4 %all-to-all-start = ((bf16[16,96,512]{2,1,0:T(8,128)(2,1)}), bf16[16,96,512]{2,1,0:T(8,128)(2,1)}, u32[]{:S(2)}, u32[]{:S(2)}) async-start(bf16[16,96,512]{2,1,0:T(8,128)(2,1)} %cast.3), calls=%async_computation | async-start | bytes 3145728 | tf_op jit(solution)/shard_map/all_to_all | solution.py:585
  21.0 3.3 %cast.4 = bf16[16,96,512]{2,1,0:T(8,128)(2,1)} custom-call(f32[4608,512]{1,0:T(8,128)} %bitcast.34), custom_call_target="tpu_custom_call" | custom-call | tf_op jit(solution)/shard_map/cast/pallas_call | solution.py:569
  24.3 48.8 %all-to-all-done = bf16[16,96,512]{2,1,0:T(8,128)(2,1)} async-done(((bf16[16,96,512]{2,1,0:T(8,128)(2,1)}), bf16[16,96,512]{2,1,0:T(8,128)(2,1)}, u32[]{:S(2)}, u32[]{:S(2)}) %all-to-all-start) | async-done | bytes 1572896 | tf_op jit(solution)/shard_map/all_to_all | solution.py:585
  73.1 6.1 %all-to-all-start.1 = ((bf16[16,96,512]{2,1,0:T(8,128)(2,1)}), bf16[16,96,512]{2,1,0:T(8,128)(2,1)}, u32[]{:S(2)}, u32[]{:S(2)}) async-start(bf16[16,96,512]{2,1,0:T(8,128)(2,1)} %cast.4), calls=%async_computation.1 | async-start | bytes 3145728 | tf_op jit(solution)/shard_map/all_to_all | solution.py:585
  79.3 1.5 collective-permute-start
  80.8 3.2 %cast.5.__0_ = bf16[16,96,512]{2,1,0:T(8,128)(2,1)} custom-call(f32[4608,512]{1,0:T(8,128)} %bitcast.35), custom_call_target="tpu_custom_call" | custom-call | tf_op jit(solution)/shard_map/cast/pallas_call | solution.py:569
  84.1 32.2 %collective-permute-done.__1_.g_ref.g_oth = bf16[1536,512]{1,0:T(8,128)(2,1)} collective-permute-done((bf16[1536,512]{1,0:T(8,128)(2,1)}, bf16[1536,512]{1,0:T(8,128)(2,1)}, u32[]{:S(2)}, u32[]{:S(2)}) %collective-permute-start) | collective-permute-done | bytes 1572896 | tf_op jit(solution)/shard_map/ppermute | solution.py:589
  116.2 0.0 copy-start.3
  116.2 0.3 all-to-all-done.1
  116.5 9.2 %all-to-all-start.2 = ((bf16[16,96,512]{2,1,0:T(8,128)(2,1)}), bf16[16,96,512]{2,1,0:T(8,128)(2,1)}, u32[]{:S(2)}, u32[]{:S(2)}) async-start(bf16[16,96,512]{2,1,0:T(8,128)(2,1)} %tie.3), calls=%async_computation.2 | async-start | bytes 3145728 | tf_op jit(solution)/shard_map/all_to_all | solution.py:585
  125.7 0.0 all-gather.8.cloned.1.call-start
  125.8 1.5 collective-permute-start.1
  127.3 0.0 copy-done.3
  127.3 0.6 dynamic_slice.3
  128.0 1.3 stack.36.info
  129.2 0.0 all-gather.6.cloned.1.call-done.x_ref
  129.2 10.7 %gate_up.2 = (bf16[640,512]{1,0:T(8,128)(2,1)}, bf16[640,128]{1,0:T(8,128)(2,1)}, f32[16,128]{1,0:T(8,128)}) custom-call(s32[5]{0:T(128)} %stack.36.info, s32[16]{0:T(128)} %lengths_ref.5, s32[16]{0:T(128)} %constant.33.clone.ring_ref, bf16[2048,1664]{1,0:T(8,128)(2,1)} %all-gather.6.cloned.1.call-done.x_ref, bf16[1536,512]{1,0:T(8,128)(2,1)} %bitcast.10.g_ref.g_own, ...), custom_call_target="tpu_custom_call" | custom-call | tf_op jit(solution)/shard_map/gate_up/pallas_call | solution.py:632
  139.9 17.9 %all-to-all-done.2 = bf16[16,96,512]{2,1,0:T(8,128)(2,1)} async-done(((bf16[16,96,512]{2,1,0:T(8,128)(2,1)}), bf16[16,96,512]{2,1,0:T(8,128)(2,1)}, u32[]{:S(2)}, u32[]{:S(2)}) %all-to-all-start.2) | async-done | bytes 1572896 | tf_op jit(solution)/shard_map/all_to_all | solution.py:585
  157.8 0.0 all-gather.8.cloned.1.call-update
  157.8 4.3 %own_down.1 = (bf16[512,1536]{1,0:T(8,128)(2,1)}, bf16[128,1536]{1,0:T(8,128)(2,1)}, f32[16,1536]{1,0:T(8,128)}) custom-call(bf16[640,512]{1,0:T(8,128)(2,1)} %get-tuple-element.23.__1_.hidden_any, f32[16,128]{1,0:T(8,128)} %get-tuple-element.24.share_any, bf16[1536,512]{1,0:T(8,128)(2,1)} %tie.4.d_any), custom_call_target="tpu_custom_call" | custom-call | tf_op jit(solution)/shard_map/own_down/pallas_call | solution.py:677
  162.1 0.7 collective-permute-done.1.__1_.u_ref.u_oth
  162.8 8.5 %all-to-all-start.4 = ((bf16[16,32,1536]{2,1,0:T(8,128)(2,1)}), bf16[16,32,1536]{2,1,0:T(8,128)(2,1)}, u32[]{:S(2)}, u32[]{:S(2)}) async-start(bf16[16,32,1536]{2,1,0:T(8,128)(2,1)} %bitcast.36), calls=%async_computation.4 | async-start | bytes 3145728 | tf_op jit(solution)/shard_map/all_to_all | solution.py:658
  171.3 11.1 %gate_up.3 = (bf16[656,512]{1,0:T(8,128)(2,1)}, f32[16,128]{1,0:T(8,128)}, f32[16,1536]{1,0:T(8,128)}) custom-call(s32[5]{0:T(128)} %stack.36.info, s32[16]{0:T(128)} %lengths_ref.5, s32[16]{0:T(128)} %constant.33.clone.ring_ref, bf16[2048,1664]{1,0:T(8,128)(2,1)} %all-gather.6.cloned.1.call-done.x_ref, ...), custom_call_target="tpu_custom_call" | custom-call | tf_op jit(solution)/shard_map/gate_up/pallas_call | solution.py:632
  182.4 24.8 %all-gather.8.cloned.1.call-done = bf16[3072,512]{1,0:T(8,128)(2,1)} async-done(((bf16[1536,512]{1,0:T(8,128)(2,1)}), bf16[3072,512]{1,0:T(8,128)(2,1)}) %all-gather.8.cloned.1.call-update) | async-done | bytes 3145744 | tf_op jit(solution)/shard_map/all_gather | solution.py:676
  207.3 6.3 %oth_down.1 = (bf16[640,1536]{1,0:T(8,128)(2,1)}, bf16[16,2304]{1,0:T(8,128)(2,1)}) custom-call(s32[5]{0:T(128)} %stack.36.info, bf16[656,512]{1,0:T(8,128)(2,1)} %get-tuple-element.26.hidden_any, f32[16,128]{1,0:T(8,128)} %get-tuple-element.27.share_any, bf16[640,128]{1,0:T(8,128)(2,1)} %get-tuple-element.28.spot_any, ...), custom_call_target="tpu_custom_call" | custom-call | tf_op jit(solution)/shard_map/oth_down/pallas_call | solution.py:702
  213.6 0.0 all-to-all-done.4
  213.6 5.7 %all-to-all-start.3 = ((bf16[16,40,1536]{2,1,0:T(8,128)(2,1)}), bf16[16,40,1536]{2,1,0:T(8,128)(2,1)}, u32[]{:S(2)}, u32[]{:S(2)}) async-start(bf16[16,40,1536]{2,1,0:T(8,128)(2,1)} %bitcast.39), calls=%async_computation.3 | async-start | bytes 3932160 | tf_op jit(solution)/shard_map/all_to_all | solution.py:658
  219.3 0.0 all-gather.10.cloned.1.call-start
  219.3 0.7 all-gather.10.cloned.1.call-update
  220.0 3.1 %mix.1 = (bf16[384,512]{1,0:T(8,128)(2,1)}, bf16[384,640]{1,0:T(8,128)(2,1)}) custom-call(s32[5]{0:T(128)} %stack.36.info, bf16[128,1664]{1,0:T(8,128)(2,1)} %get-tuple-element.20.rank_ref.refs_0_, bf16[384,128]{1,0:T(8,128)(2,1)} %get-tuple-element.21.pieces_ref), custom_call_target="tpu_custom_call" | custom-call | tf_op jit(solution)/shard_map/mix/pallas_call | solution.py:743
  223.1 4.0 %first.1.base_any = f32[128,1536]{1,0:T(8,128)} custom-call(bf16[384,512]{1,0:T(8,128)(2,1)} %get-tuple-element.32.mix_ref, bf16[512,1536]{1,0:T(8,128)(2,1)} %bitcast.17.back_ref, bf16[128,1536]{1,0:T(8,128)(2,1)} %bitcast.41), custom_call_target="tpu_custom_call" | custom-call | tf_op jit(solution)/shard_map/first/pallas_call | solution.py:766
  227.1 0.0 copy-start
  227.1 0.0 copy-start.1
  227.1 0.0 copy-start.5
  227.1 8.4 %place.1._ = bf16[3,1536,1024]{2,1,0:T(8,128)(2,1)} custom-call(s32[5]{0:T(128)} %stack.36.info, bf16[1536,512]{1,0:T(8,128)(2,1)} %bitcast.10.g_ref.g_own, bf16[1536,512]{1,0:T(8,128)(2,1)} %collective-permute-done.__1_.g_ref.g_oth, bf16[1536,512]{1,0:T(8,128)(2,1)} %bitcast.11.u_ref.u_own, bf16[1536,512]{1,0:T(8,128)(2,1)} %collective-permute-done.1.__1_.u_ref.u_oth, ...), custom_call_target="tpu_custom_call" | custom-call | tf_op jit(solution)/shard_map/place/pallas_call | solution.py:729
  235.5 34.7 %all-gather.10.cloned.1.call-done = bf16[256,2304]{1,0:T(8,128)(2,1)} async-done(((bf16[16,2304]{1,0:T(8,128)(2,1)}), bf16[256,2304]{1,0:T(8,128)(2,1)}) %all-gather.10.cloned.1.call-update) | async-done | bytes 1179664 | tf_op jit(solution)/shard_map/all_gather | solution.py:726
  270.2 1.2 convert_reduce_fusion
  271.5 0.0 copy-done
  271.5 0.1 multiply_reduce_fusion
  271.6 0.0 copy-done.1
  271.6 0.0 copy-done.5
  271.6 5.2 %select_reduce_fusion = (f32[16]{0:T(128)S(1)}, f32[16]{0:T(128)}) fusion(s32[2048]{0:T(1024)S(1)} %iota_add_fusion, s32[16]{0:T(128)S(1)} %copy-done.5, bf16[2048,1536]{1,0:T(8,128)(2,1)} %param.16, f32[1536]{0:T(1024)S(1)} %copy-done.1, f32[16]{0:T(128)S(1)} %add_rsqrt_fusion, f32[16,1536]{1,0:T(8,128)S(1)} %copy-done, f32[16,1536]{1,0:T(8,128)S(1)} %convert_reduce_fusion), kind=kOutput, calls=%fused_computation.1 | convolution fusion | flops 100917216 | bytes 6502656 | tf_op jit(solution)/shard_map/dot_general | solution.py:783
  276.9 0.0 all-to-all-done.3
  276.9 0.0 copy-start.2
  276.9 0.0 copy-start.4
  276.9 4.7 %combine.1 = (bf16[128,1536]{1,0:T(8,128)(2,1)}, f32[1,128]{1,0:T(1,128)}) custom-call(s32[5]{0:T(128)} %stack.36.info, bf16[384,640]{1,0:T(8,128)(2,1)} %get-tuple-element.22.mix_any, bf16[640,1536]{1,0:T(8,128)(2,1)} %bitcast.15.back_any, f32[128,1536]{1,0:T(8,128)} %first.1.base_any, bf16[3,1536,1024]{2,1,0:T(8,128)(2,1)} %place.1._, f32[1,16]{1,0:T(1,128)} %bitcast.44), custom_call_target="tpu_custom_call" | custom-call | tf_op jit(solution)/shard_map/combine/pallas_call | solution.py:793
  281.6 0.6 compare_select_fusion
  282.2 0.0 copy-done.2
  282.2 11.7 %all_to_all.30 = f32[16,3,16]{2,1,0:T(4,128)S(1)} all-to-all(f32[16,3,16]{2,1,0:T(4,128)S(1)} %broadcast_in_dim.29), channel_id=1, replica_groups=mesh['blk'=16,'rep'=2] {'blk'}, dimensions={0} | all-to-all | bytes 6144 | tf_op jit(solution)/shard_map/all_to_all | solution.py:813
  293.9 0.0 copy-done.4
  294.0 0.6 pad_maximum_fusion.1
  (12 shorter events, 0.1 us)
Async XLA Ops:
  7.2 122.1 %all-gather.6.cloned.1.call-start = ((), (), s32[]{:S(2)}) async-start(), calls=%async_computation.6 | async-start | bytes 7241728 | tf_op jit(solution)/shard_map/all_gather | solution.py:627
  13.6 59.5 %all-to-all-start = ((bf16[16,96,512]{2,1,0:T(8,128)(2,1)}), bf16[16,96,512]{2,1,0:T(8,128)(2,1)}, u32[]{:S(2)}, u32[]{:S(2)}) async-start(bf16[16,96,512]{2,1,0:T(8,128)(2,1)} %cast.3), calls=%async_computation | async-start | bytes 3145728 | tf_op jit(solution)/shard_map/all_to_all | solution.py:585
  73.1 43.4 %all-to-all-start.1 = ((bf16[16,96,512]{2,1,0:T(8,128)(2,1)}), bf16[16,96,512]{2,1,0:T(8,128)(2,1)}, u32[]{:S(2)}, u32[]{:S(2)}) async-start(bf16[16,96,512]{2,1,0:T(8,128)(2,1)} %cast.4), calls=%async_computation.1 | async-start | bytes 3145728 | tf_op jit(solution)/shard_map/all_to_all | solution.py:585
  79.3 37.0 %collective-permute-start = (bf16[1536,512]{1,0:T(8,128)(2,1)}, bf16[1536,512]{1,0:T(8,128)(2,1)}, u32[]{:S(2)}, u32[]{:S(2)}) collective-permute-start(bf16[1536,512]{1,0:T(8,128)(2,1)} %bitcast.10.g_ref.g_own), channel_id=1, source_target_pairs={{0,1},{1,0},{2,3},{3,2},{4,5},{5,4},{6,7},{7,6},{8,9},{9,8},{10,11... | collective-permute-start | bytes 4718600 | tf_op jit(solution)/shard_map/ppermute | solution.py:589
  116.2 11.1 %copy-start.3 = (s32[16]{0:T(128)S(1)}, s32[16]{0:T(128)}, u32[]{:S(2)}) copy-start(s32[16]{0:T(128)} %lengths_ref.5) | copy-start | bytes 196
  116.5 41.2 %all-to-all-start.2 = ((bf16[16,96,512]{2,1,0:T(8,128)(2,1)}), bf16[16,96,512]{2,1,0:T(8,128)(2,1)}, u32[]{:S(2)}, u32[]{:S(2)}) async-start(bf16[16,96,512]{2,1,0:T(8,128)(2,1)} %tie.3), calls=%async_computation.2 | async-start | bytes 3145728 | tf_op jit(solution)/shard_map/all_to_all | solution.py:585
  125.7 81.5 %all-gather.8.cloned.1.call-start = ((), (), s32[]{:S(2)}) async-start(), calls=%async_computation.7 | async-start | bytes 4718592 | tf_op jit(solution)/shard_map/all_gather | solution.py:676
  125.8 37.0 %collective-permute-start.1 = (bf16[1536,512]{1,0:T(8,128)(2,1)}, bf16[1536,512]{1,0:T(8,128)(2,1)}, u32[]{:S(2)}, u32[]{:S(2)}) collective-permute-start(bf16[1536,512]{1,0:T(8,128)(2,1)} %bitcast.11.u_ref.u_own), channel_id=1, source_target_pairs={{0,1},{1,0},{2,3},{3,2},{4,5},{5,4},{6,7},{7,6},{8,9},{9,8},{10,11... | collective-permute-start | bytes 4718600 | tf_op jit(solution)/shard_map/ppermute | solution.py:589
  162.8 50.8 %all-to-all-start.4 = ((bf16[16,32,1536]{2,1,0:T(8,128)(2,1)}), bf16[16,32,1536]{2,1,0:T(8,128)(2,1)}, u32[]{:S(2)}, u32[]{:S(2)}) async-start(bf16[16,32,1536]{2,1,0:T(8,128)(2,1)} %bitcast.36), calls=%async_computation.4 | async-start | bytes 3145728 | tf_op jit(solution)/shard_map/all_to_all | solution.py:658
  213.6 63.3 %all-to-all-start.3 = ((bf16[16,40,1536]{2,1,0:T(8,128)(2,1)}), bf16[16,40,1536]{2,1,0:T(8,128)(2,1)}, u32[]{:S(2)}, u32[]{:S(2)}) async-start(bf16[16,40,1536]{2,1,0:T(8,128)(2,1)} %bitcast.39), calls=%async_computation.3 | async-start | bytes 3932160 | tf_op jit(solution)/shard_map/all_to_all | solution.py:658
  219.3 50.9 %all-gather.10.cloned.1.call-start = ((), (), s32[]{:S(2)}) async-start(), calls=%async_computation.8 | async-start | bytes 1253376 | tf_op jit(solution)/shard_map/all_gather | solution.py:726
  227.1 44.4 %copy-start = (f32[16,1536]{1,0:T(8,128)S(1)}, f32[16,1536]{1,0:T(8,128)}, u32[]{:S(2)}) copy-start(f32[16,1536]{1,0:T(8,128)} %get-tuple-element.33) | copy-start | bytes 294916
  227.1 44.5 %copy-start.1 = (f32[1536]{0:T(1024)S(1)}, f32[1536]{0:T(1024)}, u32[]{:S(2)}) copy-start(f32[1536]{0:T(1024)} %param.17) | copy-start | bytes 18436
  227.1 44.5 %copy-start.5 = (s32[16]{0:T(128)S(1)}, s32[16]{0:T(128)}, u32[]{:S(2)}) copy-start(s32[16]{0:T(128)} %param.18) | copy-start | bytes 196
  276.9 5.3 %copy-start.2 = (f32[16]{0:T(128)S(1)}, f32[16]{0:T(128)}, u32[]{:S(2)}) copy-start(f32[16]{0:T(128)} %get-tuple-element.38) | copy-start | bytes 196
  276.9 17.1 %copy-start.4 = (s32[16]{0:T(128)S(1)}, s32[16]{0:T(128)}, u32[]{:S(2)}) copy-start(s32[16]{0:T(128)} %lengths_ref.5) | copy-start | bytes 196
Sparse Core Ops, SparseCore 0:
  10.4 95.0 all-gather.5
  157.9 49.3 all-gather.7
  221.7 48.4 all-gather.9

commit v20 on v17

--- a/solution.py
+++ b/solution.py
@@ -367,7 +367,7 @@
 
 
 def oth_down_kernel(
-    info,
+    _,
     hidden_any,
     share_any,
     spot_any,
@@ -391,12 +391,11 @@
     chunks, size = d.shape[:2]
     rows = out_any.shape[0]
     copy = pltpu.make_async_copy
-    other = 1 - info[2]
     sources = (hidden_any, share_any, spot_any, late_any, base_any, part_any)
     targets = (hidden, share, spot, late, base, part)
     downs = started(
         [
-            copy(d_any.at[other, k * size : (k + 1) * size], d.at[k], sems.at[1, k])
+            copy(d_any.at[k * size : (k + 1) * size], d.at[k], sems.at[1, k])
             for k in range(chunks)
         ]
     )
@@ -489,13 +488,13 @@
     )
 
 
-def place_kernel(info, g_own, g_oth, u_own, u_oth, d_both, _, out_ref):
+def place_kernel(info, g_own, g_oth, u_both, d_own, d_oth, _, out_ref):
     left = info[2] == 0
-    for k, (own, oth) in enumerate(((g_own[...], g_oth[...]), (u_own[...], u_oth[...]))):
+    for k, (own, oth) in ((0, (g_own[...], g_oth[...])), (2, (d_own[...], d_oth[...]))):
         out_ref[k, :, :FF] = jnp.where(left, own, oth)
         out_ref[k, :, FF:] = jnp.where(left, oth, own)
-    out_ref[2, :, :FF] = d_both[0]
-    out_ref[2, :, FF:] = d_both[1]
+    out_ref[1, :, :FF] = u_both[0]
+    out_ref[1, :, FF:] = u_both[1]
 
 
 def cast_kernel(first_row, blocks, x_ref, *refs):
@@ -608,21 +607,23 @@
     g_own = moved(turned(0, row_ext))
     g_oth = swapped(g_own)
     u_own = moved(turned(1))
-    u_oth = swapped(u_own)
+    u_both = lax.all_gather(u_own, "rep", axis=0)
     d_own = moved(tied(turned(2), g_oth))
 
     tokens = lax.all_gather(row_ext, "blk", axis_index_groups=[list(RING)], axis=0, tiled=True)
 
     ring = jnp.array(RING, jnp.int32)
 
-    def hidden_of(kernel, outs, picked, operands, specs):
+    other = pl.BlockSpec((None, width, FF), lambda i, info, *_: (1 - info[2], 0, 0))
+
+    def hidden_of(kernel, outs, picked, operands, up, specs):
         return pl.pallas_call(
             kernel,
             grid_spec=pltpu.PrefetchScalarGridSpec(
                 num_scalar_prefetch=3,
                 grid=(GROUPS,),
                 in_specs=[pl.BlockSpec((blk_count // GROUPS * rows, width + LANES), lambda i, *_: (i, 0))]
-                + [whole((width, FF))] * 2
+                + [whole((width, FF)), up]
                 + specs,
                 out_specs=[whole(out.shape) for out in outs],
                 scratch_shapes=[
@@ -657,10 +658,11 @@
         [bf16(first + extra, FF), bf16(second, extra), f32(blk_count, LANES)],
         first + extra,
         (g_own, u_own),
+        whole((width, FF)),
         [],
     )
     d_own = tied(d_own, own_hidden)
-    d_both = lax.all_gather(d_own, "rep", axis=0)
+    d_oth = swapped(d_own)
     own_out, late_out, own_part = pl.pallas_call(
         own_down_kernel,
         in_specs=[anywhere] * 3,
@@ -677,13 +679,13 @@
         compiler_params=pltpu.CompilerParams(vmem_limit_bytes=VMEM),
         name="own_down",
     )(own_hidden, own_share, d_own)
-    own_out = tied(own_out, u_oth)
     own_back = returned(own_out)
     oth_hidden, oth_share, base_part = hidden_of(
         oth_kernel,
         [bf16(second + blk_count, FF), f32(blk_count, LANES), f32(blk_count, width)],
         second + blk_count,
-        (g_oth, u_oth, resid, own_out),
+        (g_oth, u_both, resid, own_out),
+        other,
         [whole((rows, width)), anywhere],
     )
     oth_out, last_part = pl.pallas_call(
@@ -709,7 +711,7 @@
         out_shape=[bf16(second, width), f32(blk_count, width)],
         compiler_params=params(),
         name="oth_down",
-    )(info, oth_hidden, oth_share, spot, late_out, base_part, own_part, d_both)
+    )(info, oth_hidden, oth_share, spot, late_out, base_part, own_part, d_oth)
     last_parts = lax.all_gather(last_part, "blk", axis_index_groups=[list(RING)], axis=0)
     oth_back = returned(oth_out)
 
@@ -718,14 +720,16 @@
         grid_spec=pltpu.PrefetchScalarGridSpec(
             num_scalar_prefetch=1,
             grid=(4,),
-            in_specs=[pl.BlockSpec((quarter, FF), lambda i, *_: (i, 0))] * 4
-            + [pl.BlockSpec((2, quarter, FF), lambda i, *_: (0, i, 0)), anywhere],
+            in_specs=[pl.BlockSpec((quarter, FF), lambda i, *_: (i, 0))] * 2
+            + [pl.BlockSpec((2, quarter, FF), lambda i, *_: (0, i, 0))]
+            + [pl.BlockSpec((quarter, FF), lambda i, *_: (i, 0))] * 2
+            + [anywhere],
             out_specs=pl.BlockSpec((3, quarter, 2 * FF), lambda i, *_: (0, i, 0)),
         ),
         out_shape=jax.ShapeDtypeStruct((3, width, 2 * FF), jnp.bfloat16),
         compiler_params=params(),
         name="place",
-    )(info, g_own, g_oth, u_own, u_oth, d_both, oth_out)
+    )(info, g_own, g_oth, u_both, d_own, d_oth, oth_out)
 
     first_mix, second_mix = pl.pallas_call(
         mix_kernel,

time: 299 us -> 300 us (level)
    all_gather x1, waiting for transfers between devices: 24.7 us -> 1.34 us  [paired(): u_both = lax.all_gather(u_own, 'rep', axis=0)]
    ppermute x2, waiting for transfers between devices: 32.9 us -> 55.5 us  [swapped(): return lax.ppermute(x, 'rep', [(0, 1), (1, 0)])]
where the time goes in v20:
time: 300 us; the launch traced here: 299 us
  waiting for transfers between devices  157 us (52%)
  Pallas kernels  64.8 us (22%)
  starting transfers between devices  41.1 us (14%)
  between operations  13.9 us (5%)
  blocking collectives  11.9 us (4%)
  matrix products  5.18 us (2%)
    all_to_all x3, waiting for transfers between devices, moved(): own = lax.all_to_all(x, 'blk', split_axis=0, concat_axis=0, tiled=True)  67.9 us
    ppermute x2, waiting for transfers between devices, swapped(): return lax.ppermute(x, 'rep', [(0, 1), (1, 0)])  55.5 us
    all_gather x1, waiting for transfers between devices, paired(): lax.all_gather(last_part, 'blk', axis_index_groups=[list(RING)], axis=0)  31.7 us
    all_to_all x3, starting transfers between devices, moved(): own = lax.all_to_all(x, 'blk', split_axis=0, concat_axis=0, tiled=True)  22.8 us
    pallas_call x2, Pallas kernels, hidden_of(): pl.pallas_call(kernel, grid_spec=pltpu.PrefetchScalarGridSpec(num_scalar_...  21.4 us
    all_to_all x2, starting transfers between devices, returned(): x = lax.all_to_all(x, 'blk', split_axis=0, concat_axis=0, tiled=True)  15 us
    all_to_all x1, blocking collectives, everywhere(): lax.all_to_all(copies, 'blk', split_axis=0, concat_axis=0, tiled=True)  11.9 us
    pallas_call x3, Pallas kernels, turned(): pl.pallas_call(functools.partial(cast_kernel, k * shard_rows * blk_count,...  9.77 us
  transfers between devices with their start and end apart: 10, of which 7 were waited for; matrix products, arithmetic and copies ran while one was open for 3% of the time, Pallas kernels for 19%

profile of v20, /device:TPU:0, one launch (start us, length us, event | category | flops | bytes accessed | tf_op | source)
XLA Modules:
  0.0 298.8 jit_solution(9018207393829264888)
XLA Ops:
  7.2 0.0 all-gather.5.cloned.1.call-start
  7.2 3.0 %prep.1 = (bf16[128,1664]{1,0:T(8,128)(2,1)}, bf16[384,128]{1,0:T(8,128)(2,1)}) custom-call(s32[16]{0:T(128)} %lengths_ref.5, s32[1]{0:T(128)} %bitcast.3.blk_ref, bf16[128,1536]{1,0:T(8,128)(2,1)} %bitcast.38, s32[8,128]{1,0:T(8,128)} %bitcast.45, f32[8,128]{1,0:T(8,128)} %bitcast.46, f32[1536]{0:T(1024)} %gain_ref.1), custom_call_target="tpu_custom_call" | custom-call | tf_op jit(solution)/shard_map/prep/pallas_call | solution.py:587
  10.2 0.0 all-gather.5.cloned.1.call-update
  10.3 3.3 %cast.3 = bf16[16,96,512]{2,1,0:T(8,128)(2,1)} custom-call(f32[4608,512]{1,0:T(8,128)} %bitcast.33, bf16[128,1664]{1,0:T(8,128)(2,1)} %get-tuple-element.20.rank_ref.refs_0_), custom_call_target="tpu_custom_call" | custom-call | tf_op jit(solution)/shard_map/cast/pallas_call | solution.py:555
  13.5 7.4 %all-to-all-start = ((bf16[16,96,512]{2,1,0:T(8,128)(2,1)}), bf16[16,96,512]{2,1,0:T(8,128)(2,1)}, u32[]{:S(2)}, u32[]{:S(2)}) async-start(bf16[16,96,512]{2,1,0:T(8,128)(2,1)} %cast.3), calls=%async_computation | async-start | bytes 3145728 | tf_op jit(solution)/shard_map/all_to_all | solution.py:571
  21.0 3.3 %cast.4 = bf16[16,96,512]{2,1,0:T(8,128)(2,1)} custom-call(f32[4608,512]{1,0:T(8,128)} %bitcast.34), custom_call_target="tpu_custom_call" | custom-call | tf_op jit(solution)/shard_map/cast/pallas_call | solution.py:555
  24.2 48.8 %all-to-all-done = bf16[16,96,512]{2,1,0:T(8,128)(2,1)} async-done(((bf16[16,96,512]{2,1,0:T(8,128)(2,1)}), bf16[16,96,512]{2,1,0:T(8,128)(2,1)}, u32[]{:S(2)}, u32[]{:S(2)}) %all-to-all-start) | async-done | bytes 1572896 | tf_op jit(solution)/shard_map/all_to_all | solution.py:571
  73.0 6.1 %all-to-all-start.1 = ((bf16[16,96,512]{2,1,0:T(8,128)(2,1)}), bf16[16,96,512]{2,1,0:T(8,128)(2,1)}, u32[]{:S(2)}, u32[]{:S(2)}) async-start(bf16[16,96,512]{2,1,0:T(8,128)(2,1)} %cast.4), calls=%async_computation.1 | async-start | bytes 3145728 | tf_op jit(solution)/shard_map/all_to_all | solution.py:571
  79.2 1.6 collective-permute-start
  80.8 3.2 %cast.5.__0_ = bf16[16,96,512]{2,1,0:T(8,128)(2,1)} custom-call(f32[4608,512]{1,0:T(8,128)} %bitcast.35), custom_call_target="tpu_custom_call" | custom-call | tf_op jit(solution)/shard_map/cast/pallas_call | solution.py:555
  84.0 32.2 %collective-permute-done.__1_.g_ref.g_oth = bf16[1536,512]{1,0:T(8,128)(2,1)} collective-permute-done((bf16[1536,512]{1,0:T(8,128)(2,1)}, bf16[1536,512]{1,0:T(8,128)(2,1)}, u32[]{:S(2)}, u32[]{:S(2)}) %collective-permute-start) | collective-permute-done | bytes 1572896 | tf_op jit(solution)/shard_map/ppermute | solution.py:575
  116.2 0.3 all-to-all-done.1
  116.5 9.2 %all-to-all-start.2 = ((bf16[16,96,512]{2,1,0:T(8,128)(2,1)}), bf16[16,96,512]{2,1,0:T(8,128)(2,1)}, u32[]{:S(2)}, u32[]{:S(2)}) async-start(bf16[16,96,512]{2,1,0:T(8,128)(2,1)} %tie.2), calls=%async_computation.2 | async-start | bytes 3145728 | tf_op jit(solution)/shard_map/all_to_all | solution.py:571
  125.6 0.0 copy-start.2
  125.7 0.0 all-gather.7.cloned.1.call-start
  125.7 0.7 all-gather.7.cloned.1.call-update
  126.4 0.0 copy-done.2
  126.4 0.6 dynamic_slice.3
  127.0 1.2 stack.36.info._
  128.3 0.0 all-gather.5.cloned.1.call-done.x_ref
  128.3 10.6 %gate_up.2 = (bf16[640,512]{1,0:T(8,128)(2,1)}, bf16[640,128]{1,0:T(8,128)(2,1)}, f32[16,128]{1,0:T(8,128)}) custom-call(s32[5]{0:T(128)} %stack.36.info._, s32[16]{0:T(128)} %lengths_ref.5, s32[16]{0:T(128)} %constant.33.clone.ring_ref, bf16[2048,1664]{1,0:T(8,128)(2,1)} %all-gather.5.cloned.1.call-done.x_ref, bf16[1536,512]{1,0:T(8,128)(2,1)} %bitcast.10.g_ref.g_own, ...), custom_call_target="tpu_custom_call" | custom-call | tf_op jit(solution)/shard_map/gate_up/pallas_call | solution.py:620
  138.9 18.8 %all-to-all-done.2 = bf16[16,96,512]{2,1,0:T(8,128)(2,1)} async-done(((bf16[16,96,512]{2,1,0:T(8,128)(2,1)}), bf16[16,96,512]{2,1,0:T(8,128)(2,1)}, u32[]{:S(2)}, u32[]{:S(2)}) %all-to-all-start.2) | async-done | bytes 1572896 | tf_op jit(solution)/shard_map/all_to_all | solution.py:571
  157.7 4.3 %own_down.1 = (bf16[512,1536]{1,0:T(8,128)(2,1)}, bf16[128,1536]{1,0:T(8,128)(2,1)}, f32[16,1536]{1,0:T(8,128)}) custom-call(bf16[640,512]{1,0:T(8,128)(2,1)} %get-tuple-element.23.__1_.hidden_any, f32[16,128]{1,0:T(8,128)} %get-tuple-element.24.share_any, bf16[1536,512]{1,0:T(8,128)(2,1)} %tie.3.d_any.d_own), custom_call_target="tpu_custom_call" | custom-call | tf_op jit(solution)/shard_map/own_down/pallas_call | solution.py:666
  162.0 9.2 %all-to-all-start.4 = ((bf16[16,32,1536]{2,1,0:T(8,128)(2,1)}), bf16[16,32,1536]{2,1,0:T(8,128)(2,1)}, u32[]{:S(2)}, u32[]{:S(2)}) async-start(bf16[16,32,1536]{2,1,0:T(8,128)(2,1)} %bitcast.37), calls=%async_computation.4 | async-start | bytes 3145728 | tf_op jit(solution)/shard_map/all_to_all | solution.py:646
  171.2 0.2 all-gather.9.cloned.1.call-start
  171.4 1.5 collective-permute-start.1
  172.9 1.3 all-gather.7.cloned.1.call-done.u_ref.u_both
  174.3 10.8 %gate_up.3 = (bf16[656,512]{1,0:T(8,128)(2,1)}, f32[16,128]{1,0:T(8,128)}, f32[16,1536]{1,0:T(8,128)}) custom-call(s32[5]{0:T(128)} %stack.36.info._, s32[16]{0:T(128)} %lengths_ref.5, s32[16]{0:T(128)} %constant.33.clone.ring_ref, bf16[2048,1664]{1,0:T(8,128)(2,1)} %all-gather.5.cloned.1.call-done.x_ref, ...), custom_call_target="tpu_custom_call" | custom-call | tf_op jit(solution)/shard_map/gate_up/pallas_call | solution.py:620
  185.0 23.4 %collective-permute-done.1.d_any.d_oth = bf16[1536,512]{1,0:T(8,128)(2,1)} collective-permute-done((bf16[1536,512]{1,0:T(8,128)(2,1)}, bf16[1536,512]{1,0:T(8,128)(2,1)}, u32[]{:S(2)}, u32[]{:S(2)}) %collective-permute-start.1) | collective-permute-done | bytes 1572896 | tf_op jit(solution)/shard_map/ppermute | solution.py:575
  208.4 6.3 %oth_down.1 = (bf16[640,1536]{1,0:T(8,128)(2,1)}, f32[16,1536]{1,0:T(8,128)}) custom-call(s32[5]{0:T(128)} %stack.36.info._, bf16[656,512]{1,0:T(8,128)(2,1)} %get-tuple-element.26.hidden_any, f32[16,128]{1,0:T(8,128)} %get-tuple-element.27.share_any, bf16[640,128]{1,0:T(8,128)(2,1)} %get-tuple-element.28.spot_any, ...), custom_call_target="tpu_custom_call" | custom-call | tf_op jit(solution)/shard_map/oth_down/pallas_call | solution.py:691
  214.7 0.0 all-gather.9.cloned.1.call-update
  214.7 0.0 all-to-all-done.4
  214.7 5.8 %all-to-all-start.3 = ((bf16[16,40,1536]{2,1,0:T(8,128)(2,1)}), bf16[16,40,1536]{2,1,0:T(8,128)(2,1)}, u32[]{:S(2)}, u32[]{:S(2)}) async-start(bf16[16,40,1536]{2,1,0:T(8,128)(2,1)} %bitcast.36), calls=%async_computation.3 | async-start | bytes 3932160 | tf_op jit(solution)/shard_map/all_to_all | solution.py:646
  220.6 3.0 %mix.1 = (bf16[384,512]{1,0:T(8,128)(2,1)}, bf16[384,640]{1,0:T(8,128)(2,1)}) custom-call(s32[5]{0:T(128)} %stack.36.info._, bf16[128,1664]{1,0:T(8,128)(2,1)} %get-tuple-element.20.rank_ref.refs_0_, bf16[384,128]{1,0:T(8,128)(2,1)} %get-tuple-element.21.pieces_ref), custom_call_target="tpu_custom_call" | custom-call | tf_op jit(solution)/shard_map/mix/pallas_call | solution.py:734
  223.6 8.2 %place.1._ = bf16[3,1536,1024]{2,1,0:T(8,128)(2,1)} custom-call(s32[5]{0:T(128)} %stack.36.info._, bf16[1536,512]{1,0:T(8,128)(2,1)} %bitcast.10.g_ref.g_own, bf16[1536,512]{1,0:T(8,128)(2,1)} %collective-permute-done.__1_.g_ref.g_oth, bf16[2,1536,512]{2,1,0:T(8,128)(2,1)} %all-gather.7.cloned.1.call-done.u_ref.u_both, bf16[1536,512]{1,0:T(8,128)(2,1)} %tie.3.d_any.d_own, ...), custom_call_target="tpu_custom_call" | custom-call | tf_op jit(solution)/shard_map/place/pallas_call | solution.py:718
  231.8 4.0 %first.1.base_any = f32[128,1536]{1,0:T(8,128)} custom-call(bf16[384,512]{1,0:T(8,128)(2,1)} %get-tuple-element.33.mix_ref, bf16[512,1536]{1,0:T(8,128)(2,1)} %bitcast.17.back_ref, bf16[128,1536]{1,0:T(8,128)(2,1)} %bitcast.40), custom_call_target="tpu_custom_call" | custom-call | tf_op jit(solution)/shard_map/first/pallas_call | solution.py:757
  235.9 0.0 copy-start
  235.9 0.0 copy-start.4
  235.9 31.7 %all-gather.9.cloned.1.call-done = f32[256,1536]{1,0:T(8,128)} async-done(((f32[16,1536]{1,0:T(8,128)}), f32[256,1536]{1,0:T(8,128)}) %all-gather.9.cloned.1.call-update) | async-done | bytes 1572880 | tf_op jit(solution)/shard_map/all_gather | solution.py:715
  267.6 1.5 reduce_sum.36
  269.1 0.1 multiply_reduce_fusion
  269.2 0.0 copy-done
  269.2 0.0 copy-done.4
  269.2 5.2 %select_reduce_fusion = (f32[16]{0:T(128)S(1)}, f32[16]{0:T(128)}) fusion(s32[2048]{0:T(1024)S(1)} %iota_add_fusion, s32[16]{0:T(128)S(1)} %copy-done.4, bf16[2048,1536]{1,0:T(8,128)(2,1)} %param.16, f32[16,1536]{1,0:T(8,128)S(1)} %reduce_sum.36, f32[1536]{0:T(1024)S(1)} %copy-done, f32[16]{0:T(128)S(1)} %add_rsqrt_fusion), kind=kOutput, calls=%fused_computation | convolution fusion | flops 100892640 | bytes 6404352 | tf_op jit(solution)/shard_map/dot_general | solution.py:772
  274.4 0.0 all-to-all-done.3
  274.4 0.0 copy-start.1
  274.4 0.0 copy-start.3
  274.4 4.7 %combine.1 = (bf16[128,1536]{1,0:T(8,128)(2,1)}, f32[1,128]{1,0:T(1,128)}) custom-call(s32[5]{0:T(128)} %stack.36.info._, bf16[384,640]{1,0:T(8,128)(2,1)} %get-tuple-element.22.mix_any, bf16[640,1536]{1,0:T(8,128)(2,1)} %bitcast.15.back_any, f32[128,1536]{1,0:T(8,128)} %first.1.base_any, bf16[3,1536,1024]{2,1,0:T(8,128)(2,1)} %place.1._, f32[1,16]{1,0:T(1,128)} %bitcast.43), custom_call_target="tpu_custom_call" | custom-call | tf_op jit(solution)/shard_map/combine/pallas_call | solution.py:782
  279.1 0.6 compare_select_fusion
  279.7 0.0 copy-done.1
  279.8 11.9 %all_to_all.30 = f32[16,3,16]{2,1,0:T(4,128)S(1)} all-to-all(f32[16,3,16]{2,1,0:T(4,128)S(1)} %broadcast_in_dim.29), channel_id=1, replica_groups=mesh['blk'=16,'rep'=2] {'blk'}, dimensions={0} | all-to-all | bytes 6144 | tf_op jit(solution)/shard_map/all_to_all | solution.py:802
  291.7 0.0 copy-done.3
  291.7 0.6 pad_maximum_fusion.1
  (11 shorter events, 0.1 us)
Async XLA Ops:
  7.2 121.1 %all-gather.5.cloned.1.call-start = ((), (), s32[]{:S(2)}) async-start(), calls=%async_computation.6 | async-start | bytes 7241728 | tf_op jit(solution)/shard_map/all_gather | solution.py:613
  13.5 59.5 %all-to-all-start = ((bf16[16,96,512]{2,1,0:T(8,128)(2,1)}), bf16[16,96,512]{2,1,0:T(8,128)(2,1)}, u32[]{:S(2)}, u32[]{:S(2)}) async-start(bf16[16,96,512]{2,1,0:T(8,128)(2,1)} %cast.3), calls=%async_computation | async-start | bytes 3145728 | tf_op jit(solution)/shard_map/all_to_all | solution.py:571
  73.0 43.4 %all-to-all-start.1 = ((bf16[16,96,512]{2,1,0:T(8,128)(2,1)}), bf16[16,96,512]{2,1,0:T(8,128)(2,1)}, u32[]{:S(2)}, u32[]{:S(2)}) async-start(bf16[16,96,512]{2,1,0:T(8,128)(2,1)} %cast.4), calls=%async_computation.1 | async-start | bytes 3145728 | tf_op jit(solution)/shard_map/all_to_all | solution.py:571
  79.2 37.0 %collective-permute-start = (bf16[1536,512]{1,0:T(8,128)(2,1)}, bf16[1536,512]{1,0:T(8,128)(2,1)}, u32[]{:S(2)}, u32[]{:S(2)}) collective-permute-start(bf16[1536,512]{1,0:T(8,128)(2,1)} %bitcast.10.g_ref.g_own), channel_id=1, source_target_pairs={{0,1},{1,0},{2,3},{3,2},{4,5},{5,4},{6,7},{7,6},{8,9},{9,8},{10,11... | collective-permute-start | bytes 4718600 | tf_op jit(solution)/shard_map/ppermute | solution.py:575
  116.5 41.2 %all-to-all-start.2 = ((bf16[16,96,512]{2,1,0:T(8,128)(2,1)}), bf16[16,96,512]{2,1,0:T(8,128)(2,1)}, u32[]{:S(2)}, u32[]{:S(2)}) async-start(bf16[16,96,512]{2,1,0:T(8,128)(2,1)} %tie.2), calls=%async_computation.2 | async-start | bytes 3145728 | tf_op jit(solution)/shard_map/all_to_all | solution.py:571
  125.6 0.8 copy-start.2
  125.7 48.6 %all-gather.7.cloned.1.call-start = ((), (), s32[]{:S(2)}) async-start(), calls=%async_computation.7 | async-start | bytes 4718592 | tf_op jit(solution)/shard_map/all_gather | solution.py:610
  162.0 52.7 %all-to-all-start.4 = ((bf16[16,32,1536]{2,1,0:T(8,128)(2,1)}), bf16[16,32,1536]{2,1,0:T(8,128)(2,1)}, u32[]{:S(2)}, u32[]{:S(2)}) async-start(bf16[16,32,1536]{2,1,0:T(8,128)(2,1)} %bitcast.37), calls=%async_computation.4 | async-start | bytes 3145728 | tf_op jit(solution)/shard_map/all_to_all | solution.py:646
  171.2 96.4 %all-gather.9.cloned.1.call-start = ((), (), s32[]{:S(2)}) async-start(), calls=%async_computation.8 | async-start | bytes 1671168 | tf_op jit(solution)/shard_map/all_gather | solution.py:715
  171.4 37.0 %collective-permute-start.1 = (bf16[1536,512]{1,0:T(8,128)(2,1)}, bf16[1536,512]{1,0:T(8,128)(2,1)}, u32[]{:S(2)}, u32[]{:S(2)}) collective-permute-start(bf16[1536,512]{1,0:T(8,128)(2,1)} %tie.3.d_any.d_own), channel_id=1, source_target_pairs={{0,1},{1,0},{2,3},{3,2},{4,5},{5,4},{6,7},{7,6},{8,9},{9,8},{10,11... | collective-permute-start | bytes 4718600 | tf_op jit(solution)/shard_map/ppermute | solution.py:575
  214.7 59.7 %all-to-all-start.3 = ((bf16[16,40,1536]{2,1,0:T(8,128)(2,1)}), bf16[16,40,1536]{2,1,0:T(8,128)(2,1)}, u32[]{:S(2)}, u32[]{:S(2)}) async-start(bf16[16,40,1536]{2,1,0:T(8,128)(2,1)} %bitcast.36), calls=%async_computation.3 | async-start | bytes 3932160 | tf_op jit(solution)/shard_map/all_to_all | solution.py:646
  235.9 33.3 %copy-start = (f32[1536]{0:T(1024)S(1)}, f32[1536]{0:T(1024)}, u32[]{:S(2)}) copy-start(f32[1536]{0:T(1024)} %param.17) | copy-start | bytes 18436
  235.9 33.3 %copy-start.4 = (s32[16]{0:T(128)S(1)}, s32[16]{0:T(128)}, u32[]{:S(2)}) copy-start(s32[16]{0:T(128)} %param.18) | copy-start | bytes 196
  274.4 5.3 %copy-start.1 = (f32[16]{0:T(128)S(1)}, f32[16]{0:T(128)}, u32[]{:S(2)}) copy-start(f32[16]{0:T(128)} %get-tuple-element.38) | copy-start | bytes 196
  274.4 17.3 %copy-start.3 = (s32[16]{0:T(128)S(1)}, s32[16]{0:T(128)}, u32[]{:S(2)}) copy-start(s32[16]{0:T(128)} %lengths_ref.5) | copy-start | bytes 196
Sparse Core Ops, SparseCore 0:
  10.4 95.0 all-gather.4
  128.0 46.1 all-gather.6
  214.8 52.6 all-gather.8

commit v21 on v17

--- a/solution.py
+++ b/solution.py
@@ -766,14 +766,14 @@
         * final_gain
     ).astype(jnp.bfloat16)
     logits = lax.dot_general(
-        final, unembed, (((1,), (1,)), ((), ())), preferred_element_type=jnp.float32
+        unembed, final, (((1,), (1,)), ((), ())), preferred_element_type=jnp.float32
     )
     vocab_base = blk * unembed.shape[0]
     target_hit = (
-        target_ids[:, None] == vocab_base + jnp.arange(unembed.shape[0], dtype=jnp.int32)[None, :]
-    )
-    target_part = jnp.sum(jnp.where(target_hit, logits, 0.0), axis=1)
-    top_part = jnp.max(logits, axis=1)
+        target_ids[None, :] == vocab_base + jnp.arange(unembed.shape[0], dtype=jnp.int32)[:, None]
+    )
+    target_part = jnp.sum(jnp.where(target_hit, logits, 0.0), axis=0)
+    top_part = jnp.max(logits, axis=0)
 
     out_rows, square = pl.pallas_call(
         combine_kernel,

time: 299 us -> 299 us (level)
  no operation moved by 1% of the time
where the time goes in v21:
time: 299 us; the launch traced here: 298 us
  waiting for transfers between devices  156 us (52%)
  Pallas kernels  65.2 us (22%)
  starting transfers between devices  40.3 us (13%)
  between operations  13.9 us (5%)
  blocking collectives  12.3 us (4%)
  matrix products  5.19 us (2%)
  other arithmetic  3.17 us (1%)
    all_to_all x3, waiting for transfers between devices, moved(): own = lax.all_to_all(x, 'blk', split_axis=0, concat_axis=0, tiled=True)  67 us
    ppermute x2, waiting for transfers between devices, swapped(): return lax.ppermute(x, 'rep', [(0, 1), (1, 0)])  32.9 us
    all_gather x1, waiting for transfers between devices, paired(): lax.all_gather(last_part, 'blk', axis_index_groups=[list(RING)], axis=0)  31.6 us
    all_gather x1, waiting for transfers between devices, paired(): d_both = lax.all_gather(d_own, 'rep', axis=0)  24.7 us
    all_to_all x3, starting transfers between devices, moved(): own = lax.all_to_all(x, 'blk', split_axis=0, concat_axis=0, tiled=True)  22.8 us
    pallas_call x2, Pallas kernels, hidden_of(): pl.pallas_call(kernel, grid_spec=pltpu.PrefetchScalarGridSpec(num_scalar_...  21.7 us
    all_to_all x2, starting transfers between devices, returned(): x = lax.all_to_all(x, 'blk', split_axis=0, concat_axis=0, tiled=True)  14.2 us
    all_to_all x1, blocking collectives, everywhere(): lax.all_to_all(copies, 'blk', split_axis=0, concat_axis=0, tiled=True)  12.3 us
  transfers between devices with their start and end apart: 10, of which 7 were waited for; matrix products, arithmetic and copies ran while one was open for 3% of the time, Pallas kernels for 19%

profile of v21, /device:TPU:0, one launch (start us, length us, event | category | flops | bytes accessed | tf_op | source)
XLA Modules:
  0.0 298.2 jit_solution(17547406880831273156)
XLA Ops:
  7.2 0.0 all-gather.6.cloned.1.call-start
  7.2 3.0 %prep.1 = (bf16[128,1664]{1,0:T(8,128)(2,1)}, bf16[384,128]{1,0:T(8,128)(2,1)}) custom-call(s32[16]{0:T(128)} %lengths_ref.5, s32[1]{0:T(128)} %bitcast.3.blk_ref, bf16[128,1536]{1,0:T(8,128)(2,1)} %bitcast.44, s32[8,128]{1,0:T(8,128)} %bitcast.51, f32[8,128]{1,0:T(8,128)} %bitcast.52, f32[1536]{0:T(1024)} %gain_ref.1), custom_call_target="tpu_custom_call" | custom-call | tf_op jit(solution)/shard_map/prep/pallas_call | solution.py:588
  10.2 0.0 all-gather.6.cloned.1.call-update
  10.2 3.3 %cast.3 = bf16[16,96,512]{2,1,0:T(8,128)(2,1)} custom-call(f32[4608,512]{1,0:T(8,128)} %bitcast.37, bf16[128,1664]{1,0:T(8,128)(2,1)} %get-tuple-element.20.rank_ref.refs_0_), custom_call_target="tpu_custom_call" | custom-call | tf_op jit(solution)/shard_map/cast/pallas_call | solution.py:556
  13.5 7.4 %all-to-all-start = ((bf16[16,96,512]{2,1,0:T(8,128)(2,1)}), bf16[16,96,512]{2,1,0:T(8,128)(2,1)}, u32[]{:S(2)}, u32[]{:S(2)}) async-start(bf16[16,96,512]{2,1,0:T(8,128)(2,1)} %cast.3), calls=%async_computation | async-start | bytes 3145728 | tf_op jit(solution)/shard_map/all_to_all | solution.py:572
  21.0 3.3 %cast.4 = bf16[16,96,512]{2,1,0:T(8,128)(2,1)} custom-call(f32[4608,512]{1,0:T(8,128)} %bitcast.38), custom_call_target="tpu_custom_call" | custom-call | tf_op jit(solution)/shard_map/cast/pallas_call | solution.py:556
  24.2 48.8 %all-to-all-done = bf16[16,96,512]{2,1,0:T(8,128)(2,1)} async-done(((bf16[16,96,512]{2,1,0:T(8,128)(2,1)}), bf16[16,96,512]{2,1,0:T(8,128)(2,1)}, u32[]{:S(2)}, u32[]{:S(2)}) %all-to-all-start) | async-done | bytes 1572896 | tf_op jit(solution)/shard_map/all_to_all | solution.py:572
  73.0 6.1 %all-to-all-start.1 = ((bf16[16,96,512]{2,1,0:T(8,128)(2,1)}), bf16[16,96,512]{2,1,0:T(8,128)(2,1)}, u32[]{:S(2)}, u32[]{:S(2)}) async-start(bf16[16,96,512]{2,1,0:T(8,128)(2,1)} %cast.4), calls=%async_computation.1 | async-start | bytes 3145728 | tf_op jit(solution)/shard_map/all_to_all | solution.py:572
  79.2 1.6 collective-permute-start
  80.7 3.2 %cast.5.__0_ = bf16[16,96,512]{2,1,0:T(8,128)(2,1)} custom-call(f32[4608,512]{1,0:T(8,128)} %bitcast.39), custom_call_target="tpu_custom_call" | custom-call | tf_op jit(solution)/shard_map/cast/pallas_call | solution.py:556
  84.0 32.2 %collective-permute-done.__1_.g_ref.g_oth = bf16[1536,512]{1,0:T(8,128)(2,1)} collective-permute-done((bf16[1536,512]{1,0:T(8,128)(2,1)}, bf16[1536,512]{1,0:T(8,128)(2,1)}, u32[]{:S(2)}, u32[]{:S(2)}) %collective-permute-start) | collective-permute-done | bytes 1572896 | tf_op jit(solution)/shard_map/ppermute | solution.py:576
  116.2 0.0 copy-start.2
  116.2 0.3 all-to-all-done.1
  116.4 9.2 %all-to-all-start.2 = ((bf16[16,96,512]{2,1,0:T(8,128)(2,1)}), bf16[16,96,512]{2,1,0:T(8,128)(2,1)}, u32[]{:S(2)}, u32[]{:S(2)}) async-start(bf16[16,96,512]{2,1,0:T(8,128)(2,1)} %tie.3), calls=%async_computation.2 | async-start | bytes 3145728 | tf_op jit(solution)/shard_map/all_to_all | solution.py:572
  125.6 0.0 all-gather.8.cloned.1.call-start
  125.7 1.5 collective-permute-start.1
  127.2 0.0 copy-done.2
  127.2 0.6 dynamic_slice.3
  127.9 1.2 stack.36.info
  129.1 0.0 all-gather.6.cloned.1.call-done.x_ref
  129.1 10.6 %gate_up.2 = (bf16[640,512]{1,0:T(8,128)(2,1)}, bf16[640,128]{1,0:T(8,128)(2,1)}, f32[16,128]{1,0:T(8,128)}) custom-call(s32[5]{0:T(128)} %stack.36.info, s32[16]{0:T(128)} %lengths_ref.5, s32[16]{0:T(128)} %constant.33.clone.ring_ref, bf16[2048,1664]{1,0:T(8,128)(2,1)} %all-gather.6.cloned.1.call-done.x_ref, bf16[1536,512]{1,0:T(8,128)(2,1)} %bitcast.10.g_ref.g_own, ...), custom_call_target="tpu_custom_call" | custom-call | tf_op jit(solution)/shard_map/gate_up/pallas_call | solution.py:619
  139.7 17.9 %all-to-all-done.2 = bf16[16,96,512]{2,1,0:T(8,128)(2,1)} async-done(((bf16[16,96,512]{2,1,0:T(8,128)(2,1)}), bf16[16,96,512]{2,1,0:T(8,128)(2,1)}, u32[]{:S(2)}, u32[]{:S(2)}) %all-to-all-start.2) | async-done | bytes 1572896 | tf_op jit(solution)/shard_map/all_to_all | solution.py:572
  157.7 0.0 all-gather.8.cloned.1.call-update
  157.7 4.3 %own_down.1 = (bf16[512,1536]{1,0:T(8,128)(2,1)}, bf16[128,1536]{1,0:T(8,128)(2,1)}, f32[16,1536]{1,0:T(8,128)}) custom-call(bf16[640,512]{1,0:T(8,128)(2,1)} %get-tuple-element.23.__1_.hidden_any, f32[16,128]{1,0:T(8,128)} %get-tuple-element.24.share_any, bf16[1536,512]{1,0:T(8,128)(2,1)} %tie.4.d_any), custom_call_target="tpu_custom_call" | custom-call | tf_op jit(solution)/shard_map/own_down/pallas_call | solution.py:664
  162.0 0.7 collective-permute-done.1.__1_.u_ref.u_oth
  162.7 8.5 %all-to-all-start.4 = ((bf16[16,32,1536]{2,1,0:T(8,128)(2,1)}), bf16[16,32,1536]{2,1,0:T(8,128)(2,1)}, u32[]{:S(2)}, u32[]{:S(2)}) async-start(bf16[16,32,1536]{2,1,0:T(8,128)(2,1)} %bitcast.40), calls=%async_computation.4 | async-start | bytes 3145728 | tf_op jit(solution)/shard_map/all_to_all | solution.py:645
  171.2 0.2 all-gather.10.cloned.1.call-start
  171.4 11.1 %gate_up.3 = (bf16[656,512]{1,0:T(8,128)(2,1)}, f32[16,128]{1,0:T(8,128)}, f32[16,1536]{1,0:T(8,128)}) custom-call(s32[5]{0:T(128)} %stack.36.info, s32[16]{0:T(128)} %lengths_ref.5, s32[16]{0:T(128)} %constant.33.clone.ring_ref, bf16[2048,1664]{1,0:T(8,128)(2,1)} %all-gather.6.cloned.1.call-done.x_ref, ...), custom_call_target="tpu_custom_call" | custom-call | tf_op jit(solution)/shard_map/gate_up/pallas_call | solution.py:619
  182.5 24.7 %all-gather.8.cloned.1.call-done = bf16[3072,512]{1,0:T(8,128)(2,1)} async-done(((bf16[1536,512]{1,0:T(8,128)(2,1)}), bf16[3072,512]{1,0:T(8,128)(2,1)}) %all-gather.8.cloned.1.call-update) | async-done | bytes 3145744 | tf_op jit(solution)/shard_map/all_gather | solution.py:663
  207.2 6.3 %oth_down.1 = (bf16[640,1536]{1,0:T(8,128)(2,1)}, f32[16,1536]{1,0:T(8,128)}) custom-call(s32[5]{0:T(128)} %stack.36.info, bf16[656,512]{1,0:T(8,128)(2,1)} %get-tuple-element.26.hidden_any, f32[16,128]{1,0:T(8,128)} %get-tuple-element.27.share_any, bf16[640,128]{1,0:T(8,128)(2,1)} %get-tuple-element.28.spot_any, ...), custom_call_target="tpu_custom_call" | custom-call | tf_op jit(solution)/shard_map/oth_down/pallas_call | solution.py:689
  213.4 0.0 all-gather.10.cloned.1.call-update
  213.5 0.0 all-to-all-done.4
  213.5 5.7 %all-to-all-start.3 = ((bf16[16,40,1536]{2,1,0:T(8,128)(2,1)}), bf16[16,40,1536]{2,1,0:T(8,128)(2,1)}, u32[]{:S(2)}, u32[]{:S(2)}) async-start(bf16[16,40,1536]{2,1,0:T(8,128)(2,1)} %bitcast.43), calls=%async_computation.3 | async-start | bytes 3932160 | tf_op jit(solution)/shard_map/all_to_all | solution.py:645
  219.2 3.0 %mix.1 = (bf16[384,512]{1,0:T(8,128)(2,1)}, bf16[384,640]{1,0:T(8,128)(2,1)}) custom-call(s32[5]{0:T(128)} %stack.36.info, bf16[128,1664]{1,0:T(8,128)(2,1)} %get-tuple-element.20.rank_ref.refs_0_, bf16[384,128]{1,0:T(8,128)(2,1)} %get-tuple-element.21.pieces_ref), custom_call_target="tpu_custom_call" | custom-call | tf_op jit(solution)/shard_map/mix/pallas_call | solution.py:730
  222.2 4.0 %first.1.base_any = f32[128,1536]{1,0:T(8,128)} custom-call(bf16[384,512]{1,0:T(8,128)(2,1)} %get-tuple-element.33.mix_ref, bf16[512,1536]{1,0:T(8,128)(2,1)} %bitcast.17.back_ref, bf16[128,1536]{1,0:T(8,128)(2,1)} %bitcast.46), custom_call_target="tpu_custom_call" | custom-call | tf_op jit(solution)/shard_map/first/pallas_call | solution.py:753
  226.3 8.3 %place.1._ = bf16[3,1536,1024]{2,1,0:T(8,128)(2,1)} custom-call(s32[5]{0:T(128)} %stack.36.info, bf16[1536,512]{1,0:T(8,128)(2,1)} %bitcast.10.g_ref.g_own, bf16[1536,512]{1,0:T(8,128)(2,1)} %collective-permute-done.__1_.g_ref.g_oth, bf16[1536,512]{1,0:T(8,128)(2,1)} %bitcast.11.u_ref.u_own, bf16[1536,512]{1,0:T(8,128)(2,1)} %collective-permute-done.1.__1_.u_ref.u_oth, ...), custom_call_target="tpu_custom_call" | custom-call | tf_op jit(solution)/shard_map/place/pallas_call | solution.py:716
  234.5 0.0 copy-start
  234.5 31.6 %all-gather.10.cloned.1.call-done = f32[256,1536]{1,0:T(8,128)} async-done(((f32[16,1536]{1,0:T(8,128)}), f32[256,1536]{1,0:T(8,128)}) %all-gather.10.cloned.1.call-update) | async-done | bytes 1572880 | tf_op jit(solution)/shard_map/all_gather | solution.py:713
  266.1 1.5 reduce_sum.36
  267.6 0.1 multiply_reduce_fusion
  267.7 0.0 copy-done
  267.7 0.0 copy-start.4
  267.7 5.2 %fusion.4 = (f32[16]{0:T(128)}, f32[16,2048]{1,0:T(8,128)S(1)}) fusion(bf16[2048,1536]{1,0:T(8,128)(2,1)} %param.16, f32[16,1536]{1,0:T(8,128)S(1)} %reduce_sum.36, f32[1536]{0:T(1024)S(1)} %copy-done, f32[16]{0:T(128)S(1)} %add_rsqrt_fusion), kind=kOutput, calls=%fused_computation.15 | convolution fusion | flops 100794352 | bytes 6527104 | tf_op jit(solution)/shard_map/dot_general | solution.py:768
  272.9 0.0 copy-done.4
  272.9 0.2 fusion
  273.1 0.0 all-to-all-done.3
  273.1 0.0 copy-start.1
  273.1 0.0 copy-start.3
  273.2 4.8 %combine.1 = (bf16[128,1536]{1,0:T(8,128)(2,1)}, f32[1,128]{1,0:T(1,128)}) custom-call(s32[5]{0:T(128)} %stack.36.info, bf16[384,640]{1,0:T(8,128)(2,1)} %get-tuple-element.22.mix_any, bf16[640,1536]{1,0:T(8,128)(2,1)} %bitcast.15.back_any, f32[128,1536]{1,0:T(8,128)} %first.1.base_any, bf16[3,1536,1024]{2,1,0:T(8,128)(2,1)} %place.1._, f32[1,16]{1,0:T(1,128)} %bitcast.49), custom_call_target="tpu_custom_call" | custom-call | tf_op jit(solution)/shard_map/combine/pallas_call | solution.py:778
  277.9 0.7 compare_select_fusion
  278.6 0.0 copy-done.1
  278.6 12.3 %all_to_all.30 = f32[16,3,16]{2,1,0:T(4,128)S(1)} all-to-all(f32[16,3,16]{2,1,0:T(4,128)S(1)} %broadcast_in_dim.29), channel_id=1, replica_groups=mesh['blk'=16,'rep'=2] {'blk'}, dimensions={0} | all-to-all | bytes 6144 | tf_op jit(solution)/shard_map/all_to_all | solution.py:798
  291.0 0.0 copy-done.3
  291.1 0.6 pad_maximum_fusion.1
  (12 shorter events, 0.1 us)
Async XLA Ops:
  7.2 121.9 %all-gather.6.cloned.1.call-start = ((), (), s32[]{:S(2)}) async-start(), calls=%async_computation.6 | async-start | bytes 7241728 | tf_op jit(solution)/shard_map/all_gather | solution.py:614
  13.5 59.5 %all-to-all-start = ((bf16[16,96,512]{2,1,0:T(8,128)(2,1)}), bf16[16,96,512]{2,1,0:T(8,128)(2,1)}, u32[]{:S(2)}, u32[]{:S(2)}) async-start(bf16[16,96,512]{2,1,0:T(8,128)(2,1)} %cast.3), calls=%async_computation | async-start | bytes 3145728 | tf_op jit(solution)/shard_map/all_to_all | solution.py:572
  73.0 43.4 %all-to-all-start.1 = ((bf16[16,96,512]{2,1,0:T(8,128)(2,1)}), bf16[16,96,512]{2,1,0:T(8,128)(2,1)}, u32[]{:S(2)}, u32[]{:S(2)}) async-start(bf16[16,96,512]{2,1,0:T(8,128)(2,1)} %cast.4), calls=%async_computation.1 | async-start | bytes 3145728 | tf_op jit(solution)/shard_map/all_to_all | solution.py:572
  79.2 37.0 %collective-permute-start = (bf16[1536,512]{1,0:T(8,128)(2,1)}, bf16[1536,512]{1,0:T(8,128)(2,1)}, u32[]{:S(2)}, u32[]{:S(2)}) collective-permute-start(bf16[1536,512]{1,0:T(8,128)(2,1)} %bitcast.10.g_ref.g_own), channel_id=1, source_target_pairs={{0,1},{1,0},{2,3},{3,2},{4,5},{5,4},{6,7},{7,6},{8,9},{9,8},{10,11... | collective-permute-start | bytes 4718600 | tf_op jit(solution)/shard_map/ppermute | solution.py:576
  116.2 11.1 %copy-start.2 = (s32[16]{0:T(128)S(1)}, s32[16]{0:T(128)}, u32[]{:S(2)}) copy-start(s32[16]{0:T(128)} %lengths_ref.5) | copy-start | bytes 196
  116.4 41.2 %all-to-all-start.2 = ((bf16[16,96,512]{2,1,0:T(8,128)(2,1)}), bf16[16,96,512]{2,1,0:T(8,128)(2,1)}, u32[]{:S(2)}, u32[]{:S(2)}) async-start(bf16[16,96,512]{2,1,0:T(8,128)(2,1)} %tie.3), calls=%async_computation.2 | async-start | bytes 3145728 | tf_op jit(solution)/shard_map/all_to_all | solution.py:572
  125.6 81.5 %all-gather.8.cloned.1.call-start = ((), (), s32[]{:S(2)}) async-start(), calls=%async_computation.7 | async-start | bytes 4718592 | tf_op jit(solution)/shard_map/all_gather | solution.py:663
  125.7 37.0 %collective-permute-start.1 = (bf16[1536,512]{1,0:T(8,128)(2,1)}, bf16[1536,512]{1,0:T(8,128)(2,1)}, u32[]{:S(2)}, u32[]{:S(2)}) collective-permute-start(bf16[1536,512]{1,0:T(8,128)(2,1)} %bitcast.11.u_ref.u_own), channel_id=1, source_target_pairs={{0,1},{1,0},{2,3},{3,2},{4,5},{5,4},{6,7},{7,6},{8,9},{9,8},{10,11... | collective-permute-start | bytes 4718600 | tf_op jit(solution)/shard_map/ppermute | solution.py:576
  162.7 50.8 %all-to-all-start.4 = ((bf16[16,32,1536]{2,1,0:T(8,128)(2,1)}), bf16[16,32,1536]{2,1,0:T(8,128)(2,1)}, u32[]{:S(2)}, u32[]{:S(2)}) async-start(bf16[16,32,1536]{2,1,0:T(8,128)(2,1)} %bitcast.40), calls=%async_computation.4 | async-start | bytes 3145728 | tf_op jit(solution)/shard_map/all_to_all | solution.py:645
  171.2 94.9 %all-gather.10.cloned.1.call-start = ((), (), s32[]{:S(2)}) async-start(), calls=%async_computation.8 | async-start | bytes 1671168 | tf_op jit(solution)/shard_map/all_gather | solution.py:713
  213.5 59.6 %all-to-all-start.3 = ((bf16[16,40,1536]{2,1,0:T(8,128)(2,1)}), bf16[16,40,1536]{2,1,0:T(8,128)(2,1)}, u32[]{:S(2)}, u32[]{:S(2)}) async-start(bf16[16,40,1536]{2,1,0:T(8,128)(2,1)} %bitcast.43), calls=%async_computation.3 | async-start | bytes 3932160 | tf_op jit(solution)/shard_map/all_to_all | solution.py:645
  234.5 33.2 %copy-start = (f32[1536]{0:T(1024)S(1)}, f32[1536]{0:T(1024)}, u32[]{:S(2)}) copy-start(f32[1536]{0:T(1024)} %param.17) | copy-start | bytes 18436
  267.7 5.2 %copy-start.4 = (s32[16]{0:T(128)S(1)}, s32[16]{0:T(128)}, u32[]{:S(2)}) copy-start(s32[16]{0:T(128)} %param.18) | copy-start | bytes 196
  273.1 5.5 %copy-start.1 = (f32[16]{0:T(128)S(1)}, f32[16]{0:T(128)}, u32[]{:S(2)}) copy-start(f32[16]{0:T(128)} %get-tuple-element.37) | copy-start | bytes 196
  273.1 17.9 %copy-start.3 = (s32[16]{0:T(128)S(1)}, s32[16]{0:T(128)}, u32[]{:S(2)}) copy-start(s32[16]{0:T(128)} %lengths_ref.5) | copy-start | bytes 196
Sparse Core Ops, SparseCore 0:
  10.4 95.0 all-gather.5
  157.8 49.3 all-gather.7
  213.6 52.4 all-gather.9

commit v22 on v17

--- a/solution.py
+++ b/solution.py
@@ -460,7 +460,7 @@
 
 
 def combine_kernel(
-    info, mix_any, back_any, base_any, _, __, out_ref, square_ref, mix, back, base, sems
+    info, mix_any, back_any, base_any, _, out_ref, square_ref, mix, back, base, sems
 ):
     chunks, size = back.shape[:2]
     rows = base.shape[0]
@@ -780,7 +780,7 @@
         grid_spec=pltpu.PrefetchScalarGridSpec(
             num_scalar_prefetch=1,
             grid=(1,),
-            in_specs=[anywhere] * 5,
+            in_specs=[anywhere] * 4,
             out_specs=[whole((rows, width)), whole((1, LANES))],
             scratch_shapes=[
                 pltpu.VMEM((3 * rows, second), jnp.bfloat16),
@@ -792,7 +792,7 @@
         out_shape=[bf16(rows, width), f32(1, LANES)],
         compiler_params=params(),
         name="combine",
-    )(info, second_mix, oth_back, base, server, top_part[None])
+    )(info, second_mix, oth_back, base, server)
 
     def everywhere(copies):
         return lax.all_to_all(copies, "blk", split_axis=0, concat_axis=0, tiled=True)

time: 299 us -> 298 us (level)
  no operation moved by 1% of the time
where the time goes in v22:
time: 298 us; the launch traced here: 297 us
  waiting for transfers between devices  156 us (52%)
  Pallas kernels  65.1 us (22%)
  starting transfers between devices  40.3 us (14%)
  between operations  13.9 us (5%)
  blocking collectives  12.4 us (4%)
  matrix products  4.63 us (2%)
    all_to_all x3, waiting for transfers between devices, moved(): own = lax.all_to_all(x, 'blk', split_axis=0, concat_axis=0, tiled=True)  67.1 us
    ppermute x2, waiting for transfers between devices, swapped(): return lax.ppermute(x, 'rep', [(0, 1), (1, 0)])  32.9 us
    all_gather x1, waiting for transfers between devices, paired(): lax.all_gather(last_part, 'blk', axis_index_groups=[list(RING)], axis=0)  31.6 us
    all_gather x1, waiting for transfers between devices, paired(): d_both = lax.all_gather(d_own, 'rep', axis=0)  24.7 us
    all_to_all x3, starting transfers between devices, moved(): own = lax.all_to_all(x, 'blk', split_axis=0, concat_axis=0, tiled=True)  22.8 us
    pallas_call x2, Pallas kernels, hidden_of(): pl.pallas_call(kernel, grid_spec=pltpu.PrefetchScalarGridSpec(num_scalar_...  21.7 us
    all_to_all x2, starting transfers between devices, returned(): x = lax.all_to_all(x, 'blk', split_axis=0, concat_axis=0, tiled=True)  14.1 us
    all_to_all x1, blocking collectives, everywhere(): lax.all_to_all(copies, 'blk', split_axis=0, concat_axis=0, tiled=True)  12.4 us
  transfers between devices with their start and end apart: 10, of which 7 were waited for; matrix products, arithmetic and copies ran while one was open for 3% of the time, Pallas kernels for 19%

profile of v22, /device:TPU:0, one launch (start us, length us, event | category | flops | bytes accessed | tf_op | source)
XLA Modules:
  0.0 297.4 jit_solution(4025579605666274243)
XLA Ops:
  7.2 0.0 all-gather.6.cloned.1.call-start
  7.2 3.0 %prep.1 = (bf16[128,1664]{1,0:T(8,128)(2,1)}, bf16[384,128]{1,0:T(8,128)(2,1)}) custom-call(s32[16]{0:T(128)} %lengths_ref.5, s32[1]{0:T(128)} %bitcast.3.blk_ref, bf16[128,1536]{1,0:T(8,128)(2,1)} %bitcast.40, s32[8,128]{1,0:T(8,128)} %bitcast.45, f32[8,128]{1,0:T(8,128)} %bitcast.46, f32[1536]{0:T(1024)} %gain_ref.1), custom_call_target="tpu_custom_call" | custom-call | tf_op jit(solution)/shard_map/prep/pallas_call | solution.py:588
  10.2 0.0 all-gather.6.cloned.1.call-update
  10.3 3.2 %cast.3 = bf16[16,96,512]{2,1,0:T(8,128)(2,1)} custom-call(f32[4608,512]{1,0:T(8,128)} %bitcast.33, bf16[128,1664]{1,0:T(8,128)(2,1)} %get-tuple-element.20.rank_ref.refs_0_), custom_call_target="tpu_custom_call" | custom-call | tf_op jit(solution)/shard_map/cast/pallas_call | solution.py:556
  13.5 7.5 %all-to-all-start = ((bf16[16,96,512]{2,1,0:T(8,128)(2,1)}), bf16[16,96,512]{2,1,0:T(8,128)(2,1)}, u32[]{:S(2)}, u32[]{:S(2)}) async-start(bf16[16,96,512]{2,1,0:T(8,128)(2,1)} %cast.3), calls=%async_computation | async-start | bytes 3145728 | tf_op jit(solution)/shard_map/all_to_all | solution.py:572
  21.0 3.3 %cast.4 = bf16[16,96,512]{2,1,0:T(8,128)(2,1)} custom-call(f32[4608,512]{1,0:T(8,128)} %bitcast.34), custom_call_target="tpu_custom_call" | custom-call | tf_op jit(solution)/shard_map/cast/pallas_call | solution.py:556
  24.2 48.8 %all-to-all-done = bf16[16,96,512]{2,1,0:T(8,128)(2,1)} async-done(((bf16[16,96,512]{2,1,0:T(8,128)(2,1)}), bf16[16,96,512]{2,1,0:T(8,128)(2,1)}, u32[]{:S(2)}, u32[]{:S(2)}) %all-to-all-start) | async-done | bytes 1572896 | tf_op jit(solution)/shard_map/all_to_all | solution.py:572
  73.0 6.1 %all-to-all-start.1 = ((bf16[16,96,512]{2,1,0:T(8,128)(2,1)}), bf16[16,96,512]{2,1,0:T(8,128)(2,1)}, u32[]{:S(2)}, u32[]{:S(2)}) async-start(bf16[16,96,512]{2,1,0:T(8,128)(2,1)} %cast.4), calls=%async_computation.1 | async-start | bytes 3145728 | tf_op jit(solution)/shard_map/all_to_all | solution.py:572
  79.2 1.5 collective-permute-start
  80.7 3.2 %cast.5.__0_ = bf16[16,96,512]{2,1,0:T(8,128)(2,1)} custom-call(f32[4608,512]{1,0:T(8,128)} %bitcast.35), custom_call_target="tpu_custom_call" | custom-call | tf_op jit(solution)/shard_map/cast/pallas_call | solution.py:556
  84.0 32.2 %collective-permute-done.__1_.g_ref.g_oth = bf16[1536,512]{1,0:T(8,128)(2,1)} collective-permute-done((bf16[1536,512]{1,0:T(8,128)(2,1)}, bf16[1536,512]{1,0:T(8,128)(2,1)}, u32[]{:S(2)}, u32[]{:S(2)}) %collective-permute-start) | collective-permute-done | bytes 1572896 | tf_op jit(solution)/shard_map/ppermute | solution.py:576
  116.2 0.0 copy-start.1
  116.2 0.3 all-to-all-done.1
  116.5 9.2 %all-to-all-start.2 = ((bf16[16,96,512]{2,1,0:T(8,128)(2,1)}), bf16[16,96,512]{2,1,0:T(8,128)(2,1)}, u32[]{:S(2)}, u32[]{:S(2)}) async-start(bf16[16,96,512]{2,1,0:T(8,128)(2,1)} %tie.3), calls=%async_computation.2 | async-start | bytes 3145728 | tf_op jit(solution)/shard_map/all_to_all | solution.py:572
  125.7 0.0 all-gather.8.cloned.1.call-start
  125.7 1.5 collective-permute-start.1
  127.3 0.0 copy-done.1
  127.3 0.6 dynamic_slice.3
  127.8 1.2 stack.38.info
  129.1 0.0 all-gather.6.cloned.1.call-done.x_ref
  129.1 10.6 %gate_up.2 = (bf16[640,512]{1,0:T(8,128)(2,1)}, bf16[640,128]{1,0:T(8,128)(2,1)}, f32[16,128]{1,0:T(8,128)}) custom-call(s32[5]{0:T(128)} %stack.38.info, s32[16]{0:T(128)} %lengths_ref.5, s32[16]{0:T(128)} %constant.33.clone.ring_ref, bf16[2048,1664]{1,0:T(8,128)(2,1)} %all-gather.6.cloned.1.call-done.x_ref, bf16[1536,512]{1,0:T(8,128)(2,1)} %bitcast.10.g_ref.g_own, ...), custom_call_target="tpu_custom_call" | custom-call | tf_op jit(solution)/shard_map/gate_up/pallas_call | solution.py:619
  139.7 18.0 %all-to-all-done.2 = bf16[16,96,512]{2,1,0:T(8,128)(2,1)} async-done(((bf16[16,96,512]{2,1,0:T(8,128)(2,1)}), bf16[16,96,512]{2,1,0:T(8,128)(2,1)}, u32[]{:S(2)}, u32[]{:S(2)}) %all-to-all-start.2) | async-done | bytes 1572896 | tf_op jit(solution)/shard_map/all_to_all | solution.py:572
  157.7 0.0 all-gather.8.cloned.1.call-update
  157.7 4.3 %own_down.1 = (bf16[512,1536]{1,0:T(8,128)(2,1)}, bf16[128,1536]{1,0:T(8,128)(2,1)}, f32[16,1536]{1,0:T(8,128)}) custom-call(bf16[640,512]{1,0:T(8,128)(2,1)} %get-tuple-element.23.__1_.hidden_any, f32[16,128]{1,0:T(8,128)} %get-tuple-element.24.share_any, bf16[1536,512]{1,0:T(8,128)(2,1)} %tie.4.d_any), custom_call_target="tpu_custom_call" | custom-call | tf_op jit(solution)/shard_map/own_down/pallas_call | solution.py:664
  162.0 0.7 collective-permute-done.1.__1_.u_ref.u_oth
  162.7 8.5 %all-to-all-start.4 = ((bf16[16,32,1536]{2,1,0:T(8,128)(2,1)}), bf16[16,32,1536]{2,1,0:T(8,128)(2,1)}, u32[]{:S(2)}, u32[]{:S(2)}) async-start(bf16[16,32,1536]{2,1,0:T(8,128)(2,1)} %bitcast.36), calls=%async_computation.4 | async-start | bytes 3145728 | tf_op jit(solution)/shard_map/all_to_all | solution.py:645
  171.2 0.2 all-gather.10.cloned.1.call-start
  171.4 11.1 %gate_up.3 = (bf16[656,512]{1,0:T(8,128)(2,1)}, f32[16,128]{1,0:T(8,128)}, f32[16,1536]{1,0:T(8,128)}) custom-call(s32[5]{0:T(128)} %stack.38.info, s32[16]{0:T(128)} %lengths_ref.5, s32[16]{0:T(128)} %constant.33.clone.ring_ref, bf16[2048,1664]{1,0:T(8,128)(2,1)} %all-gather.6.cloned.1.call-done.x_ref, ...), custom_call_target="tpu_custom_call" | custom-call | tf_op jit(solution)/shard_map/gate_up/pallas_call | solution.py:619
  182.5 24.7 %all-gather.8.cloned.1.call-done = bf16[3072,512]{1,0:T(8,128)(2,1)} async-done(((bf16[1536,512]{1,0:T(8,128)(2,1)}), bf16[3072,512]{1,0:T(8,128)(2,1)}) %all-gather.8.cloned.1.call-update) | async-done | bytes 3145744 | tf_op jit(solution)/shard_map/all_gather | solution.py:663
  207.2 6.3 %oth_down.1 = (bf16[640,1536]{1,0:T(8,128)(2,1)}, f32[16,1536]{1,0:T(8,128)}) custom-call(s32[5]{0:T(128)} %stack.38.info, bf16[656,512]{1,0:T(8,128)(2,1)} %get-tuple-element.26.hidden_any, f32[16,128]{1,0:T(8,128)} %get-tuple-element.27.share_any, bf16[640,128]{1,0:T(8,128)(2,1)} %get-tuple-element.28.spot_any, ...), custom_call_target="tpu_custom_call" | custom-call | tf_op jit(solution)/shard_map/oth_down/pallas_call | solution.py:689
  213.5 0.0 all-gather.10.cloned.1.call-update
  213.6 0.0 all-to-all-done.4
  213.6 5.7 %all-to-all-start.3 = ((bf16[16,40,1536]{2,1,0:T(8,128)(2,1)}), bf16[16,40,1536]{2,1,0:T(8,128)(2,1)}, u32[]{:S(2)}, u32[]{:S(2)}) async-start(bf16[16,40,1536]{2,1,0:T(8,128)(2,1)} %bitcast.39), calls=%async_computation.3 | async-start | bytes 3932160 | tf_op jit(solution)/shard_map/all_to_all | solution.py:645
  219.3 3.0 %mix.1 = (bf16[384,512]{1,0:T(8,128)(2,1)}, bf16[384,640]{1,0:T(8,128)(2,1)}) custom-call(s32[5]{0:T(128)} %stack.38.info, bf16[128,1664]{1,0:T(8,128)(2,1)} %get-tuple-element.20.rank_ref.refs_0_, bf16[384,128]{1,0:T(8,128)(2,1)} %get-tuple-element.21.pieces_ref), custom_call_target="tpu_custom_call" | custom-call | tf_op jit(solution)/shard_map/mix/pallas_call | solution.py:730
  222.3 4.0 %first.1.base_any = f32[128,1536]{1,0:T(8,128)} custom-call(bf16[384,512]{1,0:T(8,128)(2,1)} %get-tuple-element.33.mix_ref, bf16[512,1536]{1,0:T(8,128)(2,1)} %bitcast.17.back_ref, bf16[128,1536]{1,0:T(8,128)(2,1)} %bitcast.42), custom_call_target="tpu_custom_call" | custom-call | tf_op jit(solution)/shard_map/first/pallas_call | solution.py:753
  226.3 8.3 %place.1._ = bf16[3,1536,1024]{2,1,0:T(8,128)(2,1)} custom-call(s32[5]{0:T(128)} %stack.38.info, bf16[1536,512]{1,0:T(8,128)(2,1)} %bitcast.10.g_ref.g_own, bf16[1536,512]{1,0:T(8,128)(2,1)} %collective-permute-done.__1_.g_ref.g_oth, bf16[1536,512]{1,0:T(8,128)(2,1)} %bitcast.11.u_ref.u_own, bf16[1536,512]{1,0:T(8,128)(2,1)} %collective-permute-done.1.__1_.u_ref.u_oth, ...), custom_call_target="tpu_custom_call" | custom-call | tf_op jit(solution)/shard_map/place/pallas_call | solution.py:716
  234.6 0.0 copy-start
  234.6 0.0 copy-start.3
  234.6 31.6 %all-gather.10.cloned.1.call-done = f32[256,1536]{1,0:T(8,128)} async-done(((f32[16,1536]{1,0:T(8,128)}), f32[256,1536]{1,0:T(8,128)}) %all-gather.10.cloned.1.call-update) | async-done | bytes 1572880 | tf_op jit(solution)/shard_map/all_gather | solution.py:713
  266.2 1.5 reduce_sum.36
  267.7 0.1 multiply_reduce_fusion
  267.8 0.0 copy-done
  267.8 0.0 copy-done.3
  267.8 4.6 %fusion.3 = (f32[16]{0:T(128)S(1)}, f32[16]{0:T(128)S(1)}) fusion(s32[2048]{0:T(1024)S(1)} %iota_add_fusion, s32[16]{0:T(128)S(1)} %copy-done.3, bf16[2048,1536]{1,0:T(8,128)(2,1)} %param.16, f32[16,1536]{1,0:T(8,128)S(1)} %reduce_sum.36, f32[1536]{0:T(1024)S(1)} %copy-done, f32[16]{0:T(128)S(1)} %add_rsqrt_fusion), kind=kOutput, calls=%fused_computation.14 | convolution fusion | flops 100892640 | bytes 6404352 | tf_op jit(solution)/shard_map/dot_general | solution.py:768
  272.4 0.0 all-to-all-done.3
  272.5 0.0 copy-start.2
  272.5 4.7 %combine.1 = (bf16[128,1536]{1,0:T(8,128)(2,1)}, f32[1,128]{1,0:T(1,128)}) custom-call(s32[5]{0:T(128)} %stack.38.info, bf16[384,640]{1,0:T(8,128)(2,1)} %get-tuple-element.22.mix_any, bf16[640,1536]{1,0:T(8,128)(2,1)} %bitcast.15.back_any, f32[128,1536]{1,0:T(8,128)} %first.1.base_any, bf16[3,1536,1024]{2,1,0:T(8,128)(2,1)} %place.1._), custom_call_target="tpu_custom_call" | custom-call | tf_op jit(solution)/shard_map/combine/pallas_call | solution.py:778
  277.2 0.6 compare_select_fusion
  277.8 12.4 %all_to_all.30 = f32[16,3,16]{2,1,0:T(4,128)S(1)} all-to-all(f32[16,3,16]{2,1,0:T(4,128)S(1)} %broadcast_in_dim.25), channel_id=1, replica_groups=mesh['blk'=16,'rep'=2] {'blk'}, dimensions={0} | all-to-all | bytes 6144 | tf_op jit(solution)/shard_map/all_to_all | solution.py:798
  290.2 0.0 copy-done.2
  290.3 0.6 pad_maximum_fusion.1
  (12 shorter events, 0.1 us)
Async XLA Ops:
  7.2 121.9 %all-gather.6.cloned.1.call-start = ((), (), s32[]{:S(2)}) async-start(), calls=%async_computation.6 | async-start | bytes 7241728 | tf_op jit(solution)/shard_map/all_gather | solution.py:614
  13.5 59.6 %all-to-all-start = ((bf16[16,96,512]{2,1,0:T(8,128)(2,1)}), bf16[16,96,512]{2,1,0:T(8,128)(2,1)}, u32[]{:S(2)}, u32[]{:S(2)}) async-start(bf16[16,96,512]{2,1,0:T(8,128)(2,1)} %cast.3), calls=%async_computation | async-start | bytes 3145728 | tf_op jit(solution)/shard_map/all_to_all | solution.py:572
  73.0 43.4 %all-to-all-start.1 = ((bf16[16,96,512]{2,1,0:T(8,128)(2,1)}), bf16[16,96,512]{2,1,0:T(8,128)(2,1)}, u32[]{:S(2)}, u32[]{:S(2)}) async-start(bf16[16,96,512]{2,1,0:T(8,128)(2,1)} %cast.4), calls=%async_computation.1 | async-start | bytes 3145728 | tf_op jit(solution)/shard_map/all_to_all | solution.py:572
  79.2 37.0 %collective-permute-start = (bf16[1536,512]{1,0:T(8,128)(2,1)}, bf16[1536,512]{1,0:T(8,128)(2,1)}, u32[]{:S(2)}, u32[]{:S(2)}) collective-permute-start(bf16[1536,512]{1,0:T(8,128)(2,1)} %bitcast.10.g_ref.g_own), channel_id=1, source_target_pairs={{0,1},{1,0},{2,3},{3,2},{4,5},{5,4},{6,7},{7,6},{8,9},{9,8},{10,11... | collective-permute-start | bytes 4718600 | tf_op jit(solution)/shard_map/ppermute | solution.py:576
  116.2 11.1 %copy-start.1 = (s32[16]{0:T(128)S(1)}, s32[16]{0:T(128)}, u32[]{:S(2)}) copy-start(s32[16]{0:T(128)} %lengths_ref.5) | copy-start | bytes 196
  116.5 41.2 %all-to-all-start.2 = ((bf16[16,96,512]{2,1,0:T(8,128)(2,1)}), bf16[16,96,512]{2,1,0:T(8,128)(2,1)}, u32[]{:S(2)}, u32[]{:S(2)}) async-start(bf16[16,96,512]{2,1,0:T(8,128)(2,1)} %tie.3), calls=%async_computation.2 | async-start | bytes 3145728 | tf_op jit(solution)/shard_map/all_to_all | solution.py:572
  125.7 81.5 %all-gather.8.cloned.1.call-start = ((), (), s32[]{:S(2)}) async-start(), calls=%async_computation.7 | async-start | bytes 4718592 | tf_op jit(solution)/shard_map/all_gather | solution.py:663
  125.7 37.0 %collective-permute-start.1 = (bf16[1536,512]{1,0:T(8,128)(2,1)}, bf16[1536,512]{1,0:T(8,128)(2,1)}, u32[]{:S(2)}, u32[]{:S(2)}) collective-permute-start(bf16[1536,512]{1,0:T(8,128)(2,1)} %bitcast.11.u_ref.u_own), channel_id=1, source_target_pairs={{0,1},{1,0},{2,3},{3,2},{4,5},{5,4},{6,7},{7,6},{8,9},{9,8},{10,11... | collective-permute-start | bytes 4718600 | tf_op jit(solution)/shard_map/ppermute | solution.py:576
  162.7 50.8 %all-to-all-start.4 = ((bf16[16,32,1536]{2,1,0:T(8,128)(2,1)}), bf16[16,32,1536]{2,1,0:T(8,128)(2,1)}, u32[]{:S(2)}, u32[]{:S(2)}) async-start(bf16[16,32,1536]{2,1,0:T(8,128)(2,1)} %bitcast.36), calls=%async_computation.4 | async-start | bytes 3145728 | tf_op jit(solution)/shard_map/all_to_all | solution.py:645
  171.2 95.0 %all-gather.10.cloned.1.call-start = ((), (), s32[]{:S(2)}) async-start(), calls=%async_computation.8 | async-start | bytes 1671168 | tf_op jit(solution)/shard_map/all_gather | solution.py:713
  213.6 58.9 %all-to-all-start.3 = ((bf16[16,40,1536]{2,1,0:T(8,128)(2,1)}), bf16[16,40,1536]{2,1,0:T(8,128)(2,1)}, u32[]{:S(2)}, u32[]{:S(2)}) async-start(bf16[16,40,1536]{2,1,0:T(8,128)(2,1)} %bitcast.39), calls=%async_computation.3 | async-start | bytes 3932160 | tf_op jit(solution)/shard_map/all_to_all | solution.py:645
  234.6 33.2 %copy-start = (f32[1536]{0:T(1024)S(1)}, f32[1536]{0:T(1024)}, u32[]{:S(2)}) copy-start(f32[1536]{0:T(1024)} %param.17) | copy-start | bytes 18436
  234.6 33.2 %copy-start.3 = (s32[16]{0:T(128)S(1)}, s32[16]{0:T(128)}, u32[]{:S(2)}) copy-start(s32[16]{0:T(128)} %param.18) | copy-start | bytes 196
  272.5 17.8 %copy-start.2 = (s32[16]{0:T(128)S(1)}, s32[16]{0:T(128)}, u32[]{:S(2)}) copy-start(s32[16]{0:T(128)} %lengths_ref.5) | copy-start | bytes 196
Sparse Core Ops, SparseCore 0:
  10.4 95.0 all-gather.5
  157.8 49.3 all-gather.7
  213.7 52.4 all-gather.9
